TPU v7x, 128 devices: a whole 4x4x4 slice. The times are simulated.
128 devices in a mesh: tm: 16 (over x_lo, y, core), tensor: 2 (over x_hi), section: 4 (over z).
Axes of the slice: x: 4 (x_hi: 2, x_lo: 2; x = x_hi * 2 + x_lo), y: 4, z: 4, core: 2. Of those that a mesh axis runs over, the one named last changes fastest.
Arguments:
- frames: bfloat16 [32768, 1280], P(('tm', 'section')), may hold values from -6 to 6
- returned: bfloat16 [32768, 1280], P('tm', 'section'), may hold values from -6 to 6
- norm_gain: float32 [1280], replicated, may hold values from 0.5 to 1.5
- weight_in: bfloat16 [2, 1280, 1280], P(None, None, 'tensor'), may hold values from -0.15625 to 0.15625
- kernel: float32 [31, 1280], P(None, 'tensor'), may hold values from -1.5 to 1.5
- weight_out: bfloat16 [1280, 1280], P('tensor'), may hold values from -0.15625 to 0.15625
- block_utt: int32 [256], replicated, may hold values from 0 to 63, as said below
- block_fill: int32 [256], replicated, may hold values from 1 to 128, as said below
Outputs:
- grad_frames: bfloat16 [32768, 1280], P(('tm', 'section'))
- grad_in: float32 [2, 1280, 1280], P(None, ('tm', 'section'), 'tensor')
- grad_out: float32 [1280, 1280], P('tensor', ('tm', 'section'))
- grad_kernel: float32 [31, 1280], P(None, 'tensor')
- grad_gain: float32 [1280], replicated
Inputs may be any that keep to these rules, and one draw needn't show every extreme that they name: `block_utt`: there are exactly 64 utterances. Utterance numbers start at 0 in the first block, never fall, and rise by at most one from a block to the next; every utterance begins at a block's first frame. `block_fill`: every block holds 128 valid frames except the last block of an utterance, whose valid frames come first and the rest is padding.
All inputs are finite; a program needn't handle non-finite values.
Results may differ from a plain program's by a relative error of at most 0.0065.
Values may be sent and summed in bfloat16 or wider, within the bound.
No kernel may reach another device: no remote copies, remote signals or barrier semaphores. Data moves between devices by JAX's collectives and lax.ppermute only.
A program may use at most 128 MiB of HBM per device.

v0:
```python
import jax
import jax.numpy as jnp
from jax import lax
from jax.sharding import PartitionSpec as P

BLOCK = 128


epsilon = 1e-05


def extended(shard, sides, width):
    for axis, dim in sides:
        peers, length = (lax.axis_size(axis), shard.shape[dim])
        up = [(i, (i + 1) % peers) for i in range(peers - 1)]
        down = [(j, i) for i, j in up]
        last = lax.slice_in_dim(shard, length - width, length, axis=dim)
        initial = lax.slice_in_dim(shard, 0, width, axis=dim)
        before = lax.ppermute(last, axis, up)
        after = lax.ppermute(initial, axis, down)
        shard = jnp.concatenate([before, shard, after], axis=dim)
    return shard


def body(frames, returned, norm_gain, weight_in, kernel, weight_out, block_utt, block_fill):
    frame_count = frames.shape[0]
    tap_count = kernel.shape[0]
    half_taps = tap_count // 2
    shard_index = lax.axis_index(("tm", "section"))
    total_frames = lax.axis_size(("tm", "section")) * frame_count
    first_frame = shard_index * frame_count
    ext_pos = first_frame - half_taps + jnp.arange(frame_count + 2 * half_taps, dtype=jnp.int32)
    inside = (ext_pos >= 0) & (ext_pos < total_frames)
    clipped = jnp.clip(ext_pos, 0, total_frames - 1) // BLOCK
    ext_utt = jnp.where(inside, jnp.take(block_utt, clipped), -1)
    frame_utt = ext_utt[half_taps : half_taps + frame_count]
    frame_pos = ext_pos[half_taps : half_taps + frame_count]
    frame_fill = jnp.take(block_fill, frame_pos // BLOCK)
    valid_frame = frame_pos % BLOCK < frame_fill
    valid_col = valid_frame.astype(jnp.float32)[:, None]
    arrived = lax.all_to_all(returned, "section", split_axis=0, concat_axis=1, tiled=True)
    grad_rows = jnp.where(valid_frame[:, None], arrived, jnp.zeros_like(arrived))
    as_float = frames.astype(jnp.float32)
    center = as_float - jnp.mean(as_float, axis=1, keepdims=True)
    inv_scale = lax.rsqrt(jnp.mean(center * center, axis=1, keepdims=True) + epsilon)
    unit_frames = center * inv_scale
    normed = (unit_frames * norm_gain).astype(jnp.bfloat16)
    value_proj = jnp.dot(normed, weight_in[0], preferred_element_type=jnp.float32)
    gate_proj = jnp.dot(normed, weight_in[1], preferred_element_type=jnp.float32)
    gate_sigmoid = jax.nn.sigmoid(gate_proj)
    gated_units = (valid_col * value_proj * gate_sigmoid).astype(jnp.bfloat16)
    units_ext = extended(gated_units, ((("tm", "section"), 0),), half_taps).astype(jnp.float32)
    conv_out = jnp.zeros(gated_units.shape, jnp.float32)
    for offset in range(tap_count):
        same_utt = (ext_utt[offset : offset + frame_count] == frame_utt)[:, None]
        conv_out = conv_out + kernel[offset] * jnp.where(
            same_utt, units_ext[offset : offset + frame_count], 0.0
        )
    conv_sigmoid = jax.nn.sigmoid(conv_out)
    activated = (conv_out * conv_sigmoid).astype(jnp.bfloat16)
    out_term = jnp.dot(activated.T, grad_rows, preferred_element_type=jnp.float32)
    grad_activated = jnp.dot(grad_rows, weight_out.T, preferred_element_type=jnp.float32)
    grad_conv = grad_activated * (conv_sigmoid + conv_out * conv_sigmoid * (1.0 - conv_sigmoid))
    conv_ext = extended(grad_conv, ((("tm", "section"), 0),), half_taps)
    kernel_rows = []
    grad_units = jnp.zeros(grad_conv.shape, jnp.float32)
    for offset in range(tap_count):
        same_utt = (ext_utt[offset : offset + frame_count] == frame_utt)[:, None]
        kernel_rows.append(
            jnp.sum(
                jnp.where(same_utt, units_ext[offset : offset + frame_count], 0.0) * grad_conv,
                axis=0,
            )
        )
        back_offset = 2 * half_taps - offset
        back_same = (ext_utt[back_offset : back_offset + frame_count] == frame_utt)[:, None]
        grad_units = grad_units + kernel[offset] * jnp.where(
            back_same, conv_ext[back_offset : back_offset + frame_count], 0.0
        )
    kernel_part = jnp.stack(kernel_rows)
    grad_units = grad_units * valid_col
    grad_value = (grad_units * gate_sigmoid).astype(jnp.bfloat16)
    grad_gate = (grad_units * value_proj * gate_sigmoid * (1.0 - gate_sigmoid)).astype(jnp.bfloat16)
    in_term = jnp.stack(
        [
            jnp.dot(normed.T, grad_value, preferred_element_type=jnp.float32),
            jnp.dot(normed.T, grad_gate, preferred_element_type=jnp.float32),
        ]
    )
    normed_part = jnp.dot(grad_value, weight_in[0].T, preferred_element_type=jnp.float32) + jnp.dot(
        grad_gate, weight_in[1].T, preferred_element_type=jnp.float32
    )
    grad_in, grad_out = (
        lax.psum_scatter(in_term, ("tm", "section"), scatter_dimension=1, tiled=True),
        lax.psum_scatter(out_term, ("tm", "section"), scatter_dimension=1, tiled=True),
    )
    grad_normed = lax.psum(normed_part, "tensor")
    scaled_grad = grad_normed * norm_gain
    norm_back = inv_scale * (
        scaled_grad
        - jnp.mean(scaled_grad, axis=1, keepdims=True)
        - unit_frames * jnp.mean(scaled_grad * unit_frames, axis=1, keepdims=True)
    )
    grad_frames = (arrived.astype(jnp.float32) + norm_back).astype(jnp.bfloat16)
    grad_kernel, grad_gain = lax.psum(
        (kernel_part, jnp.sum(grad_normed * unit_frames, axis=0)), ("tm", "section")
    )
    return (grad_frames, grad_in, grad_out, grad_kernel, grad_gain)


def solution(mesh):
    in_specs = (
        P(("tm", "section"), None),
        P("tm", "section"),
        P(),
        P(None, None, "tensor"),
        P(None, "tensor"),
        P("tensor", None),
        P(),
        P(),
    )
    out_specs = (
        P(("tm", "section"), None),
        P(None, ("tm", "section"), "tensor"),
        P("tensor", ("tm", "section")),
        P(None, "tensor"),
        P(),
    )
    return jax.shard_map(body, mesh=mesh, in_specs=in_specs, out_specs=out_specs, check_vma=False)
```

profile of v0, /device:TPU:0, one launch (start us, length us, event | category | flops | bytes accessed | tf_op | source)
XLA Modules:
  0.0 769.5 jit_solution(2482033433576290457)
XLA Ops:
  7.2 0.0 copy-start
  7.2 2.6 copy.25
  9.8 5.5 all-to-all-start
  15.3 0.2 convert_reduce_fusion
  15.6 0.5 fusion.13
  16.2 0.0 copy-start.2
  16.2 3.9 gather_fusion
  20.1 0.0 copy-start.17
  20.2 0.1 compare_select_fusion.2
  20.3 3.5 gather_fusion.1
  23.8 0.1 fusion.181
  23.9 0.0 copy-start.12
  23.9 2.9 fusion.19
  26.7 0.0 copy-start.16
  26.8 2.5 multiply_convert_fusion.2
  29.3 1.3 collective-permute-start.1
  30.6 4.6 collective-permute-start
  35.1 0.1 slice_compare_fusion.26
  35.2 0.1 slice_compare_fusion.27
  35.3 0.1 slice_compare_fusion.28
  35.4 0.1 slice_compare_fusion.29
  35.5 0.1 slice_reduce_fusion.30
  35.6 0.1 slice_reduce_fusion.29
  35.7 0.0 collective-permute-done.1
  35.7 0.9 collective-permute-done
  36.6 0.1 maximum_convert_fusion
  36.7 8.5 %multiply_add_fusion = f32[512,640]{1,0:T(8,128)} fusion(f32[542,640]{1,0:T(8,128)S(1)} %maximum_convert_fusion, f32[640]{0:T(1024)S(1)} %get-tuple-element.83, f32[640]{0:T(1024)S(1)} %get-tuple-element.84, f32[640]{0:T(1024)S(1)} %get-tuple-element.55, f32[640]{0:T(1024)S(1)} %get-tuple-element.56, f32[640]{0:T(1024)S(1)} %get-tuple-element.57, ...), kind=kLoop, calls=%fused_computation.275 | loop fusion | flops 29818880 | bytes 42037760 | tf_op jit(solution)/shard_map/add | solution.py:56
  45.2 0.0 all-to-all-done
  45.2 3.9 multiply_reduce_fusion.28
  49.1 0.0 copy-start.3
  49.1 4.2 collective-permute-start.3
  53.4 1.6 collective-permute-start.2
  55.0 2.6 multiply_reduce_fusion.19
  57.6 0.0 collective-permute-done.3
  57.6 1.8 collective-permute-done.2
  59.4 11.1 %multiply_convert_fusion = (bf16[512,640]{1,0:T(8,128)(2,1)S(1)}, f32[512,640]{1,0:T(8,128)S(1)}) fusion(f32[512,640]{1,0:T(8,128)S(1)} %copy-done.7, f32[512,640]{1,0:T(8,128)S(1)} %copy-done.11, f32[512]{0:T(512)S(1)} %get-tuple-element.90, f32[512,640]{1,0:T(8,128)S(1)} %get-tuple-element.130, f32[15,640]{1,0:T(8,128)S(1)} %collective-permute-done.3, ...), kind=kLoop, calls=%fused_computation.272 | loop fusion | flops 41615360 | bytes 6071808 | tf_op jit(solution)/shard_map/convert_element_type | solution.py:83
  70.5 0.0 copy-start.13
  70.5 0.1 multiply_convert_fusion.1
  70.7 2.0 copy-done.13
  72.7 1.2 fusion.17
  74.0 2.7 convolution_add_fusion
  76.7 0.0 all-reduce.6.cloned.1.call-update
  76.7 0.0 all-reduce.8.cloned.1.call-start
  76.8 0.0 copy-start.4
  76.8 4.0 multiply_reduce_fusion.2
  81.1 2.6 multiply_reduce_fusion.1
  83.8 2.6 stack.139
  86.4 4.8 fusion.156
  91.2 1.4 convolution_bitcast_fusion
  92.6 1.4 convolution_bitcast_fusion.1
  94.0 0.4 pad_maximum_fusion
  94.5 12.4 %copy.22 = f32[2,1280,640]{2,0,1:T(2,128)} copy(f32[2,1280,640]{2,1,0:T(8,128)S(1)} %pad_maximum_fusion) | data formatting | bytes 13107200 | tf_op jit(solution)/shard_map/stack | solution.py:84
  106.8 0.0 all-reduce.8.cloned.1.call-update
  106.9 0.6 copy-done.18
  107.5 0.6 dynamic-slice
  108.7 2.5 copy.21
  111.2 60.1 %all-reduce.6.cloned.1.call-done = f32[512,1280]{1,0:T(8,128)} async-done(((f32[512,1280]{1,0:T(8,128)}), f32[512,1280]{1,0:T(8,128)}) %all-reduce.6.cloned.1.call-update) | async-done | bytes 2621456 | tf_op jit(solution)/shard_map/psum | solution.py:97
  171.3 2.8 fusion.12
  174.0 146.2 %psum.23 = f32[1280]{0:T(1024)} all-reduce(f32[1280]{0:T(1024)S(1)} %get-tuple-element.20), channel_id=1, replica_groups=mesh['tm'=16,'tensor'=2,'section'=4] {'tm','section'}, use_global_device_ids=true, to_apply=%region_40.41 | all-reduce | flops 1280 | bytes 10240 | tf_op jit(solution)/shard_map/psum | solution.py:105
  320.3 4.2 fusion.11
  324.5 433.6 %all-reduce.8.cloned.1.call-done = (f32[2,1280,640]{2,0,1:T(2,128)}, f32[640,1280]{0,1:T(8,128)}, f32[31,640]{1,0:T(8,128)}) async-done(((f32[2,1280,640]{2,0,1:T(2,128)}, f32[640,1280]{0,1:T(8,128)}, f32[31,640]{1,0:T(8,128)}), (f32[2,1280,640]{2,0,1:T(2,128)}, f32[640,1280]{0,1:T(8,128)}, f32[31,640]{1,0:T(8,128)})) %all-reduce.8.cloned.1.call-update) | async-done | bytes 9909776
  758.1 1.5 constant_dynamic-slice_fusion.1
  759.6 1.5 constant_dynamic-slice_fusion
  761.1 1.5 copy.30
  (70 shorter events, 0.3 us)
Async XLA Ops:
  7.2 38.1 %copy-start = (bf16[640,1280]{1,0:T(8,128)(2,1)S(1)}, bf16[640,1280]{1,0:T(8,128)(2,1)}, u32[]{:S(2)}) copy-start(bf16[640,1280]{1,0:T(8,128)(2,1)} %param.13) | copy-start | bytes 4915204
  9.8 5.5 copy-start.5
  9.8 35.4 %all-to-all-start = ((bf16[4,512,320]{1,2,0:T(8,128)(2,1)}), bf16[4,512,320]{1,2,0:T(8,128)(2,1)}, u32[]{:S(2)}, u32[]{:S(2)}) async-start(bf16[4,512,320]{1,2,0:T(8,128)(2,1)} %bitcast.37), calls=%async_computation | async-start | bytes 2621440 | tf_op jit(solution)/shard_map/all_to_all | solution.py:41
  15.3 155.9 %all-reduce.6.cloned.1.call-start = ((), (), s32[]{:S(2)}) async-start(), calls=%async_computation.1 | async-start | bytes 5242880 | tf_op jit(solution)/shard_map/psum | solution.py:97
  15.3 0.8 copy-start.1
  16.2 4.1 copy-start.2
  20.1 3.7 copy-start.17
  23.9 2.9 copy-start.12
  26.7 2.5 copy-start.10
  26.7 8.7 %copy-start.16 = (f32[31,640]{1,0:T(8,128)S(1)}, f32[31,640]{1,0:T(8,128)}, u32[]{:S(2)}) copy-start(f32[31,640]{1,0:T(8,128)} %param.12) | copy-start | bytes 238084
  29.3 6.5 collective-permute-start.1
  30.6 6.0 collective-permute-start
  49.1 10.3 %copy-start.3 = (f32[512,640]{1,0:T(8,128)}, f32[512,640]{1,0:T(8,128)S(1)}, u32[]{:S(2)}) copy-start(f32[512,640]{1,0:T(8,128)S(1)} %get-tuple-element.130) | copy-start | bytes 3932164
  49.1 8.4 %collective-permute-start.3 = (f32[15,640]{1,0:T(8,128)S(1)}, f32[15,640]{1,0:T(8,128)S(1)}, u32[]{:S(2)}, u32[]{:S(2)}) collective-permute-start(f32[15,640]{1,0:T(8,128)S(1)} %get-tuple-element.95), channel_id=1, source_target_pairs={{0,1},{1,2},{2,3},{3,8},{8,9},{9,10},{10,11},{11,16},{16,17},{17,1... | collective-permute-start | bytes 115208 | tf_op jit(solution)/shard_map/ppermute | solution.py:19
  53.3 6.1 copy-start.7
  53.3 6.0 copy-start.11
  53.4 6.0 collective-permute-start.2
  70.5 3.4 copy-start.8
  70.5 2.2 copy-start.13
  72.7 1.2 copy-start.14
  76.7 681.3 %all-reduce.8.cloned.1.call-start = ((), (), s32[]{:S(2)}) async-start(), calls=%async_computation.2 | async-start | bytes 19824640
  76.8 4.3 copy-start.4
  86.4 4.8 copy-start.6
  86.4 4.8 copy-start.9
  91.2 1.4 copy-start.15
  106.8 0.7 copy-start.18
Sparse Core Ops, SparseCore 0:
  76.8 94.3 all-reduce.5
  174.8 583.2 all-reduce.7
where the time goes:
time: 770 us
  waiting for transfers between devices  496 us (64%)
  blocking collectives  146 us (19%)
  other arithmetic  37.8 us (5%)
  local copies, waits for them, and re-layouts  35.7 us (5%)
  matrix products  20.8 us (3%)
  starting transfers between devices  17.2 us (2%)
  between operations  15.3 us (2%)
    unnamed x3, waiting for transfers between devices  434 us
    psum x1, blocking collectives, body(): lax.psum((kernel_part, jnp.sum(grad_normed * unit_frames, axis=0)), ('tm'...  146 us
    psum x1, waiting for transfers between devices, body(): grad_normed = lax.psum(normed_part, 'tensor')  60.1 us
  transfers between devices with their start and end apart: 7, of which 4 were waited for; matrix products, arithmetic and copies ran while one was open for 8% of the time, Pallas kernels for 0%

commit v1 on v0

v1 whole, which is shorter than its diff:
```python
import jax
import jax.numpy as jnp
import numpy as np
from jax import lax
from jax.sharding import Mesh
from jax.sharding import PartitionSpec as P

BLOCK = 128
EPSILON = 1e-05
BF16 = jnp.bfloat16
F32 = jnp.float32

FRAMES = ("xl", "y", "core", "section")
CHIPS = ("xl", "y", "section")
EVERY = ("xl", "y", "core", "tensor", "section")


def swap(value, axis):
    return lax.ppermute(value, axis, [(0, 1), (1, 0)])


def extended(shard, width):
    peers, length = (lax.axis_size(FRAMES), shard.shape[0])
    up = [(i, (i + 1) % peers) for i in range(peers - 1)]
    down = [(j, i) for i, j in up]
    before = lax.ppermute(shard[length - width :], FRAMES, up)
    after = lax.ppermute(shard[:width], FRAMES, down)
    return jnp.concatenate([before, shard, after], axis=0)


def core_rows(array, core):
    parts = array.reshape(8, 2, 80, array.shape[1])
    return lax.dynamic_index_in_dim(parts, core, 1, keepdims=False).reshape(640, array.shape[1])


def body(frames, returned, norm_gain, weight_in, kernel, weight_out, block_utt, block_fill):
    frame_count = frames.shape[0]
    tap_count = kernel.shape[0]
    half_taps = tap_count // 2
    core = lax.axis_index("core")
    first_block = lax.axis_index(FRAMES) * (frame_count // BLOCK)
    blocks = frame_count // BLOCK
    arrived = lax.all_to_all(returned, "section", split_axis=0, concat_axis=1, tiled=True)

    padded_utt = jnp.concatenate([jnp.full((1,), -1, jnp.int32), block_utt, jnp.full((1,), -1, jnp.int32)])
    near_utt = lax.dynamic_slice(padded_utt, (first_block,), (blocks + 2,))
    fill = lax.dynamic_slice(block_fill, (first_block,), (blocks,))
    frame_utt = jnp.broadcast_to(near_utt[1:-1, None], (blocks, BLOCK)).reshape(-1)
    ext_utt = jnp.concatenate(
        [
            jnp.broadcast_to(near_utt[:1], (half_taps,)),
            frame_utt,
            jnp.broadcast_to(near_utt[-1:], (half_taps,)),
        ]
    )
    valid_frame = (jnp.arange(BLOCK, dtype=jnp.int32)[None, :] < fill[:, None]).reshape(-1)
    valid_col = valid_frame.astype(F32)[:, None]

    as_float = frames.astype(F32)
    center = as_float - jnp.mean(as_float, axis=1, keepdims=True)
    inv_scale = lax.rsqrt(jnp.mean(center * center, axis=1, keepdims=True) + EPSILON)
    unit_frames = center * inv_scale
    normed = (unit_frames * norm_gain).astype(BF16)
    value_proj = jnp.dot(normed, weight_in[0], preferred_element_type=F32)
    gate_proj = jnp.dot(normed, weight_in[1], preferred_element_type=F32)
    gate_sigmoid = jax.nn.sigmoid(gate_proj)
    gated_units = (valid_col * value_proj * gate_sigmoid).astype(BF16)
    units_ext = extended(gated_units, half_taps).astype(F32)
    conv_out = jnp.zeros(gated_units.shape, F32)
    for offset in range(tap_count):
        same_utt = (ext_utt[offset : offset + frame_count] == frame_utt)[:, None]
        conv_out = conv_out + kernel[offset] * jnp.where(
            same_utt, units_ext[offset : offset + frame_count], 0.0
        )
    conv_sigmoid = jax.nn.sigmoid(conv_out)
    activated = (conv_out * conv_sigmoid).astype(BF16)

    grad_rows = jnp.where(valid_frame[:, None], arrived, jnp.zeros_like(arrived))
    grad_activated = jnp.dot(grad_rows, weight_out.T, preferred_element_type=F32)
    grad_conv = grad_activated * (conv_sigmoid + conv_out * conv_sigmoid * (1.0 - conv_sigmoid))
    conv_ext = extended(grad_conv, half_taps)
    kernel_rows = []
    grad_units = jnp.zeros(grad_conv.shape, F32)
    for offset in range(tap_count):
        same_utt = (ext_utt[offset : offset + frame_count] == frame_utt)[:, None]
        kernel_rows.append(
            jnp.sum(
                jnp.where(same_utt, units_ext[offset : offset + frame_count], 0.0) * grad_conv,
                axis=0,
            )
        )
        back_offset = 2 * half_taps - offset
        back_same = (ext_utt[back_offset : back_offset + frame_count] == frame_utt)[:, None]
        grad_units = grad_units + kernel[offset] * jnp.where(
            back_same, conv_ext[back_offset : back_offset + frame_count], 0.0
        )
    kernel_part = jnp.stack(kernel_rows)
    grad_units = grad_units * valid_col
    grad_value = (grad_units * gate_sigmoid).astype(BF16)
    grad_gate = (grad_units * value_proj * gate_sigmoid * (1.0 - gate_sigmoid)).astype(BF16)

    normed_part = jnp.dot(grad_value, weight_in[0].T, preferred_element_type=F32) + jnp.dot(
        grad_gate, weight_in[1].T, preferred_element_type=F32
    )
    sent = normed_part.astype(BF16)
    other = swap(sent, "tensor")
    gain_part = jnp.sum(normed_part * unit_frames, axis=0)

    normed_t, rows_t = normed.T, grad_rows.T
    early = jnp.stack([core_rows(normed_t, 1 - core), core_rows(rows_t, 1 - core)])
    early_peer = swap(early, "core")
    activated_peer = swap(activated, "core")
    late = jnp.concatenate([grad_value, grad_gate], axis=1)
    late_peer = swap(late, "core")
    in_part = jnp.dot(core_rows(normed_t, core), late, preferred_element_type=F32) + jnp.dot(
        early_peer[0], late_peer, preferred_element_type=F32
    )
    out_part = jnp.dot(core_rows(rows_t, core), activated, preferred_element_type=F32) + jnp.dot(
        early_peer[1], activated_peer, preferred_element_type=F32
    )
    parts = jnp.concatenate([in_part.astype(BF16), out_part.astype(BF16)], axis=1)
    parts = lax.all_to_all(parts.reshape(32, 20, 1920), CHIPS, 0, 0)
    weights_sum = jnp.sum(parts.astype(F32), axis=0)
    grad_in = jnp.stack([weights_sum[:, :640], weights_sum[:, 640:1280]])
    grad_out = weights_sum[:, 1280:].T

    taps = kernel_part.reshape(64, -1)
    taps = jnp.sum(lax.all_to_all(taps, FRAMES, 0, 0), axis=0)
    taps = lax.all_to_all(jnp.broadcast_to(taps[None], (64, taps.shape[0])), FRAMES, 0, 0)
    grad_kernel = taps.reshape(kernel.shape)

    gains = lax.all_to_all(jnp.broadcast_to(gain_part[None], (128, gain_part.shape[0])), EVERY, 0, 0)
    grad_gain = jnp.sum(gains, axis=0)

    grad_normed = sent.astype(F32) + other.astype(F32)
    scaled_grad = grad_normed * norm_gain
    norm_back = inv_scale * (
        scaled_grad
        - jnp.mean(scaled_grad, axis=1, keepdims=True)
        - unit_frames * jnp.mean(scaled_grad * unit_frames, axis=1, keepdims=True)
    )
    grad_frames = (arrived.astype(F32) + norm_back).astype(BF16)
    return (grad_frames, grad_in, grad_out, grad_kernel, grad_gain)


def solution(mesh):
    split = Mesh(
        np.asarray(mesh.devices).reshape(2, 4, 2, 2, 4), ("xl", "y", "core", "tensor", "section")
    )
    outer = ("xl", "y", "core")
    in_specs = (
        P(FRAMES, None),
        P(outer, "section"),
        P(),
        P(None, None, "tensor"),
        P(None, "tensor"),
        P("tensor", None),
        P(),
        P(),
    )
    out_specs = (
        P(FRAMES, None),
        P(None, FRAMES, "tensor"),
        P("tensor", FRAMES),
        P(None, "tensor"),
        P(),
    )
    return jax.shard_map(body, mesh=split, in_specs=in_specs, out_specs=out_specs, check_vma=False)
```

time: 770 us -> 246 us (0.32)
  waiting for transfers between devices: 496 us -> 66.3 us
  blocking collectives: 146 us -> 0 us
  other arithmetic: 37.8 us -> 80.8 us
  starting transfers between devices: 17.2 us -> 49.6 us
  between operations: 15.3 us -> 1.36 us
  local copies, waits for them, and re-layouts: 35.7 us -> 23.9 us
    unnamed x3 -> x0, waiting for transfers between devices: 434 us -> none
    psum x1 -> x0, blocking collectives: 146 us -> none  [body(): lax.psum((kernel_part, jnp.sum(grad_normed * unit_frames, axis=0)), ('tm'...]
    psum x1 -> x0, waiting for transfers between devices: 60.1 us -> none  [body(): grad_normed = lax.psum(normed_part, 'tensor')]
    all_to_all x0 -> x4, waiting for transfers between devices: none -> 41.3 us  [the longest x1 27.4 us: body(): parts = lax.all_to_all(parts.reshape(32, 20, 1920), CHIPS, 0, 0)]
    convert_element_type x5, other arithmetic: 15.7 us -> 53.3 us  [the longest x1 38.7 us: body(): (grad_units * value_proj * gate_sigmoid * (1.0 - gate_sigmoid)).astype(BF16)]
    all_to_all x0 -> x4, starting transfers between devices: none -> 25.9 us  [the longest x1 8.86 us: body(): taps = jnp.sum(lax.all_to_all(taps, FRAMES, 0, 0), axis=0)]
    ppermute x4 -> x8, waiting for transfers between devices: 2.68 us -> 21.8 us  [the longest x4 20.2 us: swap(): return lax.ppermute(value, axis, [(0, 1), (1, 0)])]
    another operation x1 -> x0, local copies, waits for them, and re-layouts: 12.4 us -> none  [body(): jnp.stack([jnp.dot(normed.T, grad_value, preferred_element_type=jnp.float...]
  transfers between devices with their start and end apart: 7 -> 13, of which waited for: 4 -> 7; matrix products, arithmetic and copies ran while one was open for 8% -> 26% of each run, Pallas kernels for 0% -> 0%
where the time goes in v1:
time: 246 us; the launch traced here: 242 us
  other arithmetic  80.8 us (33%)
  waiting for transfers between devices  66.3 us (27%)
  starting transfers between devices  49.6 us (20%)
  local copies, waits for them, and re-layouts  23.9 us (10%)
  matrix products  20.3 us (8%)
    convert_element_type x1, other arithmetic, body(): (grad_units * value_proj * gate_sigmoid * (1.0 - gate_sigmoid)).astype(BF16)  38.7 us
    all_to_all x1, waiting for transfers between devices, body(): parts = lax.all_to_all(parts.reshape(32, 20, 1920), CHIPS, 0, 0)  27.4 us
    ppermute x4, waiting for transfers between devices, swap(): return lax.ppermute(value, axis, [(0, 1), (1, 0)])  20.2 us
    convert_element_type x1, other arithmetic, body(): activated = (conv_out * conv_sigmoid).astype(BF16)  8.89 us
    all_to_all x1, starting transfers between devices, body(): taps = jnp.sum(lax.all_to_all(taps, FRAMES, 0, 0), axis=0)  8.86 us
    ppermute x2, starting transfers between devices, extended(): before = lax.ppermute(shard[length - width:], FRAMES, up)  8.45 us
    all_to_all x1, waiting for transfers between devices, body(): taps = jnp.sum(lax.all_to_all(taps, FRAMES, 0, 0), axis=0)  8.12 us
    reduce_sum x3, other arithmetic, body(): jnp.sum(jnp.where(same_utt, units_ext[offset:offset + frame_count], 0.0)...  7.83 us
  transfers between devices with their start and end apart: 13, of which 7 were waited for; matrix products, arithmetic and copies ran while one was open for 26% of the time, Pallas kernels for 0%

profile of v1, /device:TPU:0, one launch (start us, length us, event | category | flops | bytes accessed | tf_op | source)
XLA Modules:
  0.0 242.2 jit_solution(16708922955319975915)
XLA Ops:
  0.7 0.9 dynamic_slice.20
  1.7 1.6 convert_reduce_fusion.1
  3.2 0.5 fusion.14
  3.8 2.9 %fusion.21 = f32[512,640]{1,0:T(8,128)S(1)} fusion(bf16[2,1280,640]{2,1,0:T(8,128)(2,1)} %param.11, bf16[512,1280]{1,0:T(8,128)(2,1)S(1)} %copy-done.4, f32[1280]{0:T(1024)S(1)} %copy-done.23, f32[512]{0:T(512)S(1)} %add_rsqrt_fusion, f32[512]{0:T(512)S(1)} %broadcast_multiply_fusion.2), kind=kOutput, calls=%fused_computation.56 | convolution fusion | flops 842137600 | bytes 4269056 | tf_op jit(solution)/shard_map/dot_general | solution.py:64
  6.6 2.5 %multiply_convert_fusion.2 = (bf16[512,640]{1,0:T(8,128)(2,1)S(1)}, f32[512,640]{1,0:T(8,128)}) fusion(f32[512,640]{1,0:T(8,128)S(1)} %fusion.21, f32[512]{0:T(512)S(1)} %get-tuple-element.149, bf16[2,1280,640]{2,1,0:T(8,128)(2,1)S(1)} %copy-done.19, bf16[512,1280]{1,0:T(8,128)(2,1)S(1)} %copy-done.4, f32[1280]{0:T(1024)S(1)} %copy-done.23, ...), kind=kOutput, calls=%fused_computation.279 | convolution fusion | flops 844103680 | bytes 6240256 | tf_op jit(solution)/shard_map/dot_general | solution.py:65
  9.2 3.9 %collective-permute-start = (bf16[15,640]{1,0:T(8,128)(2,1)S(1)}, bf16[15,640]{1,0:T(8,128)(2,1)S(1)}, u32[]{:S(2)}, u32[]{:S(2)}) collective-permute-start(bf16[15,640]{1,0:T(8,128)(2,1)S(1)} %get-tuple-element.111), channel_id=1, source_target_pairs={{0,1},{1,2},{2,3},{3,8},{8,9},{9,10},{10,11},{11,16},{16,17},{17,1... | collective-permute-start | bytes 57608 | tf_op jit(solution)/shard_map/ppermute | solution.py:26
  13.1 1.3 collective-permute-start.1
  14.4 1.2 copy.52
  15.6 6.2 %all-to-all-start = ((bf16[4,512,320]{1,2,0:T(8,128)(2,1)}), bf16[4,512,320]{1,2,0:T(8,128)(2,1)}, u32[]{:S(2)}, u32[]{:S(2)}) async-start(bf16[4,512,320]{1,2,0:T(8,128)(2,1)} %bitcast.98), calls=%async_computation | async-start | bytes 2621440 | tf_op jit(solution)/shard_map/all_to_all | solution.py:43
  22.0 0.6 fusion.169
  22.6 1.4 bitcast_compare_fusion.28
  24.0 1.4 bitcast_compare_fusion.27
  25.4 1.4 bitcast_compare_fusion.15
  26.8 0.7 bitcast_compare_fusion.24
  27.8 1.2 maximum_convert_fusion
  29.0 8.9 %fusion.159 = (bf16[512,640]{1,0:T(8,128)(2,1)}, f32[512,640]{1,0:T(8,128)}) fusion(f32[542,640]{1,0:T(8,128)S(1)} %maximum_convert_fusion, pred[512]{0:T(512)(128)(4,1)S(1)} %get-tuple-element.145, f32[640]{0:T(1024)S(1)} %get-tuple-element.98, pred[512]{0:T(512)(128)(4,1)S(1)} %get-tuple-element.131, f32[640]{0:T(1024)S(1)} %get-tuple-element.99, ...), kind=kLoop, calls=%fused_computation.283 | loop fusion | flops 31457280 | bytes 42693120 | tf_op jit(solution)/shard_map/convert_element_type | solution.py:76
  37.9 3.2 %all-to-all-done = bf16[4,512,320]{1,2,0:T(8,128)(2,1)} async-done(((bf16[4,512,320]{1,2,0:T(8,128)(2,1)}), bf16[4,512,320]{1,2,0:T(8,128)(2,1)}, u32[]{:S(2)}, u32[]{:S(2)}) %all-to-all-start) | async-done | bytes 1310752 | tf_op jit(solution)/shard_map/all_to_all | solution.py:43
  41.0 1.5 broadcast_select_fusion
  42.8 2.2 multiply_reduce_fusion.27
  45.0 1.0 copy-done.1
  46.0 1.3 collective-permute-start.2
  47.3 4.5 %collective-permute-start.3 = (f32[15,640]{1,0:T(8,128)S(1)}, f32[15,640]{1,0:T(8,128)S(1)}, u32[]{:S(2)}, u32[]{:S(2)}) collective-permute-start(f32[15,640]{1,0:T(8,128)S(1)} %get-tuple-element.110), channel_id=1, source_target_pairs={{0,1},{1,2},{2,3},{3,8},{8,9},{9,10},{10,11},{11,16},{16,17},{17,1... | collective-permute-start | bytes 115208 | tf_op jit(solution)/shard_map/ppermute | solution.py:26
  51.9 1.6 collective-permute-done.3
  53.5 38.7 %multiply_convert_fusion = (bf16[512,640]{1,0:T(8,128)(2,1)S(1)}, f32[512,640]{1,0:T(8,128)S(1)}) fusion(f32[512,640]{1,0:T(8,128)} %get-tuple-element.151, f32[512,640]{1,0:T(8,128)} %copy-done.17, f32[512]{0:T(512)S(1)} %get-tuple-element.149, f32[512,640]{1,0:T(8,128)} %copy-done.1, f32[15,640]{1,0:T(8,128)S(1)} %collective-permute-done.3, ...), kind=kLoop, calls=%fused_computation.275 | loop fusion | flops 41615360 | bytes 6071808 | tf_op jit(solution)/shard_map/convert_element_type | solution.py:100
  92.4 2.0 copy-done.20
  94.4 1.2 fusion.19
  95.6 1.3 fusion.170
  96.9 3.3 %collective-permute-start.4 = (bf16[512,1280]{1,0:T(8,128)(2,1)S(1)}, bf16[512,1280]{1,0:T(8,128)(2,1)S(1)}, u32[]{:S(2)}, u32[]{:S(2)}) collective-permute-start(bf16[512,1280]{1,0:T(8,128)(2,1)S(1)} %get-tuple-element.152), channel_id=1, source_target_pairs={{0,4},{4,0},{1,5},{5,1},{2,6},{6,2},{3,7},{7,3},{8,12},{12,8},{9,1... | collective-permute-start | bytes 3932168 | tf_op jit(solution)/shard_map/ppermute | solution.py:19
  100.2 2.6 %multiply_reduce_fusion = (f32[640]{0:T(1024)S(1)}, f32[640]{0:T(1024)S(1)}, f32[640]{0:T(1024)S(1)}, f32[640]{0:T(1024)S(1)}, f32[640]{0:T(1024)S(1)}, /*index=...) fusion(f32[512,640]{1,0:T(8,128)S(1)} %copy-done.2, f32[542,640]{1,0:T(8,128)S(1)} %maximum_convert_fusion, ...), kind=kLoop, calls=%fused_computation.244 | loop fusion | flops 8841600 | bytes 13134848 | tf_op jit(solution)/shard_map/reduce_sum | solution.py:87
  102.9 2.7 %multiply_reduce_fusion.1 = (f32[640]{0:T(1024)S(1)}, f32[640]{0:T(1024)S(1)}, f32[640]{0:T(1024)S(1)}, f32[640]{0:T(1024)S(1)}, f32[640]{0:T(1024)S(1)}, /*inde...) fusion(f32[512,640]{1,0:T(8,128)S(1)} %copy-done.2, f32[542,640]{1,0:T(8,128)S(1)} %maximum_convert_fusion, ...), kind=kLoop, calls=%fused_computation.245 | loop fusion | flops 8513920 | bytes 13134336 | tf_op jit(solution)/shard_map/reduce_sum | solution.py:87
  105.7 1.2 pad_maximum_fusion.3
  106.9 1.9 collective-permute-start.6
  108.8 20.2 %collective-permute-done.4 = bf16[512,1280]{1,0:T(8,128)(2,1)S(1)} collective-permute-done((bf16[512,1280]{1,0:T(8,128)(2,1)S(1)}, bf16[512,1280]{1,0:T(8,128)(2,1)S(1)}, u32[]{:S(2)}, u32[]{:S(2)}) %collective-permute-start.4) | collective-permute-done | bytes 1310752 | tf_op jit(solution)/shard_map/ppermute | solution.py:19
  129.0 2.3 fusion.15
  131.3 2.4 %copy.42 = bf16[1280,512]{1,0:T(8,128)(2,1)} copy(bf16[1280,512]{0,1:T(8,128)(2,1)} %get-tuple-element.104) | data formatting | bytes 2621440 | tf_op jit(solution)/shard_map/transpose | solution.py:109
  133.8 3.0 %constant_dynamic-slice_fusion.1 = (bf16[8,1,80,512]{3,2,1,0:T(8,128)(2,1)S(1)}, bf16[8,1,80,512]{3,2,1,0:T(8,128)(2,1)}, bf16[8,1,80,512]{3,2,1,0:T(8,128)(2,1)S(1)}, bf16[8,1,80,512]{3,2,1,0:T(8,128)(2,1)}) fusion(bf16[8,2,80,512]{3,2,1,0:T(8,128)(2,1)} %bitcast.100, s32[]{:T(128)S(6)} %select_n.297, s32[]{:T(128)S(6)} %select_n.296, ...), kind=kLoop, calls=%fused_computation.388 | loop fusion | bytes 5242888 | tf_op jit(solution)/shard_map/jit(dynamic_index_in_dim)/dynamic_slice | solution.py:33
  136.8 1.2 pad_maximum_fusion.4
  137.9 1.1 collective-permute-start.5
  139.0 2.6 %multiply_reduce_fusion.18 = (f32[640]{0:T(1024)S(1)}, f32[640]{0:T(1024)S(1)}, f32[640]{0:T(1024)S(1)}, f32[640]{0:T(1024)S(1)}, f32[640]{0:T(1024)S(1)}, /*ind...) fusion(f32[512,640]{1,0:T(8,128)S(1)} %copy-done.3, ...), kind=kLoop, calls=%fused_computation.262 | loop fusion | flops 8841600 | bytes 13134848 | tf_op jit(solution)/shard_map/reduce_sum | solution.py:87
  142.0 0.9 all_to_all.36
  142.9 8.9 %all-to-all-start.2 = ((f32[64,1,310]{2,1,0:T(1,128)}), f32[64,1,310]{2,1,0:T(1,128)S(1)}, u32[]{:S(2)}, u32[]{:S(2)}) async-start(f32[64,1,310]{2,1,0:T(1,128)} %all_to_all.36), calls=%async_computation.2 | async-start | bytes 196608 | tf_op jit(solution)/shard_map/all_to_all | solution.py:128
  151.9 8.1 %all-to-all-done.2 = f32[64,1,310]{2,1,0:T(1,128)S(1)} async-done(((f32[64,1,310]{2,1,0:T(1,128)}), f32[64,1,310]{2,1,0:T(1,128)S(1)}, u32[]{:S(2)}, u32[]{:S(2)}) %all-to-all-start.2) | async-done | bytes 79392 | tf_op jit(solution)/shard_map/all_to_all | solution.py:128
  160.1 0.7 broadcast_in_dim.612
  160.8 4.6 %all-to-all-start.3 = ((f32[64,1,310]{2,1,0:T(1,128)}), f32[64,1,310]{2,1,0:T(1,128)S(1)}, u32[]{:S(2)}, u32[]{:S(2)}) async-start(f32[64,1,310]{2,1,0:T(1,128)} %broadcast_in_dim.612), calls=%async_computation.3 | async-start | bytes 196608 | tf_op jit(solution)/shard_map/all_to_all | solution.py:129
  165.5 4.1 %fusion.162 = f32[640,1280]{1,0:T(8,128)} fusion(bf16[640,512]{1,0:T(8,128)(2,1)} %bitcast.101, bf16[512,640]{1,0:T(8,128)(2,1)S(1)} %copy-done.9, bf16[512,640]{1,0:T(8,128)(2,1)} %copy-done.10), kind=kOutput, calls=%fused_computation.395 | convolution fusion | flops 841482240 | bytes 5242880 | tf_op jit(solution)/shard_map/dot_general | solution.py:115
  169.5 0.7 fusion.171
  170.2 3.5 %all-to-all-done.3 = f32[64,1,310]{2,1,0:T(1,128)S(1)} async-done(((f32[64,1,310]{2,1,0:T(1,128)}), f32[64,1,310]{2,1,0:T(1,128)S(1)}, u32[]{:S(2)}, u32[]{:S(2)}) %all-to-all-start.3) | async-done | bytes 79392 | tf_op jit(solution)/shard_map/all_to_all | solution.py:129
  173.7 1.2 broadcast_in_dim.613
  174.9 6.8 %all-to-all-start.4 = ((f32[128,1,1280]{2,1,0:T(1,128)}), f32[128,1,1280]{2,1,0:T(1,128)}, u32[]{:S(2)}, u32[]{:S(2)}) async-start(f32[128,1,1280]{2,1,0:T(1,128)} %broadcast_in_dim.613), calls=%async_computation.4 | async-start | bytes 1310720 | tf_op jit(solution)/shard_map/all_to_all | solution.py:132
  181.7 3.5 %fusion = bf16[640,1280]{1,0:T(8,128)(2,1)S(1)} fusion(f32[640,1280]{1,0:T(8,128)} %fusion.162, bf16[512,1280]{1,0:T(8,128)(2,1)} %collective-permute-done.6, bf16[2,640,512]{2,1,0:T(8,128)(2,1)} %collective-permute-done.5), kind=kOutput, calls=%fused_computation.33 | convolution fusion | flops 840499200 | bytes 6881280 | tf_op jit(solution)/shard_map/dot_general | solution.py:115
  185.3 2.0 add_convert_fusion
  187.2 1.6 pad_maximum_fusion
  188.9 4.2 %reshape.139 = bf16[32,20,1920]{2,1,0:T(8,128)(2,1)} reshape(bf16[640,1920]{1,0:T(8,128)(2,1)} %pad_maximum_fusion) | data formatting | bytes 4915200 | tf_op jit(solution)/shard_map/reshape | solution.py:122
  193.0 2.4 all-to-all-done.4
  195.4 5.6 %all-to-all-start.1 = ((bf16[32,20,1920]{2,1,0:T(8,128)(2,1)}), bf16[32,20,1920]{2,1,0:T(8,128)(2,1)}, u32[]{:S(2)}, u32[]{:S(2)}) async-start(bf16[32,20,1920]{2,1,0:T(8,128)(2,1)} %reshape.139), calls=%async_computation.1 | async-start | bytes 5898240 | tf_op jit(solution)/shard_map/all_to_all | solution.py:122
  201.1 2.5 %copy.41 = bf16[512,1280]{1,0:T(8,128)(2,1)} copy(bf16[512,1280]{0,1:T(8,128)(2,1)} %bitcast.1) | data formatting | bytes 2621440 | tf_op jit(solution)/shard_map/all_to_all | solution.py:43
  203.6 0.2 reduce.33
  203.9 0.8 reshape.140
  204.7 4.4 %fusion.12 = bf16[512,1280]{1,0:T(8,128)(2,1)} fusion(bf16[512,1280]{1,0:T(8,128)(2,1)S(1)} %copy-done.6, bf16[512,1280]{1,0:T(8,128)(2,1)} %copy.41, bf16[512,1280]{1,0:T(8,128)(2,1)} %copy-done.12, bf16[512,1280]{1,0:T(8,128)(2,1)} %copy-done.7, f32[512]{0:T(512)S(1)} %get-tuple-element.155, f32[512]{0:T(512)S(1)} %get-tuple-element.156, ...), kind=kLoop, calls=%fused_computation.45 | loop fusion | flops 9175040 | bytes 6566912 | tf_op jit(solution)/shard_map/convert_element_type | solution.py:142
  209.1 2.1 reduce_sum.389
  211.2 27.4 %all-to-all-done.1 = bf16[32,20,1920]{2,1,0:T(8,128)(2,1)} async-done(((bf16[32,20,1920]{2,1,0:T(8,128)(2,1)}), bf16[32,20,1920]{2,1,0:T(8,128)(2,1)}, u32[]{:S(2)}, u32[]{:S(2)}) %all-to-all-start.1) | async-done | bytes 2457632 | tf_op jit(solution)/shard_map/all_to_all | solution.py:122
  238.6 2.3 convert_reduce_fusion
  240.9 0.6 slice_bitcast_fusion.4
  241.5 0.7 copy.46
  (102 shorter events, 1.6 us)
Async XLA Ops:
  0.6 41.9 %copy-start = (bf16[640,1280]{1,0:T(8,128)(2,1)S(1)}, bf16[640,1280]{1,0:T(8,128)(2,1)}, u32[]{:S(2)}) copy-start(bf16[640,1280]{1,0:T(8,128)(2,1)} %param.13) | copy-start | bytes 4915204
  0.6 2.6 %copy-start.4 = (bf16[512,1280]{1,0:T(8,128)(2,1)S(1)}, bf16[512,1280]{1,0:T(8,128)(2,1)}, u32[]{:S(2)}) copy-start(bf16[512,1280]{1,0:T(8,128)(2,1)} %param.8) | copy-start | bytes 3932164
  1.7 2.1 copy-start.23
  3.7 2.9 %copy-start.19 = (bf16[2,1280,640]{2,1,0:T(8,128)(2,1)S(1)}, bf16[2,1280,640]{2,1,0:T(8,128)(2,1)}, u32[]{:S(2)}) copy-start(bf16[2,1280,640]{2,1,0:T(8,128)(2,1)} %param.11) | copy-start | bytes 9830404
  6.6 2.5 %copy-start.17 = (f32[512,640]{1,0:T(8,128)}, f32[512,640]{1,0:T(8,128)S(1)}, u32[]{:S(2)}) copy-start(f32[512,640]{1,0:T(8,128)S(1)} %fusion.21) | copy-start | bytes 3932164
  6.6 7.7 %copy-start.16 = (bf16[2048,320]{0,1:T(8,128)(2,1)S(1)}, bf16[2048,320]{0,1:T(8,128)(2,1)}, u32[]{:S(2)}) copy-start(bf16[2048,320]{0,1:T(8,128)(2,1)} %param.9) | copy-start | bytes 3932164
  9.2 6.4 %copy-start.21 = (bf16[512,640]{1,0:T(8,128)(2,1)}, bf16[512,640]{1,0:T(8,128)(2,1)S(1)}, u32[]{:S(2)}) copy-start(bf16[512,640]{1,0:T(8,128)(2,1)S(1)} %get-tuple-element.150) | copy-start | bytes 1966084
  9.2 18.6 %collective-permute-start = (bf16[15,640]{1,0:T(8,128)(2,1)S(1)}, bf16[15,640]{1,0:T(8,128)(2,1)S(1)}, u32[]{:S(2)}, u32[]{:S(2)}) collective-permute-start(bf16[15,640]{1,0:T(8,128)(2,1)S(1)} %get-tuple-element.111), channel_id=1, source_target_pairs={{0,1},{1,2},{2,3},{3,8},{8,9},{9,10},{10,11},{11,16},{16,17},{17,1... | collective-permute-start | bytes 57608 | tf_op jit(solution)/shard_map/ppermute | solution.py:26
  13.1 14.7 %collective-permute-start.1 = (bf16[15,640]{1,0:T(8,128)(2,1)S(1)}, bf16[15,640]{1,0:T(8,128)(2,1)S(1)}, u32[]{:S(2)}, u32[]{:S(2)}) collective-permute-start(bf16[15,640]{1,0:T(8,128)(2,1)S(1)} %get-tuple-element.112), channel_id=1, source_target_pairs={{1,0},{2,1},{3,2},{8,3},{9,8},{10,9},{11,10},{16,11},{17,16},{18,1... | collective-permute-start | bytes 57608 | tf_op jit(solution)/shard_map/ppermute | solution.py:27
  15.6 6.2 %copy-start.24 = (s32[256]{0:T(256)S(1)}, s32[256]{0:T(256)}, u32[]{:S(2)}) copy-start(s32[256]{0:T(256)} %param.14) | copy-start | bytes 3076
  15.6 11.9 %copy-start.22 = (f32[31,640]{1,0:T(8,128)S(1)}, f32[31,640]{1,0:T(8,128)}, u32[]{:S(2)}) copy-start(f32[31,640]{1,0:T(8,128)} %param.12) | copy-start | bytes 238084
  15.6 25.5 %all-to-all-start = ((bf16[4,512,320]{1,2,0:T(8,128)(2,1)}), bf16[4,512,320]{1,2,0:T(8,128)(2,1)}, u32[]{:S(2)}, u32[]{:S(2)}) async-start(bf16[4,512,320]{1,2,0:T(8,128)(2,1)} %bitcast.98), calls=%async_computation | async-start | bytes 2621440 | tf_op jit(solution)/shard_map/all_to_all | solution.py:43
  41.0 1.7 copy-start.18
  42.6 2.4 copy-start.13
  44.9 1.1 copy-start.1
  46.0 5.9 %collective-permute-start.2 = (f32[15,640]{1,0:T(8,128)S(1)}, f32[15,640]{1,0:T(8,128)S(1)}, u32[]{:S(2)}, u32[]{:S(2)}) collective-permute-start(f32[15,640]{1,0:T(8,128)S(1)} %get-tuple-element.109), channel_id=1, source_target_pairs={{1,0},{2,1},{3,2},{8,3},{9,8},{10,9},{11,10},{16,11},{17,16},{18,1... | collective-permute-start | bytes 115208 | tf_op jit(solution)/shard_map/ppermute | solution.py:27
  47.3 6.2 %collective-permute-start.3 = (f32[15,640]{1,0:T(8,128)S(1)}, f32[15,640]{1,0:T(8,128)S(1)}, u32[]{:S(2)}, u32[]{:S(2)}) collective-permute-start(f32[15,640]{1,0:T(8,128)S(1)} %get-tuple-element.110), channel_id=1, source_target_pairs={{0,1},{1,2},{2,3},{3,8},{8,9},{9,10},{10,11},{11,16},{16,17},{17,1... | collective-permute-start | bytes 115208 | tf_op jit(solution)/shard_map/ppermute | solution.py:26
  53.5 38.7 %copy-start.11 = (f32[512,640]{1,0:T(8,128)S(1)}, f32[512,640]{1,0:T(8,128)}, u32[]{:S(2)}) copy-start(f32[512,640]{1,0:T(8,128)} %get-tuple-element.151) | copy-start | bytes 3932164
  92.2 13.5 %copy-start.8 = (bf16[512,640]{1,0:T(8,128)(2,1)}, bf16[512,640]{1,0:T(8,128)(2,1)S(1)}, u32[]{:S(2)}) copy-start(bf16[512,640]{1,0:T(8,128)(2,1)S(1)} %get-tuple-element.102) | copy-start | bytes 1966084
  92.2 2.2 copy-start.20
  94.4 11.3 %copy-start.10 = (bf16[512,640]{1,0:T(8,128)(2,1)}, bf16[512,640]{1,0:T(8,128)(2,1)S(1)}, u32[]{:S(2)}) copy-start(bf16[512,640]{1,0:T(8,128)(2,1)S(1)} %multiply_convert_fusion.1) | copy-start | bytes 1966084
  95.6 4.6 %copy-start.2 = (f32[512,640]{1,0:T(8,128)S(1)}, f32[512,640]{1,0:T(8,128)}, u32[]{:S(2)}) copy-start(f32[512,640]{1,0:T(8,128)} %copy-done.1) | copy-start | bytes 3932164
  96.9 32.1 %copy-start.7 = (bf16[512,1280]{1,0:T(8,128)(2,1)}, bf16[512,1280]{1,0:T(8,128)(2,1)S(1)}, u32[]{:S(2)}) copy-start(bf16[512,1280]{1,0:T(8,128)(2,1)S(1)} %get-tuple-element.152) | copy-start | bytes 3932164
  96.9 32.1 %collective-permute-start.4 = (bf16[512,1280]{1,0:T(8,128)(2,1)S(1)}, bf16[512,1280]{1,0:T(8,128)(2,1)S(1)}, u32[]{:S(2)}, u32[]{:S(2)}) collective-permute-start(bf16[512,1280]{1,0:T(8,128)(2,1)S(1)} %get-tuple-element.152), channel_id=1, source_target_pairs={{0,4},{4,0},{1,5},{5,1},{2,6},{6,2},{3,7},{7,3},{8,12},{12,8},{9,1... | collective-permute-start | bytes 3932168 | tf_op jit(solution)/shard_map/ppermute | solution.py:19
  105.7 23.3 %copy-start.5 = (bf16[512,1280]{1,0:T(8,128)(2,1)S(1)}, bf16[512,1280]{1,0:T(8,128)(2,1)}, u32[]{:S(2)}) copy-start(bf16[512,1280]{1,0:T(8,128)(2,1)} %param.8) | copy-start | bytes 3932164
  106.9 74.8 %collective-permute-start.6 = (bf16[512,1280]{1,0:T(8,128)(2,1)}, bf16[512,1280]{1,0:T(8,128)(2,1)}, u32[]{:S(2)}, u32[]{:S(2)}) collective-permute-start(bf16[512,1280]{1,0:T(8,128)(2,1)} %pad_maximum_fusion.3), channel_id=1, source_target_pairs={{0,8},{8,0},{1,9},{9,1},{2,10},{10,2},{3,11},{11,3},{4,12},{12,4},... | collective-permute-start | bytes 3932168 | tf_op jit(solution)/shard_map/ppermute | solution.py:19
  129.0 2.3 copy-start.12
  136.8 2.3 copy-start.3
  137.9 43.8 %collective-permute-start.5 = (bf16[2,640,512]{2,1,0:T(8,128)(2,1)}, bf16[2,640,512]{2,1,0:T(8,128)(2,1)}, u32[]{:S(2)}, u32[]{:S(2)}) collective-permute-start(bf16[2,640,512]{2,1,0:T(8,128)(2,1)} %pad_maximum_fusion.4), channel_id=1, source_target_pairs={{0,8},{8,0},{1,9},{9,1},{2,10},{10,2},{3,11},{11,3},{4,12},{12,4},... | collective-permute-start | bytes 3932168 | tf_op jit(solution)/shard_map/ppermute | solution.py:19
  141.6 23.8 %copy-start.9 = (bf16[512,640]{1,0:T(8,128)(2,1)S(1)}, bf16[512,640]{1,0:T(8,128)(2,1)}, u32[]{:S(2)}) copy-start(bf16[512,640]{1,0:T(8,128)(2,1)} %copy-done.8) | copy-start | bytes 1966084
  142.9 17.1 %all-to-all-start.2 = ((f32[64,1,310]{2,1,0:T(1,128)}), f32[64,1,310]{2,1,0:T(1,128)S(1)}, u32[]{:S(2)}, u32[]{:S(2)}) async-start(f32[64,1,310]{2,1,0:T(1,128)} %all_to_all.36), calls=%async_computation.2 | async-start | bytes 196608 | tf_op jit(solution)/shard_map/all_to_all | solution.py:128
  151.7 33.5 %collective-permute-start.7 = (bf16[512,640]{1,0:T(8,128)(2,1)}, bf16[512,640]{1,0:T(8,128)(2,1)}, u32[]{:S(2)}, u32[]{:S(2)}) collective-permute-start(bf16[512,640]{1,0:T(8,128)(2,1)} %get-tuple-element.100), channel_id=1, source_target_pairs={{0,8},{8,0},{1,9},{9,1},{2,10},{10,2},{3,11},{11,3},{4,12},{12,4},... | collective-permute-start | bytes 1966088 | tf_op jit(solution)/shard_map/ppermute | solution.py:19
  160.8 12.9 %all-to-all-start.3 = ((f32[64,1,310]{2,1,0:T(1,128)}), f32[64,1,310]{2,1,0:T(1,128)S(1)}, u32[]{:S(2)}, u32[]{:S(2)}) async-start(f32[64,1,310]{2,1,0:T(1,128)} %broadcast_in_dim.612), calls=%async_computation.3 | async-start | bytes 196608 | tf_op jit(solution)/shard_map/all_to_all | solution.py:129
  165.4 4.1 %copy-start.14 = (bf16[8,1,80,512]{3,2,1,0:T(8,128)(2,1)S(1)}, bf16[8,1,80,512]{3,2,1,0:T(8,128)(2,1)}, u32[]{:S(2)}) copy-start(bf16[8,1,80,512]{3,2,1,0:T(8,128)(2,1)} %get-tuple-element.108) | copy-start | bytes 1966084
  165.4 4.1 %copy-start.15 = (bf16[512,640]{1,0:T(8,128)(2,1)S(1)}, bf16[512,640]{1,0:T(8,128)(2,1)}, u32[]{:S(2)}) copy-start(bf16[512,640]{1,0:T(8,128)(2,1)} %get-tuple-element.100) | copy-start | bytes 1966084
  174.9 20.6 %all-to-all-start.4 = ((f32[128,1,1280]{2,1,0:T(1,128)}), f32[128,1,1280]{2,1,0:T(1,128)}, u32[]{:S(2)}, u32[]{:S(2)}) async-start(f32[128,1,1280]{2,1,0:T(1,128)} %broadcast_in_dim.613), calls=%async_computation.4 | async-start | bytes 1310720 | tf_op jit(solution)/shard_map/all_to_all | solution.py:132
  195.4 43.1 %all-to-all-start.1 = ((bf16[32,20,1920]{2,1,0:T(8,128)(2,1)}), bf16[32,20,1920]{2,1,0:T(8,128)(2,1)}, u32[]{:S(2)}, u32[]{:S(2)}) async-start(bf16[32,20,1920]{2,1,0:T(8,128)(2,1)} %reshape.139), calls=%async_computation.1 | async-start | bytes 5898240 | tf_op jit(solution)/shard_map/all_to_all | solution.py:122
  201.1 3.6 %copy-start.6 = (bf16[512,1280]{1,0:T(8,128)(2,1)S(1)}, bf16[512,1280]{1,0:T(8,128)(2,1)}, u32[]{:S(2)}) copy-start(bf16[512,1280]{1,0:T(8,128)(2,1)} %param.8) | copy-start | bytes 3932164

commit v2 on v1

v2 whole, which is shorter than its diff:
```python
import functools

import jax
import jax.numpy as jnp
import numpy as np
from jax import lax
from jax.experimental import pallas as pl
from jax.experimental.pallas import tpu as pltpu
from jax.sharding import Mesh
from jax.sharding import PartitionSpec as P

BLOCK = 128
HALO = 16
TAPS = 31
LANES = 128
EPSILON = 1e-05
BF16 = jnp.bfloat16
F32 = jnp.float32

FRAMES = ("xl", "y", "core", "section")
PLANE = ("y", "section")
EVERY = ("xl", "y", "core", "tensor", "section")
VMEM_LIMIT = 48 * 1024 * 1024


def params():
    return pltpu.CompilerParams(vmem_limit_bytes=VMEM_LIMIT)


def cost(flops, moved, special=0):
    return pl.CostEstimate(flops=flops, bytes_accessed=moved, transcendentals=special)


def swap(value, axis):
    return lax.ppermute(value, axis, [(0, 1), (1, 0)])


def halos(shard):
    peers = lax.axis_size(FRAMES)
    up = [(i, i + 1) for i in range(peers - 1)]
    down = [(j, i) for i, j in up]
    before = lax.ppermute(shard[shard.shape[0] - HALO :], FRAMES, up)
    after = lax.ppermute(shard[:HALO], FRAMES, down)
    return before, after


def fill_windows(win, main, before, after, same):
    blocks = win.shape[0]
    for b in range(blocks):
        lo, hi = b * BLOCK, (b + 1) * BLOCK
        prior = before[...] if b == 0 else main[lo - HALO : lo, :]
        later = after[...] if b == blocks - 1 else main[hi : hi + HALO, :]
        win[b, HALO : HALO + BLOCK, :] = main[lo:hi, :].astype(F32)
        win[b, :HALO, :] = jnp.where(same[b] == 1, prior.astype(F32), 0.0)
        win[b, HALO + BLOCK :, :] = jnp.where(same[b + 1] == 1, later.astype(F32), 0.0)


def shifted(win, b, shift):
    first = 1 if shift == 0 else 0
    return [(8 * a + shift - 1, 8 * a) for a in range(first, 4)], win[b, pl.ds(shift, BLOCK + 24), :]


def convolve(win, b, taps, flip):
    total = jnp.zeros((BLOCK, LANES), F32)
    for shift in range(8):
        steps, rows = shifted(win, b, shift)
        for k, at in steps:
            row = TAPS - 1 - k if flip else k
            total = total + taps[row : row + 1, :] * rows[at : at + BLOCK]
    return total


def valid_rows(fill, b):
    return lax.broadcasted_iota(jnp.int32, (BLOCK, LANES), 0) < fill[b]


def forward_kernel(same, fill, units, before, after, taps, activated, slope, win):
    fill_windows(win, units, before, after, same)

    def step(b, carry):
        conv = convolve(win, b, taps, False)
        q = jax.nn.sigmoid(conv)
        valid = valid_rows(fill, b)
        rows = pl.ds(pl.multiple_of(b * BLOCK, BLOCK), BLOCK)
        activated[rows, :] = jnp.where(valid, conv * q, 0.0).astype(BF16)
        slope[rows, :] = jnp.where(valid, q + conv * q * (1.0 - q), 0.0)
        return carry

    lax.fori_loop(0, win.shape[0], step, 0)


def taps_kernel(same, units, before, after, grad_conv, out, win, sums):
    fill_windows(win, units, before, after, same)
    sums[...] = jnp.zeros_like(sums)

    def step(b, carry):
        grad = grad_conv[pl.ds(pl.multiple_of(b * BLOCK, BLOCK), BLOCK), :]
        for shift in range(8):
            steps, rows = shifted(win, b, shift)
            for k, at in steps:
                terms = (rows[at : at + BLOCK] * grad).reshape(BLOCK // 8, 8, LANES)
                sums[k] += jnp.sum(terms, axis=0)
        return carry

    lax.fori_loop(0, win.shape[0], step, 0)
    out[...] = jnp.sum(sums[...], axis=1)


def backward_kernel(same, fill, grad_conv, before, after, taps, value, gate, out, win):
    fill_windows(win, grad_conv, before, after, same)

    def step(b, carry):
        grad_units = jnp.where(valid_rows(fill, b), convolve(win, b, taps, True), 0.0)
        rows = pl.ds(pl.multiple_of(b * BLOCK, BLOCK), BLOCK)
        s = gate[rows, :]
        grad_value = grad_units * s
        out[0, rows, :] = grad_value.astype(BF16)
        out[1, rows, :] = (grad_value * value[rows, :] * (1.0 - s)).astype(BF16)
        return carry

    lax.fori_loop(0, win.shape[0], step, 0)


def normed_kernel(late, weights, frames, mean, inv, out, gain):
    contract = (((1,), (1,)), ((), ()))
    part = lax.dot_general(late[0], weights[0], contract, preferred_element_type=F32)
    part = part + lax.dot_general(late[1], weights[1], contract, preferred_element_type=F32)
    out[...] = part.astype(BF16)
    unit = (frames[...].astype(F32) - mean[...]) * inv[...]
    gain[...] = jnp.sum(part * unit, axis=0, keepdims=True)


def pair_kernel(left, left_peer, right, right_peer, out):
    total = jnp.dot(left[...], right[...], preferred_element_type=F32)
    total = total + jnp.dot(left_peer[...], right_peer[...], preferred_element_type=F32)
    out[...] = total.astype(BF16)


def smem():
    return pl.BlockSpec(memory_space=pltpu.SMEM)


def lanes(rows):
    return pl.BlockSpec((rows, LANES), lambda c: (0, c))


def convolved(same, fill, units, before, after, taps):
    count, width = units.shape
    return pl.pallas_call(
        forward_kernel,
        grid=(width // LANES,),
        in_specs=[smem(), smem(), lanes(count), lanes(HALO), lanes(HALO), lanes(TAPS)],
        out_specs=[lanes(count), lanes(count)],
        out_shape=[
            jax.ShapeDtypeStruct((count, width), BF16),
            jax.ShapeDtypeStruct((count, width), F32),
        ],
        scratch_shapes=[pltpu.VMEM((count // BLOCK, BLOCK + 2 * HALO, LANES), F32)],
        compiler_params=params(),
        cost_estimate=cost(2 * TAPS * count * width, 8 * count * width, count * width),
        name="conv_forward",
    )(same, fill, units, before, after, taps)


def tap_sums(same, units, before, after, grad_conv):
    count, width = units.shape
    return pl.pallas_call(
        taps_kernel,
        grid=(width // LANES,),
        in_specs=[smem(), lanes(count), lanes(HALO), lanes(HALO), lanes(count)],
        out_specs=lanes(32),
        out_shape=jax.ShapeDtypeStruct((32, width), F32),
        scratch_shapes=[
            pltpu.VMEM((count // BLOCK, BLOCK + 2 * HALO, LANES), F32),
            pltpu.VMEM((32, 8, LANES), F32),
        ],
        compiler_params=params(),
        cost_estimate=cost(2 * TAPS * count * width, 6 * count * width),
        name="tap_gradients",
    )(same, units, before, after, grad_conv)


def projected_back(same, fill, grad_conv, before, after, taps, value, gate):
    count, width = grad_conv.shape
    return pl.pallas_call(
        backward_kernel,
        grid=(width // LANES,),
        in_specs=[
            smem(),
            smem(),
            lanes(count),
            lanes(HALO),
            lanes(HALO),
            lanes(TAPS),
            lanes(count),
            lanes(count),
        ],
        out_specs=pl.BlockSpec((2, count, LANES), lambda c: (0, 0, c)),
        out_shape=jax.ShapeDtypeStruct((2, count, width), BF16),
        scratch_shapes=[pltpu.VMEM((count // BLOCK, BLOCK + 2 * HALO, LANES), F32)],
        compiler_params=params(),
        cost_estimate=cost(2 * TAPS * count * width, 16 * count * width),
        name="conv_backward",
    )(same, fill, grad_conv, before, after, taps, value, gate)


def normed_back(late, weights, frames, mean, inv):
    count, features = frames.shape
    width = late.shape[2]
    step = 256
    return pl.pallas_call(
        normed_kernel,
        grid=(features // step,),
        in_specs=[
            pl.BlockSpec((2, count, width), lambda d: (0, 0, 0)),
            pl.BlockSpec((2, step, width), lambda d: (0, d, 0)),
            pl.BlockSpec((count, step), lambda d: (0, d)),
            pl.BlockSpec((count, 1), lambda d: (0, 0)),
            pl.BlockSpec((count, 1), lambda d: (0, 0)),
        ],
        out_specs=[
            pl.BlockSpec((count, step), lambda d: (0, d)),
            pl.BlockSpec((1, step), lambda d: (0, d)),
        ],
        out_shape=[
            jax.ShapeDtypeStruct((count, features), BF16),
            jax.ShapeDtypeStruct((1, features), F32),
        ],
        compiler_params=params(),
        cost_estimate=cost(4 * count * width * features, 4 * (count + width) * features),
        name="normed_gradient",
    )(late, weights, frames, mean, inv)


def pair_product(left, left_peer, right, right_peer, step):
    rows, count = left.shape
    groups, _, width = right.shape
    halves = width // step
    spec = pl.BlockSpec((None, count, step), lambda i: (i // halves, 0, i % halves))
    whole = pl.BlockSpec((rows, count), lambda i: (0, 0))
    return pl.pallas_call(
        pair_kernel,
        grid=(groups * halves,),
        in_specs=[whole, whole, spec, spec],
        out_specs=pl.BlockSpec((rows, step), lambda i: (0, i)),
        out_shape=jax.ShapeDtypeStruct((rows, groups * width), BF16),
        compiler_params=params(),
        cost_estimate=cost(
            4 * rows * count * groups * width, 4 * count * (rows + groups * width) + 2 * rows * groups * width
        ),
        name="weight_gradient",
    )(left, left_peer, right, right_peer)


def row_table():
    table = np.zeros((2, 1280), np.int32)
    at = 0
    for half in range(2):
        for y in range(4):
            for z in range(4):
                for xl in range(2):
                    for r in range(20):
                        for core in range(2):
                            owner = core if half else 1 - core
                            table[core, at] = ((xl * 4 + y) * 2 + owner) * 80 + z * 20 + r
                        at += 1
    return table


def picked(selection, array):
    contract = (((1,), (1,)), ((), ()))
    return lax.dot_general(selection, array, contract, preferred_element_type=F32).astype(BF16)


def finish_rows(summed, xl):
    own = lax.dynamic_index_in_dim(summed, xl, 0, keepdims=False)
    other = lax.dynamic_index_in_dim(summed, 1 - xl, 0, keepdims=False)
    return own + swap(other, "xl")


def body(frames, returned, norm_gain, weight_in, kernel, weight_out, block_utt, block_fill):
    count = frames.shape[0]
    width = weight_in.shape[2]
    blocks = count // BLOCK
    core, xl = lax.axis_index("core"), lax.axis_index("xl")
    first_block = lax.axis_index(FRAMES) * blocks
    arrived = lax.all_to_all(returned, "section", split_axis=0, concat_axis=1, tiled=True)

    edge = jnp.full((1,), -1, jnp.int32)
    padded_utt = jnp.concatenate([edge, block_utt, edge])
    near_utt = lax.dynamic_slice(padded_utt, (first_block,), (blocks + 2,))
    same = (near_utt[1:] == near_utt[:-1]).astype(jnp.int32)
    fill = lax.dynamic_slice(block_fill, (first_block,), (blocks,))
    valid_frame = (jnp.arange(BLOCK, dtype=jnp.int32)[None, :] < fill[:, None]).reshape(-1)

    as_float = frames.astype(F32)
    mean = jnp.mean(as_float, axis=1, keepdims=True)
    center = as_float - mean
    inv_scale = lax.rsqrt(jnp.mean(center * center, axis=1, keepdims=True) + EPSILON)
    normed = (center * inv_scale * norm_gain).astype(BF16)
    value_proj = jnp.dot(normed, weight_in[0], preferred_element_type=F32)
    gate_proj = jnp.dot(normed, weight_in[1], preferred_element_type=F32)
    gate_sigmoid = jax.nn.sigmoid(gate_proj)
    gated_units = jnp.where(valid_frame[:, None], value_proj * gate_sigmoid, 0.0).astype(BF16)
    units_before, units_after = halos(gated_units)

    order = lax.dynamic_index_in_dim(jnp.asarray(row_table()), core, 0, keepdims=False)
    columns = lax.broadcasted_iota(jnp.int32, (1280, 1280), 1)
    selection = (order[:, None] == columns).astype(BF16)
    normed_t = picked(selection, normed)

    activated, slope = convolved(same, fill, gated_units, units_before, units_after, kernel)
    activated_peer = swap(activated, "core")
    normed_peer = swap(normed_t[:640], "core")

    grad_activated = lax.dot_general(
        arrived, weight_out, (((1,), (1,)), ((), ())), preferred_element_type=F32
    )
    grad_conv = grad_activated * slope
    conv_before, conv_after = halos(grad_conv)
    rows_t = picked(selection, arrived)
    rows_peer = swap(rows_t[:640], "core")
    taps_part = tap_sums(same, gated_units, units_before, units_after, grad_conv)
    out_part = pair_product(
        rows_t[640:], rows_peer, activated[None], activated_peer[None], width
    )
    out_send = jnp.concatenate(
        [
            out_part.reshape(16, 40, width),
            taps_part.astype(BF16).reshape(16, 2, width),
            jnp.zeros((16, 6, width), BF16),
        ],
        axis=1,
    )
    out_got = lax.all_to_all(out_send, PLANE, 0, 0)
    out_sum = jnp.sum(out_got.astype(F32), axis=0)
    grad_out = finish_rows(out_sum[:40].reshape(2, 20, width), xl).T

    late = projected_back(
        same, fill, grad_conv, conv_before, conv_after, kernel, value_proj, gate_sigmoid
    )
    late_peer = swap(late, "core")
    sent, gain_part = normed_back(late, weight_in, frames, mean, inv_scale)
    other = swap(sent, "tensor")
    in_part = pair_product(normed_t[640:], normed_peer, late, late_peer, width)
    in_got = lax.all_to_all(in_part.reshape(16, 40, 2 * width), PLANE, 0, 0)
    in_sum = finish_rows(jnp.sum(in_got.astype(F32), axis=0).reshape(2, 20, 2 * width), xl)
    grad_in = jnp.stack([in_sum[:, :width], in_sum[:, width:]])

    tap_rows = out_sum[40:42].reshape(1, 2 * width)
    small = jnp.concatenate([tap_rows, gain_part], axis=1).astype(BF16)
    small = lax.all_to_all(jnp.broadcast_to(small, (128, small.shape[1])), EVERY, 0, 0)
    grad_gain = jnp.sum(small[:, 2 * width :].astype(F32), axis=0)
    tensor = lax.axis_index("tensor")
    tap_shares = small[:, : 2 * width].reshape(2, 4, 2, 2, 4, 2, width)
    tap_shares = lax.dynamic_index_in_dim(tap_shares, tensor, 3, keepdims=False)
    grad_kernel = jnp.sum(tap_shares.astype(F32), axis=(0, 2)).reshape(32, width)[:TAPS]

    grad_normed = sent.astype(F32) + other.astype(F32)
    scaled_grad = grad_normed * norm_gain
    unit_frames = center * inv_scale
    norm_back = inv_scale * (
        scaled_grad
        - jnp.mean(scaled_grad, axis=1, keepdims=True)
        - unit_frames * jnp.mean(scaled_grad * unit_frames, axis=1, keepdims=True)
    )
    grad_frames = (arrived.astype(F32) + norm_back).astype(BF16)
    return (grad_frames, grad_in, grad_out, grad_kernel, grad_gain)


def solution(mesh):
    split = Mesh(
        np.asarray(mesh.devices).reshape(2, 4, 2, 2, 4), ("xl", "y", "core", "tensor", "section")
    )
    outer = ("xl", "y", "core")
    in_specs = (
        P(FRAMES, None),
        P(outer, "section"),
        P(),
        P(None, None, "tensor"),
        P(None, "tensor"),
        P("tensor", None),
        P(),
        P(),
    )
    out_specs = (
        P(FRAMES, None),
        P(None, FRAMES, "tensor"),
        P("tensor", FRAMES),
        P(None, "tensor"),
        P(),
    )
    return jax.shard_map(body, mesh=split, in_specs=in_specs, out_specs=out_specs, check_vma=False)
```

time: 246 us -> 175 us (0.71)
  other arithmetic: 80.8 us -> 21 us
  waiting for transfers between devices: 66.3 us -> 27.7 us
  Pallas kernels: 0 us -> 27.5 us
  local copies, waits for them, and re-layouts: 23.9 us -> 39.1 us
  matrix products: 20.3 us -> 13.3 us
  starting transfers between devices: 49.6 us -> 42.6 us
    convert_element_type x4 -> x2, other arithmetic: 48.9 us -> 0.7 us  [the longest x1 0.62 us: body(): taps_part.astype(BF16).reshape(16, 2, width)]
    pallas_call x0 -> x6, Pallas kernels: none -> 27.5 us  [the longest x2 6.69 us: pair_product(): pl.pallas_call(pair_kernel, grid=(groups * halves,), in_specs=[whole, who...]
    all_to_all x4 -> x3, waiting for transfers between devices: 41.3 us -> 20 us  [the longest x1 9.77 us: body(): in_got = lax.all_to_all(in_part.reshape(16, 40, 2 * width), PLANE, 0, 0)]
    unnamed x51 -> x94, local copies, waits for them, and re-layouts: 4.05 us -> 24.7 us
    ppermute x4 -> x7, waiting for transfers between devices: 20.2 us -> 3.62 us  [swap(): return lax.ppermute(value, axis, [(0, 1), (1, 0)])]
    reduce_sum x7 -> x5, other arithmetic: 13.9 us -> 4.09 us  [the longest x1 1.68 us: body(): jnp.sum(in_got.astype(F32), axis=0).reshape(2, 20, 2 * width)]
    dot_general x7 -> x3, matrix products: 14.9 us -> 8.01 us  [the longest x2 5.33 us: picked(): lax.dot_general(selection, array, contract, preferred_element_type=F32)]
    broadcast_in_dim x0 -> x1, other arithmetic: none -> 6.42 us  [body(): jnp.broadcast_to(small, (128, small.shape[1]))]
  transfers between devices with their start and end apart: 13 -> 15, of which waited for: 7 -> 6; matrix products, arithmetic and copies ran while one was open for 26% -> 30% of each run, Pallas kernels for 0% -> 16%
where the time goes in v2:
time: 175 us; the launch traced here: 173 us
  starting transfers between devices  42.6 us (24%)
  local copies, waits for them, and re-layouts  39.1 us (22%)
  waiting for transfers between devices  27.7 us (16%)
  Pallas kernels  27.5 us (16%)
  other arithmetic  21 us (12%)
  matrix products  13.3 us (8%)
    unnamed x94, local copies, waits for them, and re-layouts  24.7 us
    all_to_all x1, waiting for transfers between devices, body(): in_got = lax.all_to_all(in_part.reshape(16, 40, 2 * width), PLANE, 0, 0)  9.77 us
    ppermute x2, starting transfers between devices, halos(): before = lax.ppermute(shard[shard.shape[0] - HALO:], FRAMES, up)  8.68 us
    all_to_all x1, starting transfers between devices, body(): lax.all_to_all(jnp.broadcast_to(small, (128, small.shape[1])), EVERY, 0, 0)  7.82 us
    all_to_all x1, starting transfers between devices, body(): out_got = lax.all_to_all(out_send, PLANE, 0, 0)  7.47 us
    pallas_call x2, Pallas kernels, pair_product(): pl.pallas_call(pair_kernel, grid=(groups * halves,), in_specs=[whole, who...  6.69 us
    pallas_call x1, Pallas kernels, normed_back(): pl.pallas_call(normed_kernel, grid=(features // step,), in_specs=[pl.Bloc...  6.45 us
    broadcast_in_dim x1, other arithmetic, body(): jnp.broadcast_to(small, (128, small.shape[1]))  6.42 us
  transfers between devices with their start and end apart: 15, of which 6 were waited for; matrix products, arithmetic and copies ran while one was open for 30% of the time, Pallas kernels for 16%

profile of v2, /device:TPU:0, one launch (start us, length us, event | category | flops | bytes accessed | tf_op | source)
XLA Modules:
  0.0 172.6 jit_solution(9270092557038546726)
XLA Ops:
  0.6 2.6 %copy.34 = bf16[40,4,8,512]{3,2,0,1:T(8,128)(2,1)} copy(bf16[40,4,8,512]{3,2,1,0:T(8,128)(2,1)} %bitcast.59) | data formatting | bytes 2621440 | tf_op jit(solution)/shard_map/all_to_all | solution.py:287
  3.3 5.5 %all-to-all-start = ((bf16[4,512,320]{1,2,0:T(8,128)(2,1)}), bf16[4,512,320]{1,2,0:T(8,128)(2,1)}, u32[]{:S(2)}, u32[]{:S(2)}) async-start(bf16[4,512,320]{1,2,0:T(8,128)(2,1)} %bitcast.56), calls=%async_computation | async-start | bytes 2621440 | tf_op jit(solution)/shard_map/all_to_all | solution.py:287
  9.7 2.9 %fusion.34.gate = f32[512,640]{1,0:T(8,128)S(1)} fusion(bf16[2,1280,640]{2,1,0:T(8,128)(2,1)} %weights.1, bf16[512,1280]{1,0:T(8,128)(2,1)S(1)} %copy-done.1, f32[1280]{0:T(1024)S(1)} %copy-done.36, f32[512]{0:T(512)S(1)} %add_rsqrt_fusion, f32[512]{0:T(512)S(1)} %broadcast_multiply_fusion.2), kind=kOutput, calls=%fused_computation.36 | convolution fusion | flops 843120640 | bytes 4269056 | tf_op jit(solution)/shard_map/dot_general | solution.py:302
  12.8 2.4 %select_convert_fusion = (bf16[512,640]{1,0:T(8,128)(2,1)S(1)}, f32[512,640]{1,0:T(8,128)}) fusion(f32[512,640]{1,0:T(8,128)S(1)} %fusion.34.gate, pred[512]{0:T(512)(128)(4,1)S(1)} %fusion.38, bf16[2,1280,640]{2,1,0:T(8,128)(2,1)S(1)} %copy-done.26, bf16[512,1280]{1,0:T(8,128)(2,1)S(1)} %copy-done.1, f32[1280]{0:T(1024)S(1)} %copy-done.36, ...), kind=kOutput, calls=%fused_computation.35 | convolution fusion | flops 843120640 | bytes 6238720 | tf_op jit(solution)/shard_map/dot_general | solution.py:301
  15.2 0.9 copy-done.5
  16.0 3.9 %collective-permute-start = (bf16[16,640]{1,0:T(8,128)(2,1)S(1)}, bf16[16,640]{1,0:T(8,128)(2,1)S(1)}, u32[]{:S(2)}, u32[]{:S(2)}) collective-permute-start(bf16[16,640]{1,0:T(8,128)(2,1)S(1)} %get-tuple-element.37), channel_id=1, source_target_pairs={{0,1},{1,2},{2,3},{3,8},{8,9},{9,10},{10,11},{11,16},{16,17},{17,1... | collective-permute-start | bytes 61448 | tf_op jit(solution)/shard_map/ppermute | solution.py:42
  20.0 1.3 collective-permute-start.1
  21.5 1.9 %collective-permute-done.before = bf16[16,640]{1,0:T(8,128)(2,1)S(1)} collective-permute-done((bf16[16,640]{1,0:T(8,128)(2,1)S(1)}, bf16[16,640]{1,0:T(8,128)(2,1)S(1)}, u32[]{:S(2)}, u32[]{:S(2)}) %collective-permute-start) | collective-permute-done | bytes 20512 | tf_op jit(solution)/shard_map/ppermute | solution.py:42
  23.5 2.2 %collective-permute-done.1.after = bf16[16,640]{1,0:T(8,128)(2,1)S(1)} collective-permute-done((bf16[16,640]{1,0:T(8,128)(2,1)S(1)}, bf16[16,640]{1,0:T(8,128)(2,1)S(1)}, u32[]{:S(2)}, u32[]{:S(2)}) %collective-permute-start.1) | collective-permute-done | bytes 20512 | tf_op jit(solution)/shard_map/ppermute | solution.py:43
  25.6 1.1 copy-done.6
  26.7 5.2 %conv_forward.1 = (bf16[512,640]{1,0:T(8,128)(2,1)}, f32[512,640]{1,0:T(8,128)S(1)}) custom-call(s32[5]{0:T(128)S(1)} %compare_convert_fusion.same, s32[4]{0:T(128)S(1)} %dynamic_slice.29.fill, bf16[512,640]{1,0:T(8,128)(2,1)S(1)} %copy-done.6, bf16[16,640]{1,0:T(8,128)(2,1)S(1)} %collective-permute-done.before, ...), custom_call_target="tpu_custom_call" | custom-call | flops 20316160 | bytes 2621440 | tf_op jit(solution)/shard_map/conv_forward/pallas_call | solution.py:149
  31.9 1.1 copy-done.13
  33.2 3.2 %fusion.10 = bf16[1280,512]{1,0:T(8,128)(2,1)S(1)} fusion(bf16[512,1280]{0,1:T(8,128)(2,1)} %bitcast.1, s32[1280]{0:T(1024)S(1)} %dynamic-slice_reduce_fusion), kind=kOutput, calls=%fused_computation.14 | convolution fusion | flops 1680015360 | bytes 2626560 | tf_op jit(solution)/shard_map/dot_general | solution.py:272
  36.5 1.2 fusion.42
  38.0 2.7 %fusion.46 = f32[512,640]{1,0:T(8,128)S(1)} fusion(bf16[512,1280]{0,1:T(8,128)(2,1)} %bitcast.1, bf16[640,1280]{1,0:T(8,128)(2,1)S(1)} %copy-done), kind=kOutput, calls=%fused_computation.65 | convolution fusion | flops 838860800 | bytes 4259840 | tf_op jit(solution)/shard_map/dot_general | solution.py:316
  41.5 1.1 copy-done.2
  42.6 4.8 %collective-permute-start.2 = (f32[16,640]{1,0:T(8,128)}, f32[16,640]{1,0:T(8,128)}, u32[]{:S(2)}, u32[]{:S(2)}) collective-permute-start(f32[16,640]{1,0:T(8,128)} %get-tuple-element.35), channel_id=1, source_target_pairs={{0,1},{1,2},{2,3},{3,8},{8,9},{9,10},{10,11},{11,16},{16,17},{17,1... | collective-permute-start | bytes 122888 | tf_op jit(solution)/shard_map/ppermute | solution.py:42
  47.3 1.3 collective-permute-start.3
  48.8 0.8 copy.27.mean
  49.6 0.7 pad.4.clone
  50.3 1.3 copy-done.3
  51.6 1.1 copy-done.7
  52.7 0.7 copy-done.18
  53.4 0.7 copy-done.20
  54.1 0.7 copy-done.22
  54.8 4.0 %tap_gradients.1 = f32[32,640]{1,0:T(8,128)S(1)} custom-call(s32[5]{0:T(128)S(1)} %copy-done.22, bf16[512,640]{1,0:T(8,128)(2,1)S(1)} %copy-done.7, bf16[16,640]{1,0:T(8,128)(2,1)S(1)} %copy-done.18, bf16[16,640]{1,0:T(8,128)(2,1)S(1)} %copy-done.20, f32[512,640]{1,0:T(8,128)S(1)} %copy-done.3), custom_call_target="tpu_custom_call" | custom-call | flops 20316160 | bytes 1966080 | tf_op jit(solution)/shard_map/tap_gradients/pallas_call | solution.py:167
  59.5 1.4 reshape.124
  60.9 1.3 copy-done.4
  62.2 1.3 copy-done.11
  63.5 1.3 copy-done.12
  64.8 0.7 copy-done.23
  66.1 5.2 %conv_backward.1.late.right = bf16[2,512,640]{2,1,0:T(8,128)(2,1)} custom-call(s32[5]{0:T(128)S(1)} %copy-done.23, s32[4]{0:T(128)S(1)} %copy-done.25, f32[512,640]{1,0:T(8,128)S(1)} %copy-done.4, f32[16,640]{1,0:T(8,128)} %collective-permute-done.2.before, f32[16,640]{1,0:T(8,128)} %collective-permute-done.3.after, f32[31,640]{1,0:T(8,128)S(1)} %copy-done.16, ...), custom_call_target="tpu_custom_call" | custom-call | flops 20316160 | bytes 5242880 | tf_op jit(solution)/shard_map/conv_backward/pallas_call | solution.py:185
  71.3 1.2 collective-permute-start.6
  72.6 2.7 %weight_gradient.3 = bf16[640,640]{1,0:T(8,128)(2,1)S(1)} custom-call(bf16[640,512]{1,0:T(8,128)(2,1)S(1)} %copy-done.8, bf16[640,512]{1,0:T(8,128)(2,1)} %collective-permute-done.8.left_peer, bf16[1,512,640]{2,1,0:T(8,128)(2,1)} %bitcast.13.right, bf16[1,512,640]{2,1,0:T(8,128)(2,1)} %bitcast.14.right_peer), custom_call_target="tpu_custom_call" | custom-call | flops 838860800 | bytes 3440640 | tf_op jit(solution)/shard_map/weight_gradient/pallas_call | solution.py:241
  75.3 1.2 maximum_maximum_fusion
  76.5 7.5 %all-to-all-start.2 = ((bf16[16,48,640]{2,1,0:T(8,128)(2,1)}), bf16[16,48,640]{2,1,0:T(8,128)(2,1)}, u32[]{:S(2)}, u32[]{:S(2)}) async-start(bf16[16,48,640]{2,1,0:T(8,128)(2,1)} %maximum_maximum_fusion), calls=%async_computation.2 | async-start | bytes 1966080 | tf_op jit(solution)/shard_map/all_to_all | solution.py:335
  84.0 6.4 %normed_gradient.1 = (bf16[512,1280]{1,0:T(8,128)(2,1)}, f32[1,1280]{1,0:T(1,128)S(1)}) custom-call(bf16[2,512,640]{2,1,0:T(8,128)(2,1)} %conv_backward.1.late.right, bf16[2,1280,640]{2,1,0:T(8,128)(2,1)} %weights.1, bf16[512,1280]{1,0:T(8,128)(2,1)S(1)} %copy-done.1, f32[512,1]{1,0:T(8,128)S(1)} %copy.27.mean, f32[512,1]{1,0:T(8,128)S(1)} %copy.28.inv), custom_call_target="tpu_custom_call" | custom-call | flops 1677721600 | bytes 5898240 | tf_op jit(solution)/shard_map/normed_gradient/pallas_call | solution.py:211
  90.5 2.7 %collective-permute-start.4 = (bf16[512,1280]{1,0:T(8,128)(2,1)}, bf16[512,1280]{1,0:T(8,128)(2,1)}, u32[]{:S(2)}, u32[]{:S(2)}) collective-permute-start(bf16[512,1280]{1,0:T(8,128)(2,1)} %get-tuple-element.10), channel_id=1, source_target_pairs={{0,4},{4,0},{1,5},{5,1},{2,6},{6,2},{3,7},{7,3},{8,12},{12,8},{9,1... | collective-permute-start | bytes 3932168 | tf_op jit(solution)/shard_map/ppermute | solution.py:35
  93.2 2.1 %fusion.9 = bf16[1280,512]{1,0:T(8,128)(2,1)S(1)} fusion(s32[1280]{0:T(1024)S(1)} %copy-done.40, bf16[512,1280]{1,0:T(8,128)(2,1)S(1)} %copy-done.1, f32[1280]{0:T(1024)S(1)} %copy-done.37, f32[512]{0:T(512)S(1)} %copy-done.34, f32[512]{0:T(512)S(1)} %copy-done.31), kind=kOutput, calls=%fused_computation.13 | convolution fusion | flops 1683292160 | bytes 2635776 | tf_op jit(solution)/shard_map/dot_general | solution.py:272
  95.3 1.2 fusion.43
  96.5 5.2 %all-to-all-done.2 = bf16[16,48,640]{2,1,0:T(8,128)(2,1)} async-done(((bf16[16,48,640]{2,1,0:T(8,128)(2,1)}), bf16[16,48,640]{2,1,0:T(8,128)(2,1)}, u32[]{:S(2)}, u32[]{:S(2)}) %all-to-all-start.2) | async-done | bytes 983072 | tf_op jit(solution)/shard_map/all_to_all | solution.py:335
  101.7 1.3 convert_reduce_fusion.2
  103.1 1.7 %broadcast_in_dim.40 = bf16[128,1,2560]{2,1,0:T(2,128)(2,1)} broadcast(bf16[2560]{0:T(1024)(128)(2,1)S(1)} %pad_maximum_fusion.1), dimensions={2} | broadcast | bytes 660480 | tf_op jit(solution)/shard_map/broadcast_in_dim | solution.py:352
  105.4 6.4 %reduce.5 = bf16[128,2560]{1,0:T(8,128)(2,1)} reduce(bf16[128,1,2560]{2,1,0:T(2,128)(2,1)} %broadcast_in_dim.40, bf16[]{:T(256)} %broadcast.73), dimensions={1}, to_apply=%broadcast_in_dim.40.reduce_sub_computation | reduce | bytes 1310722 | tf_op jit(solution)/shard_map/broadcast_in_dim | solution.py:352
  111.8 2.7 %reshape.130 = bf16[128,2,1280]{2,1,0:T(2,128)(2,1)} reshape(bf16[128,2560]{1,0:T(8,128)(2,1)} %reduce.5) | data formatting | bytes 1310720
  114.5 7.8 %all-to-all-start.3 = ((bf16[128,2,1280]{2,1,0:T(2,128)(2,1)}), bf16[128,2,1280]{2,1,0:T(2,128)(2,1)}, u32[]{:S(2)}, u32[]{:S(2)}) async-start(bf16[128,2,1280]{2,1,0:T(2,128)(2,1)} %reshape.130), calls=%async_computation.3 | async-start | bytes 1310720 | tf_op jit(solution)/shard_map/all_to_all | solution.py:352
  122.4 2.4 %copy.26 = bf16[512,1280]{1,0:T(8,128)(2,1)} copy(bf16[512,1280]{0,1:T(8,128)(2,1)} %bitcast.1) | data formatting | bytes 2621440 | tf_op jit(solution)/shard_map/all_to_all | solution.py:287
  124.8 1.1 copy-done.15
  125.9 4.0 %weight_gradient.2 = bf16[640,1280]{1,0:T(8,128)(2,1)S(1)} custom-call(bf16[640,512]{1,0:T(8,128)(2,1)S(1)} %copy-done.15, bf16[640,512]{1,0:T(8,128)(2,1)} %collective-permute-done.5.left_peer, bf16[2,512,640]{2,1,0:T(8,128)(2,1)} %conv_backward.1.late.right, bf16[2,512,640]{2,1,0:T(8,128)(2,1)} %collective-permute-done.6.right_peer), custom_call_target="tpu_custom_call" | custom-call | flops 1677721600 | bytes 5570560 | tf_op jit(solution)/shard_map/weight_gradient/pallas_call | solution.py:241
  129.9 1.2 copy-done.9
  131.1 5.0 %all-to-all-done.3 = bf16[128,2,1280]{2,1,0:T(2,128)(2,1)} async-done(((bf16[128,2,1280]{2,1,0:T(2,128)(2,1)}), bf16[128,2,1280]{2,1,0:T(2,128)(2,1)}, u32[]{:S(2)}, u32[]{:S(2)}) %all-to-all-start.3) | async-done | bytes 655392 | tf_op jit(solution)/shard_map/all_to_all | solution.py:352
  136.1 4.5 %all-to-all-start.1 = ((bf16[16,40,1280]{2,1,0:T(8,128)(2,1)}), bf16[16,40,1280]{2,1,0:T(8,128)(2,1)}, u32[]{:S(2)}, u32[]{:S(2)}) async-start(bf16[16,40,1280]{2,1,0:T(8,128)(2,1)} %bitcast.55), calls=%async_computation.1 | async-start | bytes 3276800 | tf_op jit(solution)/shard_map/all_to_all | solution.py:346
  140.7 2.7 %fusion.18 = (f32[512]{0:T(512)S(1)}, f32[512]{0:T(512)S(1)}) fusion(bf16[512,1280]{1,0:T(8,128)(2,1)} %collective-permute-done.4, bf16[512,1280]{1,0:T(8,128)(2,1)} %get-tuple-element.10, f32[1280]{0:T(1024)S(1)} %copy-done.38, f32[512]{0:T(512)S(1)} %copy-done.35, f32[512]{0:T(512)S(1)} %copy-done.32, bf16[512,1280]{1,0:T(8,128)(2,1)S(1)} %copy-done.1), kind=kLoop, calls=%fused_computation.23 | loop fusion | flops 6552576 | bytes 3945472 | tf_op jit(solution)/shard_map/reduce_sum | solution.py:364
  143.5 0.9 collective-permute-start.10
  144.3 4.4 %fusion.16 = bf16[512,1280]{1,0:T(8,128)(2,1)} fusion(bf16[512,1280]{1,0:T(8,128)(2,1)S(1)} %copy-done.1, bf16[512,1280]{1,0:T(8,128)(2,1)} %copy.26, bf16[512,1280]{1,0:T(8,128)(2,1)} %collective-permute-done.4, bf16[512,1280]{1,0:T(8,128)(2,1)} %get-tuple-element.10, f32[512]{0:T(512)S(1)} %get-tuple-element.42, f32[512]{0:T(512)S(1)} %get-tuple-element.43, ...), kind=kLoop, calls=%fused_computation.20 | loop fusion | flops 9175040 | bytes 6566912 | tf_op jit(solution)/shard_map/convert_element_type | solution.py:367
  149.4 4.1 %reshape.131 = bf16[128,1,2560]{2,1,0:T(2,128)(2,1)S(1)} reshape(bf16[128,2,1280]{2,1,0:T(2,128)(2,1)} %all-to-all-done.3) | data formatting | bytes 1310720
  153.6 0.8 copy-done.27
  154.7 0.7 reshape.127
  155.4 9.8 %all-to-all-done.1 = bf16[16,40,1280]{2,1,0:T(8,128)(2,1)} async-done(((bf16[16,40,1280]{2,1,0:T(8,128)(2,1)}), bf16[16,40,1280]{2,1,0:T(8,128)(2,1)}, u32[]{:S(2)}, u32[]{:S(2)}) %all-to-all-start.1) | async-done | bytes 1638432 | tf_op jit(solution)/shard_map/all_to_all | solution.py:346
  165.1 1.7 convert_reduce_fusion
  166.9 0.7 collective-permute-start.7
  167.6 0.7 convert_reduce_fusion.3
  168.2 3.6 %collective-permute-done.7 = f32[20,1280]{1,0:T(8,128)S(1)} collective-permute-done((f32[20,1280]{1,0:T(8,128)S(1)}, f32[20,1280]{1,0:T(8,128)S(1)}, u32[]{:S(2)}, u32[]{:S(2)}) %collective-permute-start.7) | collective-permute-done | bytes 102432 | tf_op jit(solution)/shard_map/ppermute | solution.py:35
  171.9 0.7 copy.29
  (121 shorter events, 5.7 us)
Async XLA Ops:
  0.6 37.4 %copy-start = (bf16[640,1280]{1,0:T(8,128)(2,1)S(1)}, bf16[640,1280]{1,0:T(8,128)(2,1)}, u32[]{:S(2)}) copy-start(bf16[640,1280]{1,0:T(8,128)(2,1)} %param.14) | copy-start | bytes 4915204
  3.3 5.5 %copy-start.44 = (s32[256]{0:T(256)S(1)}, s32[256]{0:T(256)}, u32[]{:S(2)}) copy-start(s32[256]{0:T(256)} %param.16) | copy-start | bytes 3076
  3.3 5.7 %copy-start.1 = (bf16[512,1280]{1,0:T(8,128)(2,1)S(1)}, bf16[512,1280]{1,0:T(8,128)(2,1)}, u32[]{:S(2)}) copy-start(bf16[512,1280]{1,0:T(8,128)(2,1)} %frames.1) | copy-start | bytes 3932164
  3.3 30.0 %all-to-all-start = ((bf16[4,512,320]{1,2,0:T(8,128)(2,1)}), bf16[4,512,320]{1,2,0:T(8,128)(2,1)}, u32[]{:S(2)}, u32[]{:S(2)}) async-start(bf16[4,512,320]{1,2,0:T(8,128)(2,1)} %bitcast.56), calls=%async_computation | async-start | bytes 2621440 | tf_op jit(solution)/shard_map/all_to_all | solution.py:287
  8.8 0.9 copy-start.36
  8.9 16.8 %copy-start.24 = (s32[4]{0:T(128)}, s32[4]{0:T(128)S(1)}, u32[]{:S(2)}) copy-start(s32[4]{0:T(128)S(1)} %dynamic_slice.29.fill) | copy-start | bytes 52
  9.2 3.5 %copy-start.30 = (f32[512]{0:T(512)}, f32[512]{0:T(512)S(1)}, u32[]{:S(2)}) copy-start(f32[512]{0:T(512)S(1)} %broadcast_multiply_fusion.2) | copy-start | bytes 6148
  9.7 38.9 %copy-start.33 = (f32[512]{0:T(512)}, f32[512]{0:T(512)S(1)}, u32[]{:S(2)}) copy-start(f32[512]{0:T(512)S(1)} %add_rsqrt_fusion) | copy-start | bytes 6148
  9.7 3.0 %copy-start.26 = (bf16[2,1280,640]{2,1,0:T(8,128)(2,1)S(1)}, bf16[2,1280,640]{2,1,0:T(8,128)(2,1)}, u32[]{:S(2)}) copy-start(bf16[2,1280,640]{2,1,0:T(8,128)(2,1)} %weights.1) | copy-start | bytes 9830404
  12.7 2.4 %copy-start.10 = (f32[512,640]{1,0:T(8,128)}, f32[512,640]{1,0:T(8,128)S(1)}, u32[]{:S(2)}) copy-start(f32[512,640]{1,0:T(8,128)S(1)} %fusion.34.gate) | copy-start | bytes 3932164
  12.7 8.5 %copy-start.42 = (s32[256]{0:T(256)S(1)}, s32[256]{0:T(256)}, u32[]{:S(2)}) copy-start(s32[256]{0:T(256)} %param.15) | copy-start | bytes 3076
  12.7 8.8 %copy-start.41 = (s32[2,1280]{1,0:T(2,128)S(1)}, s32[2,1280]{1,0:T(2,128)}, u32[]{:S(2)}) copy-start(s32[2,1280]{1,0:T(2,128)} %constant.75.clone) | copy-start | bytes 30724
  12.7 12.9 %copy-start.16 = (f32[31,640]{1,0:T(8,128)S(1)}, f32[31,640]{1,0:T(8,128)}, u32[]{:S(2)}) copy-start(f32[31,640]{1,0:T(8,128)} %taps.3) | copy-start | bytes 238084
  15.2 0.9 copy-start.5
  16.0 7.4 %collective-permute-start = (bf16[16,640]{1,0:T(8,128)(2,1)S(1)}, bf16[16,640]{1,0:T(8,128)(2,1)S(1)}, u32[]{:S(2)}, u32[]{:S(2)}) collective-permute-start(bf16[16,640]{1,0:T(8,128)(2,1)S(1)} %get-tuple-element.37), channel_id=1, source_target_pairs={{0,1},{1,2},{2,3},{3,8},{8,9},{9,10},{10,11},{11,16},{16,17},{17,1... | collective-permute-start | bytes 61448 | tf_op jit(solution)/shard_map/ppermute | solution.py:42
  20.0 5.7 %collective-permute-start.1 = (bf16[16,640]{1,0:T(8,128)(2,1)S(1)}, bf16[16,640]{1,0:T(8,128)(2,1)S(1)}, u32[]{:S(2)}, u32[]{:S(2)}) collective-permute-start(bf16[16,640]{1,0:T(8,128)(2,1)S(1)} %get-tuple-element.36), channel_id=1, source_target_pairs={{1,0},{2,1},{3,2},{8,3},{9,8},{10,9},{11,10},{16,11},{17,16},{18,1... | collective-permute-start | bytes 61448 | tf_op jit(solution)/shard_map/ppermute | solution.py:43
  21.5 15.0 %copy-start.21 = (s32[5]{0:T(128)}, s32[5]{0:T(128)S(1)}, u32[]{:S(2)}) copy-start(s32[5]{0:T(128)S(1)} %compare_convert_fusion.same) | copy-start | bytes 64
  21.5 15.0 %copy-start.39 = (s32[1280]{0:T(1024)}, s32[1280]{0:T(1024)S(1)}, u32[]{:S(2)}) copy-start(s32[1280]{0:T(1024)S(1)} %dynamic-slice_reduce_fusion) | copy-start | bytes 15364
  23.5 13.0 %copy-start.17 = (bf16[16,640]{1,0:T(8,128)(2,1)}, bf16[16,640]{1,0:T(8,128)(2,1)S(1)}, u32[]{:S(2)}) copy-start(bf16[16,640]{1,0:T(8,128)(2,1)S(1)} %collective-permute-done.before) | copy-start | bytes 61444
  25.6 1.1 copy-start.6
  26.7 9.8 %copy-start.19 = (bf16[16,640]{1,0:T(8,128)(2,1)}, bf16[16,640]{1,0:T(8,128)(2,1)S(1)}, u32[]{:S(2)}) copy-start(bf16[16,640]{1,0:T(8,128)(2,1)S(1)} %collective-permute-done.1.after) | copy-start | bytes 61444
  31.9 1.1 copy-start.13
  33.0 39.6 %collective-permute-start.9 = (bf16[512,640]{1,0:T(8,128)(2,1)}, bf16[512,640]{1,0:T(8,128)(2,1)}, u32[]{:S(2)}, u32[]{:S(2)}) collective-permute-start(bf16[512,640]{1,0:T(8,128)(2,1)} %get-tuple-element.11), channel_id=1, source_target_pairs={{0,8},{8,0},{1,9},{9,1},{2,10},{10,2},{3,11},{11,3},{4,12},{12,4},... | collective-permute-start | bytes 1966088 | tf_op jit(solution)/shard_map/ppermute | solution.py:35
  37.8 2.9 %copy-start.14 = (f32[512,640]{1,0:T(8,128)S(1)}, f32[512,640]{1,0:T(8,128)}, u32[]{:S(2)}) copy-start(f32[512,640]{1,0:T(8,128)} %copy-done.13) | copy-start | bytes 3932164
  37.8 34.8 %collective-permute-start.8 = (bf16[640,512]{1,0:T(8,128)(2,1)}, bf16[640,512]{1,0:T(8,128)(2,1)}, u32[]{:S(2)}, u32[]{:S(2)}) collective-permute-start(bf16[640,512]{1,0:T(8,128)(2,1)} %get-tuple-element.30), channel_id=1, source_target_pairs={{0,8},{8,0},{1,9},{9,1},{2,10},{10,2},{3,11},{11,3},{4,12},{12,4},... | collective-permute-start | bytes 1966088 | tf_op jit(solution)/shard_map/ppermute | solution.py:35
  41.5 1.1 copy-start.2
  42.6 18.3 %collective-permute-start.2 = (f32[16,640]{1,0:T(8,128)}, f32[16,640]{1,0:T(8,128)}, u32[]{:S(2)}, u32[]{:S(2)}) collective-permute-start(f32[16,640]{1,0:T(8,128)} %get-tuple-element.35), channel_id=1, source_target_pairs={{0,1},{1,2},{2,3},{3,8},{8,9},{9,10},{10,11},{11,16},{16,17},{17,1... | collective-permute-start | bytes 122888 | tf_op jit(solution)/shard_map/ppermute | solution.py:42
  47.3 13.6 %collective-permute-start.3 = (f32[16,640]{1,0:T(8,128)}, f32[16,640]{1,0:T(8,128)}, u32[]{:S(2)}, u32[]{:S(2)}) collective-permute-start(f32[16,640]{1,0:T(8,128)} %get-tuple-element.34), channel_id=1, source_target_pairs={{1,0},{2,1},{3,2},{8,3},{9,8},{10,9},{11,10},{16,11},{17,16},{18,1... | collective-permute-start | bytes 122888 | tf_op jit(solution)/shard_map/ppermute | solution.py:43
  50.3 1.3 copy-start.3
  51.6 1.1 copy-start.7
  52.7 0.7 copy-start.18
  53.4 0.7 copy-start.20
  54.1 0.7 copy-start.22
  60.9 1.3 copy-start.4
  62.2 1.3 copy-start.11
  63.5 1.3 copy-start.12
  64.8 0.7 copy-start.23
  65.5 0.6 copy-start.25
  66.1 6.5 %copy-start.8 = (bf16[640,512]{1,0:T(8,128)(2,1)S(1)}, bf16[640,512]{1,0:T(8,128)(2,1)}, u32[]{:S(2)}) copy-start(bf16[640,512]{1,0:T(8,128)(2,1)} %get-tuple-element.31.left) | copy-start | bytes 1966084
  71.3 53.5 %collective-permute-start.6 = (bf16[2,512,640]{2,1,0:T(8,128)(2,1)}, bf16[2,512,640]{2,1,0:T(8,128)(2,1)}, u32[]{:S(2)}, u32[]{:S(2)}) collective-permute-start(bf16[2,512,640]{2,1,0:T(8,128)(2,1)} %conv_backward.1.late.right), channel_id=1, source_target_pairs={{0,8},{8,0},{1,9},{9,1},{2,10},{10,2},{3,11},{11,3},{4,12},{12,4},... | collective-permute-start | bytes 3932168 | tf_op jit(solution)/shard_map/ppermute | solution.py:35
  72.6 2.7 %copy-start.29 = (bf16[16,2,640]{2,1,0:T(2,128)(2,1)S(1)}, bf16[16,2,640]{2,1,0:T(2,128)(2,1)}, u32[]{:S(2)}) copy-start(bf16[16,2,640]{2,1,0:T(2,128)(2,1)} %reshape.124) | copy-start | bytes 122884
  72.6 2.7 %copy-start.43 = (bf16[48]{0:T(256)(128)(2,1)S(1)}, bf16[48]{0:T(256)(128)(2,1)}, u32[]{:S(2)}) copy-start(bf16[48]{0:T(256)(128)(2,1)} %pad.4.clone) | copy-start | bytes 292
  76.5 25.2 %all-to-all-start.2 = ((bf16[16,48,640]{2,1,0:T(8,128)(2,1)}), bf16[16,48,640]{2,1,0:T(8,128)(2,1)}, u32[]{:S(2)}, u32[]{:S(2)}) async-start(bf16[16,48,640]{2,1,0:T(8,128)(2,1)} %maximum_maximum_fusion), calls=%async_computation.2 | async-start | bytes 1966080 | tf_op jit(solution)/shard_map/all_to_all | solution.py:335
  84.0 9.2 %copy-start.31 = (f32[512]{0:T(512)S(1)}, f32[512]{0:T(512)}, u32[]{:S(2)}) copy-start(f32[512]{0:T(512)} %copy-done.30) | copy-start | bytes 6148
  84.0 9.2 %copy-start.34 = (f32[512]{0:T(512)S(1)}, f32[512]{0:T(512)}, u32[]{:S(2)}) copy-start(f32[512]{0:T(512)} %copy-done.33) | copy-start | bytes 6148
  84.0 9.2 %copy-start.37 = (f32[1280]{0:T(1024)S(1)}, f32[1280]{0:T(1024)}, u32[]{:S(2)}) copy-start(f32[1280]{0:T(1024)} %param.11) | copy-start | bytes 15364
  84.0 9.2 %copy-start.40 = (s32[1280]{0:T(1024)S(1)}, s32[1280]{0:T(1024)}, u32[]{:S(2)}) copy-start(s32[1280]{0:T(1024)} %copy-done.39) | copy-start | bytes 15364
  90.5 50.2 %collective-permute-start.4 = (bf16[512,1280]{1,0:T(8,128)(2,1)}, bf16[512,1280]{1,0:T(8,128)(2,1)}, u32[]{:S(2)}, u32[]{:S(2)}) collective-permute-start(bf16[512,1280]{1,0:T(8,128)(2,1)} %get-tuple-element.10), channel_id=1, source_target_pairs={{0,4},{4,0},{1,5},{5,1},{2,6},{6,2},{3,7},{7,3},{8,12},{12,8},{9,1... | collective-permute-start | bytes 3932168 | tf_op jit(solution)/shard_map/ppermute | solution.py:35
  96.5 28.3 %collective-permute-start.5 = (bf16[640,512]{1,0:T(8,128)(2,1)}, bf16[640,512]{1,0:T(8,128)(2,1)}, u32[]{:S(2)}, u32[]{:S(2)}) collective-permute-start(bf16[640,512]{1,0:T(8,128)(2,1)} %get-tuple-element.32), channel_id=1, source_target_pairs={{0,8},{8,0},{1,9},{9,1},{2,10},{10,2},{3,11},{11,3},{4,12},{12,4},... | collective-permute-start | bytes 1966088 | tf_op jit(solution)/shard_map/ppermute | solution.py:35
  114.5 21.6 %all-to-all-start.3 = ((bf16[128,2,1280]{2,1,0:T(2,128)(2,1)}), bf16[128,2,1280]{2,1,0:T(2,128)(2,1)}, u32[]{:S(2)}, u32[]{:S(2)}) async-start(bf16[128,2,1280]{2,1,0:T(2,128)(2,1)} %reshape.130), calls=%async_computation.3 | async-start | bytes 1310720 | tf_op jit(solution)/shard_map/all_to_all | solution.py:352
  124.8 1.1 copy-start.15
  129.9 1.2 copy-start.9
  136.1 4.6 %copy-start.32 = (f32[512]{0:T(512)S(1)}, f32[512]{0:T(512)}, u32[]{:S(2)}) copy-start(f32[512]{0:T(512)} %copy-done.30) | copy-start | bytes 6148
  136.1 4.6 %copy-start.35 = (f32[512]{0:T(512)S(1)}, f32[512]{0:T(512)}, u32[]{:S(2)}) copy-start(f32[512]{0:T(512)} %copy-done.33) | copy-start | bytes 6148
  136.1 4.6 %copy-start.38 = (f32[1280]{0:T(1024)S(1)}, f32[1280]{0:T(1024)}, u32[]{:S(2)}) copy-start(f32[1280]{0:T(1024)} %param.11) | copy-start | bytes 15364
  136.1 29.0 %all-to-all-start.1 = ((bf16[16,40,1280]{2,1,0:T(8,128)(2,1)}), bf16[16,40,1280]{2,1,0:T(8,128)(2,1)}, u32[]{:S(2)}, u32[]{:S(2)}) async-start(bf16[16,40,1280]{2,1,0:T(8,128)(2,1)} %bitcast.55), calls=%async_computation.1 | async-start | bytes 3276800 | tf_op jit(solution)/shard_map/all_to_all | solution.py:346
  143.5 5.3 %collective-permute-start.10 = (f32[20,640]{1,0:T(8,128)S(1)}, f32[20,640]{1,0:T(8,128)S(1)}, u32[]{:S(2)}, u32[]{:S(2)}) collective-permute-start(f32[20,640]{1,0:T(8,128)S(1)} %dynamic-slice_bitcast_fusion.1), channel_id=1, source_target_pairs={{0,64},{64,0},{1,65},{65,1},{2,66},{66,2},{3,67},{67,3},{4,68},{68... | collective-permute-start | bytes 153608 | tf_op jit(solution)/shard_map/ppermute | solution.py:35
  153.6 0.8 copy-start.27
  154.5 13.1 %copy-start.28 = (bf16[128,1,2560]{2,0,1:T(8,128)(2,1)S(1)}, bf16[128,1,2560]{2,0,1:T(8,128)(2,1)}, u32[]{:S(2)}) copy-start(bf16[128,1,2560]{2,0,1:T(8,128)(2,1)} %copy-done.27) | copy-start | bytes 1966084
  166.9 5.0 %collective-permute-start.7 = (f32[20,1280]{1,0:T(8,128)S(1)}, f32[20,1280]{1,0:T(8,128)S(1)}, u32[]{:S(2)}, u32[]{:S(2)}) collective-permute-start(f32[20,1280]{1,0:T(8,128)S(1)} %dynamic-slice_bitcast_fusion), channel_id=1, source_target_pairs={{0,64},{64,0},{1,65},{65,1},{2,66},{66,2},{3,67},{67,3},{4,68},{68... | collective-permute-start | bytes 307208 | tf_op jit(solution)/shard_map/ppermute | solution.py:35

commit v3 on v2

v3 whole, which is shorter than its diff:
```python
import functools

import jax
import jax.numpy as jnp
import numpy as np
from jax import lax
from jax.experimental import pallas as pl
from jax.experimental.pallas import tpu as pltpu
from jax.sharding import Mesh
from jax.sharding import PartitionSpec as P

BLOCK = 128
HALO = 16
TAPS = 31
LANES = 128
EPSILON = 1e-05
BF16 = jnp.bfloat16
F32 = jnp.float32

FRAMES = ("xl", "y", "core", "section")
PLANE = ("y", "section")
MIB = 1024 * 1024


def params(mib=16):
    return pltpu.CompilerParams(vmem_limit_bytes=mib * MIB)


def in_hbm(array):
    return pltpu.with_memory_space_constraint(array, pltpu.HBM)


def swap(value, axis):
    return lax.ppermute(value, axis, [(0, 1), (1, 0)])


def halos(shard):
    peers = lax.axis_size(FRAMES)
    up = [(i, i + 1) for i in range(peers - 1)]
    down = [(j, i) for i, j in up]
    before = lax.ppermute(shard[shard.shape[0] - HALO :], FRAMES, up)
    after = lax.ppermute(shard[:HALO], FRAMES, down)
    return before, after


def fill_windows(win, main, before, after, same):
    blocks = win.shape[0]
    for b in range(blocks):
        lo, hi = b * BLOCK, (b + 1) * BLOCK
        prior = before[...] if b == 0 else main[lo - HALO : lo, :]
        later = after[...] if b == blocks - 1 else main[hi : hi + HALO, :]
        win[b, HALO : HALO + BLOCK, :] = main[lo:hi, :].astype(F32)
        win[b, :HALO, :] = jnp.where(same[b] == 1, prior.astype(F32), 0.0)
        win[b, HALO + BLOCK :, :] = jnp.where(same[b + 1] == 1, later.astype(F32), 0.0)


def fill_extended(win, rows, same):
    for b in range(win.shape[0]):
        lo = b * BLOCK
        hi = lo + HALO + BLOCK
        win[b, HALO : HALO + BLOCK, :] = rows[lo + HALO : hi, :].astype(F32)
        win[b, :HALO, :] = jnp.where(same[b] == 1, rows[lo : lo + HALO, :].astype(F32), 0.0)
        win[b, HALO + BLOCK :, :] = jnp.where(same[b + 1] == 1, rows[hi : hi + HALO, :].astype(F32), 0.0)


def shifted(win, b, shift):
    first = 1 if shift == 0 else 0
    return [(8 * a + shift - 1, 8 * a) for a in range(first, 4)], win[b, pl.ds(shift, BLOCK + 24), :]


def convolve(win, b, taps, flip):
    total = jnp.zeros((BLOCK, LANES), F32)
    for shift in range(8):
        steps, rows = shifted(win, b, shift)
        for k, at in steps:
            row = TAPS - 1 - k if flip else k
            total = total + taps[row : row + 1, :] * rows[at : at + BLOCK]
    return total


def valid_rows(fill, b):
    return lax.broadcasted_iota(jnp.int32, (BLOCK, LANES), 0) < fill[b]


def forward_kernel(same, fill, units, taps, activated, slope, win):
    fill_extended(win, units, same)

    def step(b, carry):
        conv = convolve(win, b, taps, False)
        q = jax.nn.sigmoid(conv)
        valid = valid_rows(fill, b)
        rows = pl.ds(pl.multiple_of(b * BLOCK, BLOCK), BLOCK)
        activated[rows, :] = jnp.where(valid, conv * q, 0.0).astype(BF16)
        slope[rows, :] = jnp.where(valid, q + conv * q * (1.0 - q), 0.0)
        return carry

    lax.fori_loop(0, win.shape[0], step, 0)


def taps_kernel(same, units, grad_conv, out, win, sums):
    fill_extended(win, units, same)
    sums[...] = jnp.zeros_like(sums)

    def step(b, carry):
        grad = grad_conv[pl.ds(pl.multiple_of(b * BLOCK, BLOCK), BLOCK), :]
        for shift in range(8):
            steps, rows = shifted(win, b, shift)
            for k, at in steps:
                terms = (rows[at : at + BLOCK] * grad).reshape(BLOCK // 8, 8, LANES)
                sums[k] += jnp.sum(terms, axis=0)
        return carry

    lax.fori_loop(0, win.shape[0], step, 0)
    out[...] = jnp.sum(sums[...], axis=1)


def backward_kernel(same, fill, grad_conv, before, after, taps, value, gate, out, win):
    fill_windows(win, grad_conv, before, after, same)

    def step(b, carry):
        grad_units = jnp.where(valid_rows(fill, b), convolve(win, b, taps, True), 0.0)
        rows = pl.ds(pl.multiple_of(b * BLOCK, BLOCK), BLOCK)
        inner = pl.ds(pl.multiple_of(b * BLOCK + HALO, HALO), BLOCK)
        s = gate[inner, :]
        grad_value = grad_units * s
        out[0, rows, :] = grad_value.astype(BF16)
        out[1, rows, :] = (grad_value * value[inner, :] * (1.0 - s)).astype(BF16)
        return carry

    lax.fori_loop(0, win.shape[0], step, 0)


def norm_kernel(frames, before, after, gain, out, out_t):
    def rows(block):
        x = block.astype(F32)
        center = x - jnp.mean(x, axis=1, keepdims=True)
        inv = lax.rsqrt(jnp.mean(center * center, axis=1, keepdims=True) + EPSILON)
        return (center * inv * gain[...]).astype(BF16)

    i = pl.program_id(0)
    normed = rows(frames[...])
    out[pl.ds(pl.multiple_of(HALO + i * BLOCK, HALO), BLOCK), :] = normed
    out_t[...] = normed.T

    @pl.when(i == 0)
    def _():
        out[:HALO, :] = rows(before[...])
        out[out.shape[0] - HALO :, :] = rows(after[...])


def chunks_kernel(rows, out, held, sems):
    count = held.shape[2]
    parts = range(held.shape[0])
    loads = [pltpu.make_async_copy(rows.at[:, pl.ds(i * count, count)], held.at[i], sems.at[0, i]) for i in parts]
    stores = [pltpu.make_async_copy(held.at[i], out.at[i], sems.at[1, i]) for i in parts]
    for load in loads:
        load.start()
    for load, store in zip(loads, stores):
        load.wait()
        store.start()
    for store in stores:
        store.wait()


def halves_kernel(core, rows, order, own, other, held, sem):
    copy = pltpu.make_async_copy(held, other, sem)
    for half, out in ((1 - core[0], held), (core[0], own)):
        for y in range(4):
            first = pl.multiple_of(y * 160 + half * 80, 16)
            second = pl.multiple_of((4 + y) * 160 + half * 80, 16)
            both = jnp.concatenate([rows[pl.ds(first, 80), :], rows[pl.ds(second, 80), :]], axis=0)
            moved = jnp.dot(order[...], both, preferred_element_type=F32)
            out[y * 160 : (y + 1) * 160, :] = moved.astype(BF16)
        if out is held:
            copy.start()
    copy.wait()


def final_kernel(sent, other, frames, arrived, gain, out, gain_part):
    x = frames[...].astype(F32)
    center = x - jnp.mean(x, axis=1, keepdims=True)
    inv = lax.rsqrt(jnp.mean(center * center, axis=1, keepdims=True) + EPSILON)
    unit = center * inv
    grad = sent[...].astype(F32) + other[...].astype(F32)
    e = grad * gain[...]
    product = grad * unit
    back = e - jnp.mean(e, axis=1, keepdims=True) - unit * jnp.mean(product * gain[...], axis=1, keepdims=True)
    out[...] = (arrived[...].astype(F32).T + inv * back).astype(BF16)

    @pl.when(pl.program_id(0) == 0)
    def _():
        gain_part[...] = jnp.zeros_like(gain_part)

    gain_part[...] += jnp.sum(product, axis=0, keepdims=True)


def pair_kernel(left, left_peer, right, right_peer, *buffers):
    out = buffers[-1]
    total = jnp.dot(left[...], right[...], preferred_element_type=F32)
    total = total + jnp.dot(left_peer[...], right_peer[...], preferred_element_type=F32)
    out[...] = total.astype(BF16)


def hbm():
    return pl.BlockSpec(memory_space=pltpu.HBM)


def smem():
    return pl.BlockSpec(memory_space=pltpu.SMEM)


def lanes(rows):
    return pl.BlockSpec((rows, LANES), lambda c: (0, c))


def convolved(same, fill, units, taps, count):
    width = units.shape[1]
    return pl.pallas_call(
        forward_kernel,
        grid=(width // LANES,),
        in_specs=[smem(), smem(), lanes(units.shape[0]), lanes(TAPS)],
        out_specs=[lanes(count), lanes(count)],
        out_shape=[
            jax.ShapeDtypeStruct((count, width), BF16),
            jax.ShapeDtypeStruct((count, width), F32),
        ],
        scratch_shapes=[pltpu.VMEM((count // BLOCK, BLOCK + 2 * HALO, LANES), F32)],
        compiler_params=params(),
        cost_estimate=pl.CostEstimate(flops=0, bytes_accessed=0, transcendentals=0),
        name="conv_forward",
    )(same, fill, units, taps)


def tap_sums(same, units, grad_conv):
    count, width = grad_conv.shape
    return pl.pallas_call(
        taps_kernel,
        grid=(width // LANES,),
        in_specs=[smem(), lanes(units.shape[0]), lanes(count)],
        out_specs=lanes(32),
        out_shape=jax.ShapeDtypeStruct((32, width), F32),
        scratch_shapes=[
            pltpu.VMEM((count // BLOCK, BLOCK + 2 * HALO, LANES), F32),
            pltpu.VMEM((32, 8, LANES), F32),
        ],
        compiler_params=params(),
        name="tap_gradients",
    )(same, units, grad_conv)


def projected_back(same, fill, grad_conv, before, after, taps, value, gate):
    count, width = grad_conv.shape
    return pl.pallas_call(
        backward_kernel,
        grid=(width // LANES,),
        in_specs=[
            smem(),
            smem(),
            lanes(count),
            lanes(HALO),
            lanes(HALO),
            lanes(TAPS),
            lanes(value.shape[0]),
            lanes(value.shape[0]),
        ],
        out_specs=pl.BlockSpec((2, count, LANES), lambda c: (0, 0, c)),
        out_shape=jax.ShapeDtypeStruct((2, count, width), BF16),
        scratch_shapes=[pltpu.VMEM((count // BLOCK, BLOCK + 2 * HALO, LANES), F32)],
        compiler_params=params(),
        name="conv_backward",
    )(same, fill, grad_conv, before, after, taps, in_hbm(value), in_hbm(gate))


def normalised(frames, before, after, gain):
    count, features = frames.shape
    edge = pl.BlockSpec((HALO, features), lambda i: (0, 0))
    return pl.pallas_call(
        norm_kernel,
        grid=(count // BLOCK,),
        in_specs=[
            pl.BlockSpec((BLOCK, features), lambda i: (i, 0)),
            edge,
            edge,
            pl.BlockSpec((1, features), lambda i: (0, 0)),
        ],
        out_specs=[
            pl.BlockSpec((count + 2 * HALO, features), lambda i: (0, 0)),
            pl.BlockSpec((features, BLOCK), lambda i: (0, i)),
        ],
        out_shape=[
            jax.ShapeDtypeStruct((count + 2 * HALO, features), BF16),
            jax.ShapeDtypeStruct((features, count), BF16),
        ],
        compiler_params=params(),
        name="layer_norm",
    )(in_hbm(frames), before, after, gain.reshape(1, features))


def frame_chunks(rows, parts):
    features, total = rows.shape
    shape = (parts, features, total // parts)
    return pl.pallas_call(
        chunks_kernel,
        in_specs=[hbm()],
        out_specs=hbm(),
        out_shape=pltpu.HBM(shape, rows.dtype),
        scratch_shapes=[pltpu.VMEM(shape, rows.dtype), pltpu.SemaphoreType.DMA((2, parts))],
        compiler_params=params(),
        name="frame_chunks",
    )(in_hbm(rows))


def halves(core, rows):
    features, count = rows.shape
    order = np.zeros((160, 160), np.float32)
    for z in range(4):
        for x in range(2):
            for r in range(20):
                order[(z * 2 + x) * 20 + r, x * 80 + z * 20 + r] = 1.0
    vmem = pl.BlockSpec(memory_space=pltpu.VMEM)
    half = jax.ShapeDtypeStruct((features // 2, count), BF16)
    return pl.pallas_call(
        halves_kernel,
        in_specs=[smem(), vmem, vmem],
        out_specs=[vmem, hbm()],
        out_shape=[half, pltpu.HBM(half.shape, BF16)],
        scratch_shapes=[pltpu.VMEM(half.shape, BF16), pltpu.SemaphoreType.DMA],
        compiler_params=params(),
        name="core_halves",
    )(core.reshape(1), rows, jnp.asarray(order, BF16))


def norm_back(sent, other, frames, arrived, gain):
    count, features = frames.shape
    block = pl.BlockSpec((BLOCK, features), lambda i: (i, 0))
    return pl.pallas_call(
        final_kernel,
        grid=(count // BLOCK,),
        in_specs=[
            block,
            block,
            block,
            pl.BlockSpec((features, BLOCK), lambda i: (0, i)),
            pl.BlockSpec((1, features), lambda i: (0, 0)),
        ],
        out_specs=[block, pl.BlockSpec((1, features), lambda i: (0, 0))],
        out_shape=[jax.ShapeDtypeStruct((count, features), BF16), jax.ShapeDtypeStruct((1, features), F32)],
        compiler_params=params(),
        cost_estimate=pl.CostEstimate(flops=40_000_000_000, bytes_accessed=100_000_000, transcendentals=0),
        name="norm_backward",
    )(in_hbm(sent), in_hbm(other), in_hbm(frames), in_hbm(arrived), gain)


def pair_product(left, left_peer, right, right_peer, groups, first, buffer=None):
    rows, count = left.shape
    made, _, width = right.shape
    spec = pl.BlockSpec((None, count, width), lambda i: (i, 0, 0))
    whole = pl.BlockSpec((rows, count), lambda i: (0, 0))
    return pl.pallas_call(
        pair_kernel,
        grid=(made,),
        in_specs=[whole, whole, spec, spec] + ([] if buffer is None else [hbm()]),
        out_specs=pl.BlockSpec((rows, width), lambda i: (0, first + i)),
        out_shape=pltpu.HBM((rows, groups * width), BF16),
        input_output_aliases={} if buffer is None else {4: 0},
        compiler_params=params(),
        name="weight_gradient",
    )(left, left_peer, right, right_peer, *([] if buffer is None else [in_hbm(buffer)]))


def ring_shares(value, axis):
    return [value] + [lax.ppermute(value, axis, [(i, (i + by) % 4) for i in range(4)]) for by in (1, 2, 3)]


def ring_sum(shares):
    own, first, second, third = [share.astype(F32) for share in shares]
    return (own + second) + (first + third)


def finish_rows(summed, xl):
    own = lax.dynamic_index_in_dim(summed, xl, 0, keepdims=False)
    other = lax.dynamic_index_in_dim(summed, 1 - xl, 0, keepdims=False)
    return own + swap(other, "xl")


def body(frames, returned, norm_gain, weight_in, kernel, weight_out, block_utt, block_fill):
    count = frames.shape[0]
    width = weight_in.shape[2]
    features = frames.shape[1]
    blocks = count // BLOCK
    core, xl = lax.axis_index("core"), lax.axis_index("xl")
    first_block = lax.axis_index(FRAMES) * blocks
    frames_before, frames_after = halos(frames)
    chunks = frame_chunks(returned.T, 4)
    arrived = lax.all_to_all(chunks, "section", 0, 0).reshape(features, count)

    edge = jnp.full((1,), -1, jnp.int32)
    near_utt = lax.dynamic_slice(jnp.concatenate([edge, block_utt, edge]), (first_block,), (blocks + 2,))
    near_fill = lax.dynamic_slice(jnp.concatenate([edge, block_fill, edge]), (first_block,), (blocks + 2,))
    same = (near_utt[1:] == near_utt[:-1]).astype(jnp.int32)
    fill = near_fill[1:-1]
    valid = (jnp.arange(BLOCK, dtype=jnp.int32)[None, :] < near_fill[:, None]).reshape(-1)
    valid = valid[BLOCK - HALO : BLOCK + count + HALO]

    normed_ext, normed_t = normalised(frames, frames_before, frames_after, norm_gain)
    value_proj = jnp.dot(normed_ext, weight_in[0], preferred_element_type=F32)
    gate_proj = jnp.dot(normed_ext, weight_in[1], preferred_element_type=F32)
    gate_sigmoid = jax.nn.sigmoid(gate_proj)
    units = jnp.where(valid[:, None], value_proj * gate_sigmoid, 0.0).astype(BF16)
    activated, slope = convolved(same, fill, units, kernel, count)
    activated_peer = swap(activated, "core")

    normed_own, normed_other = halves(core, normed_t)
    normed_peer = swap(normed_other, "core")

    arrived, normed_own, normed_other = lax.optimization_barrier((arrived, normed_own, normed_other))
    grad_activated = lax.dot_general(
        arrived, weight_out, (((0,), (1,)), ((), ())), preferred_element_type=F32
    )
    grad_conv = grad_activated * slope
    conv_before, conv_after = halos(grad_conv)
    rows_own, rows_other = halves(core, arrived)
    rows_peer = swap(rows_other, "core")
    parts = pair_product(rows_own, rows_peer, activated[None], activated_peer[None], 3, 0)

    ready, parts = lax.optimization_barrier((grad_conv, parts))
    late = projected_back(
        same, fill, ready, conv_before, conv_after, kernel, value_proj, gate_sigmoid
    )
    late_peer = swap(late, "core")
    contract = (((1,), (1,)), ((), ()))
    sent = lax.dot_general(late[0], weight_in[0], contract, preferred_element_type=F32)
    sent = sent + lax.dot_general(late[1], weight_in[1], contract, preferred_element_type=F32)
    sent = sent.astype(BF16)
    other = swap(sent, "tensor")
    parts = pair_product(normed_own, normed_peer, late, late_peer, 3, 1, parts)
    got = lax.all_to_all(parts.reshape(16, 40, 3 * width), PLANE, 0, 0)

    grad_frames, gain_part = norm_back(sent, other, frames, arrived, norm_gain.reshape(1, features))
    ready, gain_part = lax.optimization_barrier((grad_conv, gain_part))
    taps_part = tap_sums(same, units, ready)
    small = jnp.concatenate([taps_part, gain_part.reshape(2, width)], axis=0)
    small = small + swap(small, "core")
    small = (small + swap(small, "xl")).astype(BF16)
    shares = ring_shares(small, "y")
    total = jnp.sum(got.astype(F32), axis=0)
    total, shares = lax.optimization_barrier((total, shares))
    summed = finish_rows(total.reshape(2, 20, 3 * width), xl)
    small = ring_sum(ring_shares(ring_sum(shares).astype(BF16), "section"))
    grad_kernel = small[:TAPS]
    grad_gain = small[32:].reshape(features)

    grad_out = summed[:, :width].T
    grad_in = jnp.stack([summed[:, width : 2 * width], summed[:, 2 * width :]])
    return (grad_frames, grad_in, grad_out, grad_kernel, grad_gain)


def solution(mesh):
    split = Mesh(
        np.asarray(mesh.devices).reshape(2, 4, 2, 2, 4), ("xl", "y", "core", "tensor", "section")
    )
    outer = ("xl", "y", "core")
    in_specs = (
        P(FRAMES, None),
        P(outer, "section"),
        P(),
        P(None, None, "tensor"),
        P(None, "tensor"),
        P("tensor", None),
        P(),
        P(),
    )
    out_specs = (
        P(FRAMES, None),
        P(None, FRAMES, "tensor"),
        P("tensor", FRAMES),
        P(None, "tensor"),
        P(),
    )
    return jax.shard_map(body, mesh=split, in_specs=in_specs, out_specs=out_specs, check_vma=False)
```

time: 175 us -> 133 us (0.76)
  local copies, waits for them, and re-layouts: 39.1 us -> 7.71 us
  other arithmetic: 21 us -> 2.47 us
  Pallas kernels: 27.5 us -> 34.8 us
  starting transfers between devices: 42.6 us -> 46.9 us
  matrix products: 13.3 us -> 11.4 us
    unnamed x94 -> x35, local copies, waits for them, and re-layouts: 24.7 us -> 4.51 us
    all_to_all x4 -> x2, waiting for transfers between devices: 20 us -> 0.42 us  [the longest x1 0.42 us: body(): arrived = lax.all_to_all(chunks, 'section', 0, 0).reshape(features, count)]
    ppermute x7 -> x8, waiting for transfers between devices: 3.62 us -> 20.2 us  [swap(): return lax.ppermute(value, axis, [(0, 1), (1, 0)])]
    ppermute x0 -> x6, starting transfers between devices: none -> 8.64 us  [ring_shares(): lax.ppermute(value, axis, [(i, (i + by) % 4) for i in range(4)])]
    all_to_all x4 -> x2, starting transfers between devices: 25.3 us -> 16.7 us  [the longest x1 10.6 us: body(): got = lax.all_to_all(parts.reshape(16, 40, 3 * width), PLANE, 0, 0)]
    pallas_call x3 -> x7, Pallas kernels: 13.1 us -> 20.1 us  [the longest x2 6.74 us: pair_product(): pl.pallas_call(pair_kernel, grid=(made,), in_specs=[whole, whole, spec, s...]
    broadcast_in_dim x1 -> x0, other arithmetic: 6.42 us -> none  [body(): jnp.broadcast_to(small, (128, small.shape[1]))]
    ppermute x7 -> x8, starting transfers between devices: 6.03 us -> 11.9 us  [swap(): return lax.ppermute(value, axis, [(0, 1), (1, 0)])]
  transfers between devices with their start and end apart: 15 -> 20, of which waited for: 6 -> 11; matrix products, arithmetic and copies ran while one was open for 30% -> 11% of each run, Pallas kernels for 16% -> 22%
where the time goes in v3:
time: 133 us; the launch traced here: 131 us
  starting transfers between devices  46.9 us (35%)
  Pallas kernels  34.8 us (26%)
  waiting for transfers between devices  27 us (20%)
  matrix products  11.4 us (9%)
  local copies, waits for them, and re-layouts  7.71 us (6%)
  other arithmetic  2.47 us (2%)
    ppermute x8, waiting for transfers between devices, swap(): return lax.ppermute(value, axis, [(0, 1), (1, 0)])  20.2 us
    ppermute x8, starting transfers between devices, swap(): return lax.ppermute(value, axis, [(0, 1), (1, 0)])  11.9 us
    all_to_all x1, starting transfers between devices, body(): got = lax.all_to_all(parts.reshape(16, 40, 3 * width), PLANE, 0, 0)  10.6 us
    ppermute x6, starting transfers between devices, ring_shares(): lax.ppermute(value, axis, [(i, (i + by) % 4) for i in range(4)])  8.64 us
    ppermute x2, starting transfers between devices, halos(): before = lax.ppermute(shard[shard.shape[0] - HALO:], FRAMES, up)  7.06 us
    pallas_call x2, Pallas kernels, pair_product(): pl.pallas_call(pair_kernel, grid=(made,), in_specs=[whole, whole, spec, s...  6.74 us
    all_to_all x1, starting transfers between devices, body(): arrived = lax.all_to_all(chunks, 'section', 0, 0).reshape(features, count)  6.18 us
    pallas_call x1, Pallas kernels, projected_back(): pl.pallas_call(backward_kernel, grid=(width // LANES,), in_specs=[smem(),...  5.59 us
  transfers between devices with their start and end apart: 20, of which 11 were waited for; matrix products, arithmetic and copies ran while one was open for 11% of the time, Pallas kernels for 22%

profile of v3, /device:TPU:0, one launch (start us, length us, event | category | flops | bytes accessed | tf_op | source)
XLA Modules:
  0.0 131.4 jit_solution(12165365464123875134)
XLA Ops:
  0.6 0.0 copy-start
  0.6 0.9 fusion.23
  1.6 3.9 %collective-permute-start = (bf16[16,1280]{1,0:T(8,128)(2,1)S(1)}, bf16[16,1280]{1,0:T(8,128)(2,1)S(1)}, u32[]{:S(2)}, u32[]{:S(2)}) collective-permute-start(bf16[16,1280]{1,0:T(8,128)(2,1)S(1)} %get-tuple-element.60), channel_id=1, source_target_pairs={{0,1},{1,2},{2,3},{3,8},{8,9},{9,10},{10,11},{11,16},{16,17},{17,1... | collective-permute-start | bytes 122888 | tf_op jit(solution)/shard_map/ppermute | solution.py:41
  5.5 1.3 collective-permute-start.1
  6.8 2.1 %frame_chunks.1 = bf16[4,320,512]{2,1,0:T(8,128)(2,1)} custom-call(bf16[320,2048]{1,0:T(8,128)(2,1)} %bitcast.50), custom_call_target="tpu_custom_call" | custom-call | tf_op jit(solution)/shard_map/frame_chunks/pallas_call | solution.py:302
  8.9 0.0 copy-start.13
  8.9 6.2 %all-to-all-start = ((bf16[4,320,512]{2,1,0:T(8,128)(2,1)}), bf16[4,320,512]{2,1,0:T(8,128)(2,1)S(1)}, u32[]{:S(2)}, u32[]{:S(2)}) async-start(bf16[4,320,512]{2,1,0:T(8,128)(2,1)} %frame_chunks.1), calls=%async_computation | async-start | bytes 2621440 | tf_op jit(solution)/shard_map/all_to_all | solution.py:395
  15.1 0.1 pad_add_fusion
  15.2 0.1 dynamic_slice.13
  15.3 0.1 dynamic_slice.14
  15.4 0.1 fusion.20
  15.4 0.1 compare_convert_fusion.same
  15.5 0.1 slice.55.fill
  15.6 0.1 slice.58
  15.7 3.6 %layer_norm.1 = (bf16[544,1280]{1,0:T(8,128)(2,1)S(1)}, bf16[1280,512]{1,0:T(8,128)(2,1)S(1)}) custom-call(bf16[512,1280]{1,0:T(8,128)(2,1)} %frames.3, bf16[16,1280]{1,0:T(8,128)(2,1)S(1)} %collective-permute-done.before, bf16[16,1280]{1,0:T(8,128)(2,1)S(1)} %collective-permute-done.1.after, f32[1,1280]{1,0:T(1,128)S(1)} %reshape.41.gain), custom_call_target="tpu_custom_call" | custom-call | tf_op jit(solution)/shard_map/layer_norm/pallas_call | solution.py:277
  19.3 2.9 %add_divide_fusion.gate = f32[544,640]{1,0:T(8,128)S(1)} fusion(bf16[544,1280]{1,0:T(8,128)(2,1)S(1)} %get-tuple-element.30, bf16[2,1280,640]{2,1,0:T(8,128)(2,1)} %param.13), kind=kOutput, calls=%fused_computation.18 | convolution fusion | flops 892334080 | bytes 4423680 | tf_op jit(solution)/shard_map/dot_general | solution.py:407
  22.2 0.0 copy-start.6
  22.2 2.4 %select_convert_fusion = (bf16[544,640]{1,0:T(8,128)(2,1)S(1)}, f32[544,640]{1,0:T(8,128)}) fusion(f32[544,640]{1,0:T(8,128)S(1)} %add_divide_fusion.gate, pred[544]{0:T(1024)(128)(4,1)S(1)} %slice.58, bf16[544,1280]{1,0:T(8,128)(2,1)S(1)} %get-tuple-element.30, bf16[2,1280,640]{2,1,0:T(8,128)(2,1)S(1)} %copy-done.11), kind=kOutput, calls=%fused_computation.17 | convolution fusion | flops 892334080 | bytes 6513664 | tf_op jit(solution)/shard_map/dot_general | solution.py:406
  24.7 5.1 %conv_forward.1 = (bf16[512,640]{1,0:T(8,128)(2,1)}, f32[512,640]{1,0:T(8,128)S(1)}) custom-call(s32[5]{0:T(128)S(1)} %compare_convert_fusion.same, s32[4]{0:T(128)S(1)} %slice.55.fill, bf16[544,640]{1,0:T(8,128)(2,1)S(1)} %get-tuple-element.64.units, f32[31,640]{1,0:T(8,128)S(1)} %copy-done.7), custom_call_target="tpu_custom_call" | custom-call | tf_op jit(solution)/shard_map/conv_forward/pallas_call | solution.py:218
  29.8 1.1 copy-done.8
  30.8 0.4 collective-permute-start.3
  31.3 1.2 core_halves.2
  32.5 0.9 copy-done.4
  33.4 0.4 all-to-all-done
  33.8 1.2 core_halves.3
  35.0 0.1 collective-permute-start.2
  35.1 0.7 copy-done.9
  35.8 2.6 %convolution_multiply_fusion.grad_conv = f32[512,640]{1,0:T(8,128)S(1)} fusion(f32[512,640]{1,0:T(8,128)S(1)} %copy-done.9, bf16[1280,512]{1,0:T(8,128)(2,1)} %bitcast.47, bf16[640,1280]{1,0:T(8,128)(2,1)S(1)} %copy-done), kind=kOutput, calls=%fused_computation.16 | convolution fusion | flops 839188480 | bytes 5570560 | tf_op jit(solution)/shard_map/dot_general | solution.py:417
  38.4 3.2 %collective-permute-start.4 = (f32[16,640]{1,0:T(8,128)S(1)}, f32[16,640]{1,0:T(8,128)S(1)}, u32[]{:S(2)}, u32[]{:S(2)}) collective-permute-start(f32[16,640]{1,0:T(8,128)S(1)} %get-tuple-element.58), channel_id=1, source_target_pairs={{0,1},{1,2},{2,3},{3,8},{8,9},{9,10},{10,11},{11,16},{16,17},{17,1... | collective-permute-start | bytes 122888 | tf_op jit(solution)/shard_map/ppermute | solution.py:41
  41.6 1.3 collective-permute-start.5
  42.9 3.4 %weight_gradient.2.buffers_0_ = bf16[640,1920]{1,0:T(8,128)(2,1)} custom-call(bf16[640,512]{1,0:T(8,128)(2,1)S(1)} %get-tuple-element.32.left, bf16[640,512]{1,0:T(8,128)(2,1)S(1)} %collective-permute-done.2.left_peer, bf16[1,512,640]{2,1,0:T(8,128)(2,1)} %bitcast.6.right, bf16[1,512,640]{2,1,0:T(8,128)(2,1)} %bitcast.7.right_peer), custom_call_target="tpu_custom_call" | custom-call | tf_op jit(solution)/shard_map/weight_gradient/pallas_call | solution.py:359
  46.3 1.1 collective-permute-done.5.after
  47.5 5.6 %conv_backward.1.right = bf16[2,512,640]{2,1,0:T(8,128)(2,1)S(1)} custom-call(s32[5]{0:T(128)S(1)} %compare_convert_fusion.same, s32[4]{0:T(128)S(1)} %slice.55.fill, f32[512,640]{1,0:T(8,128)S(1)} %convolution_multiply_fusion.grad_conv, f32[16,640]{1,0:T(8,128)S(1)} %collective-permute-done.4.before, f32[16,640]{1,0:T(8,128)S(1)} %collective-permute-done.5.after, ...), custom_call_target="tpu_custom_call" | custom-call | tf_op jit(solution)/shard_map/conv_backward/pallas_call | solution.py:253
  53.1 1.2 fusion.1
  54.3 1.1 collective-permute-start.8
  55.4 2.3 %fusion.sent = bf16[512,1280]{1,0:T(8,128)(2,1)} fusion(f32[512,1280]{1,0:T(8,128)S(1)} %fusion.1, bf16[2,1280,640]{2,1,0:T(8,128)(2,1)S(1)} %copy-done.12, bf16[2,512,640]{2,1,0:T(8,128)(2,1)S(1)} %conv_backward.1.right), kind=kOutput, calls=%fused_computation.2 | convolution fusion | flops 840171520 | bytes 6225920 | tf_op jit(solution)/shard_map/dot_general | solution.py:432
  57.7 3.0 %collective-permute-start.6 = (bf16[512,1280]{1,0:T(8,128)(2,1)}, bf16[512,1280]{1,0:T(8,128)(2,1)}, u32[]{:S(2)}, u32[]{:S(2)}) collective-permute-start(bf16[512,1280]{1,0:T(8,128)(2,1)} %fusion.sent), channel_id=1, source_target_pairs={{0,4},{4,0},{1,5},{5,1},{2,6},{6,2},{3,7},{7,3},{8,12},{12,8},{9,1... | collective-permute-start | bytes 3932168 | tf_op jit(solution)/shard_map/ppermute | solution.py:34
  60.7 2.1 %collective-permute-done.7.left_peer = bf16[640,512]{1,0:T(8,128)(2,1)S(1)} collective-permute-done((bf16[640,512]{1,0:T(8,128)(2,1)S(1)}, bf16[640,512]{1,0:T(8,128)(2,1)S(1)}, u32[]{:S(2)}, u32[]{:S(2)}) %collective-permute-start.7) | collective-permute-done | bytes 655392 | tf_op jit(solution)/shard_map/ppermute | solution.py:34
  62.8 3.3 %weight_gradient.3 = bf16[640,1920]{1,0:T(8,128)(2,1)} custom-call(bf16[640,512]{1,0:T(8,128)(2,1)S(1)} %copy-done.5, bf16[640,512]{1,0:T(8,128)(2,1)S(1)} %collective-permute-done.7.left_peer, bf16[2,512,640]{2,1,0:T(8,128)(2,1)S(1)} %conv_backward.1.right, ...), custom_call_target="tpu_custom_call", output_to_operand_aliasing={{}: (4, {})} | custom-call | tf_op jit(solution)/shard_map/weight_gradient/pallas_call | solution.py:359
  66.2 10.6 %all-to-all-start.1 = ((bf16[16,40,1920]{2,1,0:T(8,128)(2,1)}), bf16[16,40,1920]{2,1,0:T(8,128)(2,1)}, u32[]{:S(2)}, u32[]{:S(2)}) async-start(bf16[16,40,1920]{2,1,0:T(8,128)(2,1)} %bitcast.49), calls=%async_computation.1 | async-start | bytes 4915200 | tf_op jit(solution)/shard_map/all_to_all | solution.py:437
  76.7 13.5 %collective-permute-done.6.other = bf16[512,1280]{1,0:T(8,128)(2,1)} collective-permute-done((bf16[512,1280]{1,0:T(8,128)(2,1)}, bf16[512,1280]{1,0:T(8,128)(2,1)}, u32[]{:S(2)}, u32[]{:S(2)}) %collective-permute-start.6) | collective-permute-done | bytes 1310752 | tf_op jit(solution)/shard_map/ppermute | solution.py:34
  90.2 5.2 %norm_backward.1 = (bf16[512,1280]{1,0:T(8,128)(2,1)}, f32[1,1280]{1,0:T(1,128)S(1)}) custom-call(bf16[512,1280]{1,0:T(8,128)(2,1)} %fusion.sent, bf16[512,1280]{1,0:T(8,128)(2,1)} %collective-permute-done.6.other, bf16[512,1280]{1,0:T(8,128)(2,1)} %frames.3, bf16[1280,512]{1,0:T(8,128)(2,1)} %bitcast.48, f32[1,1280]{1,0:T(1,128)S(1)} %reshape.41.gain), custom_call_target="tpu_custom_call" | custom-call | flops 40000000000 | bytes 100000000 | tf_op jit(solution)/shard_map/norm_backward/pallas_call | solution.py:336
  95.5 1.1 copy-done.3
  96.6 4.0 %tap_gradients.1 = f32[32,640]{1,0:T(8,128)S(1)} custom-call(s32[5]{0:T(128)S(1)} %compare_convert_fusion.same, bf16[544,640]{1,0:T(8,128)(2,1)S(1)} %copy-done.3, f32[512,640]{1,0:T(8,128)S(1)} %convolution_multiply_fusion.grad_conv), custom_call_target="tpu_custom_call" | custom-call | tf_op jit(solution)/shard_map/tap_gradients/pallas_call | solution.py:236
  100.6 0.1 collective-permute-start.9
  100.7 1.3 collective-permute-done.9
  102.0 6.9 %collective-permute-start.10 = (f32[34,640]{1,0:T(8,128)S(1)}, f32[34,640]{1,0:T(8,128)S(1)}, u32[]{:S(2)}, u32[]{:S(2)}) collective-permute-start(f32[34,640]{1,0:T(8,128)S(1)} %fusion.21), channel_id=1, source_target_pairs={{0,64},{64,0},{1,65},{65,1},{2,66},{66,2},{3,67},{67,3},{4,68},{68... | collective-permute-start | bytes 261128 | tf_op jit(solution)/shard_map/ppermute | solution.py:34
  108.9 3.2 %collective-permute-done.10 = f32[34,640]{1,0:T(8,128)S(1)} collective-permute-done((f32[34,640]{1,0:T(8,128)S(1)}, f32[34,640]{1,0:T(8,128)S(1)}, u32[]{:S(2)}, u32[]{:S(2)}) %collective-permute-start.10) | collective-permute-done | bytes 87072 | tf_op jit(solution)/shard_map/ppermute | solution.py:34
  112.1 0.1 collective-permute-start.11
  112.2 1.2 collective-permute-start.12
  113.4 2.0 %collective-permute-start.13 = (bf16[34,640]{1,0:T(8,128)(2,1)S(1)}, bf16[34,640]{1,0:T(8,128)(2,1)S(1)}, u32[]{:S(2)}, u32[]{:S(2)}) collective-permute-start(bf16[34,640]{1,0:T(8,128)(2,1)S(1)} %add_convert_fusion.1), channel_id=1, source_target_pairs={{0,48},{16,0},{32,16},{48,32},{1,49},{17,1},{33,17},{49,33},{2,50}... | collective-permute-start | bytes 130568 | tf_op jit(solution)/shard_map/ppermute | solution.py:372
  115.4 2.1 %convert_reduce_fusion = f32[40,1920]{1,0:T(8,128)S(1)} fusion(bf16[16,40,1920]{2,1,0:T(8,128)(2,1)} %all-to-all-done.1), kind=kLoop, calls=%fused_computation | loop fusion | flops 2380800 | bytes 2764800 | tf_op jit(solution)/shard_map/reduce_sum | solution.py:446
  117.5 0.5 collective-permute-done.11
  118.1 0.9 collective-permute-done.13
  119.0 3.8 %collective-permute-start.17 = (bf16[34,640]{1,0:T(8,128)(2,1)S(1)}, bf16[34,640]{1,0:T(8,128)(2,1)S(1)}, u32[]{:S(2)}, u32[]{:S(2)}) collective-permute-start(bf16[34,640]{1,0:T(8,128)(2,1)S(1)} %add_convert_fusion), channel_id=1, source_target_pairs={{0,3},{1,0},{2,1},{3,2},{4,7},{5,4},{6,5},{7,6},{8,11},{9,8},{10,9... | collective-permute-start | bytes 130568 | tf_op jit(solution)/shard_map/ppermute | solution.py:372
  122.8 1.5 %collective-permute-start.15 = (bf16[34,640]{1,0:T(8,128)(2,1)S(1)}, bf16[34,640]{1,0:T(8,128)(2,1)S(1)}, u32[]{:S(2)}, u32[]{:S(2)}) collective-permute-start(bf16[34,640]{1,0:T(8,128)(2,1)S(1)} %add_convert_fusion), channel_id=1, source_target_pairs={{0,2},{1,3},{2,0},{3,1},{4,6},{5,7},{6,4},{7,5},{8,10},{9,11},{10,... | collective-permute-start | bytes 130568 | tf_op jit(solution)/shard_map/ppermute | solution.py:372
  124.4 0.4 collective-permute-start.14
  124.7 0.2 collective-permute-done.17
  125.0 3.7 %collective-permute-done.16 = bf16[34,640]{1,0:T(8,128)(2,1)S(1)} collective-permute-done((bf16[34,640]{1,0:T(8,128)(2,1)S(1)}, bf16[34,640]{1,0:T(8,128)(2,1)S(1)}, u32[]{:S(2)}, u32[]{:S(2)}) %collective-permute-start.16) | collective-permute-done | bytes 43552 | tf_op jit(solution)/shard_map/ppermute | solution.py:372
  128.7 0.6 slice.77
  129.3 0.6 reshape.45
  129.9 0.1 collective-permute-done.14
  130.0 0.6 slice_bitcast_fusion.4
  130.7 0.7 copy.17
  (52 shorter events, 0.3 us)
Async XLA Ops:
  0.6 34.5 %copy-start = (bf16[640,1280]{1,0:T(8,128)(2,1)S(1)}, bf16[640,1280]{1,0:T(8,128)(2,1)}, u32[]{:S(2)}) copy-start(bf16[640,1280]{1,0:T(8,128)(2,1)} %param.15) | copy-start | bytes 4915204
  1.6 14.1 %collective-permute-start = (bf16[16,1280]{1,0:T(8,128)(2,1)S(1)}, bf16[16,1280]{1,0:T(8,128)(2,1)S(1)}, u32[]{:S(2)}, u32[]{:S(2)}) collective-permute-start(bf16[16,1280]{1,0:T(8,128)(2,1)S(1)} %get-tuple-element.60), channel_id=1, source_target_pairs={{0,1},{1,2},{2,3},{3,8},{8,9},{9,10},{10,11},{11,16},{16,17},{17,1... | collective-permute-start | bytes 122888 | tf_op jit(solution)/shard_map/ppermute | solution.py:41
  5.5 10.2 %collective-permute-start.1 = (bf16[16,1280]{1,0:T(8,128)(2,1)S(1)}, bf16[16,1280]{1,0:T(8,128)(2,1)S(1)}, u32[]{:S(2)}, u32[]{:S(2)}) collective-permute-start(bf16[16,1280]{1,0:T(8,128)(2,1)S(1)} %get-tuple-element.59), channel_id=1, source_target_pairs={{1,0},{2,1},{3,2},{8,3},{9,8},{10,9},{11,10},{16,11},{17,16},{18,1... | collective-permute-start | bytes 122888 | tf_op jit(solution)/shard_map/ppermute | solution.py:42
  8.9 6.2 %copy-start.14 = (s32[256]{0:T(256)S(1)}, s32[256]{0:T(256)}, u32[]{:S(2)}) copy-start(s32[256]{0:T(256)} %param.17) | copy-start | bytes 3076
  8.9 6.2 %copy-start.15 = (s32[256]{0:T(256)S(1)}, s32[256]{0:T(256)}, u32[]{:S(2)}) copy-start(s32[256]{0:T(256)} %param.16) | copy-start | bytes 3076
  8.9 6.6 %copy-start.13 = (f32[1280]{0:T(1024)S(1)}, f32[1280]{0:T(1024)}, u32[]{:S(2)}) copy-start(f32[1280]{0:T(1024)} %param.12) | copy-start | bytes 15364
  8.9 24.9 %all-to-all-start = ((bf16[4,320,512]{2,1,0:T(8,128)(2,1)}), bf16[4,320,512]{2,1,0:T(8,128)(2,1)S(1)}, u32[]{:S(2)}, u32[]{:S(2)}) async-start(bf16[4,320,512]{2,1,0:T(8,128)(2,1)} %frame_chunks.1), calls=%async_computation | async-start | bytes 2621440 | tf_op jit(solution)/shard_map/all_to_all | solution.py:395
  19.3 2.9 %copy-start.11 = (bf16[2,1280,640]{2,1,0:T(8,128)(2,1)S(1)}, bf16[2,1280,640]{2,1,0:T(8,128)(2,1)}, u32[]{:S(2)}) copy-start(bf16[2,1280,640]{2,1,0:T(8,128)(2,1)} %param.13) | copy-start | bytes 9830404
  22.2 2.4 %copy-start.10 = (f32[544,640]{1,0:T(8,128)}, f32[544,640]{1,0:T(8,128)S(1)}, u32[]{:S(2)}) copy-start(f32[544,640]{1,0:T(8,128)S(1)} %add_divide_fusion.gate) | copy-start | bytes 4177924
  22.2 2.4 %copy-start.7 = (f32[31,640]{1,0:T(8,128)S(1)}, f32[31,640]{1,0:T(8,128)}, u32[]{:S(2)}) copy-start(f32[31,640]{1,0:T(8,128)} %taps.3) | copy-start | bytes 238084
  22.2 9.0 %copy-start.6 = (bf16[160,160]{1,0:T(8,128)(2,1)S(1)}, bf16[160,160]{1,0:T(8,128)(2,1)}, u32[]{:S(2)}) copy-start(bf16[160,160]{1,0:T(8,128)(2,1)} %constant.46.clone.order) | copy-start | bytes 153604
  24.6 6.6 %copy-start.2 = (bf16[544,640]{1,0:T(8,128)(2,1)}, bf16[544,640]{1,0:T(8,128)(2,1)S(1)}, u32[]{:S(2)}) copy-start(bf16[544,640]{1,0:T(8,128)(2,1)S(1)} %get-tuple-element.64.units) | copy-start | bytes 2088964
  29.8 1.1 copy-start.8
  30.8 12.1 %collective-permute-start.3 = (bf16[512,640]{1,0:T(8,128)(2,1)}, bf16[512,640]{1,0:T(8,128)(2,1)}, u32[]{:S(2)}, u32[]{:S(2)}) collective-permute-start(bf16[512,640]{1,0:T(8,128)(2,1)} %get-tuple-element.34), channel_id=1, source_target_pairs={{0,8},{8,0},{1,9},{9,1},{2,10},{10,2},{3,11},{11,3},{4,12},{12,4},... | collective-permute-start | bytes 1966088 | tf_op jit(solution)/shard_map/ppermute | solution.py:34
  32.5 0.9 copy-start.4
  33.8 1.3 copy-start.1
  33.8 2.0 %copy-start.9 = (f32[512,640]{1,0:T(8,128)S(1)}, f32[512,640]{1,0:T(8,128)}, u32[]{:S(2)}) copy-start(f32[512,640]{1,0:T(8,128)} %copy-done.8) | copy-start | bytes 3932164
  35.0 7.9 %collective-permute-start.2 = (bf16[640,512]{1,0:T(8,128)(2,1)}, bf16[640,512]{1,0:T(8,128)(2,1)S(1)}, u32[]{:S(2)}, u32[]{:S(2)}) collective-permute-start(bf16[640,512]{1,0:T(8,128)(2,1)} %get-tuple-element.33), channel_id=1, source_target_pairs={{0,8},{8,0},{1,9},{9,1},{2,10},{10,2},{3,11},{11,3},{4,12},{12,4},... | collective-permute-start | bytes 1966088 | tf_op jit(solution)/shard_map/ppermute | solution.py:34
  38.4 7.9 %collective-permute-start.4 = (f32[16,640]{1,0:T(8,128)S(1)}, f32[16,640]{1,0:T(8,128)S(1)}, u32[]{:S(2)}, u32[]{:S(2)}) collective-permute-start(f32[16,640]{1,0:T(8,128)S(1)} %get-tuple-element.58), channel_id=1, source_target_pairs={{0,1},{1,2},{2,3},{3,8},{8,9},{9,10},{10,11},{11,16},{16,17},{17,1... | collective-permute-start | bytes 122888 | tf_op jit(solution)/shard_map/ppermute | solution.py:41
  41.6 5.9 %collective-permute-start.5 = (f32[16,640]{1,0:T(8,128)S(1)}, f32[16,640]{1,0:T(8,128)S(1)}, u32[]{:S(2)}, u32[]{:S(2)}) collective-permute-start(f32[16,640]{1,0:T(8,128)S(1)} %get-tuple-element.57), channel_id=1, source_target_pairs={{1,0},{2,1},{3,2},{8,3},{9,8},{10,9},{11,10},{16,11},{17,16},{18,1... | collective-permute-start | bytes 122888 | tf_op jit(solution)/shard_map/ppermute | solution.py:42
  47.5 5.6 %copy-start.12 = (bf16[2,1280,640]{2,1,0:T(8,128)(2,1)S(1)}, bf16[2,1280,640]{2,1,0:T(8,128)(2,1)}, u32[]{:S(2)}) copy-start(bf16[2,1280,640]{2,1,0:T(8,128)(2,1)} %param.13) | copy-start | bytes 9830404
  54.3 6.4 %copy-start.16 = (bf16[640,512]{1,0:T(8,128)(2,1)S(1)}, bf16[640,512]{1,0:T(8,128)(2,1)}, u32[]{:S(2)}) copy-start(bf16[640,512]{1,0:T(8,128)(2,1)} %get-tuple-element.28) | copy-start | bytes 1966084
  54.3 8.5 %copy-start.5 = (bf16[640,512]{1,0:T(8,128)(2,1)S(1)}, bf16[640,512]{1,0:T(8,128)(2,1)}, u32[]{:S(2)}) copy-start(bf16[640,512]{1,0:T(8,128)(2,1)} %copy-done.4) | copy-start | bytes 1966084
  54.3 8.5 %collective-permute-start.8 = (bf16[2,512,640]{2,1,0:T(8,128)(2,1)S(1)}, bf16[2,512,640]{2,1,0:T(8,128)(2,1)S(1)}, u32[]{:S(2)}, u32[]{:S(2)}) collective-permute-start(bf16[2,512,640]{2,1,0:T(8,128)(2,1)S(1)} %conv_backward.1.right), channel_id=1, source_target_pairs={{0,8},{8,0},{1,9},{9,1},{2,10},{10,2},{3,11},{11,3},{4,12},{12,4},... | collective-permute-start | bytes 3932168 | tf_op jit(solution)/shard_map/ppermute | solution.py:34
  57.7 32.5 %collective-permute-start.6 = (bf16[512,1280]{1,0:T(8,128)(2,1)}, bf16[512,1280]{1,0:T(8,128)(2,1)}, u32[]{:S(2)}, u32[]{:S(2)}) collective-permute-start(bf16[512,1280]{1,0:T(8,128)(2,1)} %fusion.sent), channel_id=1, source_target_pairs={{0,4},{4,0},{1,5},{5,1},{2,6},{6,2},{3,7},{7,3},{8,12},{12,8},{9,1... | collective-permute-start | bytes 3932168 | tf_op jit(solution)/shard_map/ppermute | solution.py:34
  60.7 2.1 %collective-permute-start.7 = (bf16[640,512]{1,0:T(8,128)(2,1)S(1)}, bf16[640,512]{1,0:T(8,128)(2,1)S(1)}, u32[]{:S(2)}, u32[]{:S(2)}) collective-permute-start(bf16[640,512]{1,0:T(8,128)(2,1)S(1)} %copy-done.16), channel_id=1, source_target_pairs={{0,8},{8,0},{1,9},{9,1},{2,10},{10,2},{3,11},{11,3},{4,12},{12,4},... | collective-permute-start | bytes 1966088 | tf_op jit(solution)/shard_map/ppermute | solution.py:34
  66.2 49.3 %all-to-all-start.1 = ((bf16[16,40,1920]{2,1,0:T(8,128)(2,1)}), bf16[16,40,1920]{2,1,0:T(8,128)(2,1)}, u32[]{:S(2)}, u32[]{:S(2)}) async-start(bf16[16,40,1920]{2,1,0:T(8,128)(2,1)} %bitcast.49), calls=%async_computation.1 | async-start | bytes 4915200 | tf_op jit(solution)/shard_map/all_to_all | solution.py:437
  95.5 1.1 copy-start.3
  100.6 1.4 %collective-permute-start.9 = (f32[34,640]{1,0:T(8,128)S(1)}, f32[34,640]{1,0:T(8,128)S(1)}, u32[]{:S(2)}, u32[]{:S(2)}) collective-permute-start(f32[34,640]{1,0:T(8,128)S(1)} %pad_maximum_fusion.1), channel_id=1, source_target_pairs={{0,8},{8,0},{1,9},{9,1},{2,10},{10,2},{3,11},{11,3},{4,12},{12,4},... | collective-permute-start | bytes 261128 | tf_op jit(solution)/shard_map/ppermute | solution.py:34
  102.0 10.1 %collective-permute-start.10 = (f32[34,640]{1,0:T(8,128)S(1)}, f32[34,640]{1,0:T(8,128)S(1)}, u32[]{:S(2)}, u32[]{:S(2)}) collective-permute-start(f32[34,640]{1,0:T(8,128)S(1)} %fusion.21), channel_id=1, source_target_pairs={{0,64},{64,0},{1,65},{65,1},{2,66},{66,2},{3,67},{67,3},{4,68},{68... | collective-permute-start | bytes 261128 | tf_op jit(solution)/shard_map/ppermute | solution.py:34
  112.1 5.9 %collective-permute-start.11 = (bf16[34,640]{1,0:T(8,128)(2,1)S(1)}, bf16[34,640]{1,0:T(8,128)(2,1)S(1)}, u32[]{:S(2)}, u32[]{:S(2)}) collective-permute-start(bf16[34,640]{1,0:T(8,128)(2,1)S(1)} %add_convert_fusion.1), channel_id=1, source_target_pairs={{0,16},{16,32},{32,48},{48,0},{1,17},{17,33},{33,49},{49,1},{2,18}... | collective-permute-start | bytes 130568 | tf_op jit(solution)/shard_map/ppermute | solution.py:372
  112.2 5.9 %collective-permute-start.12 = (bf16[34,640]{1,0:T(8,128)(2,1)S(1)}, bf16[34,640]{1,0:T(8,128)(2,1)S(1)}, u32[]{:S(2)}, u32[]{:S(2)}) collective-permute-start(bf16[34,640]{1,0:T(8,128)(2,1)S(1)} %add_convert_fusion.1), channel_id=1, source_target_pairs={{0,32},{16,48},{32,0},{48,16},{1,33},{17,49},{33,1},{49,17},{2,34}... | collective-permute-start | bytes 130568 | tf_op jit(solution)/shard_map/ppermute | solution.py:372
  113.4 5.5 %collective-permute-start.13 = (bf16[34,640]{1,0:T(8,128)(2,1)S(1)}, bf16[34,640]{1,0:T(8,128)(2,1)S(1)}, u32[]{:S(2)}, u32[]{:S(2)}) collective-permute-start(bf16[34,640]{1,0:T(8,128)(2,1)S(1)} %add_convert_fusion.1), channel_id=1, source_target_pairs={{0,48},{16,0},{32,16},{48,32},{1,49},{17,1},{33,17},{49,33},{2,50}... | collective-permute-start | bytes 130568 | tf_op jit(solution)/shard_map/ppermute | solution.py:372
  119.0 6.0 %collective-permute-start.17 = (bf16[34,640]{1,0:T(8,128)(2,1)S(1)}, bf16[34,640]{1,0:T(8,128)(2,1)S(1)}, u32[]{:S(2)}, u32[]{:S(2)}) collective-permute-start(bf16[34,640]{1,0:T(8,128)(2,1)S(1)} %add_convert_fusion), channel_id=1, source_target_pairs={{0,3},{1,0},{2,1},{3,2},{4,7},{5,4},{6,5},{7,6},{8,11},{9,8},{10,9... | collective-permute-start | bytes 130568 | tf_op jit(solution)/shard_map/ppermute | solution.py:372
  122.8 5.9 %collective-permute-start.16 = (bf16[34,640]{1,0:T(8,128)(2,1)S(1)}, bf16[34,640]{1,0:T(8,128)(2,1)S(1)}, u32[]{:S(2)}, u32[]{:S(2)}) collective-permute-start(bf16[34,640]{1,0:T(8,128)(2,1)S(1)} %add_convert_fusion), channel_id=1, source_target_pairs={{0,1},{1,2},{2,3},{3,0},{4,5},{5,6},{6,7},{7,4},{8,9},{9,10},{10,1... | collective-permute-start | bytes 130568 | tf_op jit(solution)/shard_map/ppermute | solution.py:372
  122.8 5.9 %collective-permute-start.15 = (bf16[34,640]{1,0:T(8,128)(2,1)S(1)}, bf16[34,640]{1,0:T(8,128)(2,1)S(1)}, u32[]{:S(2)}, u32[]{:S(2)}) collective-permute-start(bf16[34,640]{1,0:T(8,128)(2,1)S(1)} %add_convert_fusion), channel_id=1, source_target_pairs={{0,2},{1,3},{2,0},{3,1},{4,6},{5,7},{6,4},{7,5},{8,10},{9,11},{10,... | collective-permute-start | bytes 130568 | tf_op jit(solution)/shard_map/ppermute | solution.py:372
  124.4 5.6 %collective-permute-start.14 = (f32[20,1920]{1,0:T(8,128)S(1)}, f32[20,1920]{1,0:T(8,128)S(1)}, u32[]{:S(2)}, u32[]{:S(2)}) collective-permute-start(f32[20,1920]{1,0:T(8,128)S(1)} %dynamic-slice_bitcast_fusion), channel_id=1, source_target_pairs={{0,64},{64,0},{1,65},{65,1},{2,66},{66,2},{3,67},{67,3},{4,68},{68... | collective-permute-start | bytes 460808 | tf_op jit(solution)/shard_map/ppermute | solution.py:34

commit v4 on v3

--- a/solution.py
+++ b/solution.py
@@ -176,22 +176,14 @@
     copy.wait()
 
 
-def final_kernel(sent, other, frames, arrived, gain, out, gain_part):
+def final_kernel(sent, other, frames, arrived, gain, out):
     x = frames[...].astype(F32)
     center = x - jnp.mean(x, axis=1, keepdims=True)
     inv = lax.rsqrt(jnp.mean(center * center, axis=1, keepdims=True) + EPSILON)
     unit = center * inv
-    grad = sent[...].astype(F32) + other[...].astype(F32)
-    e = grad * gain[...]
-    product = grad * unit
-    back = e - jnp.mean(e, axis=1, keepdims=True) - unit * jnp.mean(product * gain[...], axis=1, keepdims=True)
+    e = (sent[...].astype(F32) + other[...].astype(F32)) * gain[...]
+    back = e - jnp.mean(e, axis=1, keepdims=True) - unit * jnp.mean(e * unit, axis=1, keepdims=True)
     out[...] = (arrived[...].astype(F32).T + inv * back).astype(BF16)
-
-    @pl.when(pl.program_id(0) == 0)
-    def _():
-        gain_part[...] = jnp.zeros_like(gain_part)
-
-    gain_part[...] += jnp.sum(product, axis=0, keepdims=True)
 
 
 def pair_kernel(left, left_peer, right, right_peer, *buffers):
@@ -244,6 +236,7 @@
             pltpu.VMEM((32, 8, LANES), F32),
         ],
         compiler_params=params(),
+        cost_estimate=pl.CostEstimate(flops=1_000_000, bytes_accessed=0, transcendentals=0),
         name="tap_gradients",
     )(same, units, grad_conv)
 
@@ -343,10 +336,10 @@
             pl.BlockSpec((features, BLOCK), lambda i: (0, i)),
             pl.BlockSpec((1, features), lambda i: (0, 0)),
         ],
-        out_specs=[block, pl.BlockSpec((1, features), lambda i: (0, 0))],
-        out_shape=[jax.ShapeDtypeStruct((count, features), BF16), jax.ShapeDtypeStruct((1, features), F32)],
-        compiler_params=params(),
-        cost_estimate=pl.CostEstimate(flops=40_000_000_000, bytes_accessed=100_000_000, transcendentals=0),
+        out_specs=block,
+        out_shape=jax.ShapeDtypeStruct((count, features), BF16),
+        compiler_params=params(),
+        cost_estimate=pl.CostEstimate(flops=12_000_000_000, bytes_accessed=10_000_000, transcendentals=0),
         name="norm_backward",
     )(in_hbm(sent), in_hbm(other), in_hbm(frames), in_hbm(arrived), gain)
 
@@ -390,8 +383,8 @@
     blocks = count // BLOCK
     core, xl = lax.axis_index("core"), lax.axis_index("xl")
     first_block = lax.axis_index(FRAMES) * blocks
+    chunks, frames = lax.optimization_barrier((frame_chunks(returned.T, 4), frames))
     frames_before, frames_after = halos(frames)
-    chunks = frame_chunks(returned.T, 4)
     arrived = lax.all_to_all(chunks, "section", 0, 0).reshape(features, count)
 
     edge = jnp.full((1,), -1, jnp.int32)
@@ -433,23 +426,31 @@
     sent = sent + lax.dot_general(late[1], weight_in[1], contract, preferred_element_type=F32)
     sent = sent.astype(BF16)
     other = swap(sent, "tensor")
+    late, sent = lax.optimization_barrier((late, sent))
     parts = pair_product(normed_own, normed_peer, late, late_peer, 3, 1, parts)
     got = lax.all_to_all(parts.reshape(16, 40, 3 * width), PLANE, 0, 0)
 
-    grad_frames, gain_part = norm_back(sent, other, frames, arrived, norm_gain.reshape(1, features))
-    ready, gain_part = lax.optimization_barrier((grad_conv, gain_part))
+    ready, sent_again, _ = lax.optimization_barrier((grad_conv, sent, parts))
     taps_part = tap_sums(same, units, ready)
+    gain_part = sent_again.astype(F32) * normed_ext[HALO : HALO + count].astype(F32)
+    gain_part = jnp.sum(gain_part, axis=0) / norm_gain
     small = jnp.concatenate([taps_part, gain_part.reshape(2, width)], axis=0)
     small = small + swap(small, "core")
-    small = (small + swap(small, "xl")).astype(BF16)
-    shares = ring_shares(small, "y")
+    gain = small[32:]
+    corner = lax.ppermute(gain, ("xl", "tensor"), [(0, 3), (1, 2), (2, 1), (3, 0)])
+    across = swap(small, "xl"), swap(gain, "tensor"), corner
+    small, across, other = lax.optimization_barrier((small, across, other))
+    gain = (small[32:] + across[1]) + (across[0][32:] + across[2])
+    small = jnp.concatenate([small[:32] + across[0][:32], gain], axis=0)
+    shares = ring_shares(small.astype(BF16), "y")
+    grad_frames = norm_back(sent, other, frames, arrived, norm_gain.reshape(1, features))
+    got, grad_frames = lax.optimization_barrier((got, grad_frames))
     total = jnp.sum(got.astype(F32), axis=0)
     total, shares = lax.optimization_barrier((total, shares))
     summed = finish_rows(total.reshape(2, 20, 3 * width), xl)
     small = ring_sum(ring_shares(ring_sum(shares).astype(BF16), "section"))
     grad_kernel = small[:TAPS]
     grad_gain = small[32:].reshape(features)
-
     grad_out = summed[:, :width].T
     grad_in = jnp.stack([summed[:, width : 2 * width], summed[:, 2 * width :]])
     return (grad_frames, grad_in, grad_out, grad_kernel, grad_gain)

time: 133 us -> 125 us (0.940)
  waiting for transfers between devices: 27 us -> 19.7 us
  other arithmetic: 2.47 us -> 4.56 us
  starting transfers between devices: 46.9 us -> 45 us
    ppermute x8 -> x9, waiting for transfers between devices: 20.2 us -> 13.3 us  [swap(): return lax.ppermute(value, axis, [(0, 1), (1, 0)])]
    ppermute x8 -> x9, starting transfers between devices: 11.9 us -> 6.32 us  [swap(): return lax.ppermute(value, axis, [(0, 1), (1, 0)])]
    ppermute x6, waiting for transfers between devices: 5.29 us -> 1.93 us  [ring_shares(): lax.ppermute(value, axis, [(i, (i + by) % 4) for i in range(4)])]
    all_to_all x1, waiting for transfers between devices: 0.01 us -> 3.18 us  [body(): got = lax.all_to_all(parts.reshape(16, 40, 3 * width), PLANE, 0, 0)]
    ppermute x0 -> x1, starting transfers between devices: none -> 3.18 us  [body(): lax.ppermute(gain, ('xl', 'tensor'), [(0, 3), (1, 2), (2, 1), (3, 0)])]
    reduce_sum x0 -> x1, other arithmetic: none -> 2.08 us  [body(): gain_part = jnp.sum(gain_part, axis=0) / norm_gain]
    unnamed x35 -> x37, local copies, waits for them, and re-layouts: 4.51 us -> 4.49 us
  transfers between devices with their start and end apart: 20 -> 22, of which waited for: 11 -> 9; matrix products, arithmetic and copies ran while one was open for 11% -> 14% of each run, Pallas kernels for 22% -> 22%
where the time goes in v4:
time: 125 us; the launch traced here: 124 us
  starting transfers between devices  45 us (36%)
  Pallas kernels  34.9 us (28%)
  waiting for transfers between devices  19.7 us (16%)
  matrix products  11.7 us (9%)
  local copies, waits for them, and re-layouts  7.58 us (6%)
  other arithmetic  4.56 us (4%)
    ppermute x9, waiting for transfers between devices, swap(): return lax.ppermute(value, axis, [(0, 1), (1, 0)])  13.3 us
    all_to_all x1, starting transfers between devices, body(): got = lax.all_to_all(parts.reshape(16, 40, 3 * width), PLANE, 0, 0)  10.7 us
    ppermute x6, starting transfers between devices, ring_shares(): lax.ppermute(value, axis, [(i, (i + by) % 4) for i in range(4)])  8.88 us
    ppermute x2, starting transfers between devices, halos(): before = lax.ppermute(shard[shard.shape[0] - HALO:], FRAMES, up)  7.31 us
    pallas_call x2, Pallas kernels, pair_product(): pl.pallas_call(pair_kernel, grid=(made,), in_specs=[whole, whole, spec, s...  6.83 us
    ppermute x9, starting transfers between devices, swap(): return lax.ppermute(value, axis, [(0, 1), (1, 0)])  6.32 us
    all_to_all x1, starting transfers between devices, body(): arrived = lax.all_to_all(chunks, 'section', 0, 0).reshape(features, count)  6.05 us
    pallas_call x1, Pallas kernels, projected_back(): pl.pallas_call(backward_kernel, grid=(width // LANES,), in_specs=[smem(),...  5.6 us
  transfers between devices with their start and end apart: 22, of which 9 were waited for; matrix products, arithmetic and copies ran while one was open for 14% of the time, Pallas kernels for 22%

profile of v4, /device:TPU:0, one launch (start us, length us, event | category | flops | bytes accessed | tf_op | source)
XLA Modules:
  0.0 124.5 jit_solution(2383143991205535953)
XLA Ops:
  0.6 2.2 %frame_chunks.1 = bf16[4,320,512]{2,1,0:T(8,128)(2,1)} custom-call(bf16[320,2048]{1,0:T(8,128)(2,1)} %bitcast.50), custom_call_target="tpu_custom_call" | custom-call | tf_op jit(solution)/shard_map/frame_chunks/pallas_call | solution.py:295
  2.9 0.8 fusion.23
  3.7 3.9 %collective-permute-start = (bf16[16,1280]{1,0:T(8,128)(2,1)S(1)}, bf16[16,1280]{1,0:T(8,128)(2,1)S(1)}, u32[]{:S(2)}, u32[]{:S(2)}) collective-permute-start(bf16[16,1280]{1,0:T(8,128)(2,1)S(1)} %get-tuple-element.78), channel_id=1, source_target_pairs={{0,1},{1,2},{2,3},{3,8},{8,9},{9,10},{10,11},{11,16},{16,17},{17,1... | collective-permute-start | bytes 122888 | tf_op jit(solution)/shard_map/ppermute | solution.py:41
  7.6 1.3 %collective-permute-start.1 = (bf16[16,1280]{1,0:T(8,128)(2,1)S(1)}, bf16[16,1280]{1,0:T(8,128)(2,1)S(1)}, u32[]{:S(2)}, u32[]{:S(2)}) collective-permute-start(bf16[16,1280]{1,0:T(8,128)(2,1)S(1)} %get-tuple-element.77), channel_id=1, source_target_pairs={{1,0},{2,1},{3,2},{8,3},{9,8},{10,9},{11,10},{16,11},{17,16},{18,1... | collective-permute-start | bytes 122888 | tf_op jit(solution)/shard_map/ppermute | solution.py:42
  8.9 6.0 %all-to-all-start = ((bf16[4,320,512]{2,1,0:T(8,128)(2,1)}), bf16[4,320,512]{2,1,0:T(8,128)(2,1)S(1)}, u32[]{:S(2)}, u32[]{:S(2)}) async-start(bf16[4,320,512]{2,1,0:T(8,128)(2,1)} %frame_chunks.1), calls=%async_computation | async-start | bytes 2621440 | tf_op jit(solution)/shard_map/all_to_all | solution.py:388
  15.0 0.1 pad_add_fusion
  15.1 0.1 dynamic_slice.14
  15.1 0.1 fusion.20
  15.2 0.1 dynamic_slice.13
  15.3 0.1 compare_convert_fusion.same
  15.4 0.1 slice.75.fill
  15.4 0.1 slice.76
  15.5 3.6 %layer_norm.1 = (bf16[544,1280]{1,0:T(8,128)(2,1)S(1)}, bf16[1280,512]{1,0:T(8,128)(2,1)S(1)}) custom-call(bf16[512,1280]{1,0:T(8,128)(2,1)} %frames.1, bf16[16,1280]{1,0:T(8,128)(2,1)S(1)} %collective-permute-done.before, bf16[16,1280]{1,0:T(8,128)(2,1)S(1)} %collective-permute-done.1.after, f32[1,1280]{1,0:T(1,128)S(1)} %reshape.41.gain), custom_call_target="tpu_custom_call" | custom-call | tf_op jit(solution)/shard_map/layer_norm/pallas_call | solution.py:270
  19.2 3.3 %add_divide_fusion.gate = f32[544,640]{1,0:T(8,128)S(1)} fusion(bf16[544,1280]{1,0:T(8,128)(2,1)S(1)} %get-tuple-element.42, bf16[2,1280,640]{2,1,0:T(8,128)(2,1)} %param.13), kind=kOutput, calls=%fused_computation.19 | convolution fusion | flops 892334080 | bytes 4423680 | tf_op jit(solution)/shard_map/dot_general | solution.py:400
  22.5 2.3 %select_convert_fusion = (bf16[544,640]{1,0:T(8,128)(2,1)S(1)}, f32[544,640]{1,0:T(8,128)}) fusion(f32[544,640]{1,0:T(8,128)S(1)} %add_divide_fusion.gate, pred[544]{0:T(1024)(128)(4,1)S(1)} %slice.76, bf16[544,1280]{1,0:T(8,128)(2,1)S(1)} %get-tuple-element.42, bf16[2,1280,640]{2,1,0:T(8,128)(2,1)S(1)} %copy-done.12), kind=kOutput, calls=%fused_computation.18 | convolution fusion | flops 892334080 | bytes 6513664 | tf_op jit(solution)/shard_map/dot_general | solution.py:399
  24.9 5.2 %conv_forward.1 = (bf16[512,640]{1,0:T(8,128)(2,1)}, f32[512,640]{1,0:T(8,128)S(1)}) custom-call(s32[5]{0:T(128)S(1)} %compare_convert_fusion.same, s32[4]{0:T(128)S(1)} %slice.75.fill, bf16[544,640]{1,0:T(8,128)(2,1)S(1)} %get-tuple-element.82.units, f32[31,640]{1,0:T(8,128)S(1)} %copy-done.8), custom_call_target="tpu_custom_call" | custom-call | tf_op jit(solution)/shard_map/conv_forward/pallas_call | solution.py:210
  30.0 1.1 copy-done.9
  31.1 0.4 collective-permute-start.4
  31.5 1.2 core_halves.2
  32.7 0.8 copy-done.5
  33.5 0.2 all-to-all-done
  33.7 1.2 core_halves.3
  34.9 0.1 collective-permute-start.3
  35.0 0.7 copy-done.10
  35.7 2.6 %convolution_multiply_fusion.grad_conv = f32[512,640]{1,0:T(8,128)S(1)} fusion(f32[512,640]{1,0:T(8,128)S(1)} %copy-done.10, bf16[1280,512]{1,0:T(8,128)(2,1)} %bitcast.47, bf16[640,1280]{1,0:T(8,128)(2,1)S(1)} %copy-done), kind=kOutput, calls=%fused_computation.17 | convolution fusion | flops 839188480 | bytes 5570560 | tf_op jit(solution)/shard_map/dot_general | solution.py:410
  38.3 3.4 %collective-permute-start.5 = (f32[16,640]{1,0:T(8,128)S(1)}, f32[16,640]{1,0:T(8,128)S(1)}, u32[]{:S(2)}, u32[]{:S(2)}) collective-permute-start(f32[16,640]{1,0:T(8,128)S(1)} %get-tuple-element.76), channel_id=1, source_target_pairs={{0,1},{1,2},{2,3},{3,8},{8,9},{9,10},{10,11},{11,16},{16,17},{17,1... | collective-permute-start | bytes 122888 | tf_op jit(solution)/shard_map/ppermute | solution.py:41
  41.7 1.3 %collective-permute-start.6 = (f32[16,640]{1,0:T(8,128)S(1)}, f32[16,640]{1,0:T(8,128)S(1)}, u32[]{:S(2)}, u32[]{:S(2)}) collective-permute-start(f32[16,640]{1,0:T(8,128)S(1)} %get-tuple-element.75), channel_id=1, source_target_pairs={{1,0},{2,1},{3,2},{8,3},{9,8},{10,9},{11,10},{16,11},{17,16},{18,1... | collective-permute-start | bytes 122888 | tf_op jit(solution)/shard_map/ppermute | solution.py:42
  43.0 3.4 %weight_gradient.2.buffers_0_ = bf16[640,1920]{1,0:T(8,128)(2,1)} custom-call(bf16[640,512]{1,0:T(8,128)(2,1)S(1)} %get-tuple-element.44.left, bf16[640,512]{1,0:T(8,128)(2,1)S(1)} %collective-permute-done.3.left_peer, bf16[1,512,640]{2,1,0:T(8,128)(2,1)} %bitcast.6.right, bf16[1,512,640]{2,1,0:T(8,128)(2,1)} %bitcast.7.right_peer), custom_call_target="tpu_custom_call" | custom-call | tf_op jit(solution)/shard_map/weight_gradient/pallas_call | solution.py:352
  46.4 1.2 collective-permute-done.6.after
  47.6 5.6 %conv_backward.1.right = bf16[2,512,640]{2,1,0:T(8,128)(2,1)S(1)} custom-call(s32[5]{0:T(128)S(1)} %compare_convert_fusion.same, s32[4]{0:T(128)S(1)} %slice.75.fill, f32[512,640]{1,0:T(8,128)S(1)} %convolution_multiply_fusion.grad_conv, f32[16,640]{1,0:T(8,128)S(1)} %collective-permute-done.5.before, f32[16,640]{1,0:T(8,128)S(1)} %collective-permute-done.6.after, ...), custom_call_target="tpu_custom_call" | custom-call | tf_op jit(solution)/shard_map/conv_backward/pallas_call | solution.py:246
  53.2 1.0 collective-permute-start.7
  54.2 0.1 collective-permute-start.2
  54.3 1.2 fusion.1
  55.5 2.3 %fusion.sent = bf16[512,1280]{1,0:T(8,128)(2,1)} fusion(f32[512,1280]{1,0:T(8,128)S(1)} %fusion.1, bf16[2,1280,640]{2,1,0:T(8,128)(2,1)S(1)} %copy-done.13, bf16[2,512,640]{2,1,0:T(8,128)(2,1)S(1)} %conv_backward.1.right), kind=kOutput, calls=%fused_computation.2 | convolution fusion | flops 840171520 | bytes 6225920 | tf_op jit(solution)/shard_map/dot_general | solution.py:425
  57.8 3.0 %collective-permute-start.12 = (bf16[512,1280]{1,0:T(8,128)(2,1)}, bf16[512,1280]{1,0:T(8,128)(2,1)}, u32[]{:S(2)}, u32[]{:S(2)}) collective-permute-start(bf16[512,1280]{1,0:T(8,128)(2,1)} %fusion.sent), channel_id=1, source_target_pairs={{0,4},{4,0},{1,5},{5,1},{2,6},{6,2},{3,7},{7,3},{8,12},{12,8},{9,1... | collective-permute-start | bytes 3932168 | tf_op jit(solution)/shard_map/ppermute | solution.py:34
  60.8 3.4 %weight_gradient.3 = bf16[640,1920]{1,0:T(8,128)(2,1)} custom-call(bf16[640,512]{1,0:T(8,128)(2,1)S(1)} %copy-done.6, bf16[640,512]{1,0:T(8,128)(2,1)S(1)} %collective-permute-done.2.left_peer, bf16[2,512,640]{2,1,0:T(8,128)(2,1)S(1)} %conv_backward.1.right, ...), custom_call_target="tpu_custom_call", output_to_operand_aliasing={{}: (4, {})} | custom-call | tf_op jit(solution)/shard_map/weight_gradient/pallas_call | solution.py:352
  64.2 10.7 %all-to-all-start.1 = ((bf16[16,40,1920]{2,1,0:T(8,128)(2,1)}), bf16[16,40,1920]{2,1,0:T(8,128)(2,1)}, u32[]{:S(2)}, u32[]{:S(2)}) async-start(bf16[16,40,1920]{2,1,0:T(8,128)(2,1)} %bitcast.49), calls=%async_computation.1 | async-start | bytes 4915200 | tf_op jit(solution)/shard_map/all_to_all | solution.py:431
  74.9 2.1 %multiply_reduce_fusion = f32[1280]{0:T(1024)S(1)} fusion(bf16[512,1280]{1,0:T(8,128)(2,1)} %fusion.sent, bf16[544,1280]{1,0:T(8,128)(2,1)} %copy-done.4), kind=kLoop, calls=%fused_computation.3 | loop fusion | flops 2620160 | bytes 2626560 | tf_op jit(solution)/shard_map/reduce_sum | solution.py:436
  77.0 1.1 copy-done.3
  78.1 4.0 %tap_gradients.1 = f32[32,640]{1,0:T(8,128)S(1)} custom-call(s32[5]{0:T(128)S(1)} %compare_convert_fusion.same, bf16[544,640]{1,0:T(8,128)(2,1)S(1)} %copy-done.3, f32[512,640]{1,0:T(8,128)S(1)} %convolution_multiply_fusion.grad_conv), custom_call_target="tpu_custom_call" | custom-call | flops 1000000 | tf_op jit(solution)/shard_map/tap_gradients/pallas_call | solution.py:228
  82.2 0.1 collective-permute-start.8
  82.2 1.3 %collective-permute-done.8 = f32[34,640]{1,0:T(8,128)S(1)} collective-permute-done((f32[34,640]{1,0:T(8,128)S(1)}, f32[34,640]{1,0:T(8,128)S(1)}, u32[]{:S(2)}, u32[]{:S(2)}) %collective-permute-start.8) | collective-permute-done | bytes 87072 | tf_op jit(solution)/shard_map/ppermute | solution.py:34
  83.6 0.1 collective-permute-start.9
  83.7 1.5 %collective-permute-start.10 = (f32[2,640]{1,0:T(2,128)S(1)}, f32[2,640]{1,0:T(2,128)S(1)}, u32[]{:S(2)}, u32[]{:S(2)}) collective-permute-start(f32[2,640]{1,0:T(2,128)S(1)} %slice.98), channel_id=1, source_target_pairs={{0,4},{4,0},{1,5},{5,1},{2,6},{6,2},{3,7},{7,3},{8,12},{12,8},{9,1... | collective-permute-start | bytes 15368 | tf_op jit(solution)/shard_map/ppermute | solution.py:34
  85.2 3.2 %collective-permute-start.11 = (f32[2,640]{1,0:T(2,128)S(1)}, f32[2,640]{1,0:T(2,128)S(1)}, u32[]{:S(2)}, u32[]{:S(2)}) collective-permute-start(f32[2,640]{1,0:T(2,128)S(1)} %slice.98), channel_id=1, source_target_pairs={{0,68},{4,64},{64,4},{68,0},{1,69},{5,65},{65,5},{69,1},{2,70},{6,... | collective-permute-start | bytes 15368 | tf_op jit(solution)/shard_map/ppermute | solution.py:440
  88.3 2.9 %collective-permute-done.12.other = bf16[512,1280]{1,0:T(8,128)(2,1)} collective-permute-done((bf16[512,1280]{1,0:T(8,128)(2,1)}, bf16[512,1280]{1,0:T(8,128)(2,1)}, u32[]{:S(2)}, u32[]{:S(2)}) %collective-permute-start.12) | collective-permute-done | bytes 1310752 | tf_op jit(solution)/shard_map/ppermute | solution.py:34
  91.2 1.7 %collective-permute-done.10 = f32[2,640]{1,0:T(2,128)S(1)} collective-permute-done((f32[2,640]{1,0:T(2,128)S(1)}, f32[2,640]{1,0:T(2,128)S(1)}, u32[]{:S(2)}, u32[]{:S(2)}) %collective-permute-start.10) | collective-permute-done | bytes 5152 | tf_op jit(solution)/shard_map/ppermute | solution.py:34
  92.9 5.1 %collective-permute-done.9 = f32[34,640]{1,0:T(8,128)S(1)} collective-permute-done((f32[34,640]{1,0:T(8,128)S(1)}, f32[34,640]{1,0:T(8,128)S(1)}, u32[]{:S(2)}, u32[]{:S(2)}) %collective-permute-start.9) | collective-permute-done | bytes 87072 | tf_op jit(solution)/shard_map/ppermute | solution.py:34
  98.1 0.1 collective-permute-start.13
  98.2 0.4 collective-permute-start.14
  98.6 2.8 %collective-permute-start.15 = (bf16[34,640]{1,0:T(8,128)(2,1)S(1)}, bf16[34,640]{1,0:T(8,128)(2,1)S(1)}, u32[]{:S(2)}, u32[]{:S(2)}) collective-permute-start(bf16[34,640]{1,0:T(8,128)(2,1)S(1)} %pad_maximum_fusion.2), channel_id=1, source_target_pairs={{0,48},{16,0},{32,16},{48,32},{1,49},{17,1},{33,17},{49,33},{2,50}... | collective-permute-start | bytes 130568 | tf_op jit(solution)/shard_map/ppermute | solution.py:365
  101.4 5.1 %norm_backward.1 = bf16[512,1280]{1,0:T(8,128)(2,1)} custom-call(bf16[512,1280]{1,0:T(8,128)(2,1)} %fusion.sent, bf16[512,1280]{1,0:T(8,128)(2,1)} %collective-permute-done.12.other, bf16[512,1280]{1,0:T(8,128)(2,1)} %frames.1, bf16[1280,512]{1,0:T(8,128)(2,1)} %bitcast.48, f32[1,1280]{1,0:T(1,128)S(1)} %reshape.41.gain), custom_call_target="tpu_custom_call" | custom-call | flops 12000000000 | bytes 10000000 | tf_op jit(solution)/shard_map/norm_backward/pallas_call | solution.py:329
  106.5 3.2 %all-to-all-done.1 = bf16[16,40,1920]{2,1,0:T(8,128)(2,1)} async-done(((bf16[16,40,1920]{2,1,0:T(8,128)(2,1)}), bf16[16,40,1920]{2,1,0:T(8,128)(2,1)}, u32[]{:S(2)}, u32[]{:S(2)}) %all-to-all-start.1) | async-done | bytes 2457632 | tf_op jit(solution)/shard_map/all_to_all | solution.py:431
  109.7 2.1 %convert_reduce_fusion = f32[40,1920]{1,0:T(8,128)S(1)} fusion(bf16[16,40,1920]{2,1,0:T(8,128)(2,1)} %all-to-all-done.1), kind=kLoop, calls=%fused_computation | loop fusion | flops 2380800 | bytes 2764800 | tf_op jit(solution)/shard_map/reduce_sum | solution.py:448
  111.8 2.3 %collective-permute-start.17 = (bf16[34,640]{1,0:T(8,128)(2,1)S(1)}, bf16[34,640]{1,0:T(8,128)(2,1)S(1)}, u32[]{:S(2)}, u32[]{:S(2)}) collective-permute-start(bf16[34,640]{1,0:T(8,128)(2,1)S(1)} %add_convert_fusion), channel_id=1, source_target_pairs={{0,2},{1,3},{2,0},{3,1},{4,6},{5,7},{6,4},{7,5},{8,10},{9,11},{10,... | collective-permute-start | bytes 130568 | tf_op jit(solution)/shard_map/ppermute | solution.py:365
  114.2 0.5 collective-permute-start.18
  114.7 2.8 %collective-permute-start.19 = (bf16[34,640]{1,0:T(8,128)(2,1)S(1)}, bf16[34,640]{1,0:T(8,128)(2,1)S(1)}, u32[]{:S(2)}, u32[]{:S(2)}) collective-permute-start(bf16[34,640]{1,0:T(8,128)(2,1)S(1)} %add_convert_fusion), channel_id=1, source_target_pairs={{0,3},{1,0},{2,1},{3,2},{4,7},{5,4},{6,5},{7,6},{8,11},{9,8},{10,9... | collective-permute-start | bytes 130568 | tf_op jit(solution)/shard_map/ppermute | solution.py:365
  117.5 0.1 collective-permute-start.16
  117.6 1.9 %collective-permute-done.18 = bf16[34,640]{1,0:T(8,128)(2,1)S(1)} collective-permute-done((bf16[34,640]{1,0:T(8,128)(2,1)S(1)}, bf16[34,640]{1,0:T(8,128)(2,1)S(1)}, u32[]{:S(2)}, u32[]{:S(2)}) %collective-permute-start.18) | collective-permute-done | bytes 43552 | tf_op jit(solution)/shard_map/ppermute | solution.py:365
  119.5 0.6 slice.102
  120.2 0.6 reshape.45
  120.8 2.3 %collective-permute-done.16 = f32[20,1920]{1,0:T(8,128)S(1)} collective-permute-done((f32[20,1920]{1,0:T(8,128)S(1)}, f32[20,1920]{1,0:T(8,128)S(1)}, u32[]{:S(2)}, u32[]{:S(2)}) %collective-permute-start.16) | collective-permute-done | bytes 153632 | tf_op jit(solution)/shard_map/ppermute | solution.py:34
  123.1 0.6 slice_bitcast_fusion.4
  123.8 0.7 copy.17
  (62 shorter events, 0.4 us)
Async XLA Ops:
  0.6 34.4 %copy-start = (bf16[640,1280]{1,0:T(8,128)(2,1)S(1)}, bf16[640,1280]{1,0:T(8,128)(2,1)}, u32[]{:S(2)}) copy-start(bf16[640,1280]{1,0:T(8,128)(2,1)} %param.15) | copy-start | bytes 4915204
  2.9 12.1 %copy-start.15 = (s32[256]{0:T(256)S(1)}, s32[256]{0:T(256)}, u32[]{:S(2)}) copy-start(s32[256]{0:T(256)} %param.17) | copy-start | bytes 3076
  2.9 12.1 %copy-start.16 = (s32[256]{0:T(256)S(1)}, s32[256]{0:T(256)}, u32[]{:S(2)}) copy-start(s32[256]{0:T(256)} %param.16) | copy-start | bytes 3076
  2.9 12.6 %copy-start.14 = (f32[1280]{0:T(1024)S(1)}, f32[1280]{0:T(1024)}, u32[]{:S(2)}) copy-start(f32[1280]{0:T(1024)} %param.12) | copy-start | bytes 15364
  3.7 11.8 %collective-permute-start = (bf16[16,1280]{1,0:T(8,128)(2,1)S(1)}, bf16[16,1280]{1,0:T(8,128)(2,1)S(1)}, u32[]{:S(2)}, u32[]{:S(2)}) collective-permute-start(bf16[16,1280]{1,0:T(8,128)(2,1)S(1)} %get-tuple-element.78), channel_id=1, source_target_pairs={{0,1},{1,2},{2,3},{3,8},{8,9},{9,10},{10,11},{11,16},{16,17},{17,1... | collective-permute-start | bytes 122888 | tf_op jit(solution)/shard_map/ppermute | solution.py:41
  7.6 7.9 %collective-permute-start.1 = (bf16[16,1280]{1,0:T(8,128)(2,1)S(1)}, bf16[16,1280]{1,0:T(8,128)(2,1)S(1)}, u32[]{:S(2)}, u32[]{:S(2)}) collective-permute-start(bf16[16,1280]{1,0:T(8,128)(2,1)S(1)} %get-tuple-element.77), channel_id=1, source_target_pairs={{1,0},{2,1},{3,2},{8,3},{9,8},{10,9},{11,10},{16,11},{17,16},{18,1... | collective-permute-start | bytes 122888 | tf_op jit(solution)/shard_map/ppermute | solution.py:42
  8.9 24.7 %all-to-all-start = ((bf16[4,320,512]{2,1,0:T(8,128)(2,1)}), bf16[4,320,512]{2,1,0:T(8,128)(2,1)S(1)}, u32[]{:S(2)}, u32[]{:S(2)}) async-start(bf16[4,320,512]{2,1,0:T(8,128)(2,1)} %frame_chunks.1), calls=%async_computation | async-start | bytes 2621440 | tf_op jit(solution)/shard_map/all_to_all | solution.py:388
  19.1 3.3 %copy-start.4 = (bf16[544,1280]{1,0:T(8,128)(2,1)}, bf16[544,1280]{1,0:T(8,128)(2,1)S(1)}, u32[]{:S(2)}) copy-start(bf16[544,1280]{1,0:T(8,128)(2,1)S(1)} %get-tuple-element.42) | copy-start | bytes 4177924
  19.1 3.3 %copy-start.12 = (bf16[2,1280,640]{2,1,0:T(8,128)(2,1)S(1)}, bf16[2,1280,640]{2,1,0:T(8,128)(2,1)}, u32[]{:S(2)}) copy-start(bf16[2,1280,640]{2,1,0:T(8,128)(2,1)} %param.13) | copy-start | bytes 9830404
  22.5 2.4 %copy-start.11 = (f32[544,640]{1,0:T(8,128)}, f32[544,640]{1,0:T(8,128)S(1)}, u32[]{:S(2)}) copy-start(f32[544,640]{1,0:T(8,128)S(1)} %add_divide_fusion.gate) | copy-start | bytes 4177924
  22.5 2.4 %copy-start.8 = (f32[31,640]{1,0:T(8,128)S(1)}, f32[31,640]{1,0:T(8,128)}, u32[]{:S(2)}) copy-start(f32[31,640]{1,0:T(8,128)} %taps.3) | copy-start | bytes 238084
  22.5 9.0 %copy-start.7 = (bf16[160,160]{1,0:T(8,128)(2,1)S(1)}, bf16[160,160]{1,0:T(8,128)(2,1)}, u32[]{:S(2)}) copy-start(bf16[160,160]{1,0:T(8,128)(2,1)} %constant.46.clone.order) | copy-start | bytes 153604
  24.9 6.6 %copy-start.2 = (bf16[544,640]{1,0:T(8,128)(2,1)}, bf16[544,640]{1,0:T(8,128)(2,1)S(1)}, u32[]{:S(2)}) copy-start(bf16[544,640]{1,0:T(8,128)(2,1)S(1)} %get-tuple-element.82.units) | copy-start | bytes 2088964
  30.0 1.1 copy-start.9
  31.1 11.9 %collective-permute-start.4 = (bf16[512,640]{1,0:T(8,128)(2,1)}, bf16[512,640]{1,0:T(8,128)(2,1)}, u32[]{:S(2)}, u32[]{:S(2)}) collective-permute-start(bf16[512,640]{1,0:T(8,128)(2,1)} %get-tuple-element.46), channel_id=1, source_target_pairs={{0,8},{8,0},{1,9},{9,1},{2,10},{10,2},{3,11},{11,3},{4,12},{12,4},... | collective-permute-start | bytes 1966088 | tf_op jit(solution)/shard_map/ppermute | solution.py:34
  32.7 0.8 copy-start.5
  33.7 1.3 %copy-start.1 = (bf16[4,320,512]{2,1,0:T(8,128)(2,1)}, bf16[4,320,512]{2,1,0:T(8,128)(2,1)S(1)}, u32[]{:S(2)}) copy-start(bf16[4,320,512]{2,1,0:T(8,128)(2,1)S(1)} %all-to-all-done) | copy-start | bytes 3932164
  33.7 2.0 %copy-start.10 = (f32[512,640]{1,0:T(8,128)S(1)}, f32[512,640]{1,0:T(8,128)}, u32[]{:S(2)}) copy-start(f32[512,640]{1,0:T(8,128)} %copy-done.9) | copy-start | bytes 3932164
  34.9 8.2 %collective-permute-start.3 = (bf16[640,512]{1,0:T(8,128)(2,1)}, bf16[640,512]{1,0:T(8,128)(2,1)S(1)}, u32[]{:S(2)}, u32[]{:S(2)}) collective-permute-start(bf16[640,512]{1,0:T(8,128)(2,1)} %get-tuple-element.45), channel_id=1, source_target_pairs={{0,8},{8,0},{1,9},{9,1},{2,10},{10,2},{3,11},{11,3},{4,12},{12,4},... | collective-permute-start | bytes 1966088 | tf_op jit(solution)/shard_map/ppermute | solution.py:34
  38.3 8.2 %collective-permute-start.5 = (f32[16,640]{1,0:T(8,128)S(1)}, f32[16,640]{1,0:T(8,128)S(1)}, u32[]{:S(2)}, u32[]{:S(2)}) collective-permute-start(f32[16,640]{1,0:T(8,128)S(1)} %get-tuple-element.76), channel_id=1, source_target_pairs={{0,1},{1,2},{2,3},{3,8},{8,9},{9,10},{10,11},{11,16},{16,17},{17,1... | collective-permute-start | bytes 122888 | tf_op jit(solution)/shard_map/ppermute | solution.py:41
  41.7 5.9 %collective-permute-start.6 = (f32[16,640]{1,0:T(8,128)S(1)}, f32[16,640]{1,0:T(8,128)S(1)}, u32[]{:S(2)}, u32[]{:S(2)}) collective-permute-start(f32[16,640]{1,0:T(8,128)S(1)} %get-tuple-element.75), channel_id=1, source_target_pairs={{1,0},{2,1},{3,2},{8,3},{9,8},{10,9},{11,10},{16,11},{17,16},{18,1... | collective-permute-start | bytes 122888 | tf_op jit(solution)/shard_map/ppermute | solution.py:42
  47.6 6.6 %copy-start.17 = (bf16[640,512]{1,0:T(8,128)(2,1)S(1)}, bf16[640,512]{1,0:T(8,128)(2,1)}, u32[]{:S(2)}) copy-start(bf16[640,512]{1,0:T(8,128)(2,1)} %get-tuple-element.39) | copy-start | bytes 1966084
  47.6 6.7 %copy-start.13 = (bf16[2,1280,640]{2,1,0:T(8,128)(2,1)S(1)}, bf16[2,1280,640]{2,1,0:T(8,128)(2,1)}, u32[]{:S(2)}) copy-start(bf16[2,1280,640]{2,1,0:T(8,128)(2,1)} %param.13) | copy-start | bytes 9830404
  53.2 7.6 %collective-permute-start.7 = (bf16[2,512,640]{2,1,0:T(8,128)(2,1)S(1)}, bf16[2,512,640]{2,1,0:T(8,128)(2,1)S(1)}, u32[]{:S(2)}, u32[]{:S(2)}) collective-permute-start(bf16[2,512,640]{2,1,0:T(8,128)(2,1)S(1)} %conv_backward.1.right), channel_id=1, source_target_pairs={{0,8},{8,0},{1,9},{9,1},{2,10},{10,2},{3,11},{11,3},{4,12},{12,4},... | collective-permute-start | bytes 3932168 | tf_op jit(solution)/shard_map/ppermute | solution.py:34
  54.2 6.6 %collective-permute-start.2 = (bf16[640,512]{1,0:T(8,128)(2,1)S(1)}, bf16[640,512]{1,0:T(8,128)(2,1)S(1)}, u32[]{:S(2)}, u32[]{:S(2)}) collective-permute-start(bf16[640,512]{1,0:T(8,128)(2,1)S(1)} %copy-done.17), channel_id=1, source_target_pairs={{0,8},{8,0},{1,9},{9,1},{2,10},{10,2},{3,11},{11,3},{4,12},{12,4},... | collective-permute-start | bytes 1966088 | tf_op jit(solution)/shard_map/ppermute | solution.py:34
  55.5 5.3 %copy-start.6 = (bf16[640,512]{1,0:T(8,128)(2,1)S(1)}, bf16[640,512]{1,0:T(8,128)(2,1)}, u32[]{:S(2)}) copy-start(bf16[640,512]{1,0:T(8,128)(2,1)} %copy-done.5) | copy-start | bytes 1966084
  57.8 33.4 %collective-permute-start.12 = (bf16[512,1280]{1,0:T(8,128)(2,1)}, bf16[512,1280]{1,0:T(8,128)(2,1)}, u32[]{:S(2)}, u32[]{:S(2)}) collective-permute-start(bf16[512,1280]{1,0:T(8,128)(2,1)} %fusion.sent), channel_id=1, source_target_pairs={{0,4},{4,0},{1,5},{5,1},{2,6},{6,2},{3,7},{7,3},{8,12},{12,8},{9,1... | collective-permute-start | bytes 3932168 | tf_op jit(solution)/shard_map/ppermute | solution.py:34
  64.2 45.5 %all-to-all-start.1 = ((bf16[16,40,1920]{2,1,0:T(8,128)(2,1)}), bf16[16,40,1920]{2,1,0:T(8,128)(2,1)}, u32[]{:S(2)}, u32[]{:S(2)}) async-start(bf16[16,40,1920]{2,1,0:T(8,128)(2,1)} %bitcast.49), calls=%async_computation.1 | async-start | bytes 4915200 | tf_op jit(solution)/shard_map/all_to_all | solution.py:431
  77.0 1.1 copy-start.3
  82.2 1.4 %collective-permute-start.8 = (f32[34,640]{1,0:T(8,128)S(1)}, f32[34,640]{1,0:T(8,128)S(1)}, u32[]{:S(2)}, u32[]{:S(2)}) collective-permute-start(f32[34,640]{1,0:T(8,128)S(1)} %pad_maximum_fusion.1), channel_id=1, source_target_pairs={{0,8},{8,0},{1,9},{9,1},{2,10},{10,2},{3,11},{11,3},{4,12},{12,4},... | collective-permute-start | bytes 261128 | tf_op jit(solution)/shard_map/ppermute | solution.py:34
  83.6 14.5 %collective-permute-start.9 = (f32[34,640]{1,0:T(8,128)S(1)}, f32[34,640]{1,0:T(8,128)S(1)}, u32[]{:S(2)}, u32[]{:S(2)}) collective-permute-start(f32[34,640]{1,0:T(8,128)S(1)} %fusion.21), channel_id=1, source_target_pairs={{0,64},{64,0},{1,65},{65,1},{2,66},{66,2},{3,67},{67,3},{4,68},{68... | collective-permute-start | bytes 261128 | tf_op jit(solution)/shard_map/ppermute | solution.py:34
  83.7 9.3 %collective-permute-start.10 = (f32[2,640]{1,0:T(2,128)S(1)}, f32[2,640]{1,0:T(2,128)S(1)}, u32[]{:S(2)}, u32[]{:S(2)}) collective-permute-start(f32[2,640]{1,0:T(2,128)S(1)} %slice.98), channel_id=1, source_target_pairs={{0,4},{4,0},{1,5},{5,1},{2,6},{6,2},{3,7},{7,3},{8,12},{12,8},{9,1... | collective-permute-start | bytes 15368 | tf_op jit(solution)/shard_map/ppermute | solution.py:34
  85.2 7.8 %collective-permute-start.11 = (f32[2,640]{1,0:T(2,128)S(1)}, f32[2,640]{1,0:T(2,128)S(1)}, u32[]{:S(2)}, u32[]{:S(2)}) collective-permute-start(f32[2,640]{1,0:T(2,128)S(1)} %slice.98), channel_id=1, source_target_pairs={{0,68},{4,64},{64,4},{68,0},{1,69},{5,65},{65,5},{69,1},{2,70},{6,... | collective-permute-start | bytes 15368 | tf_op jit(solution)/shard_map/ppermute | solution.py:440
  98.1 13.7 %collective-permute-start.13 = (bf16[34,640]{1,0:T(8,128)(2,1)S(1)}, bf16[34,640]{1,0:T(8,128)(2,1)S(1)}, u32[]{:S(2)}, u32[]{:S(2)}) collective-permute-start(bf16[34,640]{1,0:T(8,128)(2,1)S(1)} %pad_maximum_fusion.2), channel_id=1, source_target_pairs={{0,16},{16,32},{32,48},{48,0},{1,17},{17,33},{33,49},{49,1},{2,18}... | collective-permute-start | bytes 130568 | tf_op jit(solution)/shard_map/ppermute | solution.py:365
  98.2 13.6 %collective-permute-start.14 = (bf16[34,640]{1,0:T(8,128)(2,1)S(1)}, bf16[34,640]{1,0:T(8,128)(2,1)S(1)}, u32[]{:S(2)}, u32[]{:S(2)}) collective-permute-start(bf16[34,640]{1,0:T(8,128)(2,1)S(1)} %pad_maximum_fusion.2), channel_id=1, source_target_pairs={{0,32},{16,48},{32,0},{48,16},{1,33},{17,49},{33,1},{49,17},{2,34}... | collective-permute-start | bytes 130568 | tf_op jit(solution)/shard_map/ppermute | solution.py:365
  98.6 13.2 %collective-permute-start.15 = (bf16[34,640]{1,0:T(8,128)(2,1)S(1)}, bf16[34,640]{1,0:T(8,128)(2,1)S(1)}, u32[]{:S(2)}, u32[]{:S(2)}) collective-permute-start(bf16[34,640]{1,0:T(8,128)(2,1)S(1)} %pad_maximum_fusion.2), channel_id=1, source_target_pairs={{0,48},{16,0},{32,16},{48,32},{1,49},{17,1},{33,17},{49,33},{2,50}... | collective-permute-start | bytes 130568 | tf_op jit(solution)/shard_map/ppermute | solution.py:365
  111.8 5.7 %collective-permute-start.17 = (bf16[34,640]{1,0:T(8,128)(2,1)S(1)}, bf16[34,640]{1,0:T(8,128)(2,1)S(1)}, u32[]{:S(2)}, u32[]{:S(2)}) collective-permute-start(bf16[34,640]{1,0:T(8,128)(2,1)S(1)} %add_convert_fusion), channel_id=1, source_target_pairs={{0,2},{1,3},{2,0},{3,1},{4,6},{5,7},{6,4},{7,5},{8,10},{9,11},{10,... | collective-permute-start | bytes 130568 | tf_op jit(solution)/shard_map/ppermute | solution.py:365
  114.2 5.3 %collective-permute-start.18 = (bf16[34,640]{1,0:T(8,128)(2,1)S(1)}, bf16[34,640]{1,0:T(8,128)(2,1)S(1)}, u32[]{:S(2)}, u32[]{:S(2)}) collective-permute-start(bf16[34,640]{1,0:T(8,128)(2,1)S(1)} %add_convert_fusion), channel_id=1, source_target_pairs={{0,1},{1,2},{2,3},{3,0},{4,5},{5,6},{6,7},{7,4},{8,9},{9,10},{10,1... | collective-permute-start | bytes 130568 | tf_op jit(solution)/shard_map/ppermute | solution.py:365
  114.7 4.9 %collective-permute-start.19 = (bf16[34,640]{1,0:T(8,128)(2,1)S(1)}, bf16[34,640]{1,0:T(8,128)(2,1)S(1)}, u32[]{:S(2)}, u32[]{:S(2)}) collective-permute-start(bf16[34,640]{1,0:T(8,128)(2,1)S(1)} %add_convert_fusion), channel_id=1, source_target_pairs={{0,3},{1,0},{2,1},{3,2},{4,7},{5,4},{6,5},{7,6},{8,11},{9,8},{10,9... | collective-permute-start | bytes 130568 | tf_op jit(solution)/shard_map/ppermute | solution.py:365
  117.5 5.6 %collective-permute-start.16 = (f32[20,1920]{1,0:T(8,128)S(1)}, f32[20,1920]{1,0:T(8,128)S(1)}, u32[]{:S(2)}, u32[]{:S(2)}) collective-permute-start(f32[20,1920]{1,0:T(8,128)S(1)} %dynamic-slice_bitcast_fusion), channel_id=1, source_target_pairs={{0,64},{64,0},{1,65},{65,1},{2,66},{66,2},{3,67},{67,3},{4,68},{68... | collective-permute-start | bytes 460808 | tf_op jit(solution)/shard_map/ppermute | solution.py:34

commit v5 on v4

--- a/solution.py
+++ b/solution.py
@@ -26,6 +26,10 @@
     return pltpu.CompilerParams(vmem_limit_bytes=mib * MIB)
 
 
+def duration(us):
+    return pl.CostEstimate(flops=round(us * 1.15e9), bytes_accessed=0, transcendentals=0)
+
+
 def in_hbm(array):
     return pltpu.with_memory_space_constraint(array, pltpu.HBM)
 
@@ -36,19 +40,25 @@
 
 def halos(shard):
     peers = lax.axis_size(FRAMES)
-    up = [(i, i + 1) for i in range(peers - 1)]
-    down = [(j, i) for i, j in up]
-    before = lax.ppermute(shard[shard.shape[0] - HALO :], FRAMES, up)
-    after = lax.ppermute(shard[:HALO], FRAMES, down)
-    return before, after
-
-
-def fill_windows(win, main, before, after, same):
+    odd = lax.axis_index(FRAMES) % 2 == 1
+    first, last = shard[:HALO], shard[shard.shape[0] - HALO :]
+    pairs = [(i, i ^ 1) for i in range(peers)]
+    across = [(i, i + 1) for i in range(1, peers - 1, 2)]
+    across = across + [(j, i) for i, j in across]
+    inner = lax.ppermute(jnp.where(odd, first, last), FRAMES, pairs)
+    outer = lax.ppermute(jnp.where(odd, last, first), FRAMES, across)
+    return inner, outer
+
+
+def fill_windows(win, main, inner, outer, same):
+    odd = same[win.shape[0] + 1] == 1
+    before = jnp.where(odd, inner[...], outer[...])
+    after = jnp.where(odd, outer[...], inner[...])
     blocks = win.shape[0]
     for b in range(blocks):
         lo, hi = b * BLOCK, (b + 1) * BLOCK
-        prior = before[...] if b == 0 else main[lo - HALO : lo, :]
-        later = after[...] if b == blocks - 1 else main[hi : hi + HALO, :]
+        prior = before if b == 0 else main[lo - HALO : lo, :]
+        later = after if b == blocks - 1 else main[hi : hi + HALO, :]
         win[b, HALO : HALO + BLOCK, :] = main[lo:hi, :].astype(F32)
         win[b, :HALO, :] = jnp.where(same[b] == 1, prior.astype(F32), 0.0)
         win[b, HALO + BLOCK :, :] = jnp.where(same[b + 1] == 1, later.astype(F32), 0.0)
@@ -114,8 +124,8 @@
     out[...] = jnp.sum(sums[...], axis=1)
 
 
-def backward_kernel(same, fill, grad_conv, before, after, taps, value, gate, out, win):
-    fill_windows(win, grad_conv, before, after, same)
+def backward_kernel(same, fill, grad_conv, inner, outer, taps, value, gate, out, win):
+    fill_windows(win, grad_conv, inner, outer, same)
 
     def step(b, carry):
         grad_units = jnp.where(valid_rows(fill, b), convolve(win, b, taps, True), 0.0)
@@ -130,7 +140,7 @@
     lax.fori_loop(0, win.shape[0], step, 0)
 
 
-def norm_kernel(frames, before, after, gain, out, out_t):
+def norm_kernel(place, frames, inner, outer, gain, out, out_t):
     def rows(block):
         x = block.astype(F32)
         center = x - jnp.mean(x, axis=1, keepdims=True)
@@ -144,8 +154,9 @@
 
     @pl.when(i == 0)
     def _():
-        out[:HALO, :] = rows(before[...])
-        out[out.shape[0] - HALO :, :] = rows(after[...])
+        odd = place[2] % 2 == 1
+        out[:HALO, :] = rows(jnp.where(odd, inner[...].astype(F32), outer[...].astype(F32)))
+        out[out.shape[0] - HALO :, :] = rows(jnp.where(odd, outer[...].astype(F32), inner[...].astype(F32)))
 
 
 def chunks_kernel(rows, out, held, sems):
@@ -214,11 +225,11 @@
         out_specs=[lanes(count), lanes(count)],
         out_shape=[
             jax.ShapeDtypeStruct((count, width), BF16),
-            jax.ShapeDtypeStruct((count, width), F32),
+            pltpu.HBM((count, width), F32),
         ],
         scratch_shapes=[pltpu.VMEM((count // BLOCK, BLOCK + 2 * HALO, LANES), F32)],
         compiler_params=params(),
-        cost_estimate=pl.CostEstimate(flops=0, bytes_accessed=0, transcendentals=0),
+        cost_estimate=duration(5),
         name="conv_forward",
     )(same, fill, units, taps)
 
@@ -236,7 +247,7 @@
             pltpu.VMEM((32, 8, LANES), F32),
         ],
         compiler_params=params(),
-        cost_estimate=pl.CostEstimate(flops=1_000_000, bytes_accessed=0, transcendentals=0),
+        cost_estimate=duration(4),
         name="tap_gradients",
     )(same, units, grad_conv)
 
@@ -260,17 +271,19 @@
         out_shape=jax.ShapeDtypeStruct((2, count, width), BF16),
         scratch_shapes=[pltpu.VMEM((count // BLOCK, BLOCK + 2 * HALO, LANES), F32)],
         compiler_params=params(),
+        cost_estimate=duration(5.6),
         name="conv_backward",
     )(same, fill, grad_conv, before, after, taps, in_hbm(value), in_hbm(gate))
 
 
-def normalised(frames, before, after, gain):
+def normalised(place, frames, inner, outer, gain):
     count, features = frames.shape
     edge = pl.BlockSpec((HALO, features), lambda i: (0, 0))
     return pl.pallas_call(
         norm_kernel,
         grid=(count // BLOCK,),
         in_specs=[
+            smem(),
             pl.BlockSpec((BLOCK, features), lambda i: (i, 0)),
             edge,
             edge,
@@ -285,8 +298,9 @@
             jax.ShapeDtypeStruct((features, count), BF16),
         ],
         compiler_params=params(),
+        cost_estimate=duration(3.5),
         name="layer_norm",
-    )(in_hbm(frames), before, after, gain.reshape(1, features))
+    )(place, in_hbm(frames), inner, outer, gain.reshape(1, features))
 
 
 def frame_chunks(rows, parts):
@@ -299,11 +313,12 @@
         out_shape=pltpu.HBM(shape, rows.dtype),
         scratch_shapes=[pltpu.VMEM(shape, rows.dtype), pltpu.SemaphoreType.DMA((2, parts))],
         compiler_params=params(),
+        cost_estimate=duration(2),
         name="frame_chunks",
     )(in_hbm(rows))
 
 
-def halves(core, rows):
+def halves(core, rows, keep=False):
     features, count = rows.shape
     order = np.zeros((160, 160), np.float32)
     for z in range(4):
@@ -316,9 +331,10 @@
         halves_kernel,
         in_specs=[smem(), vmem, vmem],
         out_specs=[vmem, hbm()],
-        out_shape=[half, pltpu.HBM(half.shape, BF16)],
+        out_shape=[half if keep else pltpu.HBM(half.shape, BF16), pltpu.HBM(half.shape, BF16)],
         scratch_shapes=[pltpu.VMEM(half.shape, BF16), pltpu.SemaphoreType.DMA],
         compiler_params=params(),
+        cost_estimate=duration(1.2),
         name="core_halves",
     )(core.reshape(1), rows, jnp.asarray(order, BF16))
 
@@ -339,7 +355,7 @@
         out_specs=block,
         out_shape=jax.ShapeDtypeStruct((count, features), BF16),
         compiler_params=params(),
-        cost_estimate=pl.CostEstimate(flops=12_000_000_000, bytes_accessed=10_000_000, transcendentals=0),
+        cost_estimate=duration(10.4),
         name="norm_backward",
     )(in_hbm(sent), in_hbm(other), in_hbm(frames), in_hbm(arrived), gain)
 
@@ -357,17 +373,18 @@
         out_shape=pltpu.HBM((rows, groups * width), BF16),
         input_output_aliases={} if buffer is None else {4: 0},
         compiler_params=params(),
+        cost_estimate=duration(3.4),
         name="weight_gradient",
     )(left, left_peer, right, right_peer, *([] if buffer is None else [in_hbm(buffer)]))
 
 
-def ring_shares(value, axis):
-    return [value] + [lax.ppermute(value, axis, [(i, (i + by) % 4) for i in range(4)]) for by in (1, 2, 3)]
-
-
-def ring_sum(shares):
+def shares_of(value, axis):
+    return [value] + [lax.ppermute(value, axis, [(i, i ^ k) for i in range(4)]) for k in (1, 2, 3)]
+
+
+def sum_of(shares):
     own, first, second, third = [share.astype(F32) for share in shares]
-    return (own + second) + (first + third)
+    return (own + first) + (second + third)
 
 
 def finish_rows(summed, xl):
@@ -383,19 +400,20 @@
     blocks = count // BLOCK
     core, xl = lax.axis_index("core"), lax.axis_index("xl")
     first_block = lax.axis_index(FRAMES) * blocks
+    place = jnp.stack([core, lax.axis_index("y"), lax.axis_index("section")]).astype(jnp.int32)
     chunks, frames = lax.optimization_barrier((frame_chunks(returned.T, 4), frames))
-    frames_before, frames_after = halos(frames)
     arrived = lax.all_to_all(chunks, "section", 0, 0).reshape(features, count)
 
     edge = jnp.full((1,), -1, jnp.int32)
     near_utt = lax.dynamic_slice(jnp.concatenate([edge, block_utt, edge]), (first_block,), (blocks + 2,))
     near_fill = lax.dynamic_slice(jnp.concatenate([edge, block_fill, edge]), (first_block,), (blocks + 2,))
     same = (near_utt[1:] == near_utt[:-1]).astype(jnp.int32)
+    same = jnp.concatenate([same, lax.axis_index(FRAMES)[None].astype(jnp.int32) % 2])
     fill = near_fill[1:-1]
     valid = (jnp.arange(BLOCK, dtype=jnp.int32)[None, :] < near_fill[:, None]).reshape(-1)
     valid = valid[BLOCK - HALO : BLOCK + count + HALO]
 
-    normed_ext, normed_t = normalised(frames, frames_before, frames_after, norm_gain)
+    normed_ext, normed_t = normalised(place, frames, *halos(frames), norm_gain)
     value_proj = jnp.dot(normed_ext, weight_in[0], preferred_element_type=F32)
     gate_proj = jnp.dot(normed_ext, weight_in[1], preferred_element_type=F32)
     gate_sigmoid = jax.nn.sigmoid(gate_proj)
@@ -411,14 +429,15 @@
         arrived, weight_out, (((0,), (1,)), ((), ())), preferred_element_type=F32
     )
     grad_conv = grad_activated * slope
-    conv_before, conv_after = halos(grad_conv)
-    rows_own, rows_other = halves(core, arrived)
+    conv_inner, conv_outer = halos(grad_conv)
+    arrived_rows, grad_conv = lax.optimization_barrier((arrived, grad_conv))
+    rows_own, rows_other = halves(core, arrived_rows, keep=True)
     rows_peer = swap(rows_other, "core")
     parts = pair_product(rows_own, rows_peer, activated[None], activated_peer[None], 3, 0)
 
     ready, parts = lax.optimization_barrier((grad_conv, parts))
     late = projected_back(
-        same, fill, ready, conv_before, conv_after, kernel, value_proj, gate_sigmoid
+        same, fill, ready, conv_inner, conv_outer, kernel, value_proj, gate_sigmoid
     )
     late_peer = swap(late, "core")
     contract = (((1,), (1,)), ((), ()))
@@ -439,16 +458,16 @@
     gain = small[32:]
     corner = lax.ppermute(gain, ("xl", "tensor"), [(0, 3), (1, 2), (2, 1), (3, 0)])
     across = swap(small, "xl"), swap(gain, "tensor"), corner
-    small, across, other = lax.optimization_barrier((small, across, other))
+    grad_frames = norm_back(sent, other, frames, arrived, norm_gain.reshape(1, features))
+    small, across, grad_frames = lax.optimization_barrier((small, across, grad_frames))
     gain = (small[32:] + across[1]) + (across[0][32:] + across[2])
     small = jnp.concatenate([small[:32] + across[0][:32], gain], axis=0)
-    shares = ring_shares(small.astype(BF16), "y")
-    grad_frames = norm_back(sent, other, frames, arrived, norm_gain.reshape(1, features))
+    shares = shares_of(small.astype(BF16), "y")
     got, grad_frames = lax.optimization_barrier((got, grad_frames))
     total = jnp.sum(got.astype(F32), axis=0)
     total, shares = lax.optimization_barrier((total, shares))
     summed = finish_rows(total.reshape(2, 20, 3 * width), xl)
-    small = ring_sum(ring_shares(ring_sum(shares).astype(BF16), "section"))
+    small = sum_of(shares_of(sum_of(shares).astype(BF16), "section"))
     grad_kernel = small[:TAPS]
     grad_gain = small[32:].reshape(features)
     grad_out = summed[:, :width].T

time: 125 us -> 117 us (0.936)
  local copies, waits for them, and re-layouts: 7.58 us -> 4.14 us
  starting transfers between devices: 45 us -> 41.9 us
  matrix products: 11.7 us -> 10.2 us
  waiting for transfers between devices: 19.7 us -> 18.2 us
    ppermute x9, starting transfers between devices: 6.32 us -> 11.3 us  [swap(): return lax.ppermute(value, axis, [(0, 1), (1, 0)])]
    ppermute x10, starting transfers between devices: 18.8 us -> 14.2 us  [the longest x6 10.2 us: shares_of(): lax.ppermute(value, axis, [(i, i ^ k) for i in range(4)])]
    ppermute x9, waiting for transfers between devices: 13.3 us -> 8.87 us  [swap(): return lax.ppermute(value, axis, [(0, 1), (1, 0)])]
    unnamed x37, local copies, waits for them, and re-layouts: 4.49 us -> 1.88 us
    all_to_all x1, starting transfers between devices: 10.7 us -> 8.56 us  [body(): got = lax.all_to_all(parts.reshape(16, 40, 3 * width), PLANE, 0, 0)]
    all_to_all x1, waiting for transfers between devices: 0.16 us -> 2.21 us  [body(): arrived = lax.all_to_all(chunks, 'section', 0, 0).reshape(features, count)]
    dot_general x1, matrix products: 3.32 us -> 1.33 us  [body(): gate_proj = jnp.dot(normed_ext, weight_in[1], preferred_element_type=F32)]
    all_to_all x1, waiting for transfers between devices: 3.18 us -> 4.94 us  [body(): got = lax.all_to_all(parts.reshape(16, 40, 3 * width), PLANE, 0, 0)]
  transfers between devices with their start and end apart: 22 -> 22, of which waited for: 9 -> 8; matrix products, arithmetic and copies ran while one was open for 14% -> 14% of each run, Pallas kernels for 22% -> 24%
where the time goes in v5:
time: 117 us
  starting transfers between devices  41.9 us (36%)
  Pallas kernels  36 us (31%)
  waiting for transfers between devices  18.2 us (16%)
  matrix products  10.2 us (9%)
  other arithmetic  5.21 us (4%)
  local copies, waits for them, and re-layouts  4.14 us (4%)
    ppermute x9, starting transfers between devices, swap(): return lax.ppermute(value, axis, [(0, 1), (1, 0)])  11.3 us
    ppermute x6, starting transfers between devices, shares_of(): lax.ppermute(value, axis, [(i, i ^ k) for i in range(4)])  10.2 us
    ppermute x9, waiting for transfers between devices, swap(): return lax.ppermute(value, axis, [(0, 1), (1, 0)])  8.87 us
    all_to_all x1, starting transfers between devices, body(): got = lax.all_to_all(parts.reshape(16, 40, 3 * width), PLANE, 0, 0)  8.56 us
    pallas_call x2, Pallas kernels, pair_product(): pl.pallas_call(pair_kernel, grid=(made,), in_specs=[whole, whole, spec, s...  6.82 us
    all_to_all x1, starting transfers between devices, body(): arrived = lax.all_to_all(chunks, 'section', 0, 0).reshape(features, count)  6.12 us
    pallas_call x1, Pallas kernels, projected_back(): pl.pallas_call(backward_kernel, grid=(width // LANES,), in_specs=[smem(),...  5.62 us
    pallas_call x1, Pallas kernels, convolved(): pl.pallas_call(forward_kernel, grid=(width // LANES,), in_specs=[smem(),...  5.17 us
  transfers between devices with their start and end apart: 22, of which 8 were waited for; matrix products, arithmetic and copies ran while one was open for 14% of the time, Pallas kernels for 24%

profile of v5, /device:TPU:0, one launch (start us, length us, event | category | flops | bytes accessed | tf_op | source)
XLA Modules:
  0.0 116.7 jit_solution(6248408850295844597)
XLA Ops:
  0.6 0.0 copy-start
  0.7 2.2 %frame_chunks.1 = bf16[4,320,512]{2,1,0:T(8,128)(2,1)} custom-call(bf16[320,2048]{1,0:T(8,128)(2,1)} %bitcast.53), custom_call_target="tpu_custom_call" | custom-call | flops 2300000000 | tf_op jit(solution)/shard_map/frame_chunks/pallas_call | solution.py:309
  2.9 0.0 copy-start.14
  2.9 0.0 copy-start.15
  2.9 0.8 broadcast_select_fusion
  3.8 2.1 %collective-permute-start = (bf16[16,1280]{1,0:T(8,128)(2,1)S(1)}, bf16[16,1280]{1,0:T(8,128)(2,1)S(1)}, u32[]{:S(2)}, u32[]{:S(2)}) collective-permute-start(bf16[16,1280]{1,0:T(8,128)(2,1)S(1)} %get-tuple-element.82), channel_id=1, source_target_pairs={{0,1},{1,0},{2,3},{3,2},{8,9},{9,8},{10,11},{11,10},{16,17},{17,16... | collective-permute-start | bytes 122888 | tf_op jit(solution)/shard_map/ppermute | solution.py:48
  5.8 0.7 collective-permute-start.1
  6.5 6.1 %all-to-all-start = ((bf16[4,320,512]{2,1,0:T(8,128)(2,1)}), bf16[4,320,512]{2,1,0:T(8,128)(2,1)S(1)}, u32[]{:S(2)}, u32[]{:S(2)}) async-start(bf16[4,320,512]{2,1,0:T(8,128)(2,1)} %frame_chunks.1), calls=%async_computation | async-start | bytes 2621440 | tf_op jit(solution)/shard_map/all_to_all | solution.py:405
  12.6 0.1 pad_add_fusion
  12.7 0.1 dynamic_slice.14
  12.8 0.1 fusion.20
  12.9 0.1 dynamic_slice.13
  12.9 0.1 compare_convert_fusion
  13.0 0.1 pad_add_fusion.5.same
  13.1 0.1 pad_add_fusion.4.place
  13.2 0.1 slice.75.fill
  13.2 0.1 slice.76
  13.3 3.8 %layer_norm.1 = (bf16[544,1280]{1,0:T(8,128)(2,1)S(1)}, bf16[1280,512]{1,0:T(8,128)(2,1)S(1)}) custom-call(s32[3]{0:T(128)S(1)} %pad_add_fusion.4.place, bf16[512,1280]{1,0:T(8,128)(2,1)} %frames.1, bf16[16,1280]{1,0:T(8,128)(2,1)S(1)} %collective-permute-done.inner, bf16[16,1280]{1,0:T(8,128)(2,1)S(1)} %collective-permute-done.1.outer, ...), custom_call_target="tpu_custom_call" | custom-call | flops 4024999936 | tf_op jit(solution)/shard_map/layer_norm/pallas_call | solution.py:282
  17.1 1.3 %add_divide_fusion.gate = f32[544,640]{1,0:T(8,128)S(1)} fusion(bf16[544,1280]{1,0:T(8,128)(2,1)S(1)} %get-tuple-element.44, bf16[2,1280,640]{2,1,0:T(8,128)(2,1)S(1)} %copy-done.11), kind=kOutput, calls=%fused_computation.19 | convolution fusion | flops 892334080 | bytes 4423680 | tf_op jit(solution)/shard_map/dot_general | solution.py:418
  18.5 2.3 %select_convert_fusion = (bf16[544,640]{1,0:T(8,128)(2,1)S(1)}, f32[544,640]{1,0:T(8,128)}) fusion(f32[544,640]{1,0:T(8,128)S(1)} %add_divide_fusion.gate, pred[544]{0:T(1024)(128)(4,1)S(1)} %slice.76, bf16[544,1280]{1,0:T(8,128)(2,1)S(1)} %get-tuple-element.44, bf16[2,1280,640]{2,1,0:T(8,128)(2,1)S(1)} %copy-done.11), kind=kOutput, calls=%fused_computation.18 | convolution fusion | flops 892334080 | bytes 6513664 | tf_op jit(solution)/shard_map/dot_general | solution.py:417
  20.9 5.2 %conv_forward.1 = (bf16[512,640]{1,0:T(8,128)(2,1)}, f32[512,640]{1,0:T(8,128)}) custom-call(s32[6]{0:T(128)S(1)} %pad_add_fusion.5.same, s32[4]{0:T(128)S(1)} %slice.75.fill, bf16[544,640]{1,0:T(8,128)(2,1)S(1)} %get-tuple-element.86.units, f32[31,640]{1,0:T(8,128)S(1)} %copy-done.6), custom_call_target="tpu_custom_call" | custom-call | flops 5750000128 | tf_op jit(solution)/shard_map/conv_forward/pallas_call | solution.py:221
  26.0 1.3 %collective-permute-start.4 = (bf16[512,640]{1,0:T(8,128)(2,1)}, bf16[512,640]{1,0:T(8,128)(2,1)}, u32[]{:S(2)}, u32[]{:S(2)}) collective-permute-start(bf16[512,640]{1,0:T(8,128)(2,1)} %get-tuple-element.50), channel_id=1, source_target_pairs={{0,8},{8,0},{1,9},{9,1},{2,10},{10,2},{3,11},{11,3},{4,12},{12,4},... | collective-permute-start | bytes 1966088 | tf_op jit(solution)/shard_map/ppermute | solution.py:38
  27.4 2.0 %core_halves.2 = (bf16[640,512]{1,0:T(8,128)(2,1)}, bf16[640,512]{1,0:T(8,128)(2,1)}) custom-call(s32[1]{0:T(128)} %bitcast.2.core, bf16[1280,512]{1,0:T(8,128)(2,1)S(1)} %get-tuple-element.39.rows, bf16[160,160]{1,0:T(8,128)(2,1)S(1)} %copy-done.7), custom_call_target="tpu_custom_call" | custom-call | flops 1380000000 | tf_op jit(solution)/shard_map/core_halves/pallas_call | solution.py:330
  29.4 2.2 %all-to-all-done = bf16[4,320,512]{2,1,0:T(8,128)(2,1)S(1)} async-done(((bf16[4,320,512]{2,1,0:T(8,128)(2,1)}), bf16[4,320,512]{2,1,0:T(8,128)(2,1)S(1)}, u32[]{:S(2)}, u32[]{:S(2)}) %all-to-all-start) | async-done | bytes 1310752 | tf_op jit(solution)/shard_map/all_to_all | solution.py:405
  31.6 3.0 %convolution_multiply_fusion.grad_conv = f32[512,640]{1,0:T(8,128)S(1)} fusion(f32[512,640]{1,0:T(8,128)} %get-tuple-element.45, bf16[1280,512]{1,0:T(8,128)(2,1)S(1)} %bitcast.49, bf16[640,1280]{1,0:T(8,128)(2,1)S(1)} %copy-done), kind=kOutput, calls=%fused_computation.17 | convolution fusion | flops 839188480 | bytes 5570560 | tf_op jit(solution)/shard_map/dot_general | solution.py:428
  34.7 1.3 %core_halves.3 = (bf16[640,512]{1,0:T(8,128)(2,1)S(1)}, bf16[640,512]{1,0:T(8,128)(2,1)}) custom-call(s32[1]{0:T(128)} %bitcast.2.core, bf16[1280,512]{1,0:T(8,128)(2,1)S(1)} %bitcast.50, bf16[160,160]{1,0:T(8,128)(2,1)S(1)} %copy-done.7), custom_call_target="tpu_custom_call" | custom-call | flops 1380000000 | tf_op jit(solution)/shard_map/core_halves/pallas_call | solution.py:330
  36.0 0.2 collective-permute-start.3
  36.2 0.7 collective-permute-start.5
  36.8 0.7 collective-permute-start.6
  37.5 0.8 collective-permute-done.3.left_peer
  38.3 3.4 %weight_gradient.2.buffers_0_ = bf16[640,1920]{1,0:T(8,128)(2,1)} custom-call(bf16[640,512]{1,0:T(8,128)(2,1)S(1)} %get-tuple-element.48.left, bf16[640,512]{1,0:T(8,128)(2,1)S(1)} %collective-permute-done.3.left_peer, bf16[1,512,640]{2,1,0:T(8,128)(2,1)} %bitcast.9.right, bf16[1,512,640]{2,1,0:T(8,128)(2,1)} %bitcast.10.right_peer), custom_call_target="tpu_custom_call" | custom-call | flops 3910000128 | tf_op jit(solution)/shard_map/weight_gradient/pallas_call | solution.py:368
  41.8 5.6 %conv_backward.1.right = bf16[2,512,640]{2,1,0:T(8,128)(2,1)S(1)} custom-call(s32[6]{0:T(128)S(1)} %pad_add_fusion.5.same, s32[4]{0:T(128)S(1)} %slice.75.fill, f32[512,640]{1,0:T(8,128)S(1)} %convolution_multiply_fusion.grad_conv, f32[16,640]{1,0:T(8,128)S(1)} %collective-permute-done.5.inner, f32[16,640]{1,0:T(8,128)S(1)} %collective-permute-done.6.outer, ...), custom_call_target="tpu_custom_call" | custom-call | flops 6440000000 | tf_op jit(solution)/shard_map/conv_backward/pallas_call | solution.py:257
  47.4 1.7 %collective-permute-start.7 = (bf16[2,512,640]{2,1,0:T(8,128)(2,1)S(1)}, bf16[2,512,640]{2,1,0:T(8,128)(2,1)S(1)}, u32[]{:S(2)}, u32[]{:S(2)}) collective-permute-start(bf16[2,512,640]{2,1,0:T(8,128)(2,1)S(1)} %conv_backward.1.right), channel_id=1, source_target_pairs={{0,8},{8,0},{1,9},{9,1},{2,10},{10,2},{3,11},{11,3},{4,12},{12,4},... | collective-permute-start | bytes 3932168 | tf_op jit(solution)/shard_map/ppermute | solution.py:38
  49.1 0.1 collective-permute-start.2
  49.3 1.2 %fusion.1 = f32[512,1280]{1,0:T(8,128)S(1)} fusion(bf16[2,1280,640]{2,1,0:T(8,128)(2,1)S(1)} %copy-done.12, bf16[2,512,640]{2,1,0:T(8,128)(2,1)S(1)} %conv_backward.1.right), kind=kOutput, calls=%fused_computation.4 | convolution fusion | flops 838860800 | bytes 4915200 | tf_op jit(solution)/shard_map/dot_general | solution.py:445
  50.5 2.3 %fusion.sent = bf16[512,1280]{1,0:T(8,128)(2,1)} fusion(f32[512,1280]{1,0:T(8,128)S(1)} %fusion.1, bf16[2,1280,640]{2,1,0:T(8,128)(2,1)S(1)} %copy-done.12, bf16[2,512,640]{2,1,0:T(8,128)(2,1)S(1)} %conv_backward.1.right), kind=kOutput, calls=%fused_computation.2 | convolution fusion | flops 840171520 | bytes 6225920 | tf_op jit(solution)/shard_map/dot_general | solution.py:444
  52.8 3.0 %collective-permute-start.12 = (bf16[512,1280]{1,0:T(8,128)(2,1)}, bf16[512,1280]{1,0:T(8,128)(2,1)}, u32[]{:S(2)}, u32[]{:S(2)}) collective-permute-start(bf16[512,1280]{1,0:T(8,128)(2,1)} %fusion.sent), channel_id=1, source_target_pairs={{0,4},{4,0},{1,5},{5,1},{2,6},{6,2},{3,7},{7,3},{8,12},{12,8},{9,1... | collective-permute-start | bytes 3932168 | tf_op jit(solution)/shard_map/ppermute | solution.py:38
  55.8 3.4 %weight_gradient.3 = bf16[640,1920]{1,0:T(8,128)(2,1)} custom-call(bf16[640,512]{1,0:T(8,128)(2,1)S(1)} %copy-done.10, bf16[640,512]{1,0:T(8,128)(2,1)S(1)} %collective-permute-done.2.left_peer, bf16[2,512,640]{2,1,0:T(8,128)(2,1)S(1)} %conv_backward.1.right, ...), custom_call_target="tpu_custom_call", output_to_operand_aliasing={{}: (4, {})} | custom-call | flops 3910000128 | tf_op jit(solution)/shard_map/weight_gradient/pallas_call | solution.py:368
  59.2 8.6 %all-to-all-start.1 = ((bf16[16,40,1920]{2,1,0:T(8,128)(2,1)}), bf16[16,40,1920]{2,1,0:T(8,128)(2,1)}, u32[]{:S(2)}, u32[]{:S(2)}) async-start(bf16[16,40,1920]{2,1,0:T(8,128)(2,1)} %bitcast.52), calls=%async_computation.1 | async-start | bytes 4915200 | tf_op jit(solution)/shard_map/all_to_all | solution.py:450
  67.8 1.1 copy-done.9
  68.9 4.0 %tap_gradients.1 = f32[32,640]{1,0:T(8,128)S(1)} custom-call(s32[6]{0:T(128)S(1)} %pad_add_fusion.5.same, bf16[544,640]{1,0:T(8,128)(2,1)S(1)} %copy-done.9, f32[512,640]{1,0:T(8,128)S(1)} %copy-done.5), custom_call_target="tpu_custom_call" | custom-call | flops 4600000000 | tf_op jit(solution)/shard_map/tap_gradients/pallas_call | solution.py:239
  72.9 1.7 %multiply_reduce_fusion = f32[1280]{0:T(1024)S(1)} fusion(bf16[512,1280]{1,0:T(8,128)(2,1)} %fusion.sent, bf16[544,1280]{1,0:T(8,128)(2,1)S(1)} %copy-done.3), kind=kLoop, calls=%fused_computation.3 | loop fusion | flops 2620160 | bytes 2626560 | tf_op jit(solution)/shard_map/reduce_sum | solution.py:455
  74.7 0.3 collective-permute-start.8
  75.0 1.3 %collective-permute-done.8 = f32[34,640]{1,0:T(8,128)S(1)} collective-permute-done((f32[34,640]{1,0:T(8,128)S(1)}, f32[34,640]{1,0:T(8,128)S(1)}, u32[]{:S(2)}, u32[]{:S(2)}) %collective-permute-start.8) | collective-permute-done | bytes 87072 | tf_op jit(solution)/shard_map/ppermute | solution.py:38
  76.3 1.4 %collective-permute-start.9 = (f32[34,640]{1,0:T(8,128)S(1)}, f32[34,640]{1,0:T(8,128)S(1)}, u32[]{:S(2)}, u32[]{:S(2)}) collective-permute-start(f32[34,640]{1,0:T(8,128)S(1)} %fusion.21), channel_id=1, source_target_pairs={{0,64},{64,0},{1,65},{65,1},{2,66},{66,2},{3,67},{67,3},{4,68},{68... | collective-permute-start | bytes 261128 | tf_op jit(solution)/shard_map/ppermute | solution.py:38
  77.7 1.7 %collective-permute-start.10 = (f32[2,640]{1,0:T(2,128)S(1)}, f32[2,640]{1,0:T(2,128)S(1)}, u32[]{:S(2)}, u32[]{:S(2)}) collective-permute-start(f32[2,640]{1,0:T(2,128)S(1)} %slice.98), channel_id=1, source_target_pairs={{0,4},{4,0},{1,5},{5,1},{2,6},{6,2},{3,7},{7,3},{8,12},{12,8},{9,1... | collective-permute-start | bytes 15368 | tf_op jit(solution)/shard_map/ppermute | solution.py:38
  79.4 1.7 %collective-permute-start.11 = (f32[2,640]{1,0:T(2,128)S(1)}, f32[2,640]{1,0:T(2,128)S(1)}, u32[]{:S(2)}, u32[]{:S(2)}) collective-permute-start(f32[2,640]{1,0:T(2,128)S(1)} %slice.98), channel_id=1, source_target_pairs={{0,68},{4,64},{64,4},{68,0},{1,69},{5,65},{65,5},{69,1},{2,70},{6,... | collective-permute-start | bytes 15368 | tf_op jit(solution)/shard_map/ppermute | solution.py:459
  81.1 5.1 %collective-permute-done.12.other = bf16[512,1280]{1,0:T(8,128)(2,1)} collective-permute-done((bf16[512,1280]{1,0:T(8,128)(2,1)}, bf16[512,1280]{1,0:T(8,128)(2,1)}, u32[]{:S(2)}, u32[]{:S(2)}) %collective-permute-start.12) | collective-permute-done | bytes 1310752 | tf_op jit(solution)/shard_map/ppermute | solution.py:38
  86.2 5.1 %norm_backward.1 = bf16[512,1280]{1,0:T(8,128)(2,1)} custom-call(bf16[512,1280]{1,0:T(8,128)(2,1)} %fusion.sent, bf16[512,1280]{1,0:T(8,128)(2,1)} %collective-permute-done.12.other, bf16[512,1280]{1,0:T(8,128)(2,1)} %frames.1, bf16[1280,512]{1,0:T(8,128)(2,1)} %bitcast.51, f32[1,1280]{1,0:T(1,128)S(1)} %reshape.43.gain), custom_call_target="tpu_custom_call" | custom-call | flops 11960000512 | tf_op jit(solution)/shard_map/norm_backward/pallas_call | solution.py:345
  91.3 1.0 collective-permute-done.9
  92.3 2.4 %collective-permute-start.13 = (bf16[34,640]{1,0:T(8,128)(2,1)S(1)}, bf16[34,640]{1,0:T(8,128)(2,1)S(1)}, u32[]{:S(2)}, u32[]{:S(2)}) collective-permute-start(bf16[34,640]{1,0:T(8,128)(2,1)S(1)} %pad_maximum_fusion.2), channel_id=1, source_target_pairs={{0,16},{16,0},{32,48},{48,32},{1,17},{17,1},{33,49},{49,33},{2,18}... | collective-permute-start | bytes 130568 | tf_op jit(solution)/shard_map/ppermute | solution.py:382
  94.7 3.0 %collective-permute-start.14 = (bf16[34,640]{1,0:T(8,128)(2,1)S(1)}, bf16[34,640]{1,0:T(8,128)(2,1)S(1)}, u32[]{:S(2)}, u32[]{:S(2)}) collective-permute-start(bf16[34,640]{1,0:T(8,128)(2,1)S(1)} %pad_maximum_fusion.2), channel_id=1, source_target_pairs={{0,32},{16,48},{32,0},{48,16},{1,33},{17,49},{33,1},{49,17},{2,34}... | collective-permute-start | bytes 130568 | tf_op jit(solution)/shard_map/ppermute | solution.py:382
  97.7 4.9 %all-to-all-done.1 = bf16[16,40,1920]{2,1,0:T(8,128)(2,1)} async-done(((bf16[16,40,1920]{2,1,0:T(8,128)(2,1)}), bf16[16,40,1920]{2,1,0:T(8,128)(2,1)}, u32[]{:S(2)}, u32[]{:S(2)}) %all-to-all-start.1) | async-done | bytes 2457632 | tf_op jit(solution)/shard_map/all_to_all | solution.py:450
  102.7 2.1 %convert_reduce_fusion = f32[40,1920]{1,0:T(8,128)S(1)} fusion(bf16[16,40,1920]{2,1,0:T(8,128)(2,1)} %all-to-all-done.1), kind=kLoop, calls=%fused_computation | loop fusion | flops 2380800 | bytes 2764800 | tf_op jit(solution)/shard_map/reduce_sum | solution.py:467
  104.8 0.7 collective-permute-start.17
  105.5 2.5 %collective-permute-start.18 = (bf16[34,640]{1,0:T(8,128)(2,1)S(1)}, bf16[34,640]{1,0:T(8,128)(2,1)S(1)}, u32[]{:S(2)}, u32[]{:S(2)}) collective-permute-start(bf16[34,640]{1,0:T(8,128)(2,1)S(1)} %add_convert_fusion), channel_id=1, source_target_pairs={{0,2},{1,3},{2,0},{3,1},{4,6},{5,7},{6,4},{7,5},{8,10},{9,11},{10,... | collective-permute-start | bytes 130568 | tf_op jit(solution)/shard_map/ppermute | solution.py:382
  108.1 1.6 %collective-permute-start.19 = (bf16[34,640]{1,0:T(8,128)(2,1)S(1)}, bf16[34,640]{1,0:T(8,128)(2,1)S(1)}, u32[]{:S(2)}, u32[]{:S(2)}) collective-permute-start(bf16[34,640]{1,0:T(8,128)(2,1)S(1)} %add_convert_fusion), channel_id=1, source_target_pairs={{0,3},{1,2},{2,1},{3,0},{4,7},{5,6},{6,5},{7,4},{8,11},{9,10},{10,... | collective-permute-start | bytes 130568 | tf_op jit(solution)/shard_map/ppermute | solution.py:382
  109.7 1.6 %collective-permute-start.16 = (f32[20,1920]{1,0:T(8,128)S(1)}, f32[20,1920]{1,0:T(8,128)S(1)}, u32[]{:S(2)}, u32[]{:S(2)}) collective-permute-start(f32[20,1920]{1,0:T(8,128)S(1)} %dynamic-slice_bitcast_fusion), channel_id=1, source_target_pairs={{0,64},{64,0},{1,65},{65,1},{2,66},{66,2},{3,67},{67,3},{4,68},{68... | collective-permute-start | bytes 460808 | tf_op jit(solution)/shard_map/ppermute | solution.py:38
  111.3 2.1 %collective-permute-done.19 = bf16[34,640]{1,0:T(8,128)(2,1)S(1)} collective-permute-done((bf16[34,640]{1,0:T(8,128)(2,1)S(1)}, bf16[34,640]{1,0:T(8,128)(2,1)S(1)}, u32[]{:S(2)}, u32[]{:S(2)}) %collective-permute-start.19) | collective-permute-done | bytes 43552 | tf_op jit(solution)/shard_map/ppermute | solution.py:382
  113.4 0.6 slice.102
  114.1 0.6 reshape.47
  114.7 0.6 collective-permute-done.16
  115.3 0.6 slice_bitcast_fusion.4
  116.0 0.7 copy.17
  (64 shorter events, 0.4 us)
Async XLA Ops:
  0.6 31.0 %copy-start = (bf16[640,1280]{1,0:T(8,128)(2,1)S(1)}, bf16[640,1280]{1,0:T(8,128)(2,1)}, u32[]{:S(2)}) copy-start(bf16[640,1280]{1,0:T(8,128)(2,1)} %param.15) | copy-start | bytes 4915204
  2.9 9.7 %copy-start.14 = (s32[256]{0:T(256)S(1)}, s32[256]{0:T(256)}, u32[]{:S(2)}) copy-start(s32[256]{0:T(256)} %param.17) | copy-start | bytes 3076
  2.9 9.7 %copy-start.15 = (s32[256]{0:T(256)S(1)}, s32[256]{0:T(256)}, u32[]{:S(2)}) copy-start(s32[256]{0:T(256)} %param.16) | copy-start | bytes 3076
  2.9 10.3 %copy-start.13 = (f32[1280]{0:T(1024)S(1)}, f32[1280]{0:T(1024)}, u32[]{:S(2)}) copy-start(f32[1280]{0:T(1024)} %param.12) | copy-start | bytes 15364
  3.8 9.6 %collective-permute-start = (bf16[16,1280]{1,0:T(8,128)(2,1)S(1)}, bf16[16,1280]{1,0:T(8,128)(2,1)S(1)}, u32[]{:S(2)}, u32[]{:S(2)}) collective-permute-start(bf16[16,1280]{1,0:T(8,128)(2,1)S(1)} %get-tuple-element.82), channel_id=1, source_target_pairs={{0,1},{1,0},{2,3},{3,2},{8,9},{9,8},{10,11},{11,10},{16,17},{17,16... | collective-permute-start | bytes 122888 | tf_op jit(solution)/shard_map/ppermute | solution.py:48
  5.8 7.5 %collective-permute-start.1 = (bf16[16,1280]{1,0:T(8,128)(2,1)S(1)}, bf16[16,1280]{1,0:T(8,128)(2,1)S(1)}, u32[]{:S(2)}, u32[]{:S(2)}) collective-permute-start(bf16[16,1280]{1,0:T(8,128)(2,1)S(1)} %get-tuple-element.81), channel_id=1, source_target_pairs={{1,2},{3,8},{9,10},{11,16},{17,18},{19,24},{25,26},{27,32},{33,34}... | collective-permute-start | bytes 122888 | tf_op jit(solution)/shard_map/ppermute | solution.py:49
  6.5 25.1 %all-to-all-start = ((bf16[4,320,512]{2,1,0:T(8,128)(2,1)}), bf16[4,320,512]{2,1,0:T(8,128)(2,1)S(1)}, u32[]{:S(2)}, u32[]{:S(2)}) async-start(bf16[4,320,512]{2,1,0:T(8,128)(2,1)} %frame_chunks.1), calls=%async_computation | async-start | bytes 2621440 | tf_op jit(solution)/shard_map/all_to_all | solution.py:405
  13.3 3.8 %copy-start.11 = (bf16[2,1280,640]{2,1,0:T(8,128)(2,1)S(1)}, bf16[2,1280,640]{2,1,0:T(8,128)(2,1)}, u32[]{:S(2)}) copy-start(bf16[2,1280,640]{2,1,0:T(8,128)(2,1)} %param.13) | copy-start | bytes 9830404
  17.1 1.4 %copy-start.2 = (bf16[544,1280]{1,0:T(8,128)(2,1)}, bf16[544,1280]{1,0:T(8,128)(2,1)S(1)}, u32[]{:S(2)}) copy-start(bf16[544,1280]{1,0:T(8,128)(2,1)S(1)} %get-tuple-element.44) | copy-start | bytes 4177924
  18.5 2.4 %copy-start.17 = (f32[544,640]{1,0:T(8,128)}, f32[544,640]{1,0:T(8,128)S(1)}, u32[]{:S(2)}) copy-start(f32[544,640]{1,0:T(8,128)S(1)} %add_divide_fusion.gate) | copy-start | bytes 4177924
  18.5 2.4 %copy-start.6 = (f32[31,640]{1,0:T(8,128)S(1)}, f32[31,640]{1,0:T(8,128)}, u32[]{:S(2)}) copy-start(f32[31,640]{1,0:T(8,128)} %taps.3) | copy-start | bytes 238084
  20.8 5.2 %copy-start.8 = (bf16[544,640]{1,0:T(8,128)(2,1)}, bf16[544,640]{1,0:T(8,128)(2,1)S(1)}, u32[]{:S(2)}) copy-start(bf16[544,640]{1,0:T(8,128)(2,1)S(1)} %get-tuple-element.86.units) | copy-start | bytes 2088964
  20.8 6.5 %copy-start.7 = (bf16[160,160]{1,0:T(8,128)(2,1)S(1)}, bf16[160,160]{1,0:T(8,128)(2,1)}, u32[]{:S(2)}) copy-start(bf16[160,160]{1,0:T(8,128)(2,1)} %constant.73.clone.order) | copy-start | bytes 153604
  26.0 11.5 %collective-permute-start.4 = (bf16[512,640]{1,0:T(8,128)(2,1)}, bf16[512,640]{1,0:T(8,128)(2,1)}, u32[]{:S(2)}, u32[]{:S(2)}) collective-permute-start(bf16[512,640]{1,0:T(8,128)(2,1)} %get-tuple-element.50), channel_id=1, source_target_pairs={{0,8},{8,0},{1,9},{9,1},{2,10},{10,2},{3,11},{11,3},{4,12},{12,4},... | collective-permute-start | bytes 1966088 | tf_op jit(solution)/shard_map/ppermute | solution.py:38
  31.6 3.0 %copy-start.1 = (bf16[4,320,512]{2,1,0:T(8,128)(2,1)}, bf16[4,320,512]{2,1,0:T(8,128)(2,1)S(1)}, u32[]{:S(2)}) copy-start(bf16[4,320,512]{2,1,0:T(8,128)(2,1)S(1)} %all-to-all-done) | copy-start | bytes 3932164
  34.7 7.1 %copy-start.4 = (f32[512,640]{1,0:T(8,128)}, f32[512,640]{1,0:T(8,128)S(1)}, u32[]{:S(2)}) copy-start(f32[512,640]{1,0:T(8,128)S(1)} %convolution_multiply_fusion.grad_conv) | copy-start | bytes 3932164
  36.0 2.4 %collective-permute-start.3 = (bf16[640,512]{1,0:T(8,128)(2,1)}, bf16[640,512]{1,0:T(8,128)(2,1)S(1)}, u32[]{:S(2)}, u32[]{:S(2)}) collective-permute-start(bf16[640,512]{1,0:T(8,128)(2,1)} %get-tuple-element.49), channel_id=1, source_target_pairs={{0,8},{8,0},{1,9},{9,1},{2,10},{10,2},{3,11},{11,3},{4,12},{12,4},... | collective-permute-start | bytes 1966088 | tf_op jit(solution)/shard_map/ppermute | solution.py:38
  36.2 5.6 %collective-permute-start.5 = (f32[16,640]{1,0:T(8,128)S(1)}, f32[16,640]{1,0:T(8,128)S(1)}, u32[]{:S(2)}, u32[]{:S(2)}) collective-permute-start(f32[16,640]{1,0:T(8,128)S(1)} %get-tuple-element.80), channel_id=1, source_target_pairs={{0,1},{1,0},{2,3},{3,2},{8,9},{9,8},{10,11},{11,10},{16,17},{17,16... | collective-permute-start | bytes 122888 | tf_op jit(solution)/shard_map/ppermute | solution.py:48
  36.8 4.9 %collective-permute-start.6 = (f32[16,640]{1,0:T(8,128)S(1)}, f32[16,640]{1,0:T(8,128)S(1)}, u32[]{:S(2)}, u32[]{:S(2)}) collective-permute-start(f32[16,640]{1,0:T(8,128)S(1)} %get-tuple-element.79), channel_id=1, source_target_pairs={{1,2},{3,8},{9,10},{11,16},{17,18},{19,24},{25,26},{27,32},{33,34}... | collective-permute-start | bytes 122888 | tf_op jit(solution)/shard_map/ppermute | solution.py:49
  41.8 7.4 %copy-start.16 = (bf16[640,512]{1,0:T(8,128)(2,1)S(1)}, bf16[640,512]{1,0:T(8,128)(2,1)}, u32[]{:S(2)}) copy-start(bf16[640,512]{1,0:T(8,128)(2,1)} %get-tuple-element.41) | copy-start | bytes 1966084
  41.8 7.5 %copy-start.12 = (bf16[2,1280,640]{2,1,0:T(8,128)(2,1)S(1)}, bf16[2,1280,640]{2,1,0:T(8,128)(2,1)}, u32[]{:S(2)}) copy-start(bf16[2,1280,640]{2,1,0:T(8,128)(2,1)} %param.13) | copy-start | bytes 9830404
  47.4 8.4 %collective-permute-start.7 = (bf16[2,512,640]{2,1,0:T(8,128)(2,1)S(1)}, bf16[2,512,640]{2,1,0:T(8,128)(2,1)S(1)}, u32[]{:S(2)}, u32[]{:S(2)}) collective-permute-start(bf16[2,512,640]{2,1,0:T(8,128)(2,1)S(1)} %conv_backward.1.right), channel_id=1, source_target_pairs={{0,8},{8,0},{1,9},{9,1},{2,10},{10,2},{3,11},{11,3},{4,12},{12,4},... | collective-permute-start | bytes 3932168 | tf_op jit(solution)/shard_map/ppermute | solution.py:38
  49.1 6.6 %collective-permute-start.2 = (bf16[640,512]{1,0:T(8,128)(2,1)S(1)}, bf16[640,512]{1,0:T(8,128)(2,1)S(1)}, u32[]{:S(2)}, u32[]{:S(2)}) collective-permute-start(bf16[640,512]{1,0:T(8,128)(2,1)S(1)} %copy-done.16), channel_id=1, source_target_pairs={{0,8},{8,0},{1,9},{9,1},{2,10},{10,2},{3,11},{11,3},{4,12},{12,4},... | collective-permute-start | bytes 1966088 | tf_op jit(solution)/shard_map/ppermute | solution.py:38
  50.5 5.3 %copy-start.10 = (bf16[640,512]{1,0:T(8,128)(2,1)S(1)}, bf16[640,512]{1,0:T(8,128)(2,1)}, u32[]{:S(2)}) copy-start(bf16[640,512]{1,0:T(8,128)(2,1)} %get-tuple-element.42.left) | copy-start | bytes 1966084
  52.8 33.4 %collective-permute-start.12 = (bf16[512,1280]{1,0:T(8,128)(2,1)}, bf16[512,1280]{1,0:T(8,128)(2,1)}, u32[]{:S(2)}, u32[]{:S(2)}) collective-permute-start(bf16[512,1280]{1,0:T(8,128)(2,1)} %fusion.sent), channel_id=1, source_target_pairs={{0,4},{4,0},{1,5},{5,1},{2,6},{6,2},{3,7},{7,3},{8,12},{12,8},{9,1... | collective-permute-start | bytes 3932168 | tf_op jit(solution)/shard_map/ppermute | solution.py:38
  59.2 8.6 %copy-start.5 = (f32[512,640]{1,0:T(8,128)S(1)}, f32[512,640]{1,0:T(8,128)}, u32[]{:S(2)}) copy-start(f32[512,640]{1,0:T(8,128)} %copy-done.4) | copy-start | bytes 3932164
  59.2 43.5 %all-to-all-start.1 = ((bf16[16,40,1920]{2,1,0:T(8,128)(2,1)}), bf16[16,40,1920]{2,1,0:T(8,128)(2,1)}, u32[]{:S(2)}, u32[]{:S(2)}) async-start(bf16[16,40,1920]{2,1,0:T(8,128)(2,1)} %bitcast.52), calls=%async_computation.1 | async-start | bytes 4915200 | tf_op jit(solution)/shard_map/all_to_all | solution.py:450
  67.8 1.1 copy-start.9
  68.9 4.0 %copy-start.3 = (bf16[544,1280]{1,0:T(8,128)(2,1)S(1)}, bf16[544,1280]{1,0:T(8,128)(2,1)}, u32[]{:S(2)}) copy-start(bf16[544,1280]{1,0:T(8,128)(2,1)} %copy-done.2) | copy-start | bytes 4177924
  74.7 1.6 %collective-permute-start.8 = (f32[34,640]{1,0:T(8,128)S(1)}, f32[34,640]{1,0:T(8,128)S(1)}, u32[]{:S(2)}, u32[]{:S(2)}) collective-permute-start(f32[34,640]{1,0:T(8,128)S(1)} %pad_maximum_fusion.1), channel_id=1, source_target_pairs={{0,8},{8,0},{1,9},{9,1},{2,10},{10,2},{3,11},{11,3},{4,12},{12,4},... | collective-permute-start | bytes 261128 | tf_op jit(solution)/shard_map/ppermute | solution.py:38
  76.3 16.0 %collective-permute-start.9 = (f32[34,640]{1,0:T(8,128)S(1)}, f32[34,640]{1,0:T(8,128)S(1)}, u32[]{:S(2)}, u32[]{:S(2)}) collective-permute-start(f32[34,640]{1,0:T(8,128)S(1)} %fusion.21), channel_id=1, source_target_pairs={{0,64},{64,0},{1,65},{65,1},{2,66},{66,2},{3,67},{67,3},{4,68},{68... | collective-permute-start | bytes 261128 | tf_op jit(solution)/shard_map/ppermute | solution.py:38
  77.7 13.6 %collective-permute-start.10 = (f32[2,640]{1,0:T(2,128)S(1)}, f32[2,640]{1,0:T(2,128)S(1)}, u32[]{:S(2)}, u32[]{:S(2)}) collective-permute-start(f32[2,640]{1,0:T(2,128)S(1)} %slice.98), channel_id=1, source_target_pairs={{0,4},{4,0},{1,5},{5,1},{2,6},{6,2},{3,7},{7,3},{8,12},{12,8},{9,1... | collective-permute-start | bytes 15368 | tf_op jit(solution)/shard_map/ppermute | solution.py:38
  79.4 11.9 %collective-permute-start.11 = (f32[2,640]{1,0:T(2,128)S(1)}, f32[2,640]{1,0:T(2,128)S(1)}, u32[]{:S(2)}, u32[]{:S(2)}) collective-permute-start(f32[2,640]{1,0:T(2,128)S(1)} %slice.98), channel_id=1, source_target_pairs={{0,68},{4,64},{64,4},{68,0},{1,69},{5,65},{65,5},{69,1},{2,70},{6,... | collective-permute-start | bytes 15368 | tf_op jit(solution)/shard_map/ppermute | solution.py:459
  92.3 12.4 %collective-permute-start.13 = (bf16[34,640]{1,0:T(8,128)(2,1)S(1)}, bf16[34,640]{1,0:T(8,128)(2,1)S(1)}, u32[]{:S(2)}, u32[]{:S(2)}) collective-permute-start(bf16[34,640]{1,0:T(8,128)(2,1)S(1)} %pad_maximum_fusion.2), channel_id=1, source_target_pairs={{0,16},{16,0},{32,48},{48,32},{1,17},{17,1},{33,49},{49,33},{2,18}... | collective-permute-start | bytes 130568 | tf_op jit(solution)/shard_map/ppermute | solution.py:382
  94.7 10.1 %collective-permute-start.14 = (bf16[34,640]{1,0:T(8,128)(2,1)S(1)}, bf16[34,640]{1,0:T(8,128)(2,1)S(1)}, u32[]{:S(2)}, u32[]{:S(2)}) collective-permute-start(bf16[34,640]{1,0:T(8,128)(2,1)S(1)} %pad_maximum_fusion.2), channel_id=1, source_target_pairs={{0,32},{16,48},{32,0},{48,16},{1,33},{17,49},{33,1},{49,17},{2,34}... | collective-permute-start | bytes 130568 | tf_op jit(solution)/shard_map/ppermute | solution.py:382
  97.7 7.1 %collective-permute-start.15 = (bf16[34,640]{1,0:T(8,128)(2,1)S(1)}, bf16[34,640]{1,0:T(8,128)(2,1)S(1)}, u32[]{:S(2)}, u32[]{:S(2)}) collective-permute-start(bf16[34,640]{1,0:T(8,128)(2,1)S(1)} %pad_maximum_fusion.2), channel_id=1, source_target_pairs={{0,48},{16,32},{32,16},{48,0},{1,49},{17,33},{33,17},{49,1},{2,50}... | collective-permute-start | bytes 130568 | tf_op jit(solution)/shard_map/ppermute | solution.py:382
  104.8 6.4 %collective-permute-start.17 = (bf16[34,640]{1,0:T(8,128)(2,1)S(1)}, bf16[34,640]{1,0:T(8,128)(2,1)S(1)}, u32[]{:S(2)}, u32[]{:S(2)}) collective-permute-start(bf16[34,640]{1,0:T(8,128)(2,1)S(1)} %add_convert_fusion), channel_id=1, source_target_pairs={{0,1},{1,0},{2,3},{3,2},{4,5},{5,4},{6,7},{7,6},{8,9},{9,8},{10,11... | collective-permute-start | bytes 130568 | tf_op jit(solution)/shard_map/ppermute | solution.py:382
  105.5 5.7 %collective-permute-start.18 = (bf16[34,640]{1,0:T(8,128)(2,1)S(1)}, bf16[34,640]{1,0:T(8,128)(2,1)S(1)}, u32[]{:S(2)}, u32[]{:S(2)}) collective-permute-start(bf16[34,640]{1,0:T(8,128)(2,1)S(1)} %add_convert_fusion), channel_id=1, source_target_pairs={{0,2},{1,3},{2,0},{3,1},{4,6},{5,7},{6,4},{7,5},{8,10},{9,11},{10,... | collective-permute-start | bytes 130568 | tf_op jit(solution)/shard_map/ppermute | solution.py:382
  108.1 5.3 %collective-permute-start.19 = (bf16[34,640]{1,0:T(8,128)(2,1)S(1)}, bf16[34,640]{1,0:T(8,128)(2,1)S(1)}, u32[]{:S(2)}, u32[]{:S(2)}) collective-permute-start(bf16[34,640]{1,0:T(8,128)(2,1)S(1)} %add_convert_fusion), channel_id=1, source_target_pairs={{0,3},{1,2},{2,1},{3,0},{4,7},{5,6},{6,5},{7,4},{8,11},{9,10},{10,... | collective-permute-start | bytes 130568 | tf_op jit(solution)/shard_map/ppermute | solution.py:382
  109.7 5.6 %collective-permute-start.16 = (f32[20,1920]{1,0:T(8,128)S(1)}, f32[20,1920]{1,0:T(8,128)S(1)}, u32[]{:S(2)}, u32[]{:S(2)}) collective-permute-start(f32[20,1920]{1,0:T(8,128)S(1)} %dynamic-slice_bitcast_fusion), channel_id=1, source_target_pairs={{0,64},{64,0},{1,65},{65,1},{2,66},{66,2},{3,67},{67,3},{4,68},{68... | collective-permute-start | bytes 460808 | tf_op jit(solution)/shard_map/ppermute | solution.py:38

commit v6 on v5

--- a/solution.py
+++ b/solution.py
@@ -50,27 +50,35 @@
     return inner, outer
 
 
-def fill_windows(win, main, inner, outer, same):
+def each_lane_block(width, step):
+    def block(c, carry):
+        step(pl.ds(pl.multiple_of(c * LANES, LANES), LANES), c)
+        return carry
+
+    lax.fori_loop(0, width // LANES, block, 0)
+
+
+def fill_windows(win, main, inner, outer, same, lane):
     odd = same[win.shape[0] + 1] == 1
-    before = jnp.where(odd, inner[...], outer[...])
-    after = jnp.where(odd, outer[...], inner[...])
+    before = jnp.where(odd, inner[:, lane], outer[:, lane])
+    after = jnp.where(odd, outer[:, lane], inner[:, lane])
     blocks = win.shape[0]
     for b in range(blocks):
         lo, hi = b * BLOCK, (b + 1) * BLOCK
-        prior = before if b == 0 else main[lo - HALO : lo, :]
-        later = after if b == blocks - 1 else main[hi : hi + HALO, :]
-        win[b, HALO : HALO + BLOCK, :] = main[lo:hi, :].astype(F32)
+        prior = before if b == 0 else main[lo - HALO : lo, lane]
+        later = after if b == blocks - 1 else main[hi : hi + HALO, lane]
+        win[b, HALO : HALO + BLOCK, :] = main[lo:hi, lane].astype(F32)
         win[b, :HALO, :] = jnp.where(same[b] == 1, prior.astype(F32), 0.0)
         win[b, HALO + BLOCK :, :] = jnp.where(same[b + 1] == 1, later.astype(F32), 0.0)
 
 
-def fill_extended(win, rows, same):
+def fill_extended(win, rows, same, lane):
     for b in range(win.shape[0]):
         lo = b * BLOCK
         hi = lo + HALO + BLOCK
-        win[b, HALO : HALO + BLOCK, :] = rows[lo + HALO : hi, :].astype(F32)
-        win[b, :HALO, :] = jnp.where(same[b] == 1, rows[lo : lo + HALO, :].astype(F32), 0.0)
-        win[b, HALO + BLOCK :, :] = jnp.where(same[b + 1] == 1, rows[hi : hi + HALO, :].astype(F32), 0.0)
+        win[b, HALO : HALO + BLOCK, :] = rows[lo + HALO : hi, lane].astype(F32)
+        win[b, :HALO, :] = jnp.where(same[b] == 1, rows[lo : lo + HALO, lane].astype(F32), 0.0)
+        win[b, HALO + BLOCK :, :] = jnp.where(same[b + 1] == 1, rows[hi : hi + HALO, lane].astype(F32), 0.0)
 
 
 def shifted(win, b, shift):
@@ -78,13 +86,13 @@
     return [(8 * a + shift - 1, 8 * a) for a in range(first, 4)], win[b, pl.ds(shift, BLOCK + 24), :]
 
 
-def convolve(win, b, taps, flip):
+def convolve(win, b, taps, lane, flip):
     total = jnp.zeros((BLOCK, LANES), F32)
     for shift in range(8):
         steps, rows = shifted(win, b, shift)
         for k, at in steps:
             row = TAPS - 1 - k if flip else k
-            total = total + taps[row : row + 1, :] * rows[at : at + BLOCK]
+            total = total + taps[row : row + 1, lane] * rows[at : at + BLOCK]
     return total
 
 
@@ -92,52 +100,60 @@
     return lax.broadcasted_iota(jnp.int32, (BLOCK, LANES), 0) < fill[b]
 
 
-def forward_kernel(same, fill, units, taps, activated, slope, win):
-    fill_extended(win, units, same)
-
-    def step(b, carry):
-        conv = convolve(win, b, taps, False)
-        q = jax.nn.sigmoid(conv)
-        valid = valid_rows(fill, b)
-        rows = pl.ds(pl.multiple_of(b * BLOCK, BLOCK), BLOCK)
-        activated[rows, :] = jnp.where(valid, conv * q, 0.0).astype(BF16)
-        slope[rows, :] = jnp.where(valid, q + conv * q * (1.0 - q), 0.0)
-        return carry
-
-    lax.fori_loop(0, win.shape[0], step, 0)
+def forward_kernel(same, fill, units, taps, activated, slope, win, held_act, held_slope, sems):
+    def stores(lane, c):
+        return (
+            pltpu.make_async_copy(held_act.at[:, lane], activated.at[:, lane], sems.at[0, c]),
+            pltpu.make_async_copy(held_slope.at[:, lane], slope.at[:, lane], sems.at[1, c]),
+        )
+
+    def step(lane, c):
+        fill_extended(win, units, same, lane)
+        for b in range(win.shape[0]):
+            conv = convolve(win, b, taps, lane, False)
+            q = jax.nn.sigmoid(conv)
+            valid = valid_rows(fill, b)
+            rows = slice(b * BLOCK, (b + 1) * BLOCK)
+            held_act[rows, lane] = jnp.where(valid, conv * q, 0.0).astype(BF16)
+            held_slope[rows, lane] = jnp.where(valid, q + conv * q * (1.0 - q), 0.0)
+        for copy in stores(lane, c):
+            copy.start()
+
+    each_lane_block(units.shape[1], step)
+    for c in range(units.shape[1] // LANES):
+        for copy in stores(pl.ds(c * LANES, LANES), c):
+            copy.wait()
 
 
 def taps_kernel(same, units, grad_conv, out, win, sums):
-    fill_extended(win, units, same)
-    sums[...] = jnp.zeros_like(sums)
-
-    def step(b, carry):
-        grad = grad_conv[pl.ds(pl.multiple_of(b * BLOCK, BLOCK), BLOCK), :]
-        for shift in range(8):
-            steps, rows = shifted(win, b, shift)
-            for k, at in steps:
-                terms = (rows[at : at + BLOCK] * grad).reshape(BLOCK // 8, 8, LANES)
-                sums[k] += jnp.sum(terms, axis=0)
-        return carry
-
-    lax.fori_loop(0, win.shape[0], step, 0)
-    out[...] = jnp.sum(sums[...], axis=1)
+    def step(lane, c):
+        fill_extended(win, units, same, lane)
+        sums[...] = jnp.zeros_like(sums)
+        for b in range(win.shape[0]):
+            grad = grad_conv[b * BLOCK : (b + 1) * BLOCK, lane]
+            for shift in range(8):
+                steps, rows = shifted(win, b, shift)
+                for k, at in steps:
+                    terms = (rows[at : at + BLOCK] * grad).reshape(BLOCK // 8, 8, LANES)
+                    sums[k] += jnp.sum(terms, axis=0)
+        out[:, lane] = jnp.sum(sums[...], axis=1)
+
+    each_lane_block(units.shape[1], step)
 
 
 def backward_kernel(same, fill, grad_conv, inner, outer, taps, value, gate, out, win):
-    fill_windows(win, grad_conv, inner, outer, same)
-
-    def step(b, carry):
-        grad_units = jnp.where(valid_rows(fill, b), convolve(win, b, taps, True), 0.0)
-        rows = pl.ds(pl.multiple_of(b * BLOCK, BLOCK), BLOCK)
-        inner = pl.ds(pl.multiple_of(b * BLOCK + HALO, HALO), BLOCK)
-        s = gate[inner, :]
-        grad_value = grad_units * s
-        out[0, rows, :] = grad_value.astype(BF16)
-        out[1, rows, :] = (grad_value * value[inner, :] * (1.0 - s)).astype(BF16)
-        return carry
-
-    lax.fori_loop(0, win.shape[0], step, 0)
+    def step(lane, c):
+        fill_windows(win, grad_conv, inner, outer, same, lane)
+        for b in range(win.shape[0]):
+            grad_units = jnp.where(valid_rows(fill, b), convolve(win, b, taps, lane, True), 0.0)
+            rows = slice(b * BLOCK, (b + 1) * BLOCK)
+            own = slice(b * BLOCK + HALO, (b + 1) * BLOCK + HALO)
+            s = gate[own, lane]
+            grad_value = grad_units * s
+            out[0, rows, lane] = grad_value.astype(BF16)
+            out[1, rows, lane] = (grad_value * value[own, lane] * (1.0 - s)).astype(BF16)
+
+    each_lane_block(grad_conv.shape[1], step)
 
 
 def norm_kernel(place, frames, inner, outer, gain, out, out_t):
@@ -147,30 +163,45 @@
         inv = lax.rsqrt(jnp.mean(center * center, axis=1, keepdims=True) + EPSILON)
         return (center * inv * gain[...]).astype(BF16)
 
-    i = pl.program_id(0)
-    normed = rows(frames[...])
-    out[pl.ds(pl.multiple_of(HALO + i * BLOCK, HALO), BLOCK), :] = normed
-    out_t[...] = normed.T
-
-    @pl.when(i == 0)
-    def _():
-        odd = place[2] % 2 == 1
-        out[:HALO, :] = rows(jnp.where(odd, inner[...].astype(F32), outer[...].astype(F32)))
-        out[out.shape[0] - HALO :, :] = rows(jnp.where(odd, outer[...].astype(F32), inner[...].astype(F32)))
-
-
-def chunks_kernel(rows, out, held, sems):
+    for first in range(0, frames.shape[0], BLOCK):
+        normed = rows(frames[first : first + BLOCK, :])
+        out[HALO + first : HALO + first + BLOCK, :] = normed
+        out_t[:, first : first + BLOCK] = normed.T
+    odd = place[2] % 2 == 1
+    out[:HALO, :] = rows(jnp.where(odd, inner[...].astype(F32), outer[...].astype(F32)))
+    out[out.shape[0] - HALO :, :] = rows(jnp.where(odd, outer[...].astype(F32), inner[...].astype(F32)))
+
+
+def chunks_kernel(section, rows, *refs):
+    outs, held, sems = refs[:4], refs[4], refs[5]
     count = held.shape[2]
-    parts = range(held.shape[0])
-    loads = [pltpu.make_async_copy(rows.at[:, pl.ds(i * count, count)], held.at[i], sems.at[0, i]) for i in parts]
-    stores = [pltpu.make_async_copy(held.at[i], out.at[i], sems.at[1, i]) for i in parts]
-    for load in loads:
+    loads, stores = [], []
+    for k, out in enumerate(outs):
+        first = pl.multiple_of((section[0] ^ k) * count, count)
+        loads.append(pltpu.make_async_copy(rows.at[:, pl.ds(first, count)], held.at[k], sems.at[0, k]))
+        stores.append(pltpu.make_async_copy(held.at[k], out, sems.at[1, k]))
+    for load in loads[1:] + loads[:1]:
         load.start()
-    for load, store in zip(loads, stores):
-        load.wait()
-        store.start()
+    for k in (1, 2, 3, 0):
+        loads[k].wait()
+        stores[k].start()
     for store in stores:
         store.wait()
+
+
+def gradient_kernel(section, own, first, second, third, weights, slope, arrived, out, sems):
+    pieces = own, first, second, third
+    rows = own.shape[0]
+    copies = []
+    for k, piece in enumerate(pieces):
+        at = pl.multiple_of((section[0] ^ k) * rows, 64)
+        copies.append(pltpu.make_async_copy(piece, arrived.at[pl.ds(at, rows), :], sems.at[k]))
+    for copy in copies:
+        copy.start()
+    for copy in copies:
+        copy.wait()
+    grad = jnp.dot(weights[...], arrived[...], preferred_element_type=F32)
+    out[...] = grad.T * slope[...]
 
 
 def halves_kernel(core, rows, order, own, other, held, sem):
@@ -212,22 +243,27 @@
     return pl.BlockSpec(memory_space=pltpu.SMEM)
 
 
-def lanes(rows):
-    return pl.BlockSpec((rows, LANES), lambda c: (0, c))
+def vmem():
+    return pl.BlockSpec(memory_space=pltpu.VMEM)
+
+
+def windows(count):
+    return pltpu.VMEM((count // BLOCK, BLOCK + 2 * HALO, LANES), F32)
 
 
 def convolved(same, fill, units, taps, count):
     width = units.shape[1]
     return pl.pallas_call(
         forward_kernel,
-        grid=(width // LANES,),
-        in_specs=[smem(), smem(), lanes(units.shape[0]), lanes(TAPS)],
-        out_specs=[lanes(count), lanes(count)],
-        out_shape=[
-            jax.ShapeDtypeStruct((count, width), BF16),
-            pltpu.HBM((count, width), F32),
+        in_specs=[smem(), smem(), vmem(), vmem()],
+        out_specs=[hbm(), hbm()],
+        out_shape=[pltpu.HBM((count, width), BF16), pltpu.HBM((count, width), F32)],
+        scratch_shapes=[
+            windows(count),
+            pltpu.VMEM((count, width), BF16),
+            pltpu.VMEM((count, width), F32),
+            pltpu.SemaphoreType.DMA((2, width // LANES)),
         ],
-        scratch_shapes=[pltpu.VMEM((count // BLOCK, BLOCK + 2 * HALO, LANES), F32)],
         compiler_params=params(),
         cost_estimate=duration(5),
         name="conv_forward",
@@ -238,61 +274,36 @@
     count, width = grad_conv.shape
     return pl.pallas_call(
         taps_kernel,
-        grid=(width // LANES,),
-        in_specs=[smem(), lanes(units.shape[0]), lanes(count)],
-        out_specs=lanes(32),
+        in_specs=[smem(), vmem(), vmem()],
+        out_specs=vmem(),
         out_shape=jax.ShapeDtypeStruct((32, width), F32),
-        scratch_shapes=[
-            pltpu.VMEM((count // BLOCK, BLOCK + 2 * HALO, LANES), F32),
-            pltpu.VMEM((32, 8, LANES), F32),
-        ],
+        scratch_shapes=[windows(count), pltpu.VMEM((32, 8, LANES), F32)],
         compiler_params=params(),
         cost_estimate=duration(4),
         name="tap_gradients",
     )(same, units, grad_conv)
 
 
-def projected_back(same, fill, grad_conv, before, after, taps, value, gate):
+def projected_back(same, fill, grad_conv, inner, outer, taps, value, gate):
     count, width = grad_conv.shape
     return pl.pallas_call(
         backward_kernel,
-        grid=(width // LANES,),
-        in_specs=[
-            smem(),
-            smem(),
-            lanes(count),
-            lanes(HALO),
-            lanes(HALO),
-            lanes(TAPS),
-            lanes(value.shape[0]),
-            lanes(value.shape[0]),
-        ],
-        out_specs=pl.BlockSpec((2, count, LANES), lambda c: (0, 0, c)),
+        in_specs=[smem(), smem()] + [vmem()] * 6,
+        out_specs=vmem(),
         out_shape=jax.ShapeDtypeStruct((2, count, width), BF16),
-        scratch_shapes=[pltpu.VMEM((count // BLOCK, BLOCK + 2 * HALO, LANES), F32)],
+        scratch_shapes=[windows(count)],
         compiler_params=params(),
         cost_estimate=duration(5.6),
         name="conv_backward",
-    )(same, fill, grad_conv, before, after, taps, in_hbm(value), in_hbm(gate))
+    )(same, fill, grad_conv, inner, outer, taps, value, gate)
 
 
 def normalised(place, frames, inner, outer, gain):
     count, features = frames.shape
-    edge = pl.BlockSpec((HALO, features), lambda i: (0, 0))
     return pl.pallas_call(
         norm_kernel,
-        grid=(count // BLOCK,),
-        in_specs=[
-            smem(),
-            pl.BlockSpec((BLOCK, features), lambda i: (i, 0)),
-            edge,
-            edge,
-            pl.BlockSpec((1, features), lambda i: (0, 0)),
-        ],
-        out_specs=[
-            pl.BlockSpec((count + 2 * HALO, features), lambda i: (0, 0)),
-            pl.BlockSpec((features, BLOCK), lambda i: (0, i)),
-        ],
+        in_specs=[smem()] + [vmem()] * 4,
+        out_specs=[vmem(), vmem()],
         out_shape=[
             jax.ShapeDtypeStruct((count + 2 * HALO, features), BF16),
             jax.ShapeDtypeStruct((features, count), BF16),
@@ -300,22 +311,39 @@
         compiler_params=params(),
         cost_estimate=duration(3.5),
         name="layer_norm",
-    )(place, in_hbm(frames), inner, outer, gain.reshape(1, features))
-
-
-def frame_chunks(rows, parts):
+    )(place, frames, inner, outer, gain.reshape(1, features))
+
+
+def frame_chunks(section, rows):
     features, total = rows.shape
-    shape = (parts, features, total // parts)
+    count = total // 4
     return pl.pallas_call(
         chunks_kernel,
-        in_specs=[hbm()],
-        out_specs=hbm(),
-        out_shape=pltpu.HBM(shape, rows.dtype),
-        scratch_shapes=[pltpu.VMEM(shape, rows.dtype), pltpu.SemaphoreType.DMA((2, parts))],
+        in_specs=[smem(), hbm()],
+        out_specs=[hbm()] * 4,
+        out_shape=[pltpu.HBM((features, count), rows.dtype)] * 4,
+        scratch_shapes=[pltpu.VMEM((4, features, count), rows.dtype), pltpu.SemaphoreType.DMA((2, 4))],
         compiler_params=params(),
         cost_estimate=duration(2),
         name="frame_chunks",
-    )(in_hbm(rows))
+    )(section, in_hbm(rows))
+
+
+def conv_gradient(section, pieces, weights, slope):
+    features, count = 4 * pieces[0].shape[0], pieces[0].shape[1]
+    return pl.pallas_call(
+        gradient_kernel,
+        in_specs=[smem()] + [hbm()] * 4 + [vmem()] * 2,
+        out_specs=[vmem()] * 2,
+        out_shape=[
+            jax.ShapeDtypeStruct((features, count), BF16),
+            jax.ShapeDtypeStruct((count, weights.shape[0]), F32),
+        ],
+        scratch_shapes=[pltpu.SemaphoreType.DMA((4,))],
+        compiler_params=params(),
+        cost_estimate=duration(3),
+        name="conv_gradient",
+    )(section, *[in_hbm(piece) for piece in pieces], weights, slope)
 
 
 def halves(core, rows, keep=False):
@@ -325,12 +353,11 @@
         for x in range(2):
             for r in range(20):
                 order[(z * 2 + x) * 20 + r, x * 80 + z * 20 + r] = 1.0
-    vmem = pl.BlockSpec(memory_space=pltpu.VMEM)
     half = jax.ShapeDtypeStruct((features // 2, count), BF16)
     return pl.pallas_call(
         halves_kernel,
-        in_specs=[smem(), vmem, vmem],
-        out_specs=[vmem, hbm()],
+        in_specs=[smem(), vmem(), vmem()],
+        out_specs=[vmem(), hbm()],
         out_shape=[half if keep else pltpu.HBM(half.shape, BF16), pltpu.HBM(half.shape, BF16)],
         scratch_shapes=[pltpu.VMEM(half.shape, BF16), pltpu.SemaphoreType.DMA],
         compiler_params=params(),
@@ -401,8 +428,10 @@
     core, xl = lax.axis_index("core"), lax.axis_index("xl")
     first_block = lax.axis_index(FRAMES) * blocks
     place = jnp.stack([core, lax.axis_index("y"), lax.axis_index("section")]).astype(jnp.int32)
-    chunks, frames = lax.optimization_barrier((frame_chunks(returned.T, 4), frames))
-    arrived = lax.all_to_all(chunks, "section", 0, 0).reshape(features, count)
+    section = lax.axis_index("section").reshape(1)
+    *chunks, frames = lax.optimization_barrier((*frame_chunks(section, returned.T), frames))
+    for k in (1, 3, 2):
+        chunks[k] = lax.ppermute(chunks[k], "section", [(i, i ^ k) for i in range(4)])
 
     edge = jnp.full((1,), -1, jnp.int32)
     near_utt = lax.dynamic_slice(jnp.concatenate([edge, block_utt, edge]), (first_block,), (blocks + 2,))
@@ -424,11 +453,8 @@
     normed_own, normed_other = halves(core, normed_t)
     normed_peer = swap(normed_other, "core")
 
-    arrived, normed_own, normed_other = lax.optimization_barrier((arrived, normed_own, normed_other))
-    grad_activated = lax.dot_general(
-        arrived, weight_out, (((0,), (1,)), ((), ())), preferred_element_type=F32
-    )
-    grad_conv = grad_activated * slope
+    arrived, grad_conv = conv_gradient(section, chunks, weight_out, slope)
+    normed_own, normed_other, grad_conv = lax.optimization_barrier((normed_own, normed_other, grad_conv))
     conv_inner, conv_outer = halos(grad_conv)
     arrived_rows, grad_conv = lax.optimization_barrier((arrived, grad_conv))
     rows_own, rows_other = halves(core, arrived_rows, keep=True)

time: 117 us -> 113 us (0.966)
  waiting for transfers between devices: 18.2 us -> 23.5 us
  matrix products: 10.2 us -> 6.13 us
  Pallas kernels: 36 us -> 32.4 us
    ppermute x0 -> x3, starting transfers between devices: none -> 7.63 us  [body(): lax.ppermute(chunks[k], 'section', [(i, i ^ k) for i in range(4)])]
    all_to_all x1 -> x0, starting transfers between devices: 6.12 us -> none  [body(): arrived = lax.all_to_all(chunks, 'section', 0, 0).reshape(features, count)]
    ppermute x0 -> x3, waiting for transfers between devices: none -> 4.18 us  [body(): lax.ppermute(chunks[k], 'section', [(i, i ^ k) for i in range(4)])]
    ppermute x9, starting transfers between devices: 11.3 us -> 8.09 us  [swap(): return lax.ppermute(value, axis, [(0, 1), (1, 0)])]
    dot_general x1 -> x0, matrix products: 3.03 us -> none  [body(): lax.dot_general(arrived, weight_out, (((0,), (1,)), ((), ())), preferred_...]
    pallas_call x7 -> x8, Pallas kernels: 24.1 us -> 21.7 us  [the longest x1 4.66 us: convolved(): pl.pallas_call(forward_kernel, in_specs=[smem(), smem(), vmem(), vmem()],...]
    all_to_all x1 -> x0, waiting for transfers between devices: 2.21 us -> none  [body(): arrived = lax.all_to_all(chunks, 'section', 0, 0).reshape(features, count)]
    ppermute x6, waiting for transfers between devices: 2.14 us -> 3.66 us  [shares_of(): lax.ppermute(value, axis, [(i, i ^ k) for i in range(4)])]
  transfers between devices with their start and end apart: 22 -> 24, of which waited for: 8 -> 9; matrix products, arithmetic and copies ran while one was open for 14% -> 11% of each run, Pallas kernels for 24% -> 24%
where the time goes in v6:
time: 113 us
  starting transfers between devices  41.8 us (37%)
  Pallas kernels  32.4 us (29%)
  waiting for transfers between devices  23.5 us (21%)
  matrix products  6.13 us (5%)
  other arithmetic  4.39 us (4%)
  local copies, waits for them, and re-layouts  3.26 us (3%)
    ppermute x6, starting transfers between devices, shares_of(): lax.ppermute(value, axis, [(i, i ^ k) for i in range(4)])  10.5 us
    ppermute x9, waiting for transfers between devices, swap(): return lax.ppermute(value, axis, [(0, 1), (1, 0)])  9.72 us
    all_to_all x1, starting transfers between devices, body(): got = lax.all_to_all(parts.reshape(16, 40, 3 * width), PLANE, 0, 0)  9 us
    ppermute x9, starting transfers between devices, swap(): return lax.ppermute(value, axis, [(0, 1), (1, 0)])  8.09 us
    ppermute x3, starting transfers between devices, body(): lax.ppermute(chunks[k], 'section', [(i, i ^ k) for i in range(4)])  7.63 us
    all_to_all x1, waiting for transfers between devices, body(): got = lax.all_to_all(parts.reshape(16, 40, 3 * width), PLANE, 0, 0)  5.95 us
    pallas_call x2, Pallas kernels, pair_product(): pl.pallas_call(pair_kernel, grid=(made,), in_specs=[whole, whole, spec, s...  5.57 us
    pallas_call x1, Pallas kernels, norm_back(): pl.pallas_call(final_kernel, grid=(count // BLOCK,), in_specs=[block, blo...  5.13 us
  transfers between devices with their start and end apart: 24, of which 9 were waited for; matrix products, arithmetic and copies ran while one was open for 11% of the time, Pallas kernels for 24%

profile of v6, /device:TPU:0, one launch (start us, length us, event | category | flops | bytes accessed | tf_op | source)
XLA Modules:
  0.0 112.6 jit_solution(10073325782636747545)
XLA Ops:
  0.7 2.2 %frame_chunks.1 = (bf16[320,512]{1,0:T(8,128)(2,1)}, bf16[320,512]{1,0:T(8,128)(2,1)}, bf16[320,512]{1,0:T(8,128)(2,1)}, bf16[320,512]{1,0:T(8,128)(2,1)}) custom-call(s32[1]{0:T(128)} %bitcast.2.section, bf16[320,2048]{1,0:T(8,128)(2,1)} %bitcast.49), custom_call_target="tpu_custom_call" | custom-call | flops 2300000000 | tf_op jit(solution)/shard_map/frame_chunks/pallas_call | solution.py:320
  3.0 2.1 %collective-permute-start = (bf16[16,1280]{1,0:T(8,128)(2,1)S(1)}, bf16[16,1280]{1,0:T(8,128)(2,1)S(1)}, u32[]{:S(2)}, u32[]{:S(2)}) collective-permute-start(bf16[16,1280]{1,0:T(8,128)(2,1)S(1)} %get-tuple-element.100), channel_id=1, source_target_pairs={{0,1},{1,0},{2,3},{3,2},{8,9},{9,8},{10,11},{11,10},{16,17},{17,16... | collective-permute-start | bytes 122888 | tf_op jit(solution)/shard_map/ppermute | solution.py:48
  5.0 0.7 collective-permute-start.1
  5.7 4.9 %collective-permute-start.2 = (bf16[320,512]{1,0:T(8,128)(2,1)}, bf16[320,512]{1,0:T(8,128)(2,1)S(1)}, u32[]{:S(2)}, u32[]{:S(2)}) collective-permute-start(bf16[320,512]{1,0:T(8,128)(2,1)} %get-tuple-element.55), channel_id=1, source_target_pairs={{0,1},{1,0},{2,3},{3,2},{4,5},{5,4},{6,7},{7,6},{8,9},{9,8},{10,11... | collective-permute-start | bytes 983048 | tf_op jit(solution)/shard_map/ppermute | solution.py:434
  10.6 0.5 collective-permute-start.3
  11.0 2.3 %collective-permute-start.4 = (bf16[320,512]{1,0:T(8,128)(2,1)}, bf16[320,512]{1,0:T(8,128)(2,1)}, u32[]{:S(2)}, u32[]{:S(2)}) collective-permute-start(bf16[320,512]{1,0:T(8,128)(2,1)} %get-tuple-element.57), channel_id=1, source_target_pairs={{0,3},{1,2},{2,1},{3,0},{4,7},{5,6},{6,5},{7,4},{8,11},{9,10},{10,... | collective-permute-start | bytes 983048 | tf_op jit(solution)/shard_map/ppermute | solution.py:434
  13.3 0.1 pad_add_fusion
  13.4 0.1 dynamic_slice.14
  13.5 0.1 fusion.20
  13.6 0.1 dynamic_slice.13
  13.6 0.1 compare_convert_fusion
  13.7 0.1 pad_add_fusion.4.place
  13.8 0.1 pad_add_fusion.5.same
  13.9 0.1 slice.75.fill
  13.9 0.1 slice.76
  14.0 1.8 %layer_norm.1 = (bf16[544,1280]{1,0:T(8,128)(2,1)S(1)}, bf16[1280,512]{1,0:T(8,128)(2,1)S(1)}) custom-call(s32[3]{0:T(128)S(1)} %pad_add_fusion.4.place, bf16[512,1280]{1,0:T(8,128)(2,1)S(1)} %copy-done, bf16[16,1280]{1,0:T(8,128)(2,1)S(1)} %collective-permute-done.inner, bf16[16,1280]{1,0:T(8,128)(2,1)S(1)} %collective-permute-done.1.outer, ...), custom_call_target="tpu_custom_call" | custom-call | flops 4024999936 | tf_op jit(solution)/shard_map/layer_norm/pallas_call | solution.py:303
  15.8 0.1 copy-done.8
  16.0 1.3 %add_divide_fusion.gate = f32[544,640]{1,0:T(8,128)S(1)} fusion(bf16[544,1280]{1,0:T(8,128)(2,1)S(1)} %get-tuple-element.58, bf16[2,1280,640]{2,1,0:T(8,128)(2,1)S(1)} %copy-done.8), kind=kOutput, calls=%fused_computation.18 | convolution fusion | flops 892334080 | bytes 4423680 | tf_op jit(solution)/shard_map/dot_general | solution.py:447
  17.3 1.3 %select_convert_fusion = (bf16[544,640]{1,0:T(8,128)(2,1)S(1)}, f32[544,640]{1,0:T(8,128)S(1)}) fusion(f32[544,640]{1,0:T(8,128)S(1)} %add_divide_fusion.gate, pred[544]{0:T(1024)(128)(4,1)S(1)} %slice.76, bf16[544,1280]{1,0:T(8,128)(2,1)S(1)} %get-tuple-element.58, bf16[2,1280,640]{2,1,0:T(8,128)(2,1)S(1)} %copy-done.8), kind=kOutput, calls=%fused_computation.17 | convolution fusion | flops 892334080 | bytes 6513664 | tf_op jit(solution)/shard_map/dot_general | solution.py:446
  18.6 4.7 %conv_forward.1 = (bf16[512,640]{1,0:T(8,128)(2,1)}, f32[512,640]{1,0:T(8,128)}) custom-call(s32[6]{0:T(128)S(1)} %pad_add_fusion.5.same, s32[4]{0:T(128)S(1)} %slice.75.fill, bf16[544,640]{1,0:T(8,128)(2,1)S(1)} %get-tuple-element.104.units, f32[31,640]{1,0:T(8,128)S(1)} %copy-done.3), custom_call_target="tpu_custom_call" | custom-call | flops 5750000128 | tf_op jit(solution)/shard_map/conv_forward/pallas_call | solution.py:256
  23.3 0.3 collective-permute-start.7
  23.6 2.1 %core_halves.2 = (bf16[640,512]{1,0:T(8,128)(2,1)}, bf16[640,512]{1,0:T(8,128)(2,1)}) custom-call(s32[1]{0:T(128)} %bitcast.core, bf16[1280,512]{1,0:T(8,128)(2,1)S(1)} %get-tuple-element.51.rows, bf16[160,160]{1,0:T(8,128)(2,1)S(1)} %copy-done.4), custom_call_target="tpu_custom_call" | custom-call | flops 1380000000 | tf_op jit(solution)/shard_map/core_halves/pallas_call | solution.py:357
  25.7 0.4 collective-permute-done.3.second
  26.1 3.8 %collective-permute-done.4.third = bf16[320,512]{1,0:T(8,128)(2,1)} collective-permute-done((bf16[320,512]{1,0:T(8,128)(2,1)}, bf16[320,512]{1,0:T(8,128)(2,1)}, u32[]{:S(2)}, u32[]{:S(2)}) %collective-permute-start.4) | collective-permute-done | bytes 327712 | tf_op jit(solution)/shard_map/ppermute | solution.py:434
  29.9 2.6 %conv_gradient.1 = (bf16[1280,512]{1,0:T(8,128)(2,1)S(1)}, f32[512,640]{1,0:T(8,128)S(1)}) custom-call(s32[1]{0:T(128)} %bitcast.2.section, bf16[320,512]{1,0:T(8,128)(2,1)} %get-tuple-element.54.own, bf16[320,512]{1,0:T(8,128)(2,1)} %copy-done.13, bf16[320,512]{1,0:T(8,128)(2,1)} %copy-done.14, bf16[320,512]{1,0:T(8,128)(2,1)} %collective-permute-done.4.third, ...), custom_call_target="tpu_custom_call" | custom-call | flops 3449999872 | tf_op jit(solution)/shard_map/conv_gradient/pallas_call | solution.py:334
  32.5 1.2 %core_halves.3 = (bf16[640,512]{1,0:T(8,128)(2,1)S(1)}, bf16[640,512]{1,0:T(8,128)(2,1)}) custom-call(s32[1]{0:T(128)} %bitcast.core, bf16[1280,512]{1,0:T(8,128)(2,1)S(1)} %get-tuple-element.62.arrived, bf16[160,160]{1,0:T(8,128)(2,1)S(1)} %copy-done.4), custom_call_target="tpu_custom_call" | custom-call | flops 1380000000 | tf_op jit(solution)/shard_map/core_halves/pallas_call | solution.py:357
  33.6 0.1 copy-done.5
  33.7 0.1 collective-permute-start.6
  33.9 0.1 collective-permute-start.8
  34.0 0.7 collective-permute-start.9
  34.7 1.4 %collective-permute-done.6.left_peer = bf16[640,512]{1,0:T(8,128)(2,1)S(1)} collective-permute-done((bf16[640,512]{1,0:T(8,128)(2,1)}, bf16[640,512]{1,0:T(8,128)(2,1)S(1)}, u32[]{:S(2)}, u32[]{:S(2)}) %collective-permute-start.6) | collective-permute-done | bytes 655392 | tf_op jit(solution)/shard_map/ppermute | solution.py:38
  36.1 2.1 %weight_gradient.2.buffers_0_ = bf16[640,1920]{1,0:T(8,128)(2,1)} custom-call(bf16[640,512]{1,0:T(8,128)(2,1)S(1)} %get-tuple-element.66.left, bf16[640,512]{1,0:T(8,128)(2,1)S(1)} %collective-permute-done.6.left_peer, bf16[1,512,640]{2,1,0:T(8,128)(2,1)S(1)} %bitcast.46, bf16[1,512,640]{2,1,0:T(8,128)(2,1)S(1)} %bitcast.47), custom_call_target="tpu_custom_call" | custom-call | flops 3910000128 | tf_op jit(solution)/shard_map/weight_gradient/pallas_call | solution.py:395
  38.2 3.7 %conv_backward.1.right = bf16[2,512,640]{2,1,0:T(8,128)(2,1)S(1)} custom-call(s32[6]{0:T(128)S(1)} %pad_add_fusion.5.same, s32[4]{0:T(128)S(1)} %slice.75.fill, f32[512,640]{1,0:T(8,128)S(1)} %get-tuple-element.63, f32[16,640]{1,0:T(8,128)S(1)} %collective-permute-done.8.inner, f32[16,640]{1,0:T(8,128)S(1)} %collective-permute-done.9.outer, ...), custom_call_target="tpu_custom_call" | custom-call | flops 6440000000 | tf_op jit(solution)/shard_map/conv_backward/pallas_call | solution.py:289
  41.9 2.8 %collective-permute-start.10 = (bf16[2,512,640]{2,1,0:T(8,128)(2,1)S(1)}, bf16[2,512,640]{2,1,0:T(8,128)(2,1)S(1)}, u32[]{:S(2)}, u32[]{:S(2)}) collective-permute-start(bf16[2,512,640]{2,1,0:T(8,128)(2,1)S(1)} %conv_backward.1.right), channel_id=1, source_target_pairs={{0,8},{8,0},{1,9},{9,1},{2,10},{10,2},{3,11},{11,3},{4,12},{12,4},... | collective-permute-start | bytes 3932168 | tf_op jit(solution)/shard_map/ppermute | solution.py:38
  44.7 0.1 collective-permute-start.5
  44.8 1.2 %fusion.1 = f32[512,1280]{1,0:T(8,128)S(1)} fusion(bf16[2,1280,640]{2,1,0:T(8,128)(2,1)S(1)} %copy-done.8, bf16[2,512,640]{2,1,0:T(8,128)(2,1)S(1)} %conv_backward.1.right), kind=kOutput, calls=%fused_computation.4 | convolution fusion | flops 838860800 | bytes 4915200 | tf_op jit(solution)/shard_map/dot_general | solution.py:471
  46.0 2.3 %fusion.sent = bf16[512,1280]{1,0:T(8,128)(2,1)} fusion(f32[512,1280]{1,0:T(8,128)S(1)} %fusion.1, bf16[2,1280,640]{2,1,0:T(8,128)(2,1)S(1)} %copy-done.8, bf16[2,512,640]{2,1,0:T(8,128)(2,1)S(1)} %conv_backward.1.right), kind=kOutput, calls=%fused_computation.2 | convolution fusion | flops 840171520 | bytes 6225920 | tf_op jit(solution)/shard_map/dot_general | solution.py:470
  48.3 3.0 %collective-permute-start.15 = (bf16[512,1280]{1,0:T(8,128)(2,1)}, bf16[512,1280]{1,0:T(8,128)(2,1)}, u32[]{:S(2)}, u32[]{:S(2)}) collective-permute-start(bf16[512,1280]{1,0:T(8,128)(2,1)} %fusion.sent), channel_id=1, source_target_pairs={{0,4},{4,0},{1,5},{5,1},{2,6},{6,2},{3,7},{7,3},{8,12},{12,8},{9,1... | collective-permute-start | bytes 3932168 | tf_op jit(solution)/shard_map/ppermute | solution.py:38
  51.3 3.4 %weight_gradient.3 = bf16[640,1920]{1,0:T(8,128)(2,1)} custom-call(bf16[640,512]{1,0:T(8,128)(2,1)S(1)} %copy-done.6, bf16[640,512]{1,0:T(8,128)(2,1)S(1)} %collective-permute-done.5.left_peer, bf16[2,512,640]{2,1,0:T(8,128)(2,1)S(1)} %conv_backward.1.right, ...), custom_call_target="tpu_custom_call", output_to_operand_aliasing={{}: (4, {})} | custom-call | flops 3910000128 | tf_op jit(solution)/shard_map/weight_gradient/pallas_call | solution.py:395
  54.8 9.0 %all-to-all-start = ((bf16[16,40,1920]{2,1,0:T(8,128)(2,1)}), bf16[16,40,1920]{2,1,0:T(8,128)(2,1)}, u32[]{:S(2)}, u32[]{:S(2)}) async-start(bf16[16,40,1920]{2,1,0:T(8,128)(2,1)} %bitcast.48), calls=%async_computation | async-start | bytes 4915200 | tf_op jit(solution)/shard_map/all_to_all | solution.py:476
  63.8 3.6 %tap_gradients.1 = f32[32,640]{1,0:T(8,128)S(1)} custom-call(s32[6]{0:T(128)S(1)} %pad_add_fusion.5.same, bf16[544,640]{1,0:T(8,128)(2,1)S(1)} %get-tuple-element.104.units, f32[512,640]{1,0:T(8,128)S(1)} %get-tuple-element.63), custom_call_target="tpu_custom_call" | custom-call | flops 4600000000 | tf_op jit(solution)/shard_map/tap_gradients/pallas_call | solution.py:275
  67.3 1.7 %multiply_reduce_fusion = f32[1280]{0:T(1024)S(1)} fusion(bf16[512,1280]{1,0:T(8,128)(2,1)} %fusion.sent, bf16[544,1280]{1,0:T(8,128)(2,1)S(1)} %get-tuple-element.58), kind=kLoop, calls=%fused_computation.3 | loop fusion | flops 2620160 | bytes 2626560 | tf_op jit(solution)/shard_map/reduce_sum | solution.py:481
  69.1 0.1 collective-permute-start.11
  69.2 1.3 %collective-permute-done.11 = f32[34,640]{1,0:T(8,128)S(1)} collective-permute-done((f32[34,640]{1,0:T(8,128)S(1)}, f32[34,640]{1,0:T(8,128)S(1)}, u32[]{:S(2)}, u32[]{:S(2)}) %collective-permute-start.11) | collective-permute-done | bytes 87072 | tf_op jit(solution)/shard_map/ppermute | solution.py:38
  70.5 0.1 collective-permute-start.12
  70.6 1.6 %collective-permute-start.13 = (f32[2,640]{1,0:T(2,128)S(1)}, f32[2,640]{1,0:T(2,128)S(1)}, u32[]{:S(2)}, u32[]{:S(2)}) collective-permute-start(f32[2,640]{1,0:T(2,128)S(1)} %slice.96), channel_id=1, source_target_pairs={{0,4},{4,0},{1,5},{5,1},{2,6},{6,2},{3,7},{7,3},{8,12},{12,8},{9,1... | collective-permute-start | bytes 15368 | tf_op jit(solution)/shard_map/ppermute | solution.py:38
  72.2 3.1 %collective-permute-start.14 = (f32[2,640]{1,0:T(2,128)S(1)}, f32[2,640]{1,0:T(2,128)S(1)}, u32[]{:S(2)}, u32[]{:S(2)}) collective-permute-start(f32[2,640]{1,0:T(2,128)S(1)} %slice.96), channel_id=1, source_target_pairs={{0,68},{4,64},{64,4},{68,0},{1,69},{5,65},{65,5},{69,1},{2,70},{6,... | collective-permute-start | bytes 15368 | tf_op jit(solution)/shard_map/ppermute | solution.py:485
  75.3 6.4 %collective-permute-done.15.other = bf16[512,1280]{1,0:T(8,128)(2,1)} collective-permute-done((bf16[512,1280]{1,0:T(8,128)(2,1)}, bf16[512,1280]{1,0:T(8,128)(2,1)}, u32[]{:S(2)}, u32[]{:S(2)}) %collective-permute-start.15) | collective-permute-done | bytes 1310752 | tf_op jit(solution)/shard_map/ppermute | solution.py:38
  81.7 5.1 %norm_backward.1 = bf16[512,1280]{1,0:T(8,128)(2,1)} custom-call(bf16[512,1280]{1,0:T(8,128)(2,1)} %fusion.sent, bf16[512,1280]{1,0:T(8,128)(2,1)} %collective-permute-done.15.other, bf16[512,1280]{1,0:T(8,128)(2,1)} %frames.1, bf16[1280,512]{1,0:T(8,128)(2,1)} %copy-done.5, f32[1,1280]{1,0:T(1,128)S(1)} %reshape.40.gain), custom_call_target="tpu_custom_call" | custom-call | flops 11960000512 | tf_op jit(solution)/shard_map/norm_backward/pallas_call | solution.py:372
  86.9 2.7 %collective-permute-start.16 = (bf16[34,640]{1,0:T(8,128)(2,1)S(1)}, bf16[34,640]{1,0:T(8,128)(2,1)S(1)}, u32[]{:S(2)}, u32[]{:S(2)}) collective-permute-start(bf16[34,640]{1,0:T(8,128)(2,1)S(1)} %pad_maximum_fusion.2), channel_id=1, source_target_pairs={{0,16},{16,0},{32,48},{48,32},{1,17},{17,1},{33,49},{49,33},{2,18}... | collective-permute-start | bytes 130568 | tf_op jit(solution)/shard_map/ppermute | solution.py:409
  89.7 3.0 %collective-permute-start.17 = (bf16[34,640]{1,0:T(8,128)(2,1)S(1)}, bf16[34,640]{1,0:T(8,128)(2,1)S(1)}, u32[]{:S(2)}, u32[]{:S(2)}) collective-permute-start(bf16[34,640]{1,0:T(8,128)(2,1)S(1)} %pad_maximum_fusion.2), channel_id=1, source_target_pairs={{0,32},{16,48},{32,0},{48,16},{1,33},{17,49},{33,1},{49,17},{2,34}... | collective-permute-start | bytes 130568 | tf_op jit(solution)/shard_map/ppermute | solution.py:409
  92.6 6.0 %all-to-all-done = bf16[16,40,1920]{2,1,0:T(8,128)(2,1)} async-done(((bf16[16,40,1920]{2,1,0:T(8,128)(2,1)}), bf16[16,40,1920]{2,1,0:T(8,128)(2,1)}, u32[]{:S(2)}, u32[]{:S(2)}) %all-to-all-start) | async-done | bytes 2457632 | tf_op jit(solution)/shard_map/all_to_all | solution.py:476
  98.6 2.1 %convert_reduce_fusion = f32[40,1920]{1,0:T(8,128)S(1)} fusion(bf16[16,40,1920]{2,1,0:T(8,128)(2,1)} %all-to-all-done), kind=kLoop, calls=%fused_computation | loop fusion | flops 2380800 | bytes 2764800 | tf_op jit(solution)/shard_map/reduce_sum | solution.py:493
  100.8 0.8 collective-permute-start.20
  101.5 2.5 %collective-permute-start.21 = (bf16[34,640]{1,0:T(8,128)(2,1)S(1)}, bf16[34,640]{1,0:T(8,128)(2,1)S(1)}, u32[]{:S(2)}, u32[]{:S(2)}) collective-permute-start(bf16[34,640]{1,0:T(8,128)(2,1)S(1)} %add_convert_fusion), channel_id=1, source_target_pairs={{0,2},{1,3},{2,0},{3,1},{4,6},{5,7},{6,4},{7,5},{8,10},{9,11},{10,... | collective-permute-start | bytes 130568 | tf_op jit(solution)/shard_map/ppermute | solution.py:409
  104.0 1.5 %collective-permute-start.22 = (bf16[34,640]{1,0:T(8,128)(2,1)S(1)}, bf16[34,640]{1,0:T(8,128)(2,1)S(1)}, u32[]{:S(2)}, u32[]{:S(2)}) collective-permute-start(bf16[34,640]{1,0:T(8,128)(2,1)S(1)} %add_convert_fusion), channel_id=1, source_target_pairs={{0,3},{1,2},{2,1},{3,0},{4,7},{5,6},{6,5},{7,4},{8,11},{9,10},{10,... | collective-permute-start | bytes 130568 | tf_op jit(solution)/shard_map/ppermute | solution.py:409
  105.6 0.1 collective-permute-start.19
  105.7 1.4 %collective-permute-done.21 = bf16[34,640]{1,0:T(8,128)(2,1)S(1)} collective-permute-done((bf16[34,640]{1,0:T(8,128)(2,1)S(1)}, bf16[34,640]{1,0:T(8,128)(2,1)S(1)}, u32[]{:S(2)}, u32[]{:S(2)}) %collective-permute-start.21) | collective-permute-done | bytes 43552 | tf_op jit(solution)/shard_map/ppermute | solution.py:409
  107.1 2.2 %collective-permute-done.22 = bf16[34,640]{1,0:T(8,128)(2,1)S(1)} collective-permute-done((bf16[34,640]{1,0:T(8,128)(2,1)S(1)}, bf16[34,640]{1,0:T(8,128)(2,1)S(1)}, u32[]{:S(2)}, u32[]{:S(2)}) %collective-permute-start.22) | collective-permute-done | bytes 43552 | tf_op jit(solution)/shard_map/ppermute | solution.py:409
  109.4 0.6 slice.100
  110.0 0.6 reshape.44
  110.6 0.6 collective-permute-done.19
  111.2 0.6 slice_bitcast_fusion.4
  111.9 0.7 copy.17
  (62 shorter events, 0.4 us)
Async XLA Ops:
  0.7 2.3 %copy-start = (bf16[512,1280]{1,0:T(8,128)(2,1)S(1)}, bf16[512,1280]{1,0:T(8,128)(2,1)}, u32[]{:S(2)}) copy-start(bf16[512,1280]{1,0:T(8,128)(2,1)} %frames.1) | copy-start | bytes 3932164
  0.7 12.7 %copy-start.10 = (s32[256]{0:T(256)S(1)}, s32[256]{0:T(256)}, u32[]{:S(2)}) copy-start(s32[256]{0:T(256)} %param.17) | copy-start | bytes 3076
  0.7 12.7 %copy-start.11 = (s32[256]{0:T(256)S(1)}, s32[256]{0:T(256)}, u32[]{:S(2)}) copy-start(s32[256]{0:T(256)} %param.16) | copy-start | bytes 3076
  0.7 13.3 %copy-start.9 = (f32[1280]{0:T(1024)S(1)}, f32[1280]{0:T(1024)}, u32[]{:S(2)}) copy-start(f32[1280]{0:T(1024)} %param.12) | copy-start | bytes 15364
  3.0 11.1 %collective-permute-start = (bf16[16,1280]{1,0:T(8,128)(2,1)S(1)}, bf16[16,1280]{1,0:T(8,128)(2,1)S(1)}, u32[]{:S(2)}, u32[]{:S(2)}) collective-permute-start(bf16[16,1280]{1,0:T(8,128)(2,1)S(1)} %get-tuple-element.100), channel_id=1, source_target_pairs={{0,1},{1,0},{2,3},{3,2},{8,9},{9,8},{10,11},{11,10},{16,17},{17,16... | collective-permute-start | bytes 122888 | tf_op jit(solution)/shard_map/ppermute | solution.py:48
  5.0 9.0 %collective-permute-start.1 = (bf16[16,1280]{1,0:T(8,128)(2,1)S(1)}, bf16[16,1280]{1,0:T(8,128)(2,1)S(1)}, u32[]{:S(2)}, u32[]{:S(2)}) collective-permute-start(bf16[16,1280]{1,0:T(8,128)(2,1)S(1)} %get-tuple-element.99), channel_id=1, source_target_pairs={{1,2},{3,8},{9,10},{11,16},{17,18},{19,24},{25,26},{27,32},{33,34}... | collective-permute-start | bytes 122888 | tf_op jit(solution)/shard_map/ppermute | solution.py:49
  5.7 20.0 %collective-permute-start.2 = (bf16[320,512]{1,0:T(8,128)(2,1)}, bf16[320,512]{1,0:T(8,128)(2,1)S(1)}, u32[]{:S(2)}, u32[]{:S(2)}) collective-permute-start(bf16[320,512]{1,0:T(8,128)(2,1)} %get-tuple-element.55), channel_id=1, source_target_pairs={{0,1},{1,0},{2,3},{3,2},{4,5},{5,4},{6,7},{7,6},{8,9},{9,8},{10,11... | collective-permute-start | bytes 983048 | tf_op jit(solution)/shard_map/ppermute | solution.py:434
  10.6 15.5 %collective-permute-start.3 = (bf16[320,512]{1,0:T(8,128)(2,1)}, bf16[320,512]{1,0:T(8,128)(2,1)S(1)}, u32[]{:S(2)}, u32[]{:S(2)}) collective-permute-start(bf16[320,512]{1,0:T(8,128)(2,1)} %get-tuple-element.56), channel_id=1, source_target_pairs={{0,2},{1,3},{2,0},{3,1},{4,6},{5,7},{6,4},{7,5},{8,10},{9,11},{10,... | collective-permute-start | bytes 983048 | tf_op jit(solution)/shard_map/ppermute | solution.py:434
  11.0 18.8 %collective-permute-start.4 = (bf16[320,512]{1,0:T(8,128)(2,1)}, bf16[320,512]{1,0:T(8,128)(2,1)}, u32[]{:S(2)}, u32[]{:S(2)}) collective-permute-start(bf16[320,512]{1,0:T(8,128)(2,1)} %get-tuple-element.57), channel_id=1, source_target_pairs={{0,3},{1,2},{2,1},{3,0},{4,7},{5,6},{6,5},{7,4},{8,11},{9,10},{10,... | collective-permute-start | bytes 983048 | tf_op jit(solution)/shard_map/ppermute | solution.py:434
  14.0 1.9 %copy-start.8 = (bf16[2,1280,640]{2,1,0:T(8,128)(2,1)S(1)}, bf16[2,1280,640]{2,1,0:T(8,128)(2,1)}, u32[]{:S(2)}) copy-start(bf16[2,1280,640]{2,1,0:T(8,128)(2,1)} %param.13) | copy-start | bytes 9830404
  17.3 1.3 %copy-start.3 = (f32[31,640]{1,0:T(8,128)S(1)}, f32[31,640]{1,0:T(8,128)}, u32[]{:S(2)}) copy-start(f32[31,640]{1,0:T(8,128)} %taps.3) | copy-start | bytes 238084
  18.6 5.0 %copy-start.4 = (bf16[160,160]{1,0:T(8,128)(2,1)S(1)}, bf16[160,160]{1,0:T(8,128)(2,1)}, u32[]{:S(2)}) copy-start(bf16[160,160]{1,0:T(8,128)(2,1)} %constant.73.clone.order) | copy-start | bytes 153604
  23.3 11.4 %collective-permute-start.7 = (bf16[512,640]{1,0:T(8,128)(2,1)}, bf16[512,640]{1,0:T(8,128)(2,1)S(1)}, u32[]{:S(2)}, u32[]{:S(2)}) collective-permute-start(bf16[512,640]{1,0:T(8,128)(2,1)} %get-tuple-element.68), channel_id=1, source_target_pairs={{0,8},{8,0},{1,9},{9,1},{2,10},{10,2},{3,11},{11,3},{4,12},{12,4},... | collective-permute-start | bytes 1966088 | tf_op jit(solution)/shard_map/ppermute | solution.py:38
  23.6 6.3 %copy-start.1 = (bf16[640,1280]{1,0:T(8,128)(2,1)S(1)}, bf16[640,1280]{1,0:T(8,128)(2,1)}, u32[]{:S(2)}) copy-start(bf16[640,1280]{1,0:T(8,128)(2,1)} %weights.1) | copy-start | bytes 4915204
  23.6 6.3 %copy-start.7 = (f32[512,640]{1,0:T(8,128)S(1)}, f32[512,640]{1,0:T(8,128)}, u32[]{:S(2)}) copy-start(f32[512,640]{1,0:T(8,128)} %get-tuple-element.59.slope) | copy-start | bytes 3932164
  25.7 4.2 %copy-start.13 = (bf16[320,512]{1,0:T(8,128)(2,1)}, bf16[320,512]{1,0:T(8,128)(2,1)S(1)}, u32[]{:S(2)}) copy-start(bf16[320,512]{1,0:T(8,128)(2,1)S(1)} %collective-permute-done.2.first) | copy-start | bytes 983044
  26.1 3.8 %copy-start.14 = (bf16[320,512]{1,0:T(8,128)(2,1)}, bf16[320,512]{1,0:T(8,128)(2,1)S(1)}, u32[]{:S(2)}) copy-start(bf16[320,512]{1,0:T(8,128)(2,1)S(1)} %collective-permute-done.3.second) | copy-start | bytes 983044
  32.4 1.3 %copy-start.5 = (bf16[1280,512]{1,0:T(8,128)(2,1)}, bf16[1280,512]{1,0:T(8,128)(2,1)S(1)}, u32[]{:S(2)}) copy-start(bf16[1280,512]{1,0:T(8,128)(2,1)S(1)} %get-tuple-element.62.arrived) | copy-start | bytes 3932164
  32.5 3.6 %copy-start.2 = (bf16[512,640]{1,0:T(8,128)(2,1)S(1)}, bf16[512,640]{1,0:T(8,128)(2,1)}, u32[]{:S(2)}) copy-start(bf16[512,640]{1,0:T(8,128)(2,1)} %get-tuple-element.68) | copy-start | bytes 1966084
  33.7 2.3 %collective-permute-start.6 = (bf16[640,512]{1,0:T(8,128)(2,1)}, bf16[640,512]{1,0:T(8,128)(2,1)S(1)}, u32[]{:S(2)}, u32[]{:S(2)}) collective-permute-start(bf16[640,512]{1,0:T(8,128)(2,1)} %get-tuple-element.67), channel_id=1, source_target_pairs={{0,8},{8,0},{1,9},{9,1},{2,10},{10,2},{3,11},{11,3},{4,12},{12,4},... | collective-permute-start | bytes 1966088 | tf_op jit(solution)/shard_map/ppermute | solution.py:38
  33.9 4.3 %collective-permute-start.8 = (f32[16,640]{1,0:T(8,128)S(1)}, f32[16,640]{1,0:T(8,128)S(1)}, u32[]{:S(2)}, u32[]{:S(2)}) collective-permute-start(f32[16,640]{1,0:T(8,128)S(1)} %get-tuple-element.98), channel_id=1, source_target_pairs={{0,1},{1,0},{2,3},{3,2},{8,9},{9,8},{10,11},{11,10},{16,17},{17,16... | collective-permute-start | bytes 122888 | tf_op jit(solution)/shard_map/ppermute | solution.py:48
  34.0 4.2 %collective-permute-start.9 = (f32[16,640]{1,0:T(8,128)S(1)}, f32[16,640]{1,0:T(8,128)S(1)}, u32[]{:S(2)}, u32[]{:S(2)}) collective-permute-start(f32[16,640]{1,0:T(8,128)S(1)} %get-tuple-element.97), channel_id=1, source_target_pairs={{1,2},{3,8},{9,10},{11,16},{17,18},{19,24},{25,26},{27,32},{33,34}... | collective-permute-start | bytes 122888 | tf_op jit(solution)/shard_map/ppermute | solution.py:49
  38.2 6.5 %copy-start.12 = (bf16[640,512]{1,0:T(8,128)(2,1)S(1)}, bf16[640,512]{1,0:T(8,128)(2,1)}, u32[]{:S(2)}) copy-start(bf16[640,512]{1,0:T(8,128)(2,1)} %get-tuple-element.53) | copy-start | bytes 1966084
  41.9 9.4 %collective-permute-start.10 = (bf16[2,512,640]{2,1,0:T(8,128)(2,1)S(1)}, bf16[2,512,640]{2,1,0:T(8,128)(2,1)S(1)}, u32[]{:S(2)}, u32[]{:S(2)}) collective-permute-start(bf16[2,512,640]{2,1,0:T(8,128)(2,1)S(1)} %conv_backward.1.right), channel_id=1, source_target_pairs={{0,8},{8,0},{1,9},{9,1},{2,10},{10,2},{3,11},{11,3},{4,12},{12,4},... | collective-permute-start | bytes 3932168 | tf_op jit(solution)/shard_map/ppermute | solution.py:38
  44.7 6.6 %collective-permute-start.5 = (bf16[640,512]{1,0:T(8,128)(2,1)S(1)}, bf16[640,512]{1,0:T(8,128)(2,1)S(1)}, u32[]{:S(2)}, u32[]{:S(2)}) collective-permute-start(bf16[640,512]{1,0:T(8,128)(2,1)S(1)} %copy-done.12), channel_id=1, source_target_pairs={{0,8},{8,0},{1,9},{9,1},{2,10},{10,2},{3,11},{11,3},{4,12},{12,4},... | collective-permute-start | bytes 1966088 | tf_op jit(solution)/shard_map/ppermute | solution.py:38
  46.0 5.3 %copy-start.6 = (bf16[640,512]{1,0:T(8,128)(2,1)S(1)}, bf16[640,512]{1,0:T(8,128)(2,1)}, u32[]{:S(2)}) copy-start(bf16[640,512]{1,0:T(8,128)(2,1)} %get-tuple-element.61.left) | copy-start | bytes 1966084
  48.3 33.4 %collective-permute-start.15 = (bf16[512,1280]{1,0:T(8,128)(2,1)}, bf16[512,1280]{1,0:T(8,128)(2,1)}, u32[]{:S(2)}, u32[]{:S(2)}) collective-permute-start(bf16[512,1280]{1,0:T(8,128)(2,1)} %fusion.sent), channel_id=1, source_target_pairs={{0,4},{4,0},{1,5},{5,1},{2,6},{6,2},{3,7},{7,3},{8,12},{12,8},{9,1... | collective-permute-start | bytes 3932168 | tf_op jit(solution)/shard_map/ppermute | solution.py:38
  54.8 43.8 %all-to-all-start = ((bf16[16,40,1920]{2,1,0:T(8,128)(2,1)}), bf16[16,40,1920]{2,1,0:T(8,128)(2,1)}, u32[]{:S(2)}, u32[]{:S(2)}) async-start(bf16[16,40,1920]{2,1,0:T(8,128)(2,1)} %bitcast.48), calls=%async_computation | async-start | bytes 4915200 | tf_op jit(solution)/shard_map/all_to_all | solution.py:476
  69.1 1.4 %collective-permute-start.11 = (f32[34,640]{1,0:T(8,128)S(1)}, f32[34,640]{1,0:T(8,128)S(1)}, u32[]{:S(2)}, u32[]{:S(2)}) collective-permute-start(f32[34,640]{1,0:T(8,128)S(1)} %pad_maximum_fusion.1), channel_id=1, source_target_pairs={{0,8},{8,0},{1,9},{9,1},{2,10},{10,2},{3,11},{11,3},{4,12},{12,4},... | collective-permute-start | bytes 261128 | tf_op jit(solution)/shard_map/ppermute | solution.py:38
  70.5 16.4 %collective-permute-start.12 = (f32[34,640]{1,0:T(8,128)S(1)}, f32[34,640]{1,0:T(8,128)S(1)}, u32[]{:S(2)}, u32[]{:S(2)}) collective-permute-start(f32[34,640]{1,0:T(8,128)S(1)} %fusion.21), channel_id=1, source_target_pairs={{0,64},{64,0},{1,65},{65,1},{2,66},{66,2},{3,67},{67,3},{4,68},{68... | collective-permute-start | bytes 261128 | tf_op jit(solution)/shard_map/ppermute | solution.py:38
  70.6 16.2 %collective-permute-start.13 = (f32[2,640]{1,0:T(2,128)S(1)}, f32[2,640]{1,0:T(2,128)S(1)}, u32[]{:S(2)}, u32[]{:S(2)}) collective-permute-start(f32[2,640]{1,0:T(2,128)S(1)} %slice.96), channel_id=1, source_target_pairs={{0,4},{4,0},{1,5},{5,1},{2,6},{6,2},{3,7},{7,3},{8,12},{12,8},{9,1... | collective-permute-start | bytes 15368 | tf_op jit(solution)/shard_map/ppermute | solution.py:38
  72.2 14.7 %collective-permute-start.14 = (f32[2,640]{1,0:T(2,128)S(1)}, f32[2,640]{1,0:T(2,128)S(1)}, u32[]{:S(2)}, u32[]{:S(2)}) collective-permute-start(f32[2,640]{1,0:T(2,128)S(1)} %slice.96), channel_id=1, source_target_pairs={{0,68},{4,64},{64,4},{68,0},{1,69},{5,65},{65,5},{69,1},{2,70},{6,... | collective-permute-start | bytes 15368 | tf_op jit(solution)/shard_map/ppermute | solution.py:485
  86.9 13.7 %collective-permute-start.16 = (bf16[34,640]{1,0:T(8,128)(2,1)S(1)}, bf16[34,640]{1,0:T(8,128)(2,1)S(1)}, u32[]{:S(2)}, u32[]{:S(2)}) collective-permute-start(bf16[34,640]{1,0:T(8,128)(2,1)S(1)} %pad_maximum_fusion.2), channel_id=1, source_target_pairs={{0,16},{16,0},{32,48},{48,32},{1,17},{17,1},{33,49},{49,33},{2,18}... | collective-permute-start | bytes 130568 | tf_op jit(solution)/shard_map/ppermute | solution.py:409
  89.7 11.0 %collective-permute-start.17 = (bf16[34,640]{1,0:T(8,128)(2,1)S(1)}, bf16[34,640]{1,0:T(8,128)(2,1)S(1)}, u32[]{:S(2)}, u32[]{:S(2)}) collective-permute-start(bf16[34,640]{1,0:T(8,128)(2,1)S(1)} %pad_maximum_fusion.2), channel_id=1, source_target_pairs={{0,32},{16,48},{32,0},{48,16},{1,33},{17,49},{33,1},{49,17},{2,34}... | collective-permute-start | bytes 130568 | tf_op jit(solution)/shard_map/ppermute | solution.py:409
  92.6 8.1 %collective-permute-start.18 = (bf16[34,640]{1,0:T(8,128)(2,1)S(1)}, bf16[34,640]{1,0:T(8,128)(2,1)S(1)}, u32[]{:S(2)}, u32[]{:S(2)}) collective-permute-start(bf16[34,640]{1,0:T(8,128)(2,1)S(1)} %pad_maximum_fusion.2), channel_id=1, source_target_pairs={{0,48},{16,32},{32,16},{48,0},{1,49},{17,33},{33,17},{49,1},{2,50}... | collective-permute-start | bytes 130568 | tf_op jit(solution)/shard_map/ppermute | solution.py:409
  100.8 4.9 %collective-permute-start.20 = (bf16[34,640]{1,0:T(8,128)(2,1)S(1)}, bf16[34,640]{1,0:T(8,128)(2,1)S(1)}, u32[]{:S(2)}, u32[]{:S(2)}) collective-permute-start(bf16[34,640]{1,0:T(8,128)(2,1)S(1)} %add_convert_fusion), channel_id=1, source_target_pairs={{0,1},{1,0},{2,3},{3,2},{4,5},{5,4},{6,7},{7,6},{8,9},{9,8},{10,11... | collective-permute-start | bytes 130568 | tf_op jit(solution)/shard_map/ppermute | solution.py:409
  101.5 5.6 %collective-permute-start.21 = (bf16[34,640]{1,0:T(8,128)(2,1)S(1)}, bf16[34,640]{1,0:T(8,128)(2,1)S(1)}, u32[]{:S(2)}, u32[]{:S(2)}) collective-permute-start(bf16[34,640]{1,0:T(8,128)(2,1)S(1)} %add_convert_fusion), channel_id=1, source_target_pairs={{0,2},{1,3},{2,0},{3,1},{4,6},{5,7},{6,4},{7,5},{8,10},{9,11},{10,... | collective-permute-start | bytes 130568 | tf_op jit(solution)/shard_map/ppermute | solution.py:409
  104.0 5.3 %collective-permute-start.22 = (bf16[34,640]{1,0:T(8,128)(2,1)S(1)}, bf16[34,640]{1,0:T(8,128)(2,1)S(1)}, u32[]{:S(2)}, u32[]{:S(2)}) collective-permute-start(bf16[34,640]{1,0:T(8,128)(2,1)S(1)} %add_convert_fusion), channel_id=1, source_target_pairs={{0,3},{1,2},{2,1},{3,0},{4,7},{5,6},{6,5},{7,4},{8,11},{9,10},{10,... | collective-permute-start | bytes 130568 | tf_op jit(solution)/shard_map/ppermute | solution.py:409
  105.6 5.6 %collective-permute-start.19 = (f32[20,1920]{1,0:T(8,128)S(1)}, f32[20,1920]{1,0:T(8,128)S(1)}, u32[]{:S(2)}, u32[]{:S(2)}) collective-permute-start(f32[20,1920]{1,0:T(8,128)S(1)} %dynamic-slice_bitcast_fusion), channel_id=1, source_target_pairs={{0,64},{64,0},{1,65},{65,1},{2,66},{66,2},{3,67},{67,3},{4,68},{68... | collective-permute-start | bytes 460808 | tf_op jit(solution)/shard_map/ppermute | solution.py:38

commit v7 on v6

--- a/solution.py
+++ b/solution.py
@@ -228,11 +228,22 @@
     out[...] = (arrived[...].astype(F32).T + inv * back).astype(BF16)
 
 
-def pair_kernel(left, left_peer, right, right_peer, *buffers):
-    out = buffers[-1]
-    total = jnp.dot(left[...], right[...], preferred_element_type=F32)
-    total = total + jnp.dot(left_peer[...], right_peer[...], preferred_element_type=F32)
-    out[...] = total.astype(BF16)
+def pair_kernel(first, left, left_peer, right, right_peer, *refs):
+    out, held, sems = refs[-3:]
+    groups, _, width = right.shape
+    copies = []
+    for g in range(groups):
+        for at in range(0, width, 256):
+            columns = slice(at, min(at + 256, width))
+            total = jnp.dot(left[...], right[g, :, columns], preferred_element_type=F32)
+            total = total + jnp.dot(left_peer[...], right_peer[g, :, columns], preferred_element_type=F32)
+            made = pl.ds(g * width + at, columns.stop - at)
+            held[:, made] = total.astype(BF16)
+            there = pl.ds((first + g) * width + at, columns.stop - at)
+            copies.append(pltpu.make_async_copy(held.at[:, made], out.at[:, there], sems.at[len(copies)]))
+            copies[-1].start()
+    for copy in copies:
+        copy.wait()
 
 
 def hbm():
@@ -388,16 +399,14 @@
 
 
 def pair_product(left, left_peer, right, right_peer, groups, first, buffer=None):
-    rows, count = left.shape
+    rows = left.shape[0]
     made, _, width = right.shape
-    spec = pl.BlockSpec((None, count, width), lambda i: (i, 0, 0))
-    whole = pl.BlockSpec((rows, count), lambda i: (0, 0))
-    return pl.pallas_call(
-        pair_kernel,
-        grid=(made,),
-        in_specs=[whole, whole, spec, spec] + ([] if buffer is None else [hbm()]),
-        out_specs=pl.BlockSpec((rows, width), lambda i: (0, first + i)),
+    return pl.pallas_call(
+        functools.partial(pair_kernel, first),
+        in_specs=[vmem()] * 4 + ([] if buffer is None else [hbm()]),
+        out_specs=hbm(),
         out_shape=pltpu.HBM((rows, groups * width), BF16),
+        scratch_shapes=[pltpu.VMEM((rows, made * width), BF16), pltpu.SemaphoreType.DMA((3 * made,))],
         input_output_aliases={} if buffer is None else {4: 0},
         compiler_params=params(),
         cost_estimate=duration(3.4),
@@ -417,7 +426,7 @@
 def finish_rows(summed, xl):
     own = lax.dynamic_index_in_dim(summed, xl, 0, keepdims=False)
     other = lax.dynamic_index_in_dim(summed, 1 - xl, 0, keepdims=False)
-    return own + swap(other, "xl")
+    return own + swap(other.astype(BF16), "xl").astype(F32)
 
 
 def body(frames, returned, norm_gain, weight_in, kernel, weight_out, block_utt, block_fill):
@@ -466,10 +475,8 @@
         same, fill, ready, conv_inner, conv_outer, kernel, value_proj, gate_sigmoid
     )
     late_peer = swap(late, "core")
-    contract = (((1,), (1,)), ((), ()))
-    sent = lax.dot_general(late[0], weight_in[0], contract, preferred_element_type=F32)
-    sent = sent + lax.dot_general(late[1], weight_in[1], contract, preferred_element_type=F32)
-    sent = sent.astype(BF16)
+    contract = (((0, 2), (0, 2)), ((), ()))
+    sent = lax.dot_general(late, weight_in, contract, preferred_element_type=F32).astype(BF16)
     other = swap(sent, "tensor")
     late, sent = lax.optimization_barrier((late, sent))
     parts = pair_product(normed_own, normed_peer, late, late_peer, 3, 1, parts)
@@ -493,11 +500,13 @@
     total = jnp.sum(got.astype(F32), axis=0)
     total, shares = lax.optimization_barrier((total, shares))
     summed = finish_rows(total.reshape(2, 20, 3 * width), xl)
-    small = sum_of(shares_of(sum_of(shares).astype(BF16), "section"))
+    grad_out = summed[:, :width].T
+    grad_in = summed[:, width:].reshape(20, 2, width).transpose(1, 0, 2)
+    shares = shares_of(sum_of(shares).astype(BF16), "section")
+    grad_in, grad_out, shares = lax.optimization_barrier((grad_in, grad_out, shares))
+    small = sum_of(shares)
     grad_kernel = small[:TAPS]
     grad_gain = small[32:].reshape(features)
-    grad_out = summed[:, :width].T
-    grad_in = jnp.stack([summed[:, width : 2 * width], summed[:, 2 * width :]])
     return (grad_frames, grad_in, grad_out, grad_kernel, grad_gain)
 
 

time: 113 us -> 111 us (0.982)
  waiting for transfers between devices: 23.5 us -> 21.7 us
    ppermute x6, waiting for transfers between devices: 3.66 us -> 2.39 us  [shares_of(): lax.ppermute(value, axis, [(i, i ^ k) for i in range(4)])]
    dot_general x2 -> x1, matrix products: 3.5 us -> 2.95 us  [body(): lax.dot_general(late, weight_in, contract, preferred_element_type=F32)]
  transfers between devices with their start and end apart: 24 -> 24, of which waited for: 9 -> 8; matrix products, arithmetic and copies ran while one was open for 11% -> 11% of each run, Pallas kernels for 24% -> 24%
where the time goes in v7:
time: 111 us; the launch traced here: 110 us
  starting transfers between devices  41.8 us (38%)
  Pallas kernels  32 us (29%)
  waiting for transfers between devices  21.7 us (20%)
  matrix products  5.59 us (5%)
  other arithmetic  4.37 us (4%)
  local copies, waits for them, and re-layouts  3.29 us (3%)
    ppermute x6, starting transfers between devices, shares_of(): lax.ppermute(value, axis, [(i, i ^ k) for i in range(4)])  10.5 us
    ppermute x9, waiting for transfers between devices, swap(): return lax.ppermute(value, axis, [(0, 1), (1, 0)])  9.41 us
    all_to_all x1, starting transfers between devices, body(): got = lax.all_to_all(parts.reshape(16, 40, 3 * width), PLANE, 0, 0)  9.01 us
    ppermute x9, starting transfers between devices, swap(): return lax.ppermute(value, axis, [(0, 1), (1, 0)])  8.11 us
    ppermute x3, starting transfers between devices, body(): lax.ppermute(chunks[k], 'section', [(i, i ^ k) for i in range(4)])  7.63 us
    all_to_all x1, waiting for transfers between devices, body(): got = lax.all_to_all(parts.reshape(16, 40, 3 * width), PLANE, 0, 0)  5.75 us
    pallas_call x2, Pallas kernels, pair_product(): pl.pallas_call(functools.partial(pair_kernel, first), in_specs=[vmem()] *...  5.22 us
    pallas_call x1, Pallas kernels, norm_back(): pl.pallas_call(final_kernel, grid=(count // BLOCK,), in_specs=[block, blo...  5.13 us
  transfers between devices with their start and end apart: 24, of which 8 were waited for; matrix products, arithmetic and copies ran while one was open for 11% of the time, Pallas kernels for 24%

profile of v7, /device:TPU:0, one launch (start us, length us, event | category | flops | bytes accessed | tf_op | source)
XLA Modules:
  0.0 110.0 jit_solution(14918310385669400839)
XLA Ops:
  0.7 0.0 copy-start
  0.7 2.2 %frame_chunks.1 = (bf16[320,512]{1,0:T(8,128)(2,1)}, bf16[320,512]{1,0:T(8,128)(2,1)}, bf16[320,512]{1,0:T(8,128)(2,1)}, bf16[320,512]{1,0:T(8,128)(2,1)}) custom-call(s32[1]{0:T(128)} %bitcast.2.section, bf16[320,2048]{1,0:T(8,128)(2,1)} %bitcast.43), custom_call_target="tpu_custom_call" | custom-call | flops 2300000000 | tf_op jit(solution)/shard_map/frame_chunks/pallas_call | solution.py:331
  2.9 2.1 %collective-permute-start = (bf16[16,1280]{1,0:T(8,128)(2,1)S(1)}, bf16[16,1280]{1,0:T(8,128)(2,1)S(1)}, u32[]{:S(2)}, u32[]{:S(2)}) collective-permute-start(bf16[16,1280]{1,0:T(8,128)(2,1)S(1)} %get-tuple-element.102), channel_id=1, source_target_pairs={{0,1},{1,0},{2,3},{3,2},{8,9},{9,8},{10,11},{11,10},{16,17},{17,16... | collective-permute-start | bytes 122888 | tf_op jit(solution)/shard_map/ppermute | solution.py:48
  5.0 0.7 collective-permute-start.1
  5.7 4.9 %collective-permute-start.2 = (bf16[320,512]{1,0:T(8,128)(2,1)}, bf16[320,512]{1,0:T(8,128)(2,1)S(1)}, u32[]{:S(2)}, u32[]{:S(2)}) collective-permute-start(bf16[320,512]{1,0:T(8,128)(2,1)} %get-tuple-element.61), channel_id=1, source_target_pairs={{0,1},{1,0},{2,3},{3,2},{4,5},{5,4},{6,7},{7,6},{8,9},{9,8},{10,11... | collective-permute-start | bytes 983048 | tf_op jit(solution)/shard_map/ppermute | solution.py:443
  10.5 0.5 collective-permute-start.3
  11.0 2.3 %collective-permute-start.4 = (bf16[320,512]{1,0:T(8,128)(2,1)}, bf16[320,512]{1,0:T(8,128)(2,1)}, u32[]{:S(2)}, u32[]{:S(2)}) collective-permute-start(bf16[320,512]{1,0:T(8,128)(2,1)} %get-tuple-element.63), channel_id=1, source_target_pairs={{0,3},{1,2},{2,1},{3,0},{4,7},{5,6},{6,5},{7,4},{8,11},{9,10},{10,... | collective-permute-start | bytes 983048 | tf_op jit(solution)/shard_map/ppermute | solution.py:443
  13.3 0.1 pad_add_fusion
  13.4 0.1 dynamic_slice.14
  13.5 0.1 fusion.16
  13.5 0.1 dynamic_slice.13
  13.6 0.1 compare_convert_fusion
  13.7 0.1 pad_add_fusion.4.place
  13.8 0.1 pad_add_fusion.5.same
  13.9 0.1 slice.64.fill
  13.9 0.1 slice.65
  14.0 1.8 %layer_norm.1 = (bf16[544,1280]{1,0:T(8,128)(2,1)S(1)}, bf16[1280,512]{1,0:T(8,128)(2,1)S(1)}) custom-call(s32[3]{0:T(128)S(1)} %pad_add_fusion.4.place, bf16[512,1280]{1,0:T(8,128)(2,1)S(1)} %copy-done, bf16[16,1280]{1,0:T(8,128)(2,1)S(1)} %collective-permute-done.inner, bf16[16,1280]{1,0:T(8,128)(2,1)S(1)} %collective-permute-done.1.outer, ...), custom_call_target="tpu_custom_call" | custom-call | flops 4024999936 | tf_op jit(solution)/shard_map/layer_norm/pallas_call | solution.py:314
  15.8 0.1 copy-done.11
  15.9 1.4 %add_divide_fusion.gate = f32[544,640]{1,0:T(8,128)S(1)} fusion(bf16[544,1280]{1,0:T(8,128)(2,1)S(1)} %get-tuple-element.64, bf16[2,1280,640]{2,1,0:T(8,128)(2,1)S(1)} %copy-done.11), kind=kOutput, calls=%fused_computation.13 | convolution fusion | flops 892334080 | bytes 4423680 | tf_op jit(solution)/shard_map/dot_general | solution.py:456
  17.3 1.3 %select_convert_fusion = (bf16[544,640]{1,0:T(8,128)(2,1)S(1)}, f32[544,640]{1,0:T(8,128)S(1)}) fusion(f32[544,640]{1,0:T(8,128)S(1)} %add_divide_fusion.gate, pred[544]{0:T(1024)(128)(4,1)S(1)} %slice.65, bf16[544,1280]{1,0:T(8,128)(2,1)S(1)} %get-tuple-element.64, bf16[2,1280,640]{2,1,0:T(8,128)(2,1)S(1)} %copy-done.11), kind=kOutput, calls=%fused_computation.12 | convolution fusion | flops 892334080 | bytes 6513664 | tf_op jit(solution)/shard_map/dot_general | solution.py:455
  18.6 0.0 copy-start.4
  18.6 4.7 %conv_forward.1 = (bf16[512,640]{1,0:T(8,128)(2,1)}, f32[512,640]{1,0:T(8,128)}) custom-call(s32[6]{0:T(128)S(1)} %pad_add_fusion.5.same, s32[4]{0:T(128)S(1)} %slice.64.fill, bf16[544,640]{1,0:T(8,128)(2,1)S(1)} %get-tuple-element.103.units, f32[31,640]{1,0:T(8,128)S(1)} %copy-done.3), custom_call_target="tpu_custom_call" | custom-call | flops 5750000128 | tf_op jit(solution)/shard_map/conv_forward/pallas_call | solution.py:267
  23.3 0.3 collective-permute-start.7
  23.6 2.0 %core_halves.2 = (bf16[640,512]{1,0:T(8,128)(2,1)}, bf16[640,512]{1,0:T(8,128)(2,1)}) custom-call(s32[1]{0:T(128)} %bitcast.core, bf16[1280,512]{1,0:T(8,128)(2,1)S(1)} %get-tuple-element.57.rows, bf16[160,160]{1,0:T(8,128)(2,1)S(1)} %copy-done.4), custom_call_target="tpu_custom_call" | custom-call | flops 1380000000 | tf_op jit(solution)/shard_map/core_halves/pallas_call | solution.py:368
  25.6 0.4 collective-permute-done.3.second
  26.1 3.8 %collective-permute-done.4.third = bf16[320,512]{1,0:T(8,128)(2,1)} collective-permute-done((bf16[320,512]{1,0:T(8,128)(2,1)}, bf16[320,512]{1,0:T(8,128)(2,1)}, u32[]{:S(2)}, u32[]{:S(2)}) %collective-permute-start.4) | collective-permute-done | bytes 327712 | tf_op jit(solution)/shard_map/ppermute | solution.py:443
  29.9 2.6 %conv_gradient.1 = (bf16[1280,512]{1,0:T(8,128)(2,1)S(1)}, f32[512,640]{1,0:T(8,128)S(1)}) custom-call(s32[1]{0:T(128)} %bitcast.2.section, bf16[320,512]{1,0:T(8,128)(2,1)} %get-tuple-element.60.own, bf16[320,512]{1,0:T(8,128)(2,1)} %copy-done.13, bf16[320,512]{1,0:T(8,128)(2,1)} %copy-done.14, bf16[320,512]{1,0:T(8,128)(2,1)} %collective-permute-done.4.third, ...), custom_call_target="tpu_custom_call" | custom-call | flops 3449999872 | tf_op jit(solution)/shard_map/conv_gradient/pallas_call | solution.py:345
  32.4 1.2 %core_halves.3 = (bf16[640,512]{1,0:T(8,128)(2,1)S(1)}, bf16[640,512]{1,0:T(8,128)(2,1)}) custom-call(s32[1]{0:T(128)} %bitcast.core, bf16[1280,512]{1,0:T(8,128)(2,1)S(1)} %get-tuple-element.68.arrived, bf16[160,160]{1,0:T(8,128)(2,1)S(1)} %copy-done.4), custom_call_target="tpu_custom_call" | custom-call | flops 1380000000 | tf_op jit(solution)/shard_map/core_halves/pallas_call | solution.py:368
  33.6 0.1 copy-done.5
  33.8 0.1 collective-permute-start.6
  33.9 0.1 collective-permute-start.8
  34.0 0.7 collective-permute-start.9
  34.7 1.4 %collective-permute-done.6.left_peer = bf16[640,512]{1,0:T(8,128)(2,1)S(1)} collective-permute-done((bf16[640,512]{1,0:T(8,128)(2,1)}, bf16[640,512]{1,0:T(8,128)(2,1)S(1)}, u32[]{:S(2)}, u32[]{:S(2)}) %collective-permute-start.6) | collective-permute-done | bytes 655392 | tf_op jit(solution)/shard_map/ppermute | solution.py:38
  36.1 2.1 %weight_gradient.2.refs_0_ = bf16[640,1920]{1,0:T(8,128)(2,1)} custom-call(bf16[640,512]{1,0:T(8,128)(2,1)S(1)} %get-tuple-element.72.left, bf16[640,512]{1,0:T(8,128)(2,1)S(1)} %collective-permute-done.6.left_peer, bf16[1,512,640]{2,1,0:T(8,128)(2,1)S(1)} %bitcast.39, bf16[1,512,640]{2,1,0:T(8,128)(2,1)S(1)} %bitcast.40), custom_call_target="tpu_custom_call" | custom-call | flops 3910000128 | tf_op jit(solution)/shard_map/weight_gradient/pallas_call | solution.py:404
  38.2 3.7 %conv_backward.1.right = bf16[2,512,640]{2,1,0:T(8,128)(2,1)S(1)} custom-call(s32[6]{0:T(128)S(1)} %pad_add_fusion.5.same, s32[4]{0:T(128)S(1)} %slice.64.fill, f32[512,640]{1,0:T(8,128)S(1)} %get-tuple-element.69, f32[16,640]{1,0:T(8,128)S(1)} %collective-permute-done.8.inner, f32[16,640]{1,0:T(8,128)S(1)} %collective-permute-done.9.outer, ...), custom_call_target="tpu_custom_call" | custom-call | flops 6440000000 | tf_op jit(solution)/shard_map/conv_backward/pallas_call | solution.py:300
  41.9 2.8 %collective-permute-start.10 = (bf16[2,512,640]{2,1,0:T(8,128)(2,1)S(1)}, bf16[2,512,640]{2,1,0:T(8,128)(2,1)S(1)}, u32[]{:S(2)}, u32[]{:S(2)}) collective-permute-start(bf16[2,512,640]{2,1,0:T(8,128)(2,1)S(1)} %conv_backward.1.right), channel_id=1, source_target_pairs={{0,8},{8,0},{1,9},{9,1},{2,10},{10,2},{3,11},{11,3},{4,12},{12,4},... | collective-permute-start | bytes 3932168 | tf_op jit(solution)/shard_map/ppermute | solution.py:38
  44.7 0.1 collective-permute-start.5
  44.8 2.9 %fusion.sent = bf16[512,1280]{1,0:T(8,128)(2,1)} fusion(bf16[2,512,640]{2,1,0:T(8,128)(2,1)S(1)} %conv_backward.1.right, bf16[2,1280,640]{2,1,0:T(8,128)(2,1)S(1)} %copy-done.11), kind=kOutput, calls=%fused_computation.2 | convolution fusion | flops 1678376960 | bytes 5898240 | tf_op jit(solution)/shard_map/dot_general | solution.py:479
  47.8 3.0 %collective-permute-start.15 = (bf16[512,1280]{1,0:T(8,128)(2,1)}, bf16[512,1280]{1,0:T(8,128)(2,1)}, u32[]{:S(2)}, u32[]{:S(2)}) collective-permute-start(bf16[512,1280]{1,0:T(8,128)(2,1)} %fusion.sent), channel_id=1, source_target_pairs={{0,4},{4,0},{1,5},{5,1},{2,6},{6,2},{3,7},{7,3},{8,12},{12,8},{9,1... | collective-permute-start | bytes 3932168 | tf_op jit(solution)/shard_map/ppermute | solution.py:38
  50.8 3.1 %weight_gradient.3 = bf16[640,1920]{1,0:T(8,128)(2,1)} custom-call(bf16[640,512]{1,0:T(8,128)(2,1)S(1)} %copy-done.6, bf16[640,512]{1,0:T(8,128)(2,1)S(1)} %collective-permute-done.5.left_peer, bf16[2,512,640]{2,1,0:T(8,128)(2,1)S(1)} %conv_backward.1.right, ...), custom_call_target="tpu_custom_call", output_to_operand_aliasing={{}: (4, {})} | custom-call | flops 3910000128 | tf_op jit(solution)/shard_map/weight_gradient/pallas_call | solution.py:404
  53.9 9.0 %all-to-all-start = ((bf16[16,40,1920]{2,1,0:T(8,128)(2,1)}), bf16[16,40,1920]{2,1,0:T(8,128)(2,1)}, u32[]{:S(2)}, u32[]{:S(2)}) async-start(bf16[16,40,1920]{2,1,0:T(8,128)(2,1)} %bitcast.41), calls=%async_computation | async-start | bytes 4915200 | tf_op jit(solution)/shard_map/all_to_all | solution.py:483
  62.9 3.6 %tap_gradients.1 = f32[32,640]{1,0:T(8,128)S(1)} custom-call(s32[6]{0:T(128)S(1)} %pad_add_fusion.5.same, bf16[544,640]{1,0:T(8,128)(2,1)S(1)} %get-tuple-element.103.units, f32[512,640]{1,0:T(8,128)S(1)} %get-tuple-element.69), custom_call_target="tpu_custom_call" | custom-call | flops 4600000000 | tf_op jit(solution)/shard_map/tap_gradients/pallas_call | solution.py:286
  66.5 1.7 %multiply_reduce_fusion = f32[1280]{0:T(1024)S(1)} fusion(bf16[512,1280]{1,0:T(8,128)(2,1)} %fusion.sent, bf16[544,1280]{1,0:T(8,128)(2,1)S(1)} %get-tuple-element.64), kind=kLoop, calls=%fused_computation.3 | loop fusion | flops 2620160 | bytes 2626560 | tf_op jit(solution)/shard_map/reduce_sum | solution.py:488
  68.3 0.1 collective-permute-start.11
  68.4 1.3 %collective-permute-done.11 = f32[34,640]{1,0:T(8,128)S(1)} collective-permute-done((f32[34,640]{1,0:T(8,128)S(1)}, f32[34,640]{1,0:T(8,128)S(1)}, u32[]{:S(2)}, u32[]{:S(2)}) %collective-permute-start.11) | collective-permute-done | bytes 87072 | tf_op jit(solution)/shard_map/ppermute | solution.py:38
  69.7 0.1 collective-permute-start.12
  69.8 1.6 %collective-permute-start.13 = (f32[2,640]{1,0:T(2,128)S(1)}, f32[2,640]{1,0:T(2,128)S(1)}, u32[]{:S(2)}, u32[]{:S(2)}) collective-permute-start(f32[2,640]{1,0:T(2,128)S(1)} %slice.80), channel_id=1, source_target_pairs={{0,4},{4,0},{1,5},{5,1},{2,6},{6,2},{3,7},{7,3},{8,12},{12,8},{9,1... | collective-permute-start | bytes 15368 | tf_op jit(solution)/shard_map/ppermute | solution.py:38
  71.4 3.1 %collective-permute-start.14 = (f32[2,640]{1,0:T(2,128)S(1)}, f32[2,640]{1,0:T(2,128)S(1)}, u32[]{:S(2)}, u32[]{:S(2)}) collective-permute-start(f32[2,640]{1,0:T(2,128)S(1)} %slice.80), channel_id=1, source_target_pairs={{0,68},{4,64},{64,4},{68,0},{1,69},{5,65},{65,5},{69,1},{2,70},{6,... | collective-permute-start | bytes 15368 | tf_op jit(solution)/shard_map/ppermute | solution.py:492
  74.5 6.7 %collective-permute-done.15.other = bf16[512,1280]{1,0:T(8,128)(2,1)} collective-permute-done((bf16[512,1280]{1,0:T(8,128)(2,1)}, bf16[512,1280]{1,0:T(8,128)(2,1)}, u32[]{:S(2)}, u32[]{:S(2)}) %collective-permute-start.15) | collective-permute-done | bytes 1310752 | tf_op jit(solution)/shard_map/ppermute | solution.py:38
  81.2 5.1 %norm_backward.1 = bf16[512,1280]{1,0:T(8,128)(2,1)} custom-call(bf16[512,1280]{1,0:T(8,128)(2,1)} %fusion.sent, bf16[512,1280]{1,0:T(8,128)(2,1)} %collective-permute-done.15.other, bf16[512,1280]{1,0:T(8,128)(2,1)} %frames.1, bf16[1280,512]{1,0:T(8,128)(2,1)} %copy-done.5, f32[1,1280]{1,0:T(1,128)S(1)} %reshape.44.gain), custom_call_target="tpu_custom_call" | custom-call | flops 11960000512 | tf_op jit(solution)/shard_map/norm_backward/pallas_call | solution.py:383
  86.4 2.7 %collective-permute-start.16 = (bf16[34,640]{1,0:T(8,128)(2,1)S(1)}, bf16[34,640]{1,0:T(8,128)(2,1)S(1)}, u32[]{:S(2)}, u32[]{:S(2)}) collective-permute-start(bf16[34,640]{1,0:T(8,128)(2,1)S(1)} %pad_maximum_fusion.1), channel_id=1, source_target_pairs={{0,16},{16,0},{32,48},{48,32},{1,17},{17,1},{33,49},{49,33},{2,18}... | collective-permute-start | bytes 130568 | tf_op jit(solution)/shard_map/ppermute | solution.py:418
  89.1 3.0 %collective-permute-start.17 = (bf16[34,640]{1,0:T(8,128)(2,1)S(1)}, bf16[34,640]{1,0:T(8,128)(2,1)S(1)}, u32[]{:S(2)}, u32[]{:S(2)}) collective-permute-start(bf16[34,640]{1,0:T(8,128)(2,1)S(1)} %pad_maximum_fusion.1), channel_id=1, source_target_pairs={{0,32},{16,48},{32,0},{48,16},{1,33},{17,49},{33,1},{49,17},{2,34}... | collective-permute-start | bytes 130568 | tf_op jit(solution)/shard_map/ppermute | solution.py:418
  92.1 5.7 %all-to-all-done = bf16[16,40,1920]{2,1,0:T(8,128)(2,1)} async-done(((bf16[16,40,1920]{2,1,0:T(8,128)(2,1)}), bf16[16,40,1920]{2,1,0:T(8,128)(2,1)}, u32[]{:S(2)}, u32[]{:S(2)}) %all-to-all-start) | async-done | bytes 2457632 | tf_op jit(solution)/shard_map/all_to_all | solution.py:483
  97.8 2.1 %convert_reduce_fusion = f32[40,1920]{1,0:T(8,128)S(1)} fusion(bf16[16,40,1920]{2,1,0:T(8,128)(2,1)} %all-to-all-done), kind=kLoop, calls=%fused_computation | loop fusion | flops 2380800 | bytes 2764800 | tf_op jit(solution)/shard_map/reduce_sum | solution.py:500
  100.0 0.1 collective-permute-start.19
  100.2 0.7 collective-permute-start.20
  100.8 2.5 %collective-permute-start.21 = (bf16[34,640]{1,0:T(8,128)(2,1)S(1)}, bf16[34,640]{1,0:T(8,128)(2,1)S(1)}, u32[]{:S(2)}, u32[]{:S(2)}) collective-permute-start(bf16[34,640]{1,0:T(8,128)(2,1)S(1)} %add_convert_fusion), channel_id=1, source_target_pairs={{0,2},{1,3},{2,0},{3,1},{4,6},{5,7},{6,4},{7,5},{8,10},{9,11},{10,... | collective-permute-start | bytes 130568 | tf_op jit(solution)/shard_map/ppermute | solution.py:418
  103.4 1.6 %collective-permute-start.22 = (bf16[34,640]{1,0:T(8,128)(2,1)S(1)}, bf16[34,640]{1,0:T(8,128)(2,1)S(1)}, u32[]{:S(2)}, u32[]{:S(2)}) collective-permute-start(bf16[34,640]{1,0:T(8,128)(2,1)S(1)} %add_convert_fusion), channel_id=1, source_target_pairs={{0,3},{1,2},{2,1},{3,0},{4,7},{5,6},{6,5},{7,4},{8,11},{9,10},{10,... | collective-permute-start | bytes 130568 | tf_op jit(solution)/shard_map/ppermute | solution.py:418
  105.0 0.6 slice_bitcast_fusion
  105.6 0.7 reshape.48
  106.3 0.2 collective-permute-done.21
  106.5 2.2 %collective-permute-done.22 = bf16[34,640]{1,0:T(8,128)(2,1)S(1)} collective-permute-done((bf16[34,640]{1,0:T(8,128)(2,1)S(1)}, bf16[34,640]{1,0:T(8,128)(2,1)S(1)}, u32[]{:S(2)}, u32[]{:S(2)}) %collective-permute-start.22) | collective-permute-done | bytes 43552 | tf_op jit(solution)/shard_map/ppermute | solution.py:418
  108.7 0.6 slice.83
  109.4 0.6 reshape.49
  (61 shorter events, 0.4 us)
Async XLA Ops:
  0.7 2.3 %copy-start = (bf16[512,1280]{1,0:T(8,128)(2,1)S(1)}, bf16[512,1280]{1,0:T(8,128)(2,1)}, u32[]{:S(2)}) copy-start(bf16[512,1280]{1,0:T(8,128)(2,1)} %frames.1) | copy-start | bytes 3932164
  0.7 12.6 %copy-start.9 = (s32[256]{0:T(256)S(1)}, s32[256]{0:T(256)}, u32[]{:S(2)}) copy-start(s32[256]{0:T(256)} %param.17) | copy-start | bytes 3076
  0.7 12.6 %copy-start.10 = (s32[256]{0:T(256)S(1)}, s32[256]{0:T(256)}, u32[]{:S(2)}) copy-start(s32[256]{0:T(256)} %param.16) | copy-start | bytes 3076
  0.7 13.2 %copy-start.8 = (f32[1280]{0:T(1024)S(1)}, f32[1280]{0:T(1024)}, u32[]{:S(2)}) copy-start(f32[1280]{0:T(1024)} %param.12) | copy-start | bytes 15364
  2.9 11.1 %collective-permute-start = (bf16[16,1280]{1,0:T(8,128)(2,1)S(1)}, bf16[16,1280]{1,0:T(8,128)(2,1)S(1)}, u32[]{:S(2)}, u32[]{:S(2)}) collective-permute-start(bf16[16,1280]{1,0:T(8,128)(2,1)S(1)} %get-tuple-element.102), channel_id=1, source_target_pairs={{0,1},{1,0},{2,3},{3,2},{8,9},{9,8},{10,11},{11,10},{16,17},{17,16... | collective-permute-start | bytes 122888 | tf_op jit(solution)/shard_map/ppermute | solution.py:48
  5.0 9.0 %collective-permute-start.1 = (bf16[16,1280]{1,0:T(8,128)(2,1)S(1)}, bf16[16,1280]{1,0:T(8,128)(2,1)S(1)}, u32[]{:S(2)}, u32[]{:S(2)}) collective-permute-start(bf16[16,1280]{1,0:T(8,128)(2,1)S(1)} %get-tuple-element.101), channel_id=1, source_target_pairs={{1,2},{3,8},{9,10},{11,16},{17,18},{19,24},{25,26},{27,32},{33,34}... | collective-permute-start | bytes 122888 | tf_op jit(solution)/shard_map/ppermute | solution.py:49
  5.7 19.9 %collective-permute-start.2 = (bf16[320,512]{1,0:T(8,128)(2,1)}, bf16[320,512]{1,0:T(8,128)(2,1)S(1)}, u32[]{:S(2)}, u32[]{:S(2)}) collective-permute-start(bf16[320,512]{1,0:T(8,128)(2,1)} %get-tuple-element.61), channel_id=1, source_target_pairs={{0,1},{1,0},{2,3},{3,2},{4,5},{5,4},{6,7},{7,6},{8,9},{9,8},{10,11... | collective-permute-start | bytes 983048 | tf_op jit(solution)/shard_map/ppermute | solution.py:443
  10.5 15.5 %collective-permute-start.3 = (bf16[320,512]{1,0:T(8,128)(2,1)}, bf16[320,512]{1,0:T(8,128)(2,1)S(1)}, u32[]{:S(2)}, u32[]{:S(2)}) collective-permute-start(bf16[320,512]{1,0:T(8,128)(2,1)} %get-tuple-element.62), channel_id=1, source_target_pairs={{0,2},{1,3},{2,0},{3,1},{4,6},{5,7},{6,4},{7,5},{8,10},{9,11},{10,... | collective-permute-start | bytes 983048 | tf_op jit(solution)/shard_map/ppermute | solution.py:443
  11.0 18.8 %collective-permute-start.4 = (bf16[320,512]{1,0:T(8,128)(2,1)}, bf16[320,512]{1,0:T(8,128)(2,1)}, u32[]{:S(2)}, u32[]{:S(2)}) collective-permute-start(bf16[320,512]{1,0:T(8,128)(2,1)} %get-tuple-element.63), channel_id=1, source_target_pairs={{0,3},{1,2},{2,1},{3,0},{4,7},{5,6},{6,5},{7,4},{8,11},{9,10},{10,... | collective-permute-start | bytes 983048 | tf_op jit(solution)/shard_map/ppermute | solution.py:443
  14.0 1.9 %copy-start.11 = (bf16[2,1280,640]{2,1,0:T(8,128)(2,1)S(1)}, bf16[2,1280,640]{2,1,0:T(8,128)(2,1)}, u32[]{:S(2)}) copy-start(bf16[2,1280,640]{2,1,0:T(8,128)(2,1)} %param.13) | copy-start | bytes 9830404
  17.3 1.3 %copy-start.3 = (f32[31,640]{1,0:T(8,128)S(1)}, f32[31,640]{1,0:T(8,128)}, u32[]{:S(2)}) copy-start(f32[31,640]{1,0:T(8,128)} %taps.3) | copy-start | bytes 238084
  18.6 4.9 %copy-start.4 = (bf16[160,160]{1,0:T(8,128)(2,1)S(1)}, bf16[160,160]{1,0:T(8,128)(2,1)}, u32[]{:S(2)}) copy-start(bf16[160,160]{1,0:T(8,128)(2,1)} %constant.73.clone.order) | copy-start | bytes 153604
  23.3 11.4 %collective-permute-start.7 = (bf16[512,640]{1,0:T(8,128)(2,1)}, bf16[512,640]{1,0:T(8,128)(2,1)S(1)}, u32[]{:S(2)}, u32[]{:S(2)}) collective-permute-start(bf16[512,640]{1,0:T(8,128)(2,1)} %get-tuple-element.74), channel_id=1, source_target_pairs={{0,8},{8,0},{1,9},{9,1},{2,10},{10,2},{3,11},{11,3},{4,12},{12,4},... | collective-permute-start | bytes 1966088 | tf_op jit(solution)/shard_map/ppermute | solution.py:38
  23.6 6.3 %copy-start.1 = (bf16[640,1280]{1,0:T(8,128)(2,1)S(1)}, bf16[640,1280]{1,0:T(8,128)(2,1)}, u32[]{:S(2)}) copy-start(bf16[640,1280]{1,0:T(8,128)(2,1)} %weights.1) | copy-start | bytes 4915204
  23.6 6.3 %copy-start.7 = (f32[512,640]{1,0:T(8,128)S(1)}, f32[512,640]{1,0:T(8,128)}, u32[]{:S(2)}) copy-start(f32[512,640]{1,0:T(8,128)} %get-tuple-element.65.slope) | copy-start | bytes 3932164
  25.6 4.2 %copy-start.13 = (bf16[320,512]{1,0:T(8,128)(2,1)}, bf16[320,512]{1,0:T(8,128)(2,1)S(1)}, u32[]{:S(2)}) copy-start(bf16[320,512]{1,0:T(8,128)(2,1)S(1)} %collective-permute-done.2.first) | copy-start | bytes 983044
  26.1 3.8 %copy-start.14 = (bf16[320,512]{1,0:T(8,128)(2,1)}, bf16[320,512]{1,0:T(8,128)(2,1)S(1)}, u32[]{:S(2)}) copy-start(bf16[320,512]{1,0:T(8,128)(2,1)S(1)} %collective-permute-done.3.second) | copy-start | bytes 983044
  32.4 1.3 %copy-start.5 = (bf16[1280,512]{1,0:T(8,128)(2,1)}, bf16[1280,512]{1,0:T(8,128)(2,1)S(1)}, u32[]{:S(2)}) copy-start(bf16[1280,512]{1,0:T(8,128)(2,1)S(1)} %get-tuple-element.68.arrived) | copy-start | bytes 3932164
  32.4 3.6 %copy-start.2 = (bf16[512,640]{1,0:T(8,128)(2,1)S(1)}, bf16[512,640]{1,0:T(8,128)(2,1)}, u32[]{:S(2)}) copy-start(bf16[512,640]{1,0:T(8,128)(2,1)} %get-tuple-element.74) | copy-start | bytes 1966084
  33.8 2.3 %collective-permute-start.6 = (bf16[640,512]{1,0:T(8,128)(2,1)}, bf16[640,512]{1,0:T(8,128)(2,1)S(1)}, u32[]{:S(2)}, u32[]{:S(2)}) collective-permute-start(bf16[640,512]{1,0:T(8,128)(2,1)} %get-tuple-element.73), channel_id=1, source_target_pairs={{0,8},{8,0},{1,9},{9,1},{2,10},{10,2},{3,11},{11,3},{4,12},{12,4},... | collective-permute-start | bytes 1966088 | tf_op jit(solution)/shard_map/ppermute | solution.py:38
  33.9 4.3 %collective-permute-start.8 = (f32[16,640]{1,0:T(8,128)S(1)}, f32[16,640]{1,0:T(8,128)S(1)}, u32[]{:S(2)}, u32[]{:S(2)}) collective-permute-start(f32[16,640]{1,0:T(8,128)S(1)} %get-tuple-element.100), channel_id=1, source_target_pairs={{0,1},{1,0},{2,3},{3,2},{8,9},{9,8},{10,11},{11,10},{16,17},{17,16... | collective-permute-start | bytes 122888 | tf_op jit(solution)/shard_map/ppermute | solution.py:48
  34.0 4.2 %collective-permute-start.9 = (f32[16,640]{1,0:T(8,128)S(1)}, f32[16,640]{1,0:T(8,128)S(1)}, u32[]{:S(2)}, u32[]{:S(2)}) collective-permute-start(f32[16,640]{1,0:T(8,128)S(1)} %get-tuple-element.99), channel_id=1, source_target_pairs={{1,2},{3,8},{9,10},{11,16},{17,18},{19,24},{25,26},{27,32},{33,34}... | collective-permute-start | bytes 122888 | tf_op jit(solution)/shard_map/ppermute | solution.py:49
  38.2 6.5 %copy-start.12 = (bf16[640,512]{1,0:T(8,128)(2,1)S(1)}, bf16[640,512]{1,0:T(8,128)(2,1)}, u32[]{:S(2)}) copy-start(bf16[640,512]{1,0:T(8,128)(2,1)} %get-tuple-element.59) | copy-start | bytes 1966084
  41.9 8.9 %copy-start.6 = (bf16[640,512]{1,0:T(8,128)(2,1)S(1)}, bf16[640,512]{1,0:T(8,128)(2,1)}, u32[]{:S(2)}) copy-start(bf16[640,512]{1,0:T(8,128)(2,1)} %get-tuple-element.67.left) | copy-start | bytes 1966084
  41.9 8.9 %collective-permute-start.10 = (bf16[2,512,640]{2,1,0:T(8,128)(2,1)S(1)}, bf16[2,512,640]{2,1,0:T(8,128)(2,1)S(1)}, u32[]{:S(2)}, u32[]{:S(2)}) collective-permute-start(bf16[2,512,640]{2,1,0:T(8,128)(2,1)S(1)} %conv_backward.1.right), channel_id=1, source_target_pairs={{0,8},{8,0},{1,9},{9,1},{2,10},{10,2},{3,11},{11,3},{4,12},{12,4},... | collective-permute-start | bytes 3932168 | tf_op jit(solution)/shard_map/ppermute | solution.py:38
  44.7 6.1 %collective-permute-start.5 = (bf16[640,512]{1,0:T(8,128)(2,1)S(1)}, bf16[640,512]{1,0:T(8,128)(2,1)S(1)}, u32[]{:S(2)}, u32[]{:S(2)}) collective-permute-start(bf16[640,512]{1,0:T(8,128)(2,1)S(1)} %copy-done.12), channel_id=1, source_target_pairs={{0,8},{8,0},{1,9},{9,1},{2,10},{10,2},{3,11},{11,3},{4,12},{12,4},... | collective-permute-start | bytes 1966088 | tf_op jit(solution)/shard_map/ppermute | solution.py:38
  47.8 33.4 %collective-permute-start.15 = (bf16[512,1280]{1,0:T(8,128)(2,1)}, bf16[512,1280]{1,0:T(8,128)(2,1)}, u32[]{:S(2)}, u32[]{:S(2)}) collective-permute-start(bf16[512,1280]{1,0:T(8,128)(2,1)} %fusion.sent), channel_id=1, source_target_pairs={{0,4},{4,0},{1,5},{5,1},{2,6},{6,2},{3,7},{7,3},{8,12},{12,8},{9,1... | collective-permute-start | bytes 3932168 | tf_op jit(solution)/shard_map/ppermute | solution.py:38
  53.9 43.9 %all-to-all-start = ((bf16[16,40,1920]{2,1,0:T(8,128)(2,1)}), bf16[16,40,1920]{2,1,0:T(8,128)(2,1)}, u32[]{:S(2)}, u32[]{:S(2)}) async-start(bf16[16,40,1920]{2,1,0:T(8,128)(2,1)} %bitcast.41), calls=%async_computation | async-start | bytes 4915200 | tf_op jit(solution)/shard_map/all_to_all | solution.py:483
  68.3 1.4 %collective-permute-start.11 = (f32[34,640]{1,0:T(8,128)S(1)}, f32[34,640]{1,0:T(8,128)S(1)}, u32[]{:S(2)}, u32[]{:S(2)}) collective-permute-start(f32[34,640]{1,0:T(8,128)S(1)} %pad_maximum_fusion), channel_id=1, source_target_pairs={{0,8},{8,0},{1,9},{9,1},{2,10},{10,2},{3,11},{11,3},{4,12},{12,4},... | collective-permute-start | bytes 261128 | tf_op jit(solution)/shard_map/ppermute | solution.py:38
  69.7 16.6 %collective-permute-start.12 = (f32[34,640]{1,0:T(8,128)S(1)}, f32[34,640]{1,0:T(8,128)S(1)}, u32[]{:S(2)}, u32[]{:S(2)}) collective-permute-start(f32[34,640]{1,0:T(8,128)S(1)} %fusion.17), channel_id=1, source_target_pairs={{0,64},{64,0},{1,65},{65,1},{2,66},{66,2},{3,67},{67,3},{4,68},{68... | collective-permute-start | bytes 261128 | tf_op jit(solution)/shard_map/ppermute | solution.py:38
  69.8 16.5 %collective-permute-start.13 = (f32[2,640]{1,0:T(2,128)S(1)}, f32[2,640]{1,0:T(2,128)S(1)}, u32[]{:S(2)}, u32[]{:S(2)}) collective-permute-start(f32[2,640]{1,0:T(2,128)S(1)} %slice.80), channel_id=1, source_target_pairs={{0,4},{4,0},{1,5},{5,1},{2,6},{6,2},{3,7},{7,3},{8,12},{12,8},{9,1... | collective-permute-start | bytes 15368 | tf_op jit(solution)/shard_map/ppermute | solution.py:38
  71.4 15.0 %collective-permute-start.14 = (f32[2,640]{1,0:T(2,128)S(1)}, f32[2,640]{1,0:T(2,128)S(1)}, u32[]{:S(2)}, u32[]{:S(2)}) collective-permute-start(f32[2,640]{1,0:T(2,128)S(1)} %slice.80), channel_id=1, source_target_pairs={{0,68},{4,64},{64,4},{68,0},{1,69},{5,65},{65,5},{69,1},{2,70},{6,... | collective-permute-start | bytes 15368 | tf_op jit(solution)/shard_map/ppermute | solution.py:492
  86.4 13.5 %collective-permute-start.16 = (bf16[34,640]{1,0:T(8,128)(2,1)S(1)}, bf16[34,640]{1,0:T(8,128)(2,1)S(1)}, u32[]{:S(2)}, u32[]{:S(2)}) collective-permute-start(bf16[34,640]{1,0:T(8,128)(2,1)S(1)} %pad_maximum_fusion.1), channel_id=1, source_target_pairs={{0,16},{16,0},{32,48},{48,32},{1,17},{17,1},{33,49},{49,33},{2,18}... | collective-permute-start | bytes 130568 | tf_op jit(solution)/shard_map/ppermute | solution.py:418
  89.1 10.8 %collective-permute-start.17 = (bf16[34,640]{1,0:T(8,128)(2,1)S(1)}, bf16[34,640]{1,0:T(8,128)(2,1)S(1)}, u32[]{:S(2)}, u32[]{:S(2)}) collective-permute-start(bf16[34,640]{1,0:T(8,128)(2,1)S(1)} %pad_maximum_fusion.1), channel_id=1, source_target_pairs={{0,32},{16,48},{32,0},{48,16},{1,33},{17,49},{33,1},{49,17},{2,34}... | collective-permute-start | bytes 130568 | tf_op jit(solution)/shard_map/ppermute | solution.py:418
  92.1 7.9 %collective-permute-start.18 = (bf16[34,640]{1,0:T(8,128)(2,1)S(1)}, bf16[34,640]{1,0:T(8,128)(2,1)S(1)}, u32[]{:S(2)}, u32[]{:S(2)}) collective-permute-start(bf16[34,640]{1,0:T(8,128)(2,1)S(1)} %pad_maximum_fusion.1), channel_id=1, source_target_pairs={{0,48},{16,32},{32,16},{48,0},{1,49},{17,33},{33,17},{49,1},{2,50}... | collective-permute-start | bytes 130568 | tf_op jit(solution)/shard_map/ppermute | solution.py:418
  100.0 4.9 %collective-permute-start.19 = (bf16[20,1920]{1,0:T(8,128)(2,1)S(1)}, bf16[20,1920]{1,0:T(8,128)(2,1)S(1)}, u32[]{:S(2)}, u32[]{:S(2)}) collective-permute-start(bf16[20,1920]{1,0:T(8,128)(2,1)S(1)} %fusion.15), channel_id=1, source_target_pairs={{0,64},{64,0},{1,65},{65,1},{2,66},{66,2},{3,67},{67,3},{4,68},{68... | collective-permute-start | bytes 230408 | tf_op jit(solution)/shard_map/ppermute | solution.py:38
  100.2 6.2 %collective-permute-start.20 = (bf16[34,640]{1,0:T(8,128)(2,1)S(1)}, bf16[34,640]{1,0:T(8,128)(2,1)S(1)}, u32[]{:S(2)}, u32[]{:S(2)}) collective-permute-start(bf16[34,640]{1,0:T(8,128)(2,1)S(1)} %add_convert_fusion), channel_id=1, source_target_pairs={{0,1},{1,0},{2,3},{3,2},{4,5},{5,4},{6,7},{7,6},{8,9},{9,8},{10,11... | collective-permute-start | bytes 130568 | tf_op jit(solution)/shard_map/ppermute | solution.py:418
  100.8 5.6 %collective-permute-start.21 = (bf16[34,640]{1,0:T(8,128)(2,1)S(1)}, bf16[34,640]{1,0:T(8,128)(2,1)S(1)}, u32[]{:S(2)}, u32[]{:S(2)}) collective-permute-start(bf16[34,640]{1,0:T(8,128)(2,1)S(1)} %add_convert_fusion), channel_id=1, source_target_pairs={{0,2},{1,3},{2,0},{3,1},{4,6},{5,7},{6,4},{7,5},{8,10},{9,11},{10,... | collective-permute-start | bytes 130568 | tf_op jit(solution)/shard_map/ppermute | solution.py:418
  103.4 5.3 %collective-permute-start.22 = (bf16[34,640]{1,0:T(8,128)(2,1)S(1)}, bf16[34,640]{1,0:T(8,128)(2,1)S(1)}, u32[]{:S(2)}, u32[]{:S(2)}) collective-permute-start(bf16[34,640]{1,0:T(8,128)(2,1)S(1)} %add_convert_fusion), channel_id=1, source_target_pairs={{0,3},{1,2},{2,1},{3,0},{4,7},{5,6},{6,5},{7,4},{8,11},{9,10},{10,... | collective-permute-start | bytes 130568 | tf_op jit(solution)/shard_map/ppermute | solution.py:418

commit v8 on v7

--- a/solution.py
+++ b/solution.py
@@ -173,25 +173,26 @@
 
 
 def chunks_kernel(section, rows, *refs):
-    outs, held, sems = refs[:4], refs[4], refs[5]
+    outs, held, sems = refs[:3], refs[3], refs[4]
     count = held.shape[2]
     loads, stores = [], []
-    for k, out in enumerate(outs):
-        first = pl.multiple_of((section[0] ^ k) * count, count)
-        loads.append(pltpu.make_async_copy(rows.at[:, pl.ds(first, count)], held.at[k], sems.at[0, k]))
-        stores.append(pltpu.make_async_copy(held.at[k], out, sems.at[1, k]))
-    for load in loads[1:] + loads[:1]:
+    for i, out in enumerate(outs):
+        first = pl.multiple_of((section[0] ^ (i + 1)) * count, count)
+        loads.append(pltpu.make_async_copy(rows.at[:, pl.ds(first, count)], held.at[i], sems.at[0, i]))
+        stores.append(pltpu.make_async_copy(held.at[i], out, sems.at[1, i]))
+    for load in loads:
         load.start()
-    for k in (1, 2, 3, 0):
-        loads[k].wait()
-        stores[k].start()
+    for load, store in zip(loads, stores):
+        load.wait()
+        store.start()
     for store in stores:
         store.wait()
 
 
 def gradient_kernel(section, own, first, second, third, weights, slope, arrived, out, sems):
-    pieces = own, first, second, third
-    rows = own.shape[0]
+    rows, count = first.shape
+    here = pl.multiple_of(section[0] * count, count)
+    pieces = own.at[:, pl.ds(here, count)], first, second, third
     copies = []
     for k, piece in enumerate(pieces):
         at = pl.multiple_of((section[0] ^ k) * rows, 64)
@@ -331,9 +332,9 @@
     return pl.pallas_call(
         chunks_kernel,
         in_specs=[smem(), hbm()],
-        out_specs=[hbm()] * 4,
-        out_shape=[pltpu.HBM((features, count), rows.dtype)] * 4,
-        scratch_shapes=[pltpu.VMEM((4, features, count), rows.dtype), pltpu.SemaphoreType.DMA((2, 4))],
+        out_specs=[hbm()] * 3,
+        out_shape=[pltpu.HBM((features, count), rows.dtype)] * 3,
+        scratch_shapes=[pltpu.VMEM((3, features, count), rows.dtype), pltpu.SemaphoreType.DMA((2, 3))],
         compiler_params=params(),
         cost_estimate=duration(2),
         name="frame_chunks",
@@ -341,7 +342,7 @@
 
 
 def conv_gradient(section, pieces, weights, slope):
-    features, count = 4 * pieces[0].shape[0], pieces[0].shape[1]
+    features, count = 4 * pieces[1].shape[0], pieces[1].shape[1]
     return pl.pallas_call(
         gradient_kernel,
         in_specs=[smem()] + [hbm()] * 4 + [vmem()] * 2,
@@ -439,8 +440,9 @@
     place = jnp.stack([core, lax.axis_index("y"), lax.axis_index("section")]).astype(jnp.int32)
     section = lax.axis_index("section").reshape(1)
     *chunks, frames = lax.optimization_barrier((*frame_chunks(section, returned.T), frames))
-    for k in (1, 3, 2):
-        chunks[k] = lax.ppermute(chunks[k], "section", [(i, i ^ k) for i in range(4)])
+    pieces = [returned.T]
+    for k, chunk in enumerate(chunks, 1):
+        pieces.append(lax.ppermute(chunk, "section", [(i, i ^ k) for i in range(4)]))
 
     edge = jnp.full((1,), -1, jnp.int32)
     near_utt = lax.dynamic_slice(jnp.concatenate([edge, block_utt, edge]), (first_block,), (blocks + 2,))
@@ -462,7 +464,7 @@
     normed_own, normed_other = halves(core, normed_t)
     normed_peer = swap(normed_other, "core")
 
-    arrived, grad_conv = conv_gradient(section, chunks, weight_out, slope)
+    arrived, grad_conv = conv_gradient(section, pieces, weight_out, slope)
     normed_own, normed_other, grad_conv = lax.optimization_barrier((normed_own, normed_other, grad_conv))
     conv_inner, conv_outer = halos(grad_conv)
     arrived_rows, grad_conv = lax.optimization_barrier((arrived, grad_conv))

time: 111 us -> 111 us (level)
  no operation moved by 1% of the time
where the time goes in v8:
time: 111 us; the launch traced here: 110 us
  starting transfers between devices  41.8 us (38%)
  Pallas kernels  32 us (29%)
  waiting for transfers between devices  21.7 us (20%)
  matrix products  5.58 us (5%)
  other arithmetic  4.37 us (4%)
  local copies, waits for them, and re-layouts  3.28 us (3%)
    ppermute x6, starting transfers between devices, shares_of(): lax.ppermute(value, axis, [(i, i ^ k) for i in range(4)])  10.5 us
    ppermute x9, waiting for transfers between devices, swap(): return lax.ppermute(value, axis, [(0, 1), (1, 0)])  9.41 us
    all_to_all x1, starting transfers between devices, body(): got = lax.all_to_all(parts.reshape(16, 40, 3 * width), PLANE, 0, 0)  9.01 us
    ppermute x9, starting transfers between devices, swap(): return lax.ppermute(value, axis, [(0, 1), (1, 0)])  8.12 us
    ppermute x3, starting transfers between devices, body(): lax.ppermute(chunk, 'section', [(i, i ^ k) for i in range(4)])  7.63 us
    all_to_all x1, waiting for transfers between devices, body(): got = lax.all_to_all(parts.reshape(16, 40, 3 * width), PLANE, 0, 0)  5.76 us
    pallas_call x2, Pallas kernels, pair_product(): pl.pallas_call(functools.partial(pair_kernel, first), in_specs=[vmem()] *...  5.22 us
    pallas_call x1, Pallas kernels, norm_back(): pl.pallas_call(final_kernel, grid=(count // BLOCK,), in_specs=[block, blo...  5.13 us
  transfers between devices with their start and end apart: 24, of which 8 were waited for; matrix products, arithmetic and copies ran while one was open for 11% of the time, Pallas kernels for 24%

profile of v8, /device:TPU:0, one launch (start us, length us, event | category | flops | bytes accessed | tf_op | source)
XLA Modules:
  0.0 109.9 jit_solution(7702589804553715299)
XLA Ops:
  0.7 0.0 copy-start
  0.7 2.1 %frame_chunks.1 = (bf16[320,512]{1,0:T(8,128)(2,1)}, bf16[320,512]{1,0:T(8,128)(2,1)}, bf16[320,512]{1,0:T(8,128)(2,1)}) custom-call(s32[1]{0:T(128)} %bitcast.2.section, bf16[320,2048]{1,0:T(8,128)(2,1)} %bitcast.43), custom_call_target="tpu_custom_call" | custom-call | flops 2300000000 | tf_op jit(solution)/shard_map/frame_chunks/pallas_call | solution.py:332
  2.8 2.1 %collective-permute-start = (bf16[16,1280]{1,0:T(8,128)(2,1)S(1)}, bf16[16,1280]{1,0:T(8,128)(2,1)S(1)}, u32[]{:S(2)}, u32[]{:S(2)}) collective-permute-start(bf16[16,1280]{1,0:T(8,128)(2,1)S(1)} %get-tuple-element.98), channel_id=1, source_target_pairs={{0,1},{1,0},{2,3},{3,2},{8,9},{9,8},{10,11},{11,10},{16,17},{17,16... | collective-permute-start | bytes 122888 | tf_op jit(solution)/shard_map/ppermute | solution.py:48
  4.9 0.7 collective-permute-start.1
  5.6 4.9 %collective-permute-start.2 = (bf16[320,512]{1,0:T(8,128)(2,1)}, bf16[320,512]{1,0:T(8,128)(2,1)S(1)}, u32[]{:S(2)}, u32[]{:S(2)}) collective-permute-start(bf16[320,512]{1,0:T(8,128)(2,1)} %get-tuple-element.57), channel_id=1, source_target_pairs={{0,1},{1,0},{2,3},{3,2},{4,5},{5,4},{6,7},{7,6},{8,9},{9,8},{10,11... | collective-permute-start | bytes 983048 | tf_op jit(solution)/shard_map/ppermute | solution.py:445
  10.4 0.5 collective-permute-start.3
  10.9 2.3 %collective-permute-start.4 = (bf16[320,512]{1,0:T(8,128)(2,1)}, bf16[320,512]{1,0:T(8,128)(2,1)}, u32[]{:S(2)}, u32[]{:S(2)}) collective-permute-start(bf16[320,512]{1,0:T(8,128)(2,1)} %get-tuple-element.59), channel_id=1, source_target_pairs={{0,3},{1,2},{2,1},{3,0},{4,7},{5,6},{6,5},{7,4},{8,11},{9,10},{10,... | collective-permute-start | bytes 983048 | tf_op jit(solution)/shard_map/ppermute | solution.py:445
  13.2 0.1 pad_add_fusion
  13.3 0.1 dynamic_slice.14
  13.4 0.1 fusion.16
  13.4 0.1 dynamic_slice.13
  13.5 0.1 compare_convert_fusion
  13.6 0.1 pad_add_fusion.4.place
  13.7 0.1 pad_add_fusion.5.same
  13.7 0.1 slice.64.fill
  13.8 0.1 slice.65
  13.9 1.8 %layer_norm.1 = (bf16[544,1280]{1,0:T(8,128)(2,1)S(1)}, bf16[1280,512]{1,0:T(8,128)(2,1)S(1)}) custom-call(s32[3]{0:T(128)S(1)} %pad_add_fusion.4.place, bf16[512,1280]{1,0:T(8,128)(2,1)S(1)} %copy-done, bf16[16,1280]{1,0:T(8,128)(2,1)S(1)} %collective-permute-done.inner, bf16[16,1280]{1,0:T(8,128)(2,1)S(1)} %collective-permute-done.1.outer, ...), custom_call_target="tpu_custom_call" | custom-call | flops 4024999936 | tf_op jit(solution)/shard_map/layer_norm/pallas_call | solution.py:315
  15.7 0.1 copy-done.11
  15.8 1.3 %add_divide_fusion.gate = f32[544,640]{1,0:T(8,128)S(1)} fusion(bf16[544,1280]{1,0:T(8,128)(2,1)S(1)} %get-tuple-element.60, bf16[2,1280,640]{2,1,0:T(8,128)(2,1)S(1)} %copy-done.11), kind=kOutput, calls=%fused_computation.13 | convolution fusion | flops 892334080 | bytes 4423680 | tf_op jit(solution)/shard_map/dot_general | solution.py:458
  17.2 1.3 %select_convert_fusion = (bf16[544,640]{1,0:T(8,128)(2,1)S(1)}, f32[544,640]{1,0:T(8,128)S(1)}) fusion(f32[544,640]{1,0:T(8,128)S(1)} %add_divide_fusion.gate, pred[544]{0:T(1024)(128)(4,1)S(1)} %slice.65, bf16[544,1280]{1,0:T(8,128)(2,1)S(1)} %get-tuple-element.60, bf16[2,1280,640]{2,1,0:T(8,128)(2,1)S(1)} %copy-done.11), kind=kOutput, calls=%fused_computation.12 | convolution fusion | flops 892334080 | bytes 6513664 | tf_op jit(solution)/shard_map/dot_general | solution.py:457
  18.5 0.0 copy-start.4
  18.5 4.7 %conv_forward.1 = (bf16[512,640]{1,0:T(8,128)(2,1)}, f32[512,640]{1,0:T(8,128)}) custom-call(s32[6]{0:T(128)S(1)} %pad_add_fusion.5.same, s32[4]{0:T(128)S(1)} %slice.64.fill, bf16[544,640]{1,0:T(8,128)(2,1)S(1)} %get-tuple-element.99.units, f32[31,640]{1,0:T(8,128)S(1)} %copy-done.3), custom_call_target="tpu_custom_call" | custom-call | flops 5750000128 | tf_op jit(solution)/shard_map/conv_forward/pallas_call | solution.py:268
  23.2 0.3 collective-permute-start.7
  23.5 2.1 %core_halves.2 = (bf16[640,512]{1,0:T(8,128)(2,1)}, bf16[640,512]{1,0:T(8,128)(2,1)}) custom-call(s32[1]{0:T(128)} %bitcast.core, bf16[1280,512]{1,0:T(8,128)(2,1)S(1)} %get-tuple-element.54.rows, bf16[160,160]{1,0:T(8,128)(2,1)S(1)} %copy-done.4), custom_call_target="tpu_custom_call" | custom-call | flops 1380000000 | tf_op jit(solution)/shard_map/core_halves/pallas_call | solution.py:369
  25.5 0.4 collective-permute-done.3.second
  26.0 3.8 %collective-permute-done.4.third = bf16[320,512]{1,0:T(8,128)(2,1)} collective-permute-done((bf16[320,512]{1,0:T(8,128)(2,1)}, bf16[320,512]{1,0:T(8,128)(2,1)}, u32[]{:S(2)}, u32[]{:S(2)}) %collective-permute-start.4) | collective-permute-done | bytes 327712 | tf_op jit(solution)/shard_map/ppermute | solution.py:445
  29.7 2.6 %conv_gradient.1 = (bf16[1280,512]{1,0:T(8,128)(2,1)S(1)}, f32[512,640]{1,0:T(8,128)S(1)}) custom-call(s32[1]{0:T(128)} %bitcast.2.section, bf16[320,2048]{1,0:T(8,128)(2,1)} %bitcast.44, bf16[320,512]{1,0:T(8,128)(2,1)} %copy-done.13, bf16[320,512]{1,0:T(8,128)(2,1)} %copy-done.14, bf16[320,512]{1,0:T(8,128)(2,1)} %collective-permute-done.4.third, ...), custom_call_target="tpu_custom_call" | custom-call | flops 3449999872 | tf_op jit(solution)/shard_map/conv_gradient/pallas_call | solution.py:346
  32.3 1.2 %core_halves.3 = (bf16[640,512]{1,0:T(8,128)(2,1)S(1)}, bf16[640,512]{1,0:T(8,128)(2,1)}) custom-call(s32[1]{0:T(128)} %bitcast.core, bf16[1280,512]{1,0:T(8,128)(2,1)S(1)} %get-tuple-element.64.arrived, bf16[160,160]{1,0:T(8,128)(2,1)S(1)} %copy-done.4), custom_call_target="tpu_custom_call" | custom-call | flops 1380000000 | tf_op jit(solution)/shard_map/core_halves/pallas_call | solution.py:369
  33.5 0.1 copy-done.5
  33.6 0.1 collective-permute-start.6
  33.8 0.1 collective-permute-start.8
  33.9 0.7 collective-permute-start.9
  34.6 1.4 %collective-permute-done.6.left_peer = bf16[640,512]{1,0:T(8,128)(2,1)S(1)} collective-permute-done((bf16[640,512]{1,0:T(8,128)(2,1)}, bf16[640,512]{1,0:T(8,128)(2,1)S(1)}, u32[]{:S(2)}, u32[]{:S(2)}) %collective-permute-start.6) | collective-permute-done | bytes 655392 | tf_op jit(solution)/shard_map/ppermute | solution.py:38
  36.0 2.1 %weight_gradient.2.refs_0_ = bf16[640,1920]{1,0:T(8,128)(2,1)} custom-call(bf16[640,512]{1,0:T(8,128)(2,1)S(1)} %get-tuple-element.68.left, bf16[640,512]{1,0:T(8,128)(2,1)S(1)} %collective-permute-done.6.left_peer, bf16[1,512,640]{2,1,0:T(8,128)(2,1)S(1)} %bitcast.39, bf16[1,512,640]{2,1,0:T(8,128)(2,1)S(1)} %bitcast.40), custom_call_target="tpu_custom_call" | custom-call | flops 3910000128 | tf_op jit(solution)/shard_map/weight_gradient/pallas_call | solution.py:405
  38.1 3.7 %conv_backward.1.right = bf16[2,512,640]{2,1,0:T(8,128)(2,1)S(1)} custom-call(s32[6]{0:T(128)S(1)} %pad_add_fusion.5.same, s32[4]{0:T(128)S(1)} %slice.64.fill, f32[512,640]{1,0:T(8,128)S(1)} %get-tuple-element.65, f32[16,640]{1,0:T(8,128)S(1)} %collective-permute-done.8.inner, f32[16,640]{1,0:T(8,128)S(1)} %collective-permute-done.9.outer, ...), custom_call_target="tpu_custom_call" | custom-call | flops 6440000000 | tf_op jit(solution)/shard_map/conv_backward/pallas_call | solution.py:301
  41.8 2.8 %collective-permute-start.10 = (bf16[2,512,640]{2,1,0:T(8,128)(2,1)S(1)}, bf16[2,512,640]{2,1,0:T(8,128)(2,1)S(1)}, u32[]{:S(2)}, u32[]{:S(2)}) collective-permute-start(bf16[2,512,640]{2,1,0:T(8,128)(2,1)S(1)} %conv_backward.1.right), channel_id=1, source_target_pairs={{0,8},{8,0},{1,9},{9,1},{2,10},{10,2},{3,11},{11,3},{4,12},{12,4},... | collective-permute-start | bytes 3932168 | tf_op jit(solution)/shard_map/ppermute | solution.py:38
  44.6 0.1 collective-permute-start.5
  44.7 2.9 %fusion.sent = bf16[512,1280]{1,0:T(8,128)(2,1)} fusion(bf16[2,512,640]{2,1,0:T(8,128)(2,1)S(1)} %conv_backward.1.right, bf16[2,1280,640]{2,1,0:T(8,128)(2,1)S(1)} %copy-done.11), kind=kOutput, calls=%fused_computation.2 | convolution fusion | flops 1678376960 | bytes 5898240 | tf_op jit(solution)/shard_map/dot_general | solution.py:481
  47.6 3.0 %collective-permute-start.15 = (bf16[512,1280]{1,0:T(8,128)(2,1)}, bf16[512,1280]{1,0:T(8,128)(2,1)}, u32[]{:S(2)}, u32[]{:S(2)}) collective-permute-start(bf16[512,1280]{1,0:T(8,128)(2,1)} %fusion.sent), channel_id=1, source_target_pairs={{0,4},{4,0},{1,5},{5,1},{2,6},{6,2},{3,7},{7,3},{8,12},{12,8},{9,1... | collective-permute-start | bytes 3932168 | tf_op jit(solution)/shard_map/ppermute | solution.py:38
  50.7 3.1 %weight_gradient.3 = bf16[640,1920]{1,0:T(8,128)(2,1)} custom-call(bf16[640,512]{1,0:T(8,128)(2,1)S(1)} %copy-done.6, bf16[640,512]{1,0:T(8,128)(2,1)S(1)} %collective-permute-done.5.left_peer, bf16[2,512,640]{2,1,0:T(8,128)(2,1)S(1)} %conv_backward.1.right, ...), custom_call_target="tpu_custom_call", output_to_operand_aliasing={{}: (4, {})} | custom-call | flops 3910000128 | tf_op jit(solution)/shard_map/weight_gradient/pallas_call | solution.py:405
  53.8 9.0 %all-to-all-start = ((bf16[16,40,1920]{2,1,0:T(8,128)(2,1)}), bf16[16,40,1920]{2,1,0:T(8,128)(2,1)}, u32[]{:S(2)}, u32[]{:S(2)}) async-start(bf16[16,40,1920]{2,1,0:T(8,128)(2,1)} %bitcast.41), calls=%async_computation | async-start | bytes 4915200 | tf_op jit(solution)/shard_map/all_to_all | solution.py:485
  62.8 3.6 %tap_gradients.1 = f32[32,640]{1,0:T(8,128)S(1)} custom-call(s32[6]{0:T(128)S(1)} %pad_add_fusion.5.same, bf16[544,640]{1,0:T(8,128)(2,1)S(1)} %get-tuple-element.99.units, f32[512,640]{1,0:T(8,128)S(1)} %get-tuple-element.65), custom_call_target="tpu_custom_call" | custom-call | flops 4600000000 | tf_op jit(solution)/shard_map/tap_gradients/pallas_call | solution.py:287
  66.4 1.7 %multiply_reduce_fusion = f32[1280]{0:T(1024)S(1)} fusion(bf16[512,1280]{1,0:T(8,128)(2,1)} %fusion.sent, bf16[544,1280]{1,0:T(8,128)(2,1)S(1)} %get-tuple-element.60), kind=kLoop, calls=%fused_computation.3 | loop fusion | flops 2620160 | bytes 2626560 | tf_op jit(solution)/shard_map/reduce_sum | solution.py:490
  68.2 0.1 collective-permute-start.11
  68.3 1.3 %collective-permute-done.11 = f32[34,640]{1,0:T(8,128)S(1)} collective-permute-done((f32[34,640]{1,0:T(8,128)S(1)}, f32[34,640]{1,0:T(8,128)S(1)}, u32[]{:S(2)}, u32[]{:S(2)}) %collective-permute-start.11) | collective-permute-done | bytes 87072 | tf_op jit(solution)/shard_map/ppermute | solution.py:38
  69.6 0.1 collective-permute-start.12
  69.7 1.5 %collective-permute-start.13 = (f32[2,640]{1,0:T(2,128)S(1)}, f32[2,640]{1,0:T(2,128)S(1)}, u32[]{:S(2)}, u32[]{:S(2)}) collective-permute-start(f32[2,640]{1,0:T(2,128)S(1)} %slice.80), channel_id=1, source_target_pairs={{0,4},{4,0},{1,5},{5,1},{2,6},{6,2},{3,7},{7,3},{8,12},{12,8},{9,1... | collective-permute-start | bytes 15368 | tf_op jit(solution)/shard_map/ppermute | solution.py:38
  71.3 3.1 %collective-permute-start.14 = (f32[2,640]{1,0:T(2,128)S(1)}, f32[2,640]{1,0:T(2,128)S(1)}, u32[]{:S(2)}, u32[]{:S(2)}) collective-permute-start(f32[2,640]{1,0:T(2,128)S(1)} %slice.80), channel_id=1, source_target_pairs={{0,68},{4,64},{64,4},{68,0},{1,69},{5,65},{65,5},{69,1},{2,70},{6,... | collective-permute-start | bytes 15368 | tf_op jit(solution)/shard_map/ppermute | solution.py:494
  74.4 6.7 %collective-permute-done.15.other = bf16[512,1280]{1,0:T(8,128)(2,1)} collective-permute-done((bf16[512,1280]{1,0:T(8,128)(2,1)}, bf16[512,1280]{1,0:T(8,128)(2,1)}, u32[]{:S(2)}, u32[]{:S(2)}) %collective-permute-start.15) | collective-permute-done | bytes 1310752 | tf_op jit(solution)/shard_map/ppermute | solution.py:38
  81.1 5.1 %norm_backward.1 = bf16[512,1280]{1,0:T(8,128)(2,1)} custom-call(bf16[512,1280]{1,0:T(8,128)(2,1)} %fusion.sent, bf16[512,1280]{1,0:T(8,128)(2,1)} %collective-permute-done.15.other, bf16[512,1280]{1,0:T(8,128)(2,1)} %frames.1, bf16[1280,512]{1,0:T(8,128)(2,1)} %copy-done.5, f32[1,1280]{1,0:T(1,128)S(1)} %reshape.44.gain), custom_call_target="tpu_custom_call" | custom-call | flops 11960000512 | tf_op jit(solution)/shard_map/norm_backward/pallas_call | solution.py:384
  86.3 2.7 %collective-permute-start.16 = (bf16[34,640]{1,0:T(8,128)(2,1)S(1)}, bf16[34,640]{1,0:T(8,128)(2,1)S(1)}, u32[]{:S(2)}, u32[]{:S(2)}) collective-permute-start(bf16[34,640]{1,0:T(8,128)(2,1)S(1)} %pad_maximum_fusion.1), channel_id=1, source_target_pairs={{0,16},{16,0},{32,48},{48,32},{1,17},{17,1},{33,49},{49,33},{2,18}... | collective-permute-start | bytes 130568 | tf_op jit(solution)/shard_map/ppermute | solution.py:419
  89.0 2.9 %collective-permute-start.17 = (bf16[34,640]{1,0:T(8,128)(2,1)S(1)}, bf16[34,640]{1,0:T(8,128)(2,1)S(1)}, u32[]{:S(2)}, u32[]{:S(2)}) collective-permute-start(bf16[34,640]{1,0:T(8,128)(2,1)S(1)} %pad_maximum_fusion.1), channel_id=1, source_target_pairs={{0,32},{16,48},{32,0},{48,16},{1,33},{17,49},{33,1},{49,17},{2,34}... | collective-permute-start | bytes 130568 | tf_op jit(solution)/shard_map/ppermute | solution.py:419
  92.0 5.8 %all-to-all-done = bf16[16,40,1920]{2,1,0:T(8,128)(2,1)} async-done(((bf16[16,40,1920]{2,1,0:T(8,128)(2,1)}), bf16[16,40,1920]{2,1,0:T(8,128)(2,1)}, u32[]{:S(2)}, u32[]{:S(2)}) %all-to-all-start) | async-done | bytes 2457632 | tf_op jit(solution)/shard_map/all_to_all | solution.py:485
  97.7 2.1 %convert_reduce_fusion = f32[40,1920]{1,0:T(8,128)S(1)} fusion(bf16[16,40,1920]{2,1,0:T(8,128)(2,1)} %all-to-all-done), kind=kLoop, calls=%fused_computation | loop fusion | flops 2380800 | bytes 2764800 | tf_op jit(solution)/shard_map/reduce_sum | solution.py:502
  99.9 0.1 collective-permute-start.19
  100.0 0.7 collective-permute-start.20
  100.7 2.5 %collective-permute-start.21 = (bf16[34,640]{1,0:T(8,128)(2,1)S(1)}, bf16[34,640]{1,0:T(8,128)(2,1)S(1)}, u32[]{:S(2)}, u32[]{:S(2)}) collective-permute-start(bf16[34,640]{1,0:T(8,128)(2,1)S(1)} %add_convert_fusion), channel_id=1, source_target_pairs={{0,2},{1,3},{2,0},{3,1},{4,6},{5,7},{6,4},{7,5},{8,10},{9,11},{10,... | collective-permute-start | bytes 130568 | tf_op jit(solution)/shard_map/ppermute | solution.py:419
  103.3 1.6 %collective-permute-start.22 = (bf16[34,640]{1,0:T(8,128)(2,1)S(1)}, bf16[34,640]{1,0:T(8,128)(2,1)S(1)}, u32[]{:S(2)}, u32[]{:S(2)}) collective-permute-start(bf16[34,640]{1,0:T(8,128)(2,1)S(1)} %add_convert_fusion), channel_id=1, source_target_pairs={{0,3},{1,2},{2,1},{3,0},{4,7},{5,6},{6,5},{7,4},{8,11},{9,10},{10,... | collective-permute-start | bytes 130568 | tf_op jit(solution)/shard_map/ppermute | solution.py:419
  104.9 0.6 slice_bitcast_fusion
  105.5 0.7 reshape.48
  106.2 0.2 collective-permute-done.21
  106.4 2.2 %collective-permute-done.22 = bf16[34,640]{1,0:T(8,128)(2,1)S(1)} collective-permute-done((bf16[34,640]{1,0:T(8,128)(2,1)S(1)}, bf16[34,640]{1,0:T(8,128)(2,1)S(1)}, u32[]{:S(2)}, u32[]{:S(2)}) %collective-permute-start.22) | collective-permute-done | bytes 43552 | tf_op jit(solution)/shard_map/ppermute | solution.py:419
  108.6 0.6 slice.83
  109.3 0.6 reshape.49
  (61 shorter events, 0.4 us)
Async XLA Ops:
  0.7 2.2 %copy-start = (bf16[512,1280]{1,0:T(8,128)(2,1)S(1)}, bf16[512,1280]{1,0:T(8,128)(2,1)}, u32[]{:S(2)}) copy-start(bf16[512,1280]{1,0:T(8,128)(2,1)} %frames.1) | copy-start | bytes 3932164
  0.7 12.5 %copy-start.9 = (s32[256]{0:T(256)S(1)}, s32[256]{0:T(256)}, u32[]{:S(2)}) copy-start(s32[256]{0:T(256)} %param.17) | copy-start | bytes 3076
  0.7 12.5 %copy-start.10 = (s32[256]{0:T(256)S(1)}, s32[256]{0:T(256)}, u32[]{:S(2)}) copy-start(s32[256]{0:T(256)} %param.16) | copy-start | bytes 3076
  0.7 13.1 %copy-start.8 = (f32[1280]{0:T(1024)S(1)}, f32[1280]{0:T(1024)}, u32[]{:S(2)}) copy-start(f32[1280]{0:T(1024)} %param.12) | copy-start | bytes 15364
  2.8 11.1 %collective-permute-start = (bf16[16,1280]{1,0:T(8,128)(2,1)S(1)}, bf16[16,1280]{1,0:T(8,128)(2,1)S(1)}, u32[]{:S(2)}, u32[]{:S(2)}) collective-permute-start(bf16[16,1280]{1,0:T(8,128)(2,1)S(1)} %get-tuple-element.98), channel_id=1, source_target_pairs={{0,1},{1,0},{2,3},{3,2},{8,9},{9,8},{10,11},{11,10},{16,17},{17,16... | collective-permute-start | bytes 122888 | tf_op jit(solution)/shard_map/ppermute | solution.py:48
  4.9 9.0 %collective-permute-start.1 = (bf16[16,1280]{1,0:T(8,128)(2,1)S(1)}, bf16[16,1280]{1,0:T(8,128)(2,1)S(1)}, u32[]{:S(2)}, u32[]{:S(2)}) collective-permute-start(bf16[16,1280]{1,0:T(8,128)(2,1)S(1)} %get-tuple-element.97), channel_id=1, source_target_pairs={{1,2},{3,8},{9,10},{11,16},{17,18},{19,24},{25,26},{27,32},{33,34}... | collective-permute-start | bytes 122888 | tf_op jit(solution)/shard_map/ppermute | solution.py:49
  5.6 20.0 %collective-permute-start.2 = (bf16[320,512]{1,0:T(8,128)(2,1)}, bf16[320,512]{1,0:T(8,128)(2,1)S(1)}, u32[]{:S(2)}, u32[]{:S(2)}) collective-permute-start(bf16[320,512]{1,0:T(8,128)(2,1)} %get-tuple-element.57), channel_id=1, source_target_pairs={{0,1},{1,0},{2,3},{3,2},{4,5},{5,4},{6,7},{7,6},{8,9},{9,8},{10,11... | collective-permute-start | bytes 983048 | tf_op jit(solution)/shard_map/ppermute | solution.py:445
  10.4 15.5 %collective-permute-start.3 = (bf16[320,512]{1,0:T(8,128)(2,1)}, bf16[320,512]{1,0:T(8,128)(2,1)S(1)}, u32[]{:S(2)}, u32[]{:S(2)}) collective-permute-start(bf16[320,512]{1,0:T(8,128)(2,1)} %get-tuple-element.58), channel_id=1, source_target_pairs={{0,2},{1,3},{2,0},{3,1},{4,6},{5,7},{6,4},{7,5},{8,10},{9,11},{10,... | collective-permute-start | bytes 983048 | tf_op jit(solution)/shard_map/ppermute | solution.py:445
  10.9 18.8 %collective-permute-start.4 = (bf16[320,512]{1,0:T(8,128)(2,1)}, bf16[320,512]{1,0:T(8,128)(2,1)}, u32[]{:S(2)}, u32[]{:S(2)}) collective-permute-start(bf16[320,512]{1,0:T(8,128)(2,1)} %get-tuple-element.59), channel_id=1, source_target_pairs={{0,3},{1,2},{2,1},{3,0},{4,7},{5,6},{6,5},{7,4},{8,11},{9,10},{10,... | collective-permute-start | bytes 983048 | tf_op jit(solution)/shard_map/ppermute | solution.py:445
  13.9 1.9 %copy-start.11 = (bf16[2,1280,640]{2,1,0:T(8,128)(2,1)S(1)}, bf16[2,1280,640]{2,1,0:T(8,128)(2,1)}, u32[]{:S(2)}) copy-start(bf16[2,1280,640]{2,1,0:T(8,128)(2,1)} %param.13) | copy-start | bytes 9830404
  17.2 1.3 %copy-start.3 = (f32[31,640]{1,0:T(8,128)S(1)}, f32[31,640]{1,0:T(8,128)}, u32[]{:S(2)}) copy-start(f32[31,640]{1,0:T(8,128)} %taps.3) | copy-start | bytes 238084
  18.5 5.0 %copy-start.4 = (bf16[160,160]{1,0:T(8,128)(2,1)S(1)}, bf16[160,160]{1,0:T(8,128)(2,1)}, u32[]{:S(2)}) copy-start(bf16[160,160]{1,0:T(8,128)(2,1)} %constant.73.clone.order) | copy-start | bytes 153604
  23.2 11.4 %collective-permute-start.7 = (bf16[512,640]{1,0:T(8,128)(2,1)}, bf16[512,640]{1,0:T(8,128)(2,1)S(1)}, u32[]{:S(2)}, u32[]{:S(2)}) collective-permute-start(bf16[512,640]{1,0:T(8,128)(2,1)} %get-tuple-element.70), channel_id=1, source_target_pairs={{0,8},{8,0},{1,9},{9,1},{2,10},{10,2},{3,11},{11,3},{4,12},{12,4},... | collective-permute-start | bytes 1966088 | tf_op jit(solution)/shard_map/ppermute | solution.py:38
  23.5 6.3 %copy-start.1 = (bf16[640,1280]{1,0:T(8,128)(2,1)S(1)}, bf16[640,1280]{1,0:T(8,128)(2,1)}, u32[]{:S(2)}) copy-start(bf16[640,1280]{1,0:T(8,128)(2,1)} %weights.1) | copy-start | bytes 4915204
  23.5 6.3 %copy-start.7 = (f32[512,640]{1,0:T(8,128)S(1)}, f32[512,640]{1,0:T(8,128)}, u32[]{:S(2)}) copy-start(f32[512,640]{1,0:T(8,128)} %get-tuple-element.61.slope) | copy-start | bytes 3932164
  25.5 4.2 %copy-start.13 = (bf16[320,512]{1,0:T(8,128)(2,1)}, bf16[320,512]{1,0:T(8,128)(2,1)S(1)}, u32[]{:S(2)}) copy-start(bf16[320,512]{1,0:T(8,128)(2,1)S(1)} %collective-permute-done.2.first) | copy-start | bytes 983044
  25.9 3.8 %copy-start.14 = (bf16[320,512]{1,0:T(8,128)(2,1)}, bf16[320,512]{1,0:T(8,128)(2,1)S(1)}, u32[]{:S(2)}) copy-start(bf16[320,512]{1,0:T(8,128)(2,1)S(1)} %collective-permute-done.3.second) | copy-start | bytes 983044
  32.3 1.3 %copy-start.5 = (bf16[1280,512]{1,0:T(8,128)(2,1)}, bf16[1280,512]{1,0:T(8,128)(2,1)S(1)}, u32[]{:S(2)}) copy-start(bf16[1280,512]{1,0:T(8,128)(2,1)S(1)} %get-tuple-element.64.arrived) | copy-start | bytes 3932164
  32.3 3.6 %copy-start.2 = (bf16[512,640]{1,0:T(8,128)(2,1)S(1)}, bf16[512,640]{1,0:T(8,128)(2,1)}, u32[]{:S(2)}) copy-start(bf16[512,640]{1,0:T(8,128)(2,1)} %get-tuple-element.70) | copy-start | bytes 1966084
  33.6 2.3 %collective-permute-start.6 = (bf16[640,512]{1,0:T(8,128)(2,1)}, bf16[640,512]{1,0:T(8,128)(2,1)S(1)}, u32[]{:S(2)}, u32[]{:S(2)}) collective-permute-start(bf16[640,512]{1,0:T(8,128)(2,1)} %get-tuple-element.69), channel_id=1, source_target_pairs={{0,8},{8,0},{1,9},{9,1},{2,10},{10,2},{3,11},{11,3},{4,12},{12,4},... | collective-permute-start | bytes 1966088 | tf_op jit(solution)/shard_map/ppermute | solution.py:38
  33.8 4.3 %collective-permute-start.8 = (f32[16,640]{1,0:T(8,128)S(1)}, f32[16,640]{1,0:T(8,128)S(1)}, u32[]{:S(2)}, u32[]{:S(2)}) collective-permute-start(f32[16,640]{1,0:T(8,128)S(1)} %get-tuple-element.96), channel_id=1, source_target_pairs={{0,1},{1,0},{2,3},{3,2},{8,9},{9,8},{10,11},{11,10},{16,17},{17,16... | collective-permute-start | bytes 122888 | tf_op jit(solution)/shard_map/ppermute | solution.py:48
  33.9 4.2 %collective-permute-start.9 = (f32[16,640]{1,0:T(8,128)S(1)}, f32[16,640]{1,0:T(8,128)S(1)}, u32[]{:S(2)}, u32[]{:S(2)}) collective-permute-start(f32[16,640]{1,0:T(8,128)S(1)} %get-tuple-element.95), channel_id=1, source_target_pairs={{1,2},{3,8},{9,10},{11,16},{17,18},{19,24},{25,26},{27,32},{33,34}... | collective-permute-start | bytes 122888 | tf_op jit(solution)/shard_map/ppermute | solution.py:49
  38.1 6.5 %copy-start.12 = (bf16[640,512]{1,0:T(8,128)(2,1)S(1)}, bf16[640,512]{1,0:T(8,128)(2,1)}, u32[]{:S(2)}) copy-start(bf16[640,512]{1,0:T(8,128)(2,1)} %get-tuple-element.56) | copy-start | bytes 1966084
  41.8 8.9 %copy-start.6 = (bf16[640,512]{1,0:T(8,128)(2,1)S(1)}, bf16[640,512]{1,0:T(8,128)(2,1)}, u32[]{:S(2)}) copy-start(bf16[640,512]{1,0:T(8,128)(2,1)} %get-tuple-element.63.left) | copy-start | bytes 1966084
  41.8 8.9 %collective-permute-start.10 = (bf16[2,512,640]{2,1,0:T(8,128)(2,1)S(1)}, bf16[2,512,640]{2,1,0:T(8,128)(2,1)S(1)}, u32[]{:S(2)}, u32[]{:S(2)}) collective-permute-start(bf16[2,512,640]{2,1,0:T(8,128)(2,1)S(1)} %conv_backward.1.right), channel_id=1, source_target_pairs={{0,8},{8,0},{1,9},{9,1},{2,10},{10,2},{3,11},{11,3},{4,12},{12,4},... | collective-permute-start | bytes 3932168 | tf_op jit(solution)/shard_map/ppermute | solution.py:38
  44.6 6.1 %collective-permute-start.5 = (bf16[640,512]{1,0:T(8,128)(2,1)S(1)}, bf16[640,512]{1,0:T(8,128)(2,1)S(1)}, u32[]{:S(2)}, u32[]{:S(2)}) collective-permute-start(bf16[640,512]{1,0:T(8,128)(2,1)S(1)} %copy-done.12), channel_id=1, source_target_pairs={{0,8},{8,0},{1,9},{9,1},{2,10},{10,2},{3,11},{11,3},{4,12},{12,4},... | collective-permute-start | bytes 1966088 | tf_op jit(solution)/shard_map/ppermute | solution.py:38
  47.6 33.4 %collective-permute-start.15 = (bf16[512,1280]{1,0:T(8,128)(2,1)}, bf16[512,1280]{1,0:T(8,128)(2,1)}, u32[]{:S(2)}, u32[]{:S(2)}) collective-permute-start(bf16[512,1280]{1,0:T(8,128)(2,1)} %fusion.sent), channel_id=1, source_target_pairs={{0,4},{4,0},{1,5},{5,1},{2,6},{6,2},{3,7},{7,3},{8,12},{12,8},{9,1... | collective-permute-start | bytes 3932168 | tf_op jit(solution)/shard_map/ppermute | solution.py:38
  53.8 43.9 %all-to-all-start = ((bf16[16,40,1920]{2,1,0:T(8,128)(2,1)}), bf16[16,40,1920]{2,1,0:T(8,128)(2,1)}, u32[]{:S(2)}, u32[]{:S(2)}) async-start(bf16[16,40,1920]{2,1,0:T(8,128)(2,1)} %bitcast.41), calls=%async_computation | async-start | bytes 4915200 | tf_op jit(solution)/shard_map/all_to_all | solution.py:485
  68.2 1.4 %collective-permute-start.11 = (f32[34,640]{1,0:T(8,128)S(1)}, f32[34,640]{1,0:T(8,128)S(1)}, u32[]{:S(2)}, u32[]{:S(2)}) collective-permute-start(f32[34,640]{1,0:T(8,128)S(1)} %pad_maximum_fusion), channel_id=1, source_target_pairs={{0,8},{8,0},{1,9},{9,1},{2,10},{10,2},{3,11},{11,3},{4,12},{12,4},... | collective-permute-start | bytes 261128 | tf_op jit(solution)/shard_map/ppermute | solution.py:38
  69.6 16.6 %collective-permute-start.12 = (f32[34,640]{1,0:T(8,128)S(1)}, f32[34,640]{1,0:T(8,128)S(1)}, u32[]{:S(2)}, u32[]{:S(2)}) collective-permute-start(f32[34,640]{1,0:T(8,128)S(1)} %fusion.17), channel_id=1, source_target_pairs={{0,64},{64,0},{1,65},{65,1},{2,66},{66,2},{3,67},{67,3},{4,68},{68... | collective-permute-start | bytes 261128 | tf_op jit(solution)/shard_map/ppermute | solution.py:38
  69.7 16.5 %collective-permute-start.13 = (f32[2,640]{1,0:T(2,128)S(1)}, f32[2,640]{1,0:T(2,128)S(1)}, u32[]{:S(2)}, u32[]{:S(2)}) collective-permute-start(f32[2,640]{1,0:T(2,128)S(1)} %slice.80), channel_id=1, source_target_pairs={{0,4},{4,0},{1,5},{5,1},{2,6},{6,2},{3,7},{7,3},{8,12},{12,8},{9,1... | collective-permute-start | bytes 15368 | tf_op jit(solution)/shard_map/ppermute | solution.py:38
  71.3 15.0 %collective-permute-start.14 = (f32[2,640]{1,0:T(2,128)S(1)}, f32[2,640]{1,0:T(2,128)S(1)}, u32[]{:S(2)}, u32[]{:S(2)}) collective-permute-start(f32[2,640]{1,0:T(2,128)S(1)} %slice.80), channel_id=1, source_target_pairs={{0,68},{4,64},{64,4},{68,0},{1,69},{5,65},{65,5},{69,1},{2,70},{6,... | collective-permute-start | bytes 15368 | tf_op jit(solution)/shard_map/ppermute | solution.py:494
  86.3 13.5 %collective-permute-start.16 = (bf16[34,640]{1,0:T(8,128)(2,1)S(1)}, bf16[34,640]{1,0:T(8,128)(2,1)S(1)}, u32[]{:S(2)}, u32[]{:S(2)}) collective-permute-start(bf16[34,640]{1,0:T(8,128)(2,1)S(1)} %pad_maximum_fusion.1), channel_id=1, source_target_pairs={{0,16},{16,0},{32,48},{48,32},{1,17},{17,1},{33,49},{49,33},{2,18}... | collective-permute-start | bytes 130568 | tf_op jit(solution)/shard_map/ppermute | solution.py:419
  89.0 10.8 %collective-permute-start.17 = (bf16[34,640]{1,0:T(8,128)(2,1)S(1)}, bf16[34,640]{1,0:T(8,128)(2,1)S(1)}, u32[]{:S(2)}, u32[]{:S(2)}) collective-permute-start(bf16[34,640]{1,0:T(8,128)(2,1)S(1)} %pad_maximum_fusion.1), channel_id=1, source_target_pairs={{0,32},{16,48},{32,0},{48,16},{1,33},{17,49},{33,1},{49,17},{2,34}... | collective-permute-start | bytes 130568 | tf_op jit(solution)/shard_map/ppermute | solution.py:419
  92.0 7.9 %collective-permute-start.18 = (bf16[34,640]{1,0:T(8,128)(2,1)S(1)}, bf16[34,640]{1,0:T(8,128)(2,1)S(1)}, u32[]{:S(2)}, u32[]{:S(2)}) collective-permute-start(bf16[34,640]{1,0:T(8,128)(2,1)S(1)} %pad_maximum_fusion.1), channel_id=1, source_target_pairs={{0,48},{16,32},{32,16},{48,0},{1,49},{17,33},{33,17},{49,1},{2,50}... | collective-permute-start | bytes 130568 | tf_op jit(solution)/shard_map/ppermute | solution.py:419
  99.9 4.9 %collective-permute-start.19 = (bf16[20,1920]{1,0:T(8,128)(2,1)S(1)}, bf16[20,1920]{1,0:T(8,128)(2,1)S(1)}, u32[]{:S(2)}, u32[]{:S(2)}) collective-permute-start(bf16[20,1920]{1,0:T(8,128)(2,1)S(1)} %fusion.15), channel_id=1, source_target_pairs={{0,64},{64,0},{1,65},{65,1},{2,66},{66,2},{3,67},{67,3},{4,68},{68... | collective-permute-start | bytes 230408 | tf_op jit(solution)/shard_map/ppermute | solution.py:38
  100.0 6.2 %collective-permute-start.20 = (bf16[34,640]{1,0:T(8,128)(2,1)S(1)}, bf16[34,640]{1,0:T(8,128)(2,1)S(1)}, u32[]{:S(2)}, u32[]{:S(2)}) collective-permute-start(bf16[34,640]{1,0:T(8,128)(2,1)S(1)} %add_convert_fusion), channel_id=1, source_target_pairs={{0,1},{1,0},{2,3},{3,2},{4,5},{5,4},{6,7},{7,6},{8,9},{9,8},{10,11... | collective-permute-start | bytes 130568 | tf_op jit(solution)/shard_map/ppermute | solution.py:419
  100.7 5.6 %collective-permute-start.21 = (bf16[34,640]{1,0:T(8,128)(2,1)S(1)}, bf16[34,640]{1,0:T(8,128)(2,1)S(1)}, u32[]{:S(2)}, u32[]{:S(2)}) collective-permute-start(bf16[34,640]{1,0:T(8,128)(2,1)S(1)} %add_convert_fusion), channel_id=1, source_target_pairs={{0,2},{1,3},{2,0},{3,1},{4,6},{5,7},{6,4},{7,5},{8,10},{9,11},{10,... | collective-permute-start | bytes 130568 | tf_op jit(solution)/shard_map/ppermute | solution.py:419
  103.3 5.3 %collective-permute-start.22 = (bf16[34,640]{1,0:T(8,128)(2,1)S(1)}, bf16[34,640]{1,0:T(8,128)(2,1)S(1)}, u32[]{:S(2)}, u32[]{:S(2)}) collective-permute-start(bf16[34,640]{1,0:T(8,128)(2,1)S(1)} %add_convert_fusion), channel_id=1, source_target_pairs={{0,3},{1,2},{2,1},{3,0},{4,7},{5,6},{6,5},{7,4},{8,11},{9,10},{10,... | collective-permute-start | bytes 130568 | tf_op jit(solution)/shard_map/ppermute | solution.py:419

commit v9 on v8

--- a/solution.py
+++ b/solution.py
@@ -466,7 +466,7 @@
 
     arrived, grad_conv = conv_gradient(section, pieces, weight_out, slope)
     normed_own, normed_other, grad_conv = lax.optimization_barrier((normed_own, normed_other, grad_conv))
-    conv_inner, conv_outer = halos(grad_conv)
+    conv_inner, conv_outer = halos(grad_conv.astype(BF16))
     arrived_rows, grad_conv = lax.optimization_barrier((arrived, grad_conv))
     rows_own, rows_other = halves(core, arrived_rows, keep=True)
     rows_peer = swap(rows_other, "core")

time: 111 us -> 111 us (level)
  no operation moved by 1% of the time
where the time goes in v9:
time: 111 us; the launch traced here: 110 us
  starting transfers between devices  41.7 us (38%)
  Pallas kernels  32 us (29%)
  waiting for transfers between devices  21.8 us (20%)
  matrix products  5.59 us (5%)
  other arithmetic  4.44 us (4%)
  local copies, waits for them, and re-layouts  3.16 us (3%)
  between operations  1.12 us (1%)
    ppermute x6, starting transfers between devices, shares_of(): lax.ppermute(value, axis, [(i, i ^ k) for i in range(4)])  10.4 us
    ppermute x9, waiting for transfers between devices, swap(): return lax.ppermute(value, axis, [(0, 1), (1, 0)])  9.33 us
    all_to_all x1, starting transfers between devices, body(): got = lax.all_to_all(parts.reshape(16, 40, 3 * width), PLANE, 0, 0)  9.02 us
    ppermute x9, starting transfers between devices, swap(): return lax.ppermute(value, axis, [(0, 1), (1, 0)])  8.07 us
    ppermute x3, starting transfers between devices, body(): lax.ppermute(chunk, 'section', [(i, i ^ k) for i in range(4)])  7.63 us
    all_to_all x1, waiting for transfers between devices, body(): got = lax.all_to_all(parts.reshape(16, 40, 3 * width), PLANE, 0, 0)  5.85 us
    pallas_call x2, Pallas kernels, pair_product(): pl.pallas_call(functools.partial(pair_kernel, first), in_specs=[vmem()] *...  5.22 us
    pallas_call x1, Pallas kernels, norm_back(): pl.pallas_call(final_kernel, grid=(count // BLOCK,), in_specs=[block, blo...  5.13 us
  transfers between devices with their start and end apart: 24, of which 8 were waited for; matrix products, arithmetic and copies ran while one was open for 11% of the time, Pallas kernels for 24%

profile of v9, /device:TPU:0, one launch (start us, length us, event | category | flops | bytes accessed | tf_op | source)
XLA Modules:
  0.0 109.8 jit_solution(1457079130835877184)
XLA Ops:
  0.7 0.0 copy-start
  0.7 2.1 %frame_chunks.1 = (bf16[320,512]{1,0:T(8,128)(2,1)}, bf16[320,512]{1,0:T(8,128)(2,1)}, bf16[320,512]{1,0:T(8,128)(2,1)}) custom-call(s32[1]{0:T(128)} %bitcast.2.section, bf16[320,2048]{1,0:T(8,128)(2,1)} %bitcast.43), custom_call_target="tpu_custom_call" | custom-call | flops 2300000000 | tf_op jit(solution)/shard_map/frame_chunks/pallas_call | solution.py:332
  2.8 2.1 %collective-permute-start = (bf16[16,1280]{1,0:T(8,128)(2,1)S(1)}, bf16[16,1280]{1,0:T(8,128)(2,1)S(1)}, u32[]{:S(2)}, u32[]{:S(2)}) collective-permute-start(bf16[16,1280]{1,0:T(8,128)(2,1)S(1)} %get-tuple-element.96), channel_id=1, source_target_pairs={{0,1},{1,0},{2,3},{3,2},{8,9},{9,8},{10,11},{11,10},{16,17},{17,16... | collective-permute-start | bytes 122888 | tf_op jit(solution)/shard_map/ppermute | solution.py:48
  4.9 0.7 collective-permute-start.1
  5.6 4.9 %collective-permute-start.2 = (bf16[320,512]{1,0:T(8,128)(2,1)}, bf16[320,512]{1,0:T(8,128)(2,1)S(1)}, u32[]{:S(2)}, u32[]{:S(2)}) collective-permute-start(bf16[320,512]{1,0:T(8,128)(2,1)} %get-tuple-element.57), channel_id=1, source_target_pairs={{0,1},{1,0},{2,3},{3,2},{4,5},{5,4},{6,7},{7,6},{8,9},{9,8},{10,11... | collective-permute-start | bytes 983048 | tf_op jit(solution)/shard_map/ppermute | solution.py:445
  10.4 0.5 collective-permute-start.3
  10.9 2.3 %collective-permute-start.4 = (bf16[320,512]{1,0:T(8,128)(2,1)}, bf16[320,512]{1,0:T(8,128)(2,1)}, u32[]{:S(2)}, u32[]{:S(2)}) collective-permute-start(bf16[320,512]{1,0:T(8,128)(2,1)} %get-tuple-element.59), channel_id=1, source_target_pairs={{0,3},{1,2},{2,1},{3,0},{4,7},{5,6},{6,5},{7,4},{8,11},{9,10},{10,... | collective-permute-start | bytes 983048 | tf_op jit(solution)/shard_map/ppermute | solution.py:445
  13.2 0.1 pad_add_fusion
  13.3 0.1 dynamic_slice.14
  13.4 0.1 fusion.16
  13.4 0.1 dynamic_slice.13
  13.5 0.1 compare_convert_fusion
  13.6 0.1 pad_add_fusion.4.place
  13.7 0.1 pad_add_fusion.5.same
  13.7 0.1 slice.64.fill
  13.8 0.1 slice.65
  13.9 1.8 %layer_norm.1 = (bf16[544,1280]{1,0:T(8,128)(2,1)S(1)}, bf16[1280,512]{1,0:T(8,128)(2,1)S(1)}) custom-call(s32[3]{0:T(128)S(1)} %pad_add_fusion.4.place, bf16[512,1280]{1,0:T(8,128)(2,1)S(1)} %copy-done, bf16[16,1280]{1,0:T(8,128)(2,1)S(1)} %collective-permute-done.inner, bf16[16,1280]{1,0:T(8,128)(2,1)S(1)} %collective-permute-done.1.outer, ...), custom_call_target="tpu_custom_call" | custom-call | flops 4024999936 | tf_op jit(solution)/shard_map/layer_norm/pallas_call | solution.py:315
  15.7 0.1 copy-done.11
  15.8 1.3 %add_divide_fusion.gate = f32[544,640]{1,0:T(8,128)S(1)} fusion(bf16[544,1280]{1,0:T(8,128)(2,1)S(1)} %get-tuple-element.60, bf16[2,1280,640]{2,1,0:T(8,128)(2,1)S(1)} %copy-done.11), kind=kOutput, calls=%fused_computation.13 | convolution fusion | flops 892334080 | bytes 4423680 | tf_op jit(solution)/shard_map/dot_general | solution.py:458
  17.2 1.3 %select_convert_fusion = (bf16[544,640]{1,0:T(8,128)(2,1)S(1)}, f32[544,640]{1,0:T(8,128)S(1)}) fusion(f32[544,640]{1,0:T(8,128)S(1)} %add_divide_fusion.gate, pred[544]{0:T(1024)(128)(4,1)S(1)} %slice.65, bf16[544,1280]{1,0:T(8,128)(2,1)S(1)} %get-tuple-element.60, bf16[2,1280,640]{2,1,0:T(8,128)(2,1)S(1)} %copy-done.11), kind=kOutput, calls=%fused_computation.12 | convolution fusion | flops 892334080 | bytes 6513664 | tf_op jit(solution)/shard_map/dot_general | solution.py:457
  18.5 0.0 copy-start.4
  18.5 4.7 %conv_forward.1 = (bf16[512,640]{1,0:T(8,128)(2,1)}, f32[512,640]{1,0:T(8,128)}) custom-call(s32[6]{0:T(128)S(1)} %pad_add_fusion.5.same, s32[4]{0:T(128)S(1)} %slice.64.fill, bf16[544,640]{1,0:T(8,128)(2,1)S(1)} %get-tuple-element.99.units, f32[31,640]{1,0:T(8,128)S(1)} %copy-done.3), custom_call_target="tpu_custom_call" | custom-call | flops 5750000128 | tf_op jit(solution)/shard_map/conv_forward/pallas_call | solution.py:268
  23.2 0.3 collective-permute-start.7
  23.5 2.1 %core_halves.2 = (bf16[640,512]{1,0:T(8,128)(2,1)}, bf16[640,512]{1,0:T(8,128)(2,1)}) custom-call(s32[1]{0:T(128)} %bitcast.core, bf16[1280,512]{1,0:T(8,128)(2,1)S(1)} %get-tuple-element.54.rows, bf16[160,160]{1,0:T(8,128)(2,1)S(1)} %copy-done.4), custom_call_target="tpu_custom_call" | custom-call | flops 1380000000 | tf_op jit(solution)/shard_map/core_halves/pallas_call | solution.py:369
  25.5 0.4 collective-permute-done.3.second
  26.0 3.8 %collective-permute-done.4.third = bf16[320,512]{1,0:T(8,128)(2,1)} collective-permute-done((bf16[320,512]{1,0:T(8,128)(2,1)}, bf16[320,512]{1,0:T(8,128)(2,1)}, u32[]{:S(2)}, u32[]{:S(2)}) %collective-permute-start.4) | collective-permute-done | bytes 327712 | tf_op jit(solution)/shard_map/ppermute | solution.py:445
  29.7 2.6 %conv_gradient.1 = (bf16[1280,512]{1,0:T(8,128)(2,1)S(1)}, f32[512,640]{1,0:T(8,128)S(1)}) custom-call(s32[1]{0:T(128)} %bitcast.2.section, bf16[320,2048]{1,0:T(8,128)(2,1)} %bitcast.44, bf16[320,512]{1,0:T(8,128)(2,1)} %copy-done.13, bf16[320,512]{1,0:T(8,128)(2,1)} %copy-done.14, bf16[320,512]{1,0:T(8,128)(2,1)} %collective-permute-done.4.third, ...), custom_call_target="tpu_custom_call" | custom-call | flops 3449999872 | tf_op jit(solution)/shard_map/conv_gradient/pallas_call | solution.py:346
  32.3 1.3 %core_halves.3 = (bf16[640,512]{1,0:T(8,128)(2,1)S(1)}, bf16[640,512]{1,0:T(8,128)(2,1)}) custom-call(s32[1]{0:T(128)} %bitcast.core, bf16[1280,512]{1,0:T(8,128)(2,1)S(1)} %get-tuple-element.64.arrived, bf16[160,160]{1,0:T(8,128)(2,1)S(1)} %copy-done.4), custom_call_target="tpu_custom_call" | custom-call | flops 1380000000 | tf_op jit(solution)/shard_map/core_halves/pallas_call | solution.py:369
  33.6 0.2 collective-permute-start.6
  33.8 0.1 convert_element_type.60
  33.9 0.1 collective-permute-start.8
  34.0 0.7 collective-permute-start.9
  34.7 1.3 %collective-permute-done.6.left_peer = bf16[640,512]{1,0:T(8,128)(2,1)S(1)} collective-permute-done((bf16[640,512]{1,0:T(8,128)(2,1)}, bf16[640,512]{1,0:T(8,128)(2,1)S(1)}, u32[]{:S(2)}, u32[]{:S(2)}) %collective-permute-start.6) | collective-permute-done | bytes 655392 | tf_op jit(solution)/shard_map/ppermute | solution.py:38
  36.0 2.1 %weight_gradient.2.refs_0_ = bf16[640,1920]{1,0:T(8,128)(2,1)} custom-call(bf16[640,512]{1,0:T(8,128)(2,1)S(1)} %get-tuple-element.68.left, bf16[640,512]{1,0:T(8,128)(2,1)S(1)} %collective-permute-done.6.left_peer, bf16[1,512,640]{2,1,0:T(8,128)(2,1)S(1)} %bitcast.39, bf16[1,512,640]{2,1,0:T(8,128)(2,1)S(1)} %bitcast.40), custom_call_target="tpu_custom_call" | custom-call | flops 3910000128 | tf_op jit(solution)/shard_map/weight_gradient/pallas_call | solution.py:405
  38.1 3.7 %conv_backward.1.right = bf16[2,512,640]{2,1,0:T(8,128)(2,1)S(1)} custom-call(s32[6]{0:T(128)S(1)} %pad_add_fusion.5.same, s32[4]{0:T(128)S(1)} %slice.64.fill, f32[512,640]{1,0:T(8,128)S(1)} %get-tuple-element.65, bf16[16,640]{1,0:T(8,128)(2,1)S(1)} %collective-permute-done.8.inner, bf16[16,640]{1,0:T(8,128)(2,1)S(1)} %collective-permute-done.9.outer, ...), custom_call_target="tpu_custom_call" | custom-call | flops 6440000000 | tf_op jit(solution)/shard_map/conv_backward/pallas_call | solution.py:301
  41.8 2.7 %collective-permute-start.10 = (bf16[2,512,640]{2,1,0:T(8,128)(2,1)S(1)}, bf16[2,512,640]{2,1,0:T(8,128)(2,1)S(1)}, u32[]{:S(2)}, u32[]{:S(2)}) collective-permute-start(bf16[2,512,640]{2,1,0:T(8,128)(2,1)S(1)} %conv_backward.1.right), channel_id=1, source_target_pairs={{0,8},{8,0},{1,9},{9,1},{2,10},{10,2},{3,11},{11,3},{4,12},{12,4},... | collective-permute-start | bytes 3932168 | tf_op jit(solution)/shard_map/ppermute | solution.py:38
  44.5 0.1 collective-permute-start.5
  44.6 3.0 %fusion.sent = bf16[512,1280]{1,0:T(8,128)(2,1)} fusion(bf16[2,512,640]{2,1,0:T(8,128)(2,1)S(1)} %conv_backward.1.right, bf16[2,1280,640]{2,1,0:T(8,128)(2,1)S(1)} %copy-done.11), kind=kOutput, calls=%fused_computation.2 | convolution fusion | flops 1678376960 | bytes 5898240 | tf_op jit(solution)/shard_map/dot_general | solution.py:481
  47.6 3.0 %collective-permute-start.15 = (bf16[512,1280]{1,0:T(8,128)(2,1)}, bf16[512,1280]{1,0:T(8,128)(2,1)}, u32[]{:S(2)}, u32[]{:S(2)}) collective-permute-start(bf16[512,1280]{1,0:T(8,128)(2,1)} %fusion.sent), channel_id=1, source_target_pairs={{0,4},{4,0},{1,5},{5,1},{2,6},{6,2},{3,7},{7,3},{8,12},{12,8},{9,1... | collective-permute-start | bytes 3932168 | tf_op jit(solution)/shard_map/ppermute | solution.py:38
  50.6 3.1 %weight_gradient.3 = bf16[640,1920]{1,0:T(8,128)(2,1)} custom-call(bf16[640,512]{1,0:T(8,128)(2,1)S(1)} %copy-done.6, bf16[640,512]{1,0:T(8,128)(2,1)S(1)} %collective-permute-done.5.left_peer, bf16[2,512,640]{2,1,0:T(8,128)(2,1)S(1)} %conv_backward.1.right, ...), custom_call_target="tpu_custom_call", output_to_operand_aliasing={{}: (4, {})} | custom-call | flops 3910000128 | tf_op jit(solution)/shard_map/weight_gradient/pallas_call | solution.py:405
  53.7 9.0 %all-to-all-start = ((bf16[16,40,1920]{2,1,0:T(8,128)(2,1)}), bf16[16,40,1920]{2,1,0:T(8,128)(2,1)}, u32[]{:S(2)}, u32[]{:S(2)}) async-start(bf16[16,40,1920]{2,1,0:T(8,128)(2,1)} %bitcast.41), calls=%async_computation | async-start | bytes 4915200 | tf_op jit(solution)/shard_map/all_to_all | solution.py:485
  62.8 3.6 %tap_gradients.1 = f32[32,640]{1,0:T(8,128)S(1)} custom-call(s32[6]{0:T(128)S(1)} %pad_add_fusion.5.same, bf16[544,640]{1,0:T(8,128)(2,1)S(1)} %get-tuple-element.99.units, f32[512,640]{1,0:T(8,128)S(1)} %get-tuple-element.65), custom_call_target="tpu_custom_call" | custom-call | flops 4600000000 | tf_op jit(solution)/shard_map/tap_gradients/pallas_call | solution.py:287
  66.3 1.7 %multiply_reduce_fusion = f32[1280]{0:T(1024)S(1)} fusion(bf16[512,1280]{1,0:T(8,128)(2,1)} %fusion.sent, bf16[544,1280]{1,0:T(8,128)(2,1)S(1)} %get-tuple-element.60), kind=kLoop, calls=%fused_computation.3 | loop fusion | flops 2620160 | bytes 2626560 | tf_op jit(solution)/shard_map/reduce_sum | solution.py:490
  68.1 0.1 collective-permute-start.11
  68.2 1.3 %collective-permute-done.11 = f32[34,640]{1,0:T(8,128)S(1)} collective-permute-done((f32[34,640]{1,0:T(8,128)S(1)}, f32[34,640]{1,0:T(8,128)S(1)}, u32[]{:S(2)}, u32[]{:S(2)}) %collective-permute-start.11) | collective-permute-done | bytes 87072 | tf_op jit(solution)/shard_map/ppermute | solution.py:38
  69.5 0.1 collective-permute-start.12
  69.6 1.6 %collective-permute-start.13 = (f32[2,640]{1,0:T(2,128)S(1)}, f32[2,640]{1,0:T(2,128)S(1)}, u32[]{:S(2)}, u32[]{:S(2)}) collective-permute-start(f32[2,640]{1,0:T(2,128)S(1)} %slice.82), channel_id=1, source_target_pairs={{0,4},{4,0},{1,5},{5,1},{2,6},{6,2},{3,7},{7,3},{8,12},{12,8},{9,1... | collective-permute-start | bytes 15368 | tf_op jit(solution)/shard_map/ppermute | solution.py:38
  71.2 3.1 %collective-permute-start.14 = (f32[2,640]{1,0:T(2,128)S(1)}, f32[2,640]{1,0:T(2,128)S(1)}, u32[]{:S(2)}, u32[]{:S(2)}) collective-permute-start(f32[2,640]{1,0:T(2,128)S(1)} %slice.82), channel_id=1, source_target_pairs={{0,68},{4,64},{64,4},{68,0},{1,69},{5,65},{65,5},{69,1},{2,70},{6,... | collective-permute-start | bytes 15368 | tf_op jit(solution)/shard_map/ppermute | solution.py:494
  74.3 6.7 %collective-permute-done.15.other = bf16[512,1280]{1,0:T(8,128)(2,1)} collective-permute-done((bf16[512,1280]{1,0:T(8,128)(2,1)}, bf16[512,1280]{1,0:T(8,128)(2,1)}, u32[]{:S(2)}, u32[]{:S(2)}) %collective-permute-start.15) | collective-permute-done | bytes 1310752 | tf_op jit(solution)/shard_map/ppermute | solution.py:38
  81.0 5.1 %norm_backward.1 = bf16[512,1280]{1,0:T(8,128)(2,1)} custom-call(bf16[512,1280]{1,0:T(8,128)(2,1)} %fusion.sent, bf16[512,1280]{1,0:T(8,128)(2,1)} %collective-permute-done.15.other, bf16[512,1280]{1,0:T(8,128)(2,1)} %frames.1, bf16[1280,512]{1,0:T(8,128)(2,1)} %copy-done.5, f32[1,1280]{1,0:T(1,128)S(1)} %reshape.44.gain), custom_call_target="tpu_custom_call" | custom-call | flops 11960000512 | tf_op jit(solution)/shard_map/norm_backward/pallas_call | solution.py:384
  86.2 2.6 %collective-permute-start.16 = (bf16[34,640]{1,0:T(8,128)(2,1)S(1)}, bf16[34,640]{1,0:T(8,128)(2,1)S(1)}, u32[]{:S(2)}, u32[]{:S(2)}) collective-permute-start(bf16[34,640]{1,0:T(8,128)(2,1)S(1)} %pad_maximum_fusion.1), channel_id=1, source_target_pairs={{0,16},{16,0},{32,48},{48,32},{1,17},{17,1},{33,49},{49,33},{2,18}... | collective-permute-start | bytes 130568 | tf_op jit(solution)/shard_map/ppermute | solution.py:419
  88.8 3.0 %collective-permute-start.17 = (bf16[34,640]{1,0:T(8,128)(2,1)S(1)}, bf16[34,640]{1,0:T(8,128)(2,1)S(1)}, u32[]{:S(2)}, u32[]{:S(2)}) collective-permute-start(bf16[34,640]{1,0:T(8,128)(2,1)S(1)} %pad_maximum_fusion.1), channel_id=1, source_target_pairs={{0,32},{16,48},{32,0},{48,16},{1,33},{17,49},{33,1},{49,17},{2,34}... | collective-permute-start | bytes 130568 | tf_op jit(solution)/shard_map/ppermute | solution.py:419
  91.8 5.8 %all-to-all-done = bf16[16,40,1920]{2,1,0:T(8,128)(2,1)} async-done(((bf16[16,40,1920]{2,1,0:T(8,128)(2,1)}), bf16[16,40,1920]{2,1,0:T(8,128)(2,1)}, u32[]{:S(2)}, u32[]{:S(2)}) %all-to-all-start) | async-done | bytes 2457632 | tf_op jit(solution)/shard_map/all_to_all | solution.py:485
  97.7 2.1 %convert_reduce_fusion = f32[40,1920]{1,0:T(8,128)S(1)} fusion(bf16[16,40,1920]{2,1,0:T(8,128)(2,1)} %all-to-all-done), kind=kLoop, calls=%fused_computation | loop fusion | flops 2380800 | bytes 2764800 | tf_op jit(solution)/shard_map/reduce_sum | solution.py:502
  99.8 0.1 collective-permute-start.19
  100.0 0.7 collective-permute-start.20
  100.7 2.5 %collective-permute-start.21 = (bf16[34,640]{1,0:T(8,128)(2,1)S(1)}, bf16[34,640]{1,0:T(8,128)(2,1)S(1)}, u32[]{:S(2)}, u32[]{:S(2)}) collective-permute-start(bf16[34,640]{1,0:T(8,128)(2,1)S(1)} %add_convert_fusion), channel_id=1, source_target_pairs={{0,2},{1,3},{2,0},{3,1},{4,6},{5,7},{6,4},{7,5},{8,10},{9,11},{10,... | collective-permute-start | bytes 130568 | tf_op jit(solution)/shard_map/ppermute | solution.py:419
  103.2 1.6 %collective-permute-start.22 = (bf16[34,640]{1,0:T(8,128)(2,1)S(1)}, bf16[34,640]{1,0:T(8,128)(2,1)S(1)}, u32[]{:S(2)}, u32[]{:S(2)}) collective-permute-start(bf16[34,640]{1,0:T(8,128)(2,1)S(1)} %add_convert_fusion), channel_id=1, source_target_pairs={{0,3},{1,2},{2,1},{3,0},{4,7},{5,6},{6,5},{7,4},{8,11},{9,10},{10,... | collective-permute-start | bytes 130568 | tf_op jit(solution)/shard_map/ppermute | solution.py:419
  104.8 0.6 slice_bitcast_fusion
  105.4 0.7 reshape.48
  106.1 0.2 collective-permute-done.21
  106.3 2.2 %collective-permute-done.22 = bf16[34,640]{1,0:T(8,128)(2,1)S(1)} collective-permute-done((bf16[34,640]{1,0:T(8,128)(2,1)S(1)}, bf16[34,640]{1,0:T(8,128)(2,1)S(1)}, u32[]{:S(2)}, u32[]{:S(2)}) %collective-permute-start.22) | collective-permute-done | bytes 43552 | tf_op jit(solution)/shard_map/ppermute | solution.py:419
  108.5 0.6 slice.85
  109.2 0.6 reshape.49
  (62 shorter events, 0.4 us)
Async XLA Ops:
  0.7 2.2 %copy-start = (bf16[512,1280]{1,0:T(8,128)(2,1)S(1)}, bf16[512,1280]{1,0:T(8,128)(2,1)}, u32[]{:S(2)}) copy-start(bf16[512,1280]{1,0:T(8,128)(2,1)} %frames.1) | copy-start | bytes 3932164
  0.7 12.5 %copy-start.9 = (s32[256]{0:T(256)S(1)}, s32[256]{0:T(256)}, u32[]{:S(2)}) copy-start(s32[256]{0:T(256)} %param.17) | copy-start | bytes 3076
  0.7 12.5 %copy-start.10 = (s32[256]{0:T(256)S(1)}, s32[256]{0:T(256)}, u32[]{:S(2)}) copy-start(s32[256]{0:T(256)} %param.16) | copy-start | bytes 3076
  0.7 13.1 %copy-start.8 = (f32[1280]{0:T(1024)S(1)}, f32[1280]{0:T(1024)}, u32[]{:S(2)}) copy-start(f32[1280]{0:T(1024)} %param.12) | copy-start | bytes 15364
  2.8 11.1 %collective-permute-start = (bf16[16,1280]{1,0:T(8,128)(2,1)S(1)}, bf16[16,1280]{1,0:T(8,128)(2,1)S(1)}, u32[]{:S(2)}, u32[]{:S(2)}) collective-permute-start(bf16[16,1280]{1,0:T(8,128)(2,1)S(1)} %get-tuple-element.96), channel_id=1, source_target_pairs={{0,1},{1,0},{2,3},{3,2},{8,9},{9,8},{10,11},{11,10},{16,17},{17,16... | collective-permute-start | bytes 122888 | tf_op jit(solution)/shard_map/ppermute | solution.py:48
  4.9 9.0 %collective-permute-start.1 = (bf16[16,1280]{1,0:T(8,128)(2,1)S(1)}, bf16[16,1280]{1,0:T(8,128)(2,1)S(1)}, u32[]{:S(2)}, u32[]{:S(2)}) collective-permute-start(bf16[16,1280]{1,0:T(8,128)(2,1)S(1)} %get-tuple-element.95), channel_id=1, source_target_pairs={{1,2},{3,8},{9,10},{11,16},{17,18},{19,24},{25,26},{27,32},{33,34}... | collective-permute-start | bytes 122888 | tf_op jit(solution)/shard_map/ppermute | solution.py:49
  5.6 20.0 %collective-permute-start.2 = (bf16[320,512]{1,0:T(8,128)(2,1)}, bf16[320,512]{1,0:T(8,128)(2,1)S(1)}, u32[]{:S(2)}, u32[]{:S(2)}) collective-permute-start(bf16[320,512]{1,0:T(8,128)(2,1)} %get-tuple-element.57), channel_id=1, source_target_pairs={{0,1},{1,0},{2,3},{3,2},{4,5},{5,4},{6,7},{7,6},{8,9},{9,8},{10,11... | collective-permute-start | bytes 983048 | tf_op jit(solution)/shard_map/ppermute | solution.py:445
  10.4 15.5 %collective-permute-start.3 = (bf16[320,512]{1,0:T(8,128)(2,1)}, bf16[320,512]{1,0:T(8,128)(2,1)S(1)}, u32[]{:S(2)}, u32[]{:S(2)}) collective-permute-start(bf16[320,512]{1,0:T(8,128)(2,1)} %get-tuple-element.58), channel_id=1, source_target_pairs={{0,2},{1,3},{2,0},{3,1},{4,6},{5,7},{6,4},{7,5},{8,10},{9,11},{10,... | collective-permute-start | bytes 983048 | tf_op jit(solution)/shard_map/ppermute | solution.py:445
  10.9 18.8 %collective-permute-start.4 = (bf16[320,512]{1,0:T(8,128)(2,1)}, bf16[320,512]{1,0:T(8,128)(2,1)}, u32[]{:S(2)}, u32[]{:S(2)}) collective-permute-start(bf16[320,512]{1,0:T(8,128)(2,1)} %get-tuple-element.59), channel_id=1, source_target_pairs={{0,3},{1,2},{2,1},{3,0},{4,7},{5,6},{6,5},{7,4},{8,11},{9,10},{10,... | collective-permute-start | bytes 983048 | tf_op jit(solution)/shard_map/ppermute | solution.py:445
  13.9 1.9 %copy-start.11 = (bf16[2,1280,640]{2,1,0:T(8,128)(2,1)S(1)}, bf16[2,1280,640]{2,1,0:T(8,128)(2,1)}, u32[]{:S(2)}) copy-start(bf16[2,1280,640]{2,1,0:T(8,128)(2,1)} %param.13) | copy-start | bytes 9830404
  17.2 1.3 %copy-start.3 = (f32[31,640]{1,0:T(8,128)S(1)}, f32[31,640]{1,0:T(8,128)}, u32[]{:S(2)}) copy-start(f32[31,640]{1,0:T(8,128)} %taps.3) | copy-start | bytes 238084
  18.5 5.0 %copy-start.4 = (bf16[160,160]{1,0:T(8,128)(2,1)S(1)}, bf16[160,160]{1,0:T(8,128)(2,1)}, u32[]{:S(2)}) copy-start(bf16[160,160]{1,0:T(8,128)(2,1)} %constant.73.clone.order) | copy-start | bytes 153604
  23.2 11.5 %collective-permute-start.7 = (bf16[512,640]{1,0:T(8,128)(2,1)}, bf16[512,640]{1,0:T(8,128)(2,1)S(1)}, u32[]{:S(2)}, u32[]{:S(2)}) collective-permute-start(bf16[512,640]{1,0:T(8,128)(2,1)} %get-tuple-element.70), channel_id=1, source_target_pairs={{0,8},{8,0},{1,9},{9,1},{2,10},{10,2},{3,11},{11,3},{4,12},{12,4},... | collective-permute-start | bytes 1966088 | tf_op jit(solution)/shard_map/ppermute | solution.py:38
  23.5 6.3 %copy-start.1 = (bf16[640,1280]{1,0:T(8,128)(2,1)S(1)}, bf16[640,1280]{1,0:T(8,128)(2,1)}, u32[]{:S(2)}) copy-start(bf16[640,1280]{1,0:T(8,128)(2,1)} %weights.1) | copy-start | bytes 4915204
  23.5 6.3 %copy-start.7 = (f32[512,640]{1,0:T(8,128)S(1)}, f32[512,640]{1,0:T(8,128)}, u32[]{:S(2)}) copy-start(f32[512,640]{1,0:T(8,128)} %get-tuple-element.61.slope) | copy-start | bytes 3932164
  25.5 4.2 %copy-start.13 = (bf16[320,512]{1,0:T(8,128)(2,1)}, bf16[320,512]{1,0:T(8,128)(2,1)S(1)}, u32[]{:S(2)}) copy-start(bf16[320,512]{1,0:T(8,128)(2,1)S(1)} %collective-permute-done.2.first) | copy-start | bytes 983044
  25.9 3.8 %copy-start.14 = (bf16[320,512]{1,0:T(8,128)(2,1)}, bf16[320,512]{1,0:T(8,128)(2,1)S(1)}, u32[]{:S(2)}) copy-start(bf16[320,512]{1,0:T(8,128)(2,1)S(1)} %collective-permute-done.3.second) | copy-start | bytes 983044
  32.3 1.3 %copy-start.5 = (bf16[1280,512]{1,0:T(8,128)(2,1)}, bf16[1280,512]{1,0:T(8,128)(2,1)S(1)}, u32[]{:S(2)}) copy-start(bf16[1280,512]{1,0:T(8,128)(2,1)S(1)} %get-tuple-element.64.arrived) | copy-start | bytes 3932164
  33.6 2.4 %copy-start.2 = (bf16[512,640]{1,0:T(8,128)(2,1)S(1)}, bf16[512,640]{1,0:T(8,128)(2,1)}, u32[]{:S(2)}) copy-start(bf16[512,640]{1,0:T(8,128)(2,1)} %get-tuple-element.70) | copy-start | bytes 1966084
  33.6 2.4 %collective-permute-start.6 = (bf16[640,512]{1,0:T(8,128)(2,1)}, bf16[640,512]{1,0:T(8,128)(2,1)S(1)}, u32[]{:S(2)}, u32[]{:S(2)}) collective-permute-start(bf16[640,512]{1,0:T(8,128)(2,1)} %get-tuple-element.69), channel_id=1, source_target_pairs={{0,8},{8,0},{1,9},{9,1},{2,10},{10,2},{3,11},{11,3},{4,12},{12,4},... | collective-permute-start | bytes 1966088 | tf_op jit(solution)/shard_map/ppermute | solution.py:38
  33.9 4.2 %collective-permute-start.8 = (bf16[16,640]{1,0:T(8,128)(2,1)S(1)}, bf16[16,640]{1,0:T(8,128)(2,1)S(1)}, u32[]{:S(2)}, u32[]{:S(2)}) collective-permute-start(bf16[16,640]{1,0:T(8,128)(2,1)S(1)} %get-tuple-element.98), channel_id=1, source_target_pairs={{0,1},{1,0},{2,3},{3,2},{8,9},{9,8},{10,11},{11,10},{16,17},{17,16... | collective-permute-start | bytes 61448 | tf_op jit(solution)/shard_map/ppermute | solution.py:48
  34.0 4.1 %collective-permute-start.9 = (bf16[16,640]{1,0:T(8,128)(2,1)S(1)}, bf16[16,640]{1,0:T(8,128)(2,1)S(1)}, u32[]{:S(2)}, u32[]{:S(2)}) collective-permute-start(bf16[16,640]{1,0:T(8,128)(2,1)S(1)} %get-tuple-element.97), channel_id=1, source_target_pairs={{1,2},{3,8},{9,10},{11,16},{17,18},{19,24},{25,26},{27,32},{33,34}... | collective-permute-start | bytes 61448 | tf_op jit(solution)/shard_map/ppermute | solution.py:49
  38.1 6.4 %copy-start.12 = (bf16[640,512]{1,0:T(8,128)(2,1)S(1)}, bf16[640,512]{1,0:T(8,128)(2,1)}, u32[]{:S(2)}) copy-start(bf16[640,512]{1,0:T(8,128)(2,1)} %get-tuple-element.56) | copy-start | bytes 1966084
  41.8 8.8 %copy-start.6 = (bf16[640,512]{1,0:T(8,128)(2,1)S(1)}, bf16[640,512]{1,0:T(8,128)(2,1)}, u32[]{:S(2)}) copy-start(bf16[640,512]{1,0:T(8,128)(2,1)} %get-tuple-element.63.left) | copy-start | bytes 1966084
  41.8 8.7 %collective-permute-start.10 = (bf16[2,512,640]{2,1,0:T(8,128)(2,1)S(1)}, bf16[2,512,640]{2,1,0:T(8,128)(2,1)S(1)}, u32[]{:S(2)}, u32[]{:S(2)}) collective-permute-start(bf16[2,512,640]{2,1,0:T(8,128)(2,1)S(1)} %conv_backward.1.right), channel_id=1, source_target_pairs={{0,8},{8,0},{1,9},{9,1},{2,10},{10,2},{3,11},{11,3},{4,12},{12,4},... | collective-permute-start | bytes 3932168 | tf_op jit(solution)/shard_map/ppermute | solution.py:38
  44.5 6.1 %collective-permute-start.5 = (bf16[640,512]{1,0:T(8,128)(2,1)S(1)}, bf16[640,512]{1,0:T(8,128)(2,1)S(1)}, u32[]{:S(2)}, u32[]{:S(2)}) collective-permute-start(bf16[640,512]{1,0:T(8,128)(2,1)S(1)} %copy-done.12), channel_id=1, source_target_pairs={{0,8},{8,0},{1,9},{9,1},{2,10},{10,2},{3,11},{11,3},{4,12},{12,4},... | collective-permute-start | bytes 1966088 | tf_op jit(solution)/shard_map/ppermute | solution.py:38
  47.6 33.4 %collective-permute-start.15 = (bf16[512,1280]{1,0:T(8,128)(2,1)}, bf16[512,1280]{1,0:T(8,128)(2,1)}, u32[]{:S(2)}, u32[]{:S(2)}) collective-permute-start(bf16[512,1280]{1,0:T(8,128)(2,1)} %fusion.sent), channel_id=1, source_target_pairs={{0,4},{4,0},{1,5},{5,1},{2,6},{6,2},{3,7},{7,3},{8,12},{12,8},{9,1... | collective-permute-start | bytes 3932168 | tf_op jit(solution)/shard_map/ppermute | solution.py:38
  53.7 43.9 %all-to-all-start = ((bf16[16,40,1920]{2,1,0:T(8,128)(2,1)}), bf16[16,40,1920]{2,1,0:T(8,128)(2,1)}, u32[]{:S(2)}, u32[]{:S(2)}) async-start(bf16[16,40,1920]{2,1,0:T(8,128)(2,1)} %bitcast.41), calls=%async_computation | async-start | bytes 4915200 | tf_op jit(solution)/shard_map/all_to_all | solution.py:485
  68.1 1.4 %collective-permute-start.11 = (f32[34,640]{1,0:T(8,128)S(1)}, f32[34,640]{1,0:T(8,128)S(1)}, u32[]{:S(2)}, u32[]{:S(2)}) collective-permute-start(f32[34,640]{1,0:T(8,128)S(1)} %pad_maximum_fusion), channel_id=1, source_target_pairs={{0,8},{8,0},{1,9},{9,1},{2,10},{10,2},{3,11},{11,3},{4,12},{12,4},... | collective-permute-start | bytes 261128 | tf_op jit(solution)/shard_map/ppermute | solution.py:38
  69.5 16.6 %collective-permute-start.12 = (f32[34,640]{1,0:T(8,128)S(1)}, f32[34,640]{1,0:T(8,128)S(1)}, u32[]{:S(2)}, u32[]{:S(2)}) collective-permute-start(f32[34,640]{1,0:T(8,128)S(1)} %fusion.17), channel_id=1, source_target_pairs={{0,64},{64,0},{1,65},{65,1},{2,66},{66,2},{3,67},{67,3},{4,68},{68... | collective-permute-start | bytes 261128 | tf_op jit(solution)/shard_map/ppermute | solution.py:38
  69.6 16.5 %collective-permute-start.13 = (f32[2,640]{1,0:T(2,128)S(1)}, f32[2,640]{1,0:T(2,128)S(1)}, u32[]{:S(2)}, u32[]{:S(2)}) collective-permute-start(f32[2,640]{1,0:T(2,128)S(1)} %slice.82), channel_id=1, source_target_pairs={{0,4},{4,0},{1,5},{5,1},{2,6},{6,2},{3,7},{7,3},{8,12},{12,8},{9,1... | collective-permute-start | bytes 15368 | tf_op jit(solution)/shard_map/ppermute | solution.py:38
  71.2 15.0 %collective-permute-start.14 = (f32[2,640]{1,0:T(2,128)S(1)}, f32[2,640]{1,0:T(2,128)S(1)}, u32[]{:S(2)}, u32[]{:S(2)}) collective-permute-start(f32[2,640]{1,0:T(2,128)S(1)} %slice.82), channel_id=1, source_target_pairs={{0,68},{4,64},{64,4},{68,0},{1,69},{5,65},{65,5},{69,1},{2,70},{6,... | collective-permute-start | bytes 15368 | tf_op jit(solution)/shard_map/ppermute | solution.py:494
  86.2 13.5 %collective-permute-start.16 = (bf16[34,640]{1,0:T(8,128)(2,1)S(1)}, bf16[34,640]{1,0:T(8,128)(2,1)S(1)}, u32[]{:S(2)}, u32[]{:S(2)}) collective-permute-start(bf16[34,640]{1,0:T(8,128)(2,1)S(1)} %pad_maximum_fusion.1), channel_id=1, source_target_pairs={{0,16},{16,0},{32,48},{48,32},{1,17},{17,1},{33,49},{49,33},{2,18}... | collective-permute-start | bytes 130568 | tf_op jit(solution)/shard_map/ppermute | solution.py:419
  88.8 10.9 %collective-permute-start.17 = (bf16[34,640]{1,0:T(8,128)(2,1)S(1)}, bf16[34,640]{1,0:T(8,128)(2,1)S(1)}, u32[]{:S(2)}, u32[]{:S(2)}) collective-permute-start(bf16[34,640]{1,0:T(8,128)(2,1)S(1)} %pad_maximum_fusion.1), channel_id=1, source_target_pairs={{0,32},{16,48},{32,0},{48,16},{1,33},{17,49},{33,1},{49,17},{2,34}... | collective-permute-start | bytes 130568 | tf_op jit(solution)/shard_map/ppermute | solution.py:419
  91.8 8.0 %collective-permute-start.18 = (bf16[34,640]{1,0:T(8,128)(2,1)S(1)}, bf16[34,640]{1,0:T(8,128)(2,1)S(1)}, u32[]{:S(2)}, u32[]{:S(2)}) collective-permute-start(bf16[34,640]{1,0:T(8,128)(2,1)S(1)} %pad_maximum_fusion.1), channel_id=1, source_target_pairs={{0,48},{16,32},{32,16},{48,0},{1,49},{17,33},{33,17},{49,1},{2,50}... | collective-permute-start | bytes 130568 | tf_op jit(solution)/shard_map/ppermute | solution.py:419
  99.8 4.9 %collective-permute-start.19 = (bf16[20,1920]{1,0:T(8,128)(2,1)S(1)}, bf16[20,1920]{1,0:T(8,128)(2,1)S(1)}, u32[]{:S(2)}, u32[]{:S(2)}) collective-permute-start(bf16[20,1920]{1,0:T(8,128)(2,1)S(1)} %fusion.15), channel_id=1, source_target_pairs={{0,64},{64,0},{1,65},{65,1},{2,66},{66,2},{3,67},{67,3},{4,68},{68... | collective-permute-start | bytes 230408 | tf_op jit(solution)/shard_map/ppermute | solution.py:38
  100.0 6.2 %collective-permute-start.20 = (bf16[34,640]{1,0:T(8,128)(2,1)S(1)}, bf16[34,640]{1,0:T(8,128)(2,1)S(1)}, u32[]{:S(2)}, u32[]{:S(2)}) collective-permute-start(bf16[34,640]{1,0:T(8,128)(2,1)S(1)} %add_convert_fusion), channel_id=1, source_target_pairs={{0,1},{1,0},{2,3},{3,2},{4,5},{5,4},{6,7},{7,6},{8,9},{9,8},{10,11... | collective-permute-start | bytes 130568 | tf_op jit(solution)/shard_map/ppermute | solution.py:419
  100.7 5.6 %collective-permute-start.21 = (bf16[34,640]{1,0:T(8,128)(2,1)S(1)}, bf16[34,640]{1,0:T(8,128)(2,1)S(1)}, u32[]{:S(2)}, u32[]{:S(2)}) collective-permute-start(bf16[34,640]{1,0:T(8,128)(2,1)S(1)} %add_convert_fusion), channel_id=1, source_target_pairs={{0,2},{1,3},{2,0},{3,1},{4,6},{5,7},{6,4},{7,5},{8,10},{9,11},{10,... | collective-permute-start | bytes 130568 | tf_op jit(solution)/shard_map/ppermute | solution.py:419
  103.2 5.3 %collective-permute-start.22 = (bf16[34,640]{1,0:T(8,128)(2,1)S(1)}, bf16[34,640]{1,0:T(8,128)(2,1)S(1)}, u32[]{:S(2)}, u32[]{:S(2)}) collective-permute-start(bf16[34,640]{1,0:T(8,128)(2,1)S(1)} %add_convert_fusion), channel_id=1, source_target_pairs={{0,3},{1,2},{2,1},{3,0},{4,7},{5,6},{6,5},{7,4},{8,11},{9,10},{10,... | collective-permute-start | bytes 130568 | tf_op jit(solution)/shard_map/ppermute | solution.py:419
